TPU v7x, 32 devices: a whole 2x2x4 slice. The times are simulated.
32 devices in a mesh: fsdp: 4 (over y, x), dp: 8 (over z, core).
Axes of the slice: x: 2, y: 2, z: 4, core: 2. Of those that a mesh axis runs over, the one named last changes fastest.
Arguments:
- tokens: bfloat16 [10240, 2048], P(('fsdp', 'dp')), may hold values from -6 to 6
- summaries: bfloat16 [32, 50, 2048], P(('fsdp', 'dp')), may hold values from -6 to 6
- presence: int32 [32, 50], P(('fsdp', 'dp')), may hold values 0 or 1
- seg_counts: int32 [8], replicated, may hold values from 1 to 8, 32 in all
- ln1_gain: bfloat16 [2048], P(('fsdp', 'dp')), may hold values from 0.5 to 1.5
- ln1_bias: bfloat16 [2048], P(('fsdp', 'dp')), may hold values from -1.1953125 to 1.1953125
- w_query: bfloat16 [2048, 2048], P(('fsdp', 'dp')), may hold values from -0.125 to 0.125
- query_bias: bfloat16 [2048], P(('fsdp', 'dp')), may hold values from -1.796875 to 1.796875
- w_key: bfloat16 [2048, 2048], P(('fsdp', 'dp')), may hold values from -0.125 to 0.125
- w_value: bfloat16 [2048, 2048], P(('fsdp', 'dp')), may hold values from -0.125 to 0.125
- value_bias: bfloat16 [2048], P(('fsdp', 'dp')), may hold values from -1.796875 to 1.796875
- w_out: bfloat16 [2048, 2048], P(('fsdp', 'dp')), may hold values from -0.375 to 0.375
- out_bias: bfloat16 [2048], P(('fsdp', 'dp')), may hold values from -1.796875 to 1.796875
- ln2_gain: bfloat16 [2048], P(('fsdp', 'dp')), may hold values from 0.5 to 1.5
- ln2_bias: bfloat16 [2048], P(('fsdp', 'dp')), may hold values from -1.1953125 to 1.1953125
- w_up: bfloat16 [2048, 8192], P(('fsdp', 'dp')), may hold values from -0.125 to 0.125
- up_bias: bfloat16 [8192], P(('fsdp', 'dp')), may hold values from -1.796875 to 1.796875
- w_down: bfloat16 [8192, 2048], P(('fsdp', 'dp')), may hold values from -0.0625 to 0.0625
- down_bias: bfloat16 [2048], P(('fsdp', 'dp')), may hold values from -1.796875 to 1.796875
- cotangent: bfloat16 [10240, 2048], P(('fsdp', 'dp')), may hold values from -6 to 6
Outputs:
- output: bfloat16 [10240, 2048], P(('fsdp', 'dp'))
- tokens_grad: float32 [10240, 2048], P(('fsdp', 'dp'))
- summaries_grad: float32 [32, 50, 2048], P(('fsdp', 'dp'))
- ln1_gain_grad: float32 [2048], P(('fsdp', 'dp'))
- ln1_bias_grad: float32 [2048], P(('fsdp', 'dp'))
- w_query_grad: float32 [2048, 2048], P(('fsdp', 'dp'))
- query_bias_grad: float32 [2048], P(('fsdp', 'dp'))
- w_key_grad: float32 [2048, 2048], P(('fsdp', 'dp'))
- w_value_grad: float32 [2048, 2048], P(('fsdp', 'dp'))
- value_bias_grad: float32 [2048], P(('fsdp', 'dp'))
- w_out_grad: float32 [2048, 2048], P(('fsdp', 'dp'))
- out_bias_grad: float32 [2048], P(('fsdp', 'dp'))
- ln2_gain_grad: float32 [2048], P(('fsdp', 'dp'))
- ln2_bias_grad: float32 [2048], P(('fsdp', 'dp'))
- w_up_grad: float32 [2048, 8192], P(('fsdp', 'dp'))
- up_bias_grad: float32 [8192], P(('fsdp', 'dp'))
- w_down_grad: float32 [8192, 2048], P(('fsdp', 'dp'))
- down_bias_grad: float32 [2048], P(('fsdp', 'dp'))
Inputs may be any that keep to these rules, and one draw needn't show every extreme that they name: `seg_counts`: the counts add up to 32; some item has exactly 8 segments.
All inputs are finite; a program needn't handle non-finite values. No bound on the sum of `presence` on one device may be relied on, other than what follows from the above.
Results may differ from a plain program's by a relative error of at most 0.013.
Values may be sent and summed in bfloat16 or wider, within the bound.
No kernel may reach another device: no remote copies, remote signals or barrier semaphores. Data moves between devices by JAX's collectives and lax.ppermute only.
A program may use at most 448 MiB of HBM per device.

v0:
```python
import jax
import jax.numpy as jnp
from jax import lax
from jax.sharding import PartitionSpec as P

HEADS = 32


def passed_along(value, axis, steps):
    count = lax.axis_size(axis)
    leading, last = (max(0, -steps), min(count, count - steps))
    return lax.ppermute(value, axis, [(source, source + steps) for source in range(leading, last)])


def norm_apply(values, norm_gain, norm_bias):
    centre = values - jnp.mean(values, axis=-1, keepdims=True)
    spread = jnp.mean(centre * centre, axis=-1, keepdims=True)
    return centre * lax.rsqrt(spread + 1e-05) * norm_gain + norm_bias


def contract_rows(left, right):
    return lax.dot_general(
        left, right, (((0,), (0,)), ((), ())), preferred_element_type=jnp.float32
    )


def contract_cols(left, right):
    return lax.dot_general(
        left, right, (((1,), (1,)), ((), ())), preferred_element_type=jnp.float32
    )


def fetch_attention(
    gain_first, bias_first, query_mat, query_off, key_mat, value_mat, value_off, out_mat, out_off
):
    return (
        lax.all_gather(gain_first, ("fsdp", "dp"), axis=0, tiled=True),
        lax.all_gather(bias_first, ("fsdp", "dp"), axis=0, tiled=True),
        lax.all_gather(query_mat, ("fsdp", "dp"), axis=0, tiled=True),
        lax.all_gather(query_off, ("fsdp", "dp"), axis=0, tiled=True),
        lax.all_gather(key_mat, ("fsdp", "dp"), axis=0, tiled=True),
        lax.all_gather(value_mat, ("fsdp", "dp"), axis=0, tiled=True),
        lax.all_gather(value_off, ("fsdp", "dp"), axis=0, tiled=True),
        lax.all_gather(out_mat, ("fsdp", "dp"), axis=0, tiled=True),
        lax.all_gather(out_off, ("fsdp", "dp"), axis=0, tiled=True),
    )


def fetch_ffn(gain_second, bias_second, up_mat, up_off, down_mat, down_off):
    return (
        lax.all_gather(gain_second, ("fsdp", "dp"), axis=0, tiled=True),
        lax.all_gather(bias_second, ("fsdp", "dp"), axis=0, tiled=True),
        lax.all_gather(up_mat, ("fsdp", "dp"), axis=0, tiled=True),
        lax.all_gather(up_off, ("fsdp", "dp"), axis=0, tiled=True),
        lax.all_gather(down_mat, ("fsdp", "dp"), axis=0, tiled=True),
        lax.all_gather(down_off, ("fsdp", "dp"), axis=0, tiled=True),
    )


def softmax_parts(query_heads, key_heads, allowed, score_scale):
    scores = (
        jnp.einsum("qhd,khd->hqk", query_heads, key_heads, preferred_element_type=jnp.float32)
        * score_scale
    )
    return jnp.where(allowed[None], scores, -1e30)


def shards(
    tokens,
    summaries,
    presence,
    seg_counts,
    ln1_gain,
    ln1_bias,
    w_query,
    query_bias,
    w_key,
    w_value,
    value_bias,
    w_out,
    out_bias,
    ln2_gain,
    ln2_bias,
    w_up,
    up_bias,
    w_down,
    down_bias,
    cotangent,
):
    seg_len = tokens.shape[0]
    n_summary = summaries.shape[1]
    model_width = tokens.shape[1]
    head_size = model_width // HEADS
    score_scale = head_size ** (-0.5)
    total_keys = n_summary + seg_len
    position = lax.axis_index(("fsdp", "dp"))
    starts = jnp.cumsum(seg_counts) - seg_counts
    has_prev = jnp.logical_not(jnp.any(starts == position))
    prior_sum = passed_along(summaries[0], ("fsdp", "dp"), 1)
    attn_full = fetch_attention(
        ln1_gain, ln1_bias, w_query, query_bias, w_key, w_value, value_bias, w_out, out_bias
    )
    (
        gain_first,
        bias_first,
        query_mat,
        query_off,
        key_mat,
        value_mat,
        value_off,
        out_mat,
        out_off,
    ) = attn_full
    gain_one = gain_first.astype(jnp.float32)
    bias_one = bias_first.astype(jnp.float32)
    token_vals = tokens.astype(jnp.float32)
    prior_vals = prior_sum.astype(jnp.float32)
    normed_low = norm_apply(token_vals, gain_one, bias_one).astype(jnp.bfloat16)
    prior_low = norm_apply(prior_vals, gain_one, bias_one).astype(jnp.bfloat16)
    joined = jnp.concatenate([prior_low, normed_low], 0)
    query_low = (
        jnp.dot(normed_low, query_mat, preferred_element_type=jnp.float32)
        + query_off.astype(jnp.float32)
    ).astype(jnp.bfloat16)
    key_low = jnp.dot(joined, key_mat, preferred_element_type=jnp.float32).astype(jnp.bfloat16)
    value_low = (
        jnp.dot(joined, value_mat, preferred_element_type=jnp.float32)
        + value_off.astype(jnp.float32)
    ).astype(jnp.bfloat16)
    query_heads = query_low.reshape(seg_len, HEADS, head_size)
    key_heads = key_low.reshape(total_keys, HEADS, head_size)
    value_heads = value_low.reshape(total_keys, HEADS, head_size)
    row_ids = jnp.arange(seg_len, dtype=jnp.int32)[:, None]
    col_ids = jnp.arange(total_keys, dtype=jnp.int32)[None, :]
    summary_ok = jnp.concatenate(
        [jnp.logical_and(presence[0] == 1, has_prev), jnp.ones((seg_len,), dtype=jnp.bool_)]
    )
    allowed = jnp.logical_and(summary_ok[None, :], col_ids - n_summary <= row_ids)
    masked = softmax_parts(query_heads, key_heads, allowed, score_scale)
    row_max = jnp.max(masked, axis=-1, keepdims=True)
    expo_vals = jnp.exp(masked - row_max)
    row_total = jnp.sum(expo_vals, axis=-1, keepdims=True)
    log_total = row_max + jnp.log(row_total)
    probs_low = (expo_vals / row_total).astype(jnp.bfloat16)
    mixed_low = (
        jnp.einsum("hqk,khd->qhd", probs_low, value_heads, preferred_element_type=jnp.float32)
        .reshape(seg_len, model_width)
        .astype(jnp.bfloat16)
    )
    middle = (
        token_vals
        + jnp.dot(mixed_low, out_mat, preferred_element_type=jnp.float32)
        + out_off.astype(jnp.float32)
    )
    ffn_full = fetch_ffn(ln2_gain, ln2_bias, w_up, up_bias, w_down, down_bias)
    gain_second, bias_second, up_mat, up_off, down_mat, down_off = ffn_full
    gain_two = gain_second.astype(jnp.float32)
    bias_two = bias_second.astype(jnp.float32)
    second_low = norm_apply(middle, gain_two, bias_two).astype(jnp.bfloat16)
    hidden_pre = jnp.dot(second_low, up_mat, preferred_element_type=jnp.float32) + up_off.astype(
        jnp.float32
    )
    hidden_low = jax.nn.gelu(hidden_pre).astype(jnp.bfloat16)
    output = (
        middle
        + jnp.dot(hidden_low, down_mat, preferred_element_type=jnp.float32)
        + down_off.astype(jnp.float32)
    ).astype(jnp.bfloat16)
    ffn_back = fetch_ffn(ln2_gain, ln2_bias, w_up, up_bias, w_down, down_bias)
    up_mat = ffn_back[2]
    down_mat = ffn_back[4]
    cot_vals = cotangent.astype(jnp.float32)
    down_off_grad = jnp.sum(cot_vals, axis=0)
    hidden_grad = contract_cols(cotangent, down_mat)
    _, gelu_back = jax.vjp(jax.nn.gelu, hidden_pre)
    pre_low = gelu_back(hidden_grad)[0].astype(jnp.bfloat16)
    up_off_grad = jnp.sum(pre_low.astype(jnp.float32), axis=0)
    second_grad = contract_cols(pre_low, up_mat)
    _, second_back = jax.vjp(norm_apply, middle, gain_two, bias_two)
    middle_part, gain_two_grad, bias_two_grad = second_back(second_grad)
    middle_grad = cot_vals + middle_part
    down_grad = contract_rows(hidden_low, cotangent)
    up_grad = contract_rows(second_low, pre_low)
    ffn_shares = (
        lax.psum_scatter(gain_two_grad, ("fsdp", "dp"), scatter_dimension=0, tiled=True),
        lax.psum_scatter(bias_two_grad, ("fsdp", "dp"), scatter_dimension=0, tiled=True),
        lax.psum_scatter(up_grad, ("fsdp", "dp"), scatter_dimension=0, tiled=True),
        lax.psum_scatter(up_off_grad, ("fsdp", "dp"), scatter_dimension=0, tiled=True),
        lax.psum_scatter(down_grad, ("fsdp", "dp"), scatter_dimension=0, tiled=True),
        lax.psum_scatter(down_off_grad, ("fsdp", "dp"), scatter_dimension=0, tiled=True),
    )
    attn_back = fetch_attention(
        ln1_gain, ln1_bias, w_query, query_bias, w_key, w_value, value_bias, w_out, out_bias
    )
    query_mat = attn_back[2]
    key_mat = attn_back[4]
    value_mat = attn_back[5]
    out_mat = attn_back[7]
    branch_low = middle_grad.astype(jnp.bfloat16)
    out_grad = contract_rows(mixed_low, branch_low)
    out_off_grad = jnp.sum(branch_low.astype(jnp.float32), axis=0)
    mixed_grad = (
        contract_cols(branch_low, out_mat).astype(jnp.bfloat16).reshape(seg_len, HEADS, head_size)
    )
    masked_again = softmax_parts(query_heads, key_heads, allowed, score_scale)
    probs = jnp.exp(masked_again - log_total)
    probs_again = probs.astype(jnp.bfloat16)
    prob_grad = jnp.einsum(
        "qhd,khd->hqk", mixed_grad, value_heads, preferred_element_type=jnp.float32
    )
    value_grad_low = (
        jnp.einsum("hqk,qhd->khd", probs_again, mixed_grad, preferred_element_type=jnp.float32)
        .astype(jnp.bfloat16)
        .reshape(total_keys, model_width)
    )
    score_grad = (probs * (prob_grad - jnp.sum(prob_grad * probs, axis=-1, keepdims=True))).astype(
        jnp.bfloat16
    )
    query_grad_low = (
        (
            jnp.einsum("hqk,khd->qhd", score_grad, key_heads, preferred_element_type=jnp.float32)
            * score_scale
        )
        .astype(jnp.bfloat16)
        .reshape(seg_len, model_width)
    )
    key_grad_low = (
        (
            jnp.einsum("hqk,qhd->khd", score_grad, query_heads, preferred_element_type=jnp.float32)
            * score_scale
        )
        .astype(jnp.bfloat16)
        .reshape(total_keys, model_width)
    )
    query_mat_grad = contract_rows(normed_low, query_grad_low)
    query_off_grad = jnp.sum(query_grad_low.astype(jnp.float32), axis=0)
    key_mat_grad = contract_rows(joined, key_grad_low)
    value_mat_grad = contract_rows(joined, value_grad_low)
    value_off_grad = jnp.sum(value_grad_low.astype(jnp.float32), axis=0)
    joined_grad = contract_cols(key_grad_low, key_mat) + contract_cols(value_grad_low, value_mat)
    normed_grad = contract_cols(query_grad_low, query_mat) + joined_grad[n_summary:]
    _, first_back = jax.vjp(norm_apply, token_vals, gain_one, bias_one)
    token_part, gain_token, bias_token = first_back(normed_grad)
    _, prior_back = jax.vjp(norm_apply, prior_vals, gain_one, bias_one)
    prior_part, gain_prior, bias_prior = prior_back(joined_grad[:n_summary])
    tokens_grad = middle_grad + token_part
    attn_shares = (
        lax.psum_scatter(gain_token + gain_prior, ("fsdp", "dp"), scatter_dimension=0, tiled=True),
        lax.psum_scatter(bias_token + bias_prior, ("fsdp", "dp"), scatter_dimension=0, tiled=True),
        lax.psum_scatter(query_mat_grad, ("fsdp", "dp"), scatter_dimension=0, tiled=True),
        lax.psum_scatter(query_off_grad, ("fsdp", "dp"), scatter_dimension=0, tiled=True),
        lax.psum_scatter(key_mat_grad, ("fsdp", "dp"), scatter_dimension=0, tiled=True),
        lax.psum_scatter(value_mat_grad, ("fsdp", "dp"), scatter_dimension=0, tiled=True),
        lax.psum_scatter(value_off_grad, ("fsdp", "dp"), scatter_dimension=0, tiled=True),
        lax.psum_scatter(out_grad, ("fsdp", "dp"), scatter_dimension=0, tiled=True),
        lax.psum_scatter(out_off_grad, ("fsdp", "dp"), scatter_dimension=0, tiled=True),
    )
    summary_grad = passed_along(prior_part.astype(jnp.bfloat16), ("fsdp", "dp"), -1).astype(
        prior_part.dtype
    )
    return (
        output,
        tokens_grad,
        summary_grad[None],
        attn_shares[0],
        attn_shares[1],
        attn_shares[2],
        attn_shares[3],
        attn_shares[4],
        attn_shares[5],
        attn_shares[6],
        attn_shares[7],
        attn_shares[8],
        ffn_shares[0],
        ffn_shares[1],
        ffn_shares[2],
        ffn_shares[3],
        ffn_shares[4],
        ffn_shares[5],
    )


def solution(mesh):
    return jax.shard_map(
        shards,
        mesh=mesh,
        in_specs=(
            P(("fsdp", "dp"), None),
            P(("fsdp", "dp"), None, None),
            P(("fsdp", "dp"), None),
            P(),
            P(("fsdp", "dp")),
            P(("fsdp", "dp")),
            P(("fsdp", "dp"), None),
            P(("fsdp", "dp")),
            P(("fsdp", "dp"), None),
            P(("fsdp", "dp"), None),
            P(("fsdp", "dp")),
            P(("fsdp", "dp"), None),
            P(("fsdp", "dp")),
            P(("fsdp", "dp")),
            P(("fsdp", "dp")),
            P(("fsdp", "dp"), None),
            P(("fsdp", "dp")),
            P(("fsdp", "dp"), None),
            P(("fsdp", "dp")),
            P(("fsdp", "dp"), None),
        ),
        out_specs=(
            P(("fsdp", "dp"), None),
            P(("fsdp", "dp"), None),
            P(("fsdp", "dp"), None, None),
            P(("fsdp", "dp")),
            P(("fsdp", "dp")),
            P(("fsdp", "dp"), None),
            P(("fsdp", "dp")),
            P(("fsdp", "dp"), None),
            P(("fsdp", "dp"), None),
            P(("fsdp", "dp")),
            P(("fsdp", "dp"), None),
            P(("fsdp", "dp")),
            P(("fsdp", "dp")),
            P(("fsdp", "dp")),
            P(("fsdp", "dp"), None),
            P(("fsdp", "dp")),
            P(("fsdp", "dp"), None),
            P(("fsdp", "dp")),
        ),
        check_vma=False,
    )
```

profile of v0, /device:TPU:0, one launch (start us, length us, event | category | flops | bytes accessed | tf_op | source)
XLA Modules:
  0.0 3143.6 jit_solution(2411094215978760441)
XLA Ops:
  11.3 2.4 collective-permute-start
  17.3 42.8 %all-reduce.19 = (bf16[2048]{0:T(1024)(128)(2,1)S(1)}, bf16[2048]{0:T(1024)(128)(2,1)S(1)}, bf16[2048]{0:T(1024)(128)(2,1)S(1)}, bf16[2048]{0:T(1024)(128)(2,1)S...) all-reduce(bf16[2048]{0:T(1024)(128)(2,1)S(1)} %dynamic-update-slic, ...), channel_id=1, replica_groups=mesh['fsdp'=4,'dp'=8] {'fsdp','dp'}, use_global_device_ids=true, to_apply=%add.3 | all-reduce | flops 16384 | bytes 65536
  60.1 41.2 %all-gather = bf16[32,1,256]{2,1,0:T(2,128)(2,1)S(1)} all-gather(bf16[1,1,256]{2,1,0:T(2,128)(2,1)S(1)} %reshape.268), channel_id=1, replica_groups=mesh['fsdp'=4,'dp'=8] {'fsdp','dp'}, dimensions={0}, use_global_device_ids=true | all-gather | bytes 16896 | tf_op jit(solution)/shard_map/all_gather | solution.py:54
  105.5 7.3 fusion.22
  112.8 2.3 copy.53
  115.1 55.5 %all-gather.8.cloned.1.call-done = bf16[2048,2048]{1,0:T(8,128)(2,1)} async-done(((bf16[64,2048]{1,0:T(8,128)(2,1)}), bf16[2048,2048]{1,0:T(8,128)(2,1)}) %all-gather.8.cloned.1.call-update) | async-done | bytes 8388624 | tf_op jit(solution)/shard_map/all_gather | solution.py:42
  170.6 8.3 add_convert_fusion
  178.8 2.6 copy.52
  181.4 68.0 %all-gather.12.cloned.1.call-done = bf16[2048,2048]{1,0:T(8,128)(2,1)} async-done(((bf16[64,2048]{1,0:T(8,128)(2,1)}), bf16[2048,2048]{1,0:T(8,128)(2,1)}) %all-gather.12.cloned.1.call-update) | async-done | bytes 8388624 | tf_op jit(solution)/shard_map/all_gather | solution.py:41
  249.4 8.3 convolution_convert_fusion
  257.7 2.6 copy.54
  260.3 5.1 fusion.58
  265.5 4.4 fusion
  269.9 1.4 copy-done
  271.3 5.0 fusion.28
  276.3 52.0 %all-gather.14.cloned.1.call-done = bf16[2048,2048]{1,0:T(8,128)(2,1)} async-done(((bf16[64,2048]{1,0:T(8,128)(2,1)}), bf16[2048,2048]{1,0:T(8,128)(2,1)}) %all-gather.14.cloned.1.call-update) | async-done | bytes 8388624 | tf_op jit(solution)/shard_map/all_gather | solution.py:44
  328.3 5.6 fusion.59
  334.0 1.5 copy-done.3
  336.0 188.6 %all-gather.18.cloned.1.call-done = bf16[8192,2048]{1,0:T(8,128)(2,1)} async-done(((bf16[256,2048]{1,0:T(8,128)(2,1)}), bf16[8192,2048]{1,0:T(8,128)(2,1)}) %all-gather.18.cloned.1.call-update) | async-done | bytes 33554448 | tf_op jit(solution)/shard_map/all_gather | solution.py:55
  524.6 21.2 fusion.60
  545.8 174.6 %all-gather.16.cloned.1.call-done = bf16[2048,8192]{1,0:T(8,128)(2,1)} async-done(((bf16[64,8192]{1,0:T(8,128)(2,1)}), bf16[2048,8192]{1,0:T(8,128)(2,1)}) %all-gather.16.cloned.1.call-update) | async-done | bytes 33554448 | tf_op jit(solution)/shard_map/all_gather | solution.py:53
  720.4 27.1 convert_reduce_fusion
  747.6 18.4 multiply_reduce_fusion.1
  767.3 1.1 convert_reduce_fusion.5
  768.4 1.1 copy-done.24
  769.5 6.3 convolution_convert_fusion.1
  776.6 8.0 convert_reduce_fusion.3
  784.6 14.8 multiply_reduce_fusion
  799.3 11.7 multiply_convert_fusion
  811.0 1.6 multiply_convert_fusion.2
  812.6 3.7 convert_reduce_fusion.4
  817.7 6.0 fusion.61
  823.8 6.4 convolution_add_fusion.1
  830.2 4.0 fusion.53
  834.3 1.2 fusion.25
  836.4 3.5 convert_reduce_fusion.2
  841.5 9.6 fusion.62
  852.0 9.6 fusion.48
  861.7 8.5 fusion.49
  870.2 1.3 copy-done.17
  872.0 8.2 fusion.63
  880.2 1.2 copy-done.15
  881.4 31.7 %fusion.52 = f32[8192,2048]{1,0:T(8,128)} fusion(bf16[320,2048]{1,0:T(8,128)(2,1)S(1)} %copy-done.15, f32[320,8192]{1,0:T(8,128)} %get-tuple-element.113), kind=kOutput, calls=%fused_computation.109 | convolution fusion | flops 10761011200 | bytes 78905344 | tf_op jit(solution)/shard_map/dot_general | solution.py:22
  913.2 1.6 copy-done.5
  914.9 28.8 fusion.51
  944.3 1.3 fusion.56
  945.8 1.3 collective-permute-start.1
  947.1 22.8 fusion.21
  969.9 1.3 dynamic-slice
  971.1 1.3 dynamic-slice.1
  972.4 1.3 dynamic-slice.2
  973.7 1.3 dynamic-slice.3
  974.9 1.3 dynamic-slice.4
  976.2 1.3 dynamic-slice.5
  977.4 1.3 dynamic-slice.6
  978.7 1.3 dynamic-slice.8
  980.0 1.3 dynamic-slice.7
  981.3 1.2 copy.56
  982.5 173.1 %reduce-scatter.7.cloned.1.call-done = f32[64,2048]{1,0:T(8,128)} async-done(((f32[2048,2048]{1,0:T(8,128)}), f32[64,2048]{1,0:T(8,128)}) %reduce-scatter.7.cloned.1.call-update) | async-done | bytes 524304 | tf_op jit(solution)/shard_map/reduce_scatter | solution.py:250
  1155.6 187.4 %reduce-scatter.11.cloned.1.call-done = f32[64,2048]{1,0:T(8,128)} async-done(((f32[2048,2048]{1,0:T(8,128)}), f32[64,2048]{1,0:T(8,128)}) %reduce-scatter.11.cloned.1.call-update) | async-done | bytes 524304 | tf_op jit(solution)/shard_map/reduce_scatter | solution.py:253
  1343.0 187.2 %reduce-scatter.9.cloned.1.call-done = f32[64,2048]{1,0:T(8,128)} async-done(((f32[2048,2048]{1,0:T(8,128)}), f32[64,2048]{1,0:T(8,128)}) %reduce-scatter.9.cloned.1.call-update) | async-done | bytes 524304 | tf_op jit(solution)/shard_map/reduce_scatter | solution.py:252
  1530.2 187.4 %reduce-scatter.13.cloned.1.call-done = f32[64,2048]{1,0:T(8,128)} async-done(((f32[2048,2048]{1,0:T(8,128)}), f32[64,2048]{1,0:T(8,128)}) %reduce-scatter.13.cloned.1.call-update) | async-done | bytes 524304 | tf_op jit(solution)/shard_map/reduce_scatter | solution.py:255
  1717.6 710.0 %reduce-scatter.17.cloned.1.call-done = f32[256,2048]{1,0:T(8,128)} async-done(((f32[8192,2048]{1,0:T(8,128)}), f32[256,2048]{1,0:T(8,128)}) %reduce-scatter.17.cloned.1.call-update) | async-done | bytes 2097168 | tf_op jit(solution)/shard_map/reduce_scatter | solution.py:189
  2427.6 709.0 %reduce-scatter.15.cloned.1.call-done = f32[64,8192]{1,0:T(8,128)} async-done(((f32[2048,8192]{1,0:T(8,128)}), f32[64,8192]{1,0:T(8,128)}) %reduce-scatter.15.cloned.1.call-update) | async-done | bytes 2097168 | tf_op jit(solution)/shard_map/reduce_scatter | solution.py:187
  (218 shorter events, 19.7 us)
Async XLA Ops:
  7.2 4.1 copy-start.53
  7.2 6.5 copy-start.52
  7.2 8.0 copy-start.54
  7.2 8.0 copy-start.55
  7.2 8.3 copy-start.56
  7.2 8.5 copy-start.57
  7.3 8.8 copy-start.58
  7.3 9.0 copy-start.59
  7.3 9.3 copy-start.60
  7.3 9.5 copy-start.61
  7.3 9.7 copy-start.62
  7.3 94.1 %copy-start.63 = (s32[1,50]{1,0:T(1,128)S(1)}, s32[1,50]{1,0:T(1,128)}, u32[]{:S(2)}) copy-start(s32[1,50]{1,0:T(1,128)} %param.22) | copy-start | bytes 604
  7.3 94.1 %copy-start.1 = (bf16[320,2048]{1,0:T(8,128)(2,1)S(1)}, bf16[320,2048]{1,0:T(8,128)(2,1)}, u32[]{:S(2)}) copy-start(bf16[320,2048]{1,0:T(8,128)(2,1)} %param.20) | copy-start | bytes 3932164
  7.3 97.8 %all-gather.10.cloned.1.call-start = ((), (), s32[]{:S(2)}) async-start(), calls=%async_computation.7 | async-start | bytes 8650752 | tf_op jit(solution)/shard_map/all_gather | solution.py:39
  8.1 162.5 %all-gather.8.cloned.1.call-start = ((), (), s32[]{:S(2)}) async-start(), calls=%async_computation.6 | async-start | bytes 8650752 | tf_op jit(solution)/shard_map/all_gather | solution.py:42
  8.8 240.6 %all-gather.12.cloned.1.call-start = ((), (), s32[]{:S(2)}) async-start(), calls=%async_computation.8 | async-start | bytes 8650752 | tf_op jit(solution)/shard_map/all_gather | solution.py:41
  9.5 318.8 %all-gather.14.cloned.1.call-start = ((), (), s32[]{:S(2)}) async-start(), calls=%async_computation.9 | async-start | bytes 8650752 | tf_op jit(solution)/shard_map/all_gather | solution.py:44
  10.1 514.4 %all-gather.18.cloned.1.call-start = ((), (), s32[]{:S(2)}) async-start(), calls=%async_computation.11 | async-start | bytes 34603008 | tf_op jit(solution)/shard_map/all_gather | solution.py:55
  10.7 709.7 %all-gather.16.cloned.1.call-start = ((), (), s32[]{:S(2)}) async-start(), calls=%async_computation.10 | async-start | bytes 34603008 | tf_op jit(solution)/shard_map/all_gather | solution.py:53
  11.3 958.6 %all-reduce.22.cloned.1.call-start = ((), (), s32[]{:S(2)}) async-start(), calls=%async_computation.18 | async-start | bytes 196608
  11.3 92.7 %collective-permute-start = (bf16[50,2048]{1,0:T(8,128)(2,1)S(1)}, bf16[50,2048]{1,0:T(8,128)(2,1)S(1)}, u32[]{:S(2)}, u32[]{:S(2)}) collective-permute-start(bf16[50,2048]{1,0:T(8,128)(2,1)S(1)} %bitcast.88), channel_id=1, source_target_pairs={{0,1},{1,2},{2,3},{3,4},{4,5},{5,6},{6,7},{7,8},{8,9},{9,10},{10,1... | collective-permute-start | bytes 614408 | tf_op jit(solution)/shard_map/ppermute | solution.py:12
  60.0 44.9 %copy-start.32 = (f32[2048]{0:T(1024)}, f32[2048]{0:T(1024)S(1)}, u32[]{:S(2)}) copy-start(f32[2048]{0:T(1024)S(1)} %convert_element_type.125) | copy-start | bytes 24580
  60.1 705.9 %copy-start.28 = (f32[2048]{0:T(1024)}, f32[2048]{0:T(1024)S(1)}, u32[]{:S(2)}) copy-start(f32[2048]{0:T(1024)S(1)} %convert_element_type.139) | copy-start | bytes 24580
  60.1 660.3 %copy-start.30 = (f32[2048]{0:T(1024)}, f32[2048]{0:T(1024)S(1)}, u32[]{:S(2)}) copy-start(f32[2048]{0:T(1024)S(1)} %convert_element_type.140) | copy-start | bytes 24580
  105.1 144.3 %copy-start.26 = (bf16[50,2048]{1,0:T(8,128)(2,1)}, bf16[50,2048]{1,0:T(8,128)(2,1)S(1)}, u32[]{:S(2)}) copy-start(bf16[50,2048]{1,0:T(8,128)(2,1)S(1)} %fusion.41) | copy-start | bytes 614404
  115.1 145.2 %copy-start.6 = (bf16[320,2048]{0,1:T(8,128)(2,1)}, bf16[320,2048]{0,1:T(8,128)(2,1)S(1)}, u32[]{:S(2)}) copy-start(bf16[320,2048]{0,1:T(8,128)(2,1)S(1)} %copy.53) | copy-start | bytes 3932164
  265.5 5.8 copy-start
  265.5 5.8 copy-start.18
  276.3 57.7 %copy-start.16 = (bf16[32,64,320]{2,1,0:T(8,128)(2,1)}, bf16[32,64,320]{2,1,0:T(8,128)(2,1)S(1)}, u32[]{:S(2)}) copy-start(bf16[32,64,320]{2,1,0:T(8,128)(2,1)S(1)} %fusion.28) | copy-start | bytes 3932164
  334.0 432.0 %copy-start.35 = (f32[320]{0:T(512)}, f32[320]{0:T(512)S(1)}, u32[]{:S(2)}) copy-start(f32[320]{0:T(512)S(1)} %broadcast_multiply_fusion) | copy-start | bytes 3844
  335.9 430.1 %copy-start.37 = (f32[320]{0:T(512)}, f32[320]{0:T(512)S(1)}, u32[]{:S(2)}) copy-start(f32[320]{0:T(512)S(1)} %fusion.46) | copy-start | bytes 3844
  335.9 384.5 %copy-start.4 = (f32[320,2048]{1,0:T(8,128)S(1)}, f32[320,2048]{1,0:T(8,128)}, u32[]{:S(2)}) copy-start(f32[320,2048]{1,0:T(8,128)} %copy-done.3) | copy-start | bytes 7864324
  776.6 8.0 copy-start.19
  799.3 11.7 copy-start.7
  811.0 1.6 copy-start.12
  817.6 6.0 copy-start.20
  817.7 12.5 slice-start
  823.7 6.4 copy-start.2
  823.7 6.4 copy-start.21
  823.7 6.4 copy-start.33
  823.7 6.4 copy-start.40
  823.7 6.4 slice-start.1
  830.1 9.8 copy-start.34
  830.2 4.1 copy-start.44
  830.2 4.1 copy-start.42
  834.2 1.7 copy-start.9
  834.2 2.1 copy-start.14
  836.4 3.5 copy-start.23
  836.4 3.5 copy-start.46
  836.4 3.5 copy-start.48
  836.4 5.1 copy-start.11
  841.4 314.2 %reduce-scatter.7.cloned.1.call-start = ((), (), s32[]{:S(2)}) async-start(), calls=%async_computation.12 | async-start | bytes 17301504 | tf_op jit(solution)/shard_map/reduce_scatter | solution.py:250
  851.1 491.9 %reduce-scatter.11.cloned.1.call-start = ((), (), s32[]{:S(2)}) async-start(), calls=%async_computation.14 | async-start | bytes 17301504 | tf_op jit(solution)/shard_map/reduce_scatter | solution.py:253
  861.6 668.6 %reduce-scatter.9.cloned.1.call-start = ((), (), s32[]{:S(2)}) async-start(), calls=%async_computation.13 | async-start | bytes 17301504 | tf_op jit(solution)/shard_map/reduce_scatter | solution.py:252
  870.2 1.8 copy-start.25
  870.2 847.4 %reduce-scatter.13.cloned.1.call-start = ((), (), s32[]{:S(2)}) async-start(), calls=%async_computation.15 | async-start | bytes 17301504 | tf_op jit(solution)/shard_map/reduce_scatter | solution.py:255
  880.1 1547.5 %reduce-scatter.17.cloned.1.call-start = ((), (), s32[]{:S(2)}) async-start(), calls=%async_computation.17 | async-start | bytes 69206016 | tf_op jit(solution)/shard_map/reduce_scatter | solution.py:189
  913.1 1.7 copy-start.5
  913.1 1.7 copy-start.29
  913.1 1.7 copy-start.31
  913.1 1.7 copy-start.36
  913.1 1.7 copy-start.38
  913.2 2223.4 %reduce-scatter.15.cloned.1.call-start = ((), (), s32[]{:S(2)}) async-start(), calls=%async_computation.16 | async-start | bytes 69206016 | tf_op jit(solution)/shard_map/reduce_scatter | solution.py:187
  945.8 35.5 %collective-permute-start.1 = (bf16[50,2048]{1,0:T(8,128)(2,1)S(1)}, bf16[50,2048]{1,0:T(8,128)(2,1)S(1)}, u32[]{:S(2)}, u32[]{:S(2)}) collective-permute-start(bf16[50,2048]{1,0:T(8,128)(2,1)S(1)} %add_convert_fusion.2), channel_id=1, source_target_pairs={{1,0},{2,1},{3,2},{4,3},{5,4},{6,5},{7,6},{8,7},{9,8},{10,9},{11,1... | collective-permute-start | bytes 614408 | tf_op jit(solution)/shard_map/ppermute | solution.py:12
  (17 other events, 16.6 us)
Sparse Core Ops, SparseCore 0:
  11.1 80.4 all-gather.9
  94.6 75.9 all-gather.7
  173.6 75.8 all-gather.11
  252.3 75.9 all-gather.13
  331.1 193.3 all-gather.17
  527.4 192.9 all-gather.15
  841.5 123.3 all-reduce.21
  967.9 187.6 reduce-scatter.6
  1158.6 184.3 reduce-scatter.10
  1345.8 184.3 reduce-scatter.8
  1533.2 184.3 reduce-scatter.12
  1720.5 707.0 reduce-scatter.16
  2430.6 705.9 reduce-scatter.14
where the time goes:
time: 3150 us; the launch traced here: 3140 us
  waiting for transfers between devices  2700 us (86%)
  matrix products  276 us (9%)
  blocking collectives  84 us (3%)
  local copies, waits for them, and re-layouts  37.8 us (1%)
    reduce_scatter x1, waiting for transfers between devices, shards(): lax.psum_scatter(down_grad, ('fsdp', 'dp'), scatter_dimension=0, tiled=True)  710 us
    reduce_scatter x1, waiting for transfers between devices, shards(): lax.psum_scatter(up_grad, ('fsdp', 'dp'), scatter_dimension=0, tiled=True)  709 us
    all_gather x1, waiting for transfers between devices, fetch_ffn(): lax.all_gather(down_mat, ('fsdp', 'dp'), axis=0, tiled=True)  189 us
    reduce_scatter x1, waiting for transfers between devices, shards(): lax.psum_scatter(value_mat_grad, ('fsdp', 'dp'), scatter_dimension=0, til...  187 us
    reduce_scatter x1, waiting for transfers between devices, shards(): lax.psum_scatter(out_grad, ('fsdp', 'dp'), scatter_dimension=0, tiled=True)  187 us
    reduce_scatter x1, waiting for transfers between devices, shards(): lax.psum_scatter(key_mat_grad, ('fsdp', 'dp'), scatter_dimension=0, tiled...  187 us
    all_gather x1, waiting for transfers between devices, fetch_ffn(): lax.all_gather(up_mat, ('fsdp', 'dp'), axis=0, tiled=True)  175 us
    reduce_scatter x1, waiting for transfers between devices, shards(): lax.psum_scatter(query_mat_grad, ('fsdp', 'dp'), scatter_dimension=0, til...  173 us
  transfers between devices with their start and end apart: 15, of which 11 were waited for; matrix products, arithmetic and copies ran while one was open for 7% of the time, Pallas kernels for 0%

commit v1 on v0

v1 whole, which is shorter than its diff:
```python
import jax
import jax.numpy as jnp
from jax import lax
from jax.sharding import PartitionSpec as P

HEADS = 32
BOTH = ("fsdp", "dp")
PRIOR_ROWS = 64


def norm_parts(values):
    centre = values - jnp.mean(values, axis=-1, keepdims=True)
    spread = jnp.mean(centre * centre, axis=-1, keepdims=True)
    return centre, lax.rsqrt(spread + 1e-05)


def norm_apply(values, norm_gain, norm_bias):
    centre, inverse = norm_parts(values)
    return centre * inverse * norm_gain + norm_bias


def contract_rows(left, right):
    return lax.dot_general(
        left, right, (((0,), (0,)), ((), ())), preferred_element_type=jnp.float32
    )


def contract_cols(left, right):
    return lax.dot_general(
        left, right, (((1,), (1,)), ((), ())), preferred_element_type=jnp.float32
    )


def dot(left, right):
    return jnp.dot(left, right, preferred_element_type=jnp.float32)


def swap(value, rel):
    if rel == 0:
        return value
    count = lax.axis_size("fsdp")
    return lax.ppermute(value, "fsdp", [(i, i ^ rel) for i in range(count)])


def spread_out(value):
    return [swap(value, rel) for rel in range(lax.axis_size("fsdp"))]


def collect(parts):
    total = parts[0]
    for rel in range(1, len(parts)):
        total = total + swap(parts[rel].astype(jnp.bfloat16), rel).astype(jnp.float32)
    return total


def trade_blocks(blocks):
    count = lax.axis_size("fsdp")
    me = lax.axis_index("fsdp")
    out = blocks
    for rel in range(1, count):
        theirs = lax.dynamic_index_in_dim(blocks, me ^ rel, 0, keepdims=True)
        out = lax.dynamic_update_slice_in_dim(out, swap(theirs, rel), me ^ rel, 0)
    return out


def gather_small(row):
    total = lax.axis_size("fsdp") * lax.axis_size("dp")
    place = lax.axis_index(BOTH)
    step = 1
    while step < total:
        came = lax.ppermute(row, BOTH, [(i, i ^ step) for i in range(total)])
        high = (place & step) != 0
        row = jnp.concatenate([jnp.where(high, came, row), jnp.where(high, row, came)], 0)
        step *= 2
    return row


def scatter_small(rows):
    total = lax.axis_size("fsdp") * lax.axis_size("dp")
    place = lax.axis_index(BOTH)
    step = total // 2
    while step >= 1:
        high = (place & step) != 0
        lower, upper = rows[:step], rows[step:]
        sent = jnp.where(high, lower, upper)
        came = lax.ppermute(sent, BOTH, [(i, i ^ step) for i in range(total)])
        rows = jnp.where(high, upper, lower) + came
        step //= 2
    return rows[0]


def gather_dp(value, axis):
    return lax.all_gather(value, "dp", axis=axis, tiled=True)


def scatter_dp(value, axis):
    return lax.psum_scatter(value, "dp", scatter_dimension=axis, tiled=True)


def shards(
    tokens,
    summaries,
    presence,
    seg_counts,
    ln1_gain,
    ln1_bias,
    w_query,
    query_bias,
    w_key,
    w_value,
    value_bias,
    w_out,
    out_bias,
    ln2_gain,
    ln2_bias,
    w_up,
    up_bias,
    w_down,
    down_bias,
    cotangent,
):
    members = lax.axis_size("fsdp")
    columns = lax.axis_size("dp")
    total = members * columns
    me = lax.axis_index("fsdp")
    place = lax.axis_index(BOTH)
    seg_len, width = tokens.shape
    n_summary = summaries.shape[1]
    head_size = width // HEADS
    score_scale = head_size ** (-0.5)
    my_heads = HEADS // members
    my_cols = width // members
    my_ff = w_up.shape[1] // members
    row_share = w_query.shape[0]
    f32, bf16 = jnp.float32, jnp.bfloat16

    small_parts = (
        ln1_gain, ln1_bias, query_bias, value_bias, out_bias, ln2_gain, ln2_bias, up_bias,
        down_bias, presence[0].astype(bf16),
    )
    packed = gather_small(jnp.concatenate(small_parts)[None])
    smalls = []
    at = 0
    for part in small_parts:
        smalls.append(packed[:, at : at + part.shape[0]].astype(f32))
        at += part.shape[0]
    gain_one, bias_one, query_off, value_off, out_off, gain_two, bias_two, up_off, down_off = [
        part.reshape(-1) for part in smalls[:-1]
    ]
    present_all = smalls[-1]
    query_off = lax.dynamic_slice_in_dim(query_off, me * my_cols, my_cols)
    value_off = lax.dynamic_slice_in_dim(value_off, me * my_cols, my_cols)
    up_off = lax.dynamic_slice_in_dim(up_off, me * my_ff, my_ff)

    def blocks_of(weight):
        return weight.reshape(row_share, members, -1).swapaxes(0, 1)

    qkv_blocks = jnp.concatenate([blocks_of(w_query), blocks_of(w_key), blocks_of(w_value)], 2)
    qkv_mat = gather_dp(trade_blocks(qkv_blocks), 1).reshape(width, 3 * my_cols)
    out_mat = gather_dp(w_out, 0)
    up_mat = gather_dp(trade_blocks(blocks_of(w_up)), 1).reshape(width, my_ff)
    down_mat = gather_dp(w_down, 0)

    prior_own = jnp.pad(summaries[0], ((0, PRIOR_ROWS - n_summary), (0, 0)))
    group_tokens = jnp.concatenate(spread_out(tokens), 0)
    priors = []
    for rel in range(members):
        pairs = [((((i // columns) ^ rel) * columns + i % columns) - 1, i) for i in range(total)]
        priors.append(lax.ppermute(prior_own, BOTH, [pair for pair in pairs if pair[0] >= 0]))
    group_prior = jnp.concatenate(priors, 0)
    group_cot = jnp.concatenate(spread_out(cotangent), 0)

    starts = jnp.cumsum(seg_counts) - seg_counts
    group_places = (me ^ jnp.arange(members)) * columns + lax.axis_index("dp")
    has_prev = jnp.all(group_places[:, None] != starts[None, :], axis=1)
    presence_ok = present_all[group_places] == 1
    summary_ok = jnp.logical_and(presence_ok, has_prev[:, None])
    summary_ok = jnp.pad(summary_ok, ((0, 0), (0, PRIOR_ROWS - n_summary)))

    token_low = norm_apply(group_tokens.astype(f32), gain_one, bias_one).astype(bf16)
    prior_low = norm_apply(group_prior.astype(f32), gain_one, bias_one).astype(bf16)
    qkv_off = jnp.concatenate([query_off, jnp.zeros_like(query_off), value_off])
    qkv = (dot(token_low, qkv_mat) + qkv_off).astype(bf16)
    prior_kv = (dot(prior_low, qkv_mat[:, my_cols:]) + qkv_off[my_cols:]).astype(bf16)

    def heads_of(value, rows):
        return value.reshape(members, rows, my_heads, head_size)

    query_heads = heads_of(qkv[:, :my_cols], seg_len)
    key_heads = jnp.concatenate(
        [
            heads_of(qkv[:, my_cols : 2 * my_cols], seg_len),
            heads_of(prior_kv[:, :my_cols], PRIOR_ROWS),
        ],
        1,
    )
    value_heads = jnp.concatenate(
        [heads_of(qkv[:, 2 * my_cols :], seg_len), heads_of(prior_kv[:, my_cols:], PRIOR_ROWS)], 1
    )
    causal = jnp.arange(seg_len)[None, :] <= jnp.arange(seg_len)[:, None]
    allowed = jnp.concatenate(
        [
            jnp.broadcast_to(causal[None], (members, seg_len, seg_len)),
            jnp.broadcast_to(summary_ok[:, None, :], (members, seg_len, PRIOR_ROWS)),
        ],
        2,
    )[:, None]

    def masked_scores():
        scores = jnp.einsum("sqhd,skhd->shqk", query_heads, key_heads, preferred_element_type=f32)
        return jnp.where(allowed, scores * score_scale, -1e30)

    masked = masked_scores()
    row_max = jnp.max(masked, axis=-1, keepdims=True)
    expo_vals = jnp.exp(masked - row_max)
    row_total = jnp.sum(expo_vals, axis=-1, keepdims=True)
    log_total = row_max + jnp.log(row_total)
    probs_low = (expo_vals / row_total).astype(bf16)
    mixed_low = (
        jnp.einsum("shqk,skhd->sqhd", probs_low, value_heads, preferred_element_type=f32)
        .reshape(members * seg_len, my_cols)
        .astype(bf16)
    )

    def by_member(value):
        rows = value.shape[0] // members
        return [value[rel * rows : (rel + 1) * rows] for rel in range(members)]

    token_vals = tokens.astype(f32)
    middle = token_vals + collect(by_member(dot(mixed_low, out_mat))) + out_off
    second_own = norm_apply(middle, gain_two, bias_two).astype(bf16)
    second_low = jnp.concatenate(spread_out(second_own), 0)
    hidden_pre = dot(second_low, up_mat) + up_off
    hidden_low = jax.nn.gelu(hidden_pre).astype(bf16)
    output = (middle + collect(by_member(dot(hidden_low, down_mat))) + down_off).astype(bf16)

    cot_vals = cotangent.astype(f32)
    down_off_grad = jnp.sum(cot_vals, axis=0)
    hidden_grad = contract_cols(group_cot, down_mat)
    _, gelu_back = jax.vjp(jax.nn.gelu, hidden_pre)
    pre_low = gelu_back(hidden_grad)[0].astype(bf16)
    up_off_grad = jnp.sum(pre_low.astype(f32), axis=0)
    second_grad = collect(by_member(contract_cols(pre_low, up_mat)))
    _, second_back = jax.vjp(norm_apply, middle, gain_two, bias_two)
    middle_part, gain_two_grad, bias_two_grad = second_back(second_grad)
    middle_grad = cot_vals + middle_part
    down_grad = scatter_dp(contract_rows(hidden_low, group_cot).astype(bf16), 0).astype(f32)

    def to_owners(grad):
        share = scatter_dp(grad.astype(bf16).reshape(members, columns * row_share, -1), 1)
        return trade_blocks(share)

    up_blocks = to_owners(contract_rows(second_low, pre_low))
    up_grad = up_blocks.swapaxes(0, 1).reshape(row_share, members * my_ff).astype(f32)

    branch_low = middle_grad.astype(bf16)
    group_branch = jnp.concatenate(spread_out(branch_low), 0)
    out_grad = scatter_dp(contract_rows(mixed_low, group_branch).astype(bf16), 0).astype(f32)
    out_off_grad = jnp.sum(branch_low.astype(f32), axis=0)
    mixed_grad = heads_of(contract_cols(group_branch, out_mat).astype(bf16), seg_len)
    probs = jnp.exp(masked_scores() - log_total)
    probs_again = probs.astype(bf16)
    prob_grad = jnp.einsum("sqhd,skhd->shqk", mixed_grad, value_heads, preferred_element_type=f32)
    value_grad = jnp.einsum(
        "shqk,sqhd->skhd", probs_again, mixed_grad, preferred_element_type=f32
    ).astype(bf16)
    score_grad = (probs * (prob_grad - jnp.sum(prob_grad * probs, axis=-1, keepdims=True))).astype(
        bf16
    )
    query_grad = (
        jnp.einsum("shqk,skhd->sqhd", score_grad, key_heads, preferred_element_type=f32)
        * score_scale
    ).astype(bf16)
    key_grad = (
        jnp.einsum("shqk,sqhd->skhd", score_grad, query_heads, preferred_element_type=f32)
        * score_scale
    ).astype(bf16)

    def flat(value):
        return value.reshape(-1, my_cols)

    query_grad = flat(query_grad)
    query_off_grad = jnp.sum(query_grad.astype(f32), axis=0)
    value_off_grad = jnp.sum(value_grad.astype(f32), axis=(0, 1)).reshape(-1)
    token_grads = jnp.concatenate(
        [query_grad, flat(key_grad[:, :seg_len]), flat(value_grad[:, :seg_len])], 1
    )
    prior_grads = jnp.concatenate([flat(key_grad[:, seg_len:]), flat(value_grad[:, seg_len:])], 1)
    token_qkv_grad = contract_rows(token_low, token_grads)
    prior_kv_grad = contract_rows(prior_low, prior_grads)
    qkv_grad = jnp.concatenate(
        [token_qkv_grad[:, :my_cols], token_qkv_grad[:, my_cols:] + prior_kv_grad], 1
    )
    qkv_shares = to_owners(qkv_grad)
    query_mat_grad, key_mat_grad, value_mat_grad = [
        qkv_shares[:, :, part * my_cols : (part + 1) * my_cols]
        .swapaxes(0, 1)
        .reshape(row_share, width)
        .astype(f32)
        for part in range(3)
    ]
    normed_grad = collect(by_member(contract_cols(token_grads, qkv_mat)))
    prior_normed_grad = collect(by_member(contract_cols(prior_grads, qkv_mat[:, my_cols:])))
    _, first_back = jax.vjp(norm_apply, token_vals, gain_one, bias_one)
    token_part, gain_token, bias_token = first_back(normed_grad)
    prior_vals = priors[0][:n_summary].astype(f32)
    _, prior_back = jax.vjp(norm_apply, prior_vals, gain_one, bias_one)
    prior_part, gain_prior, bias_prior = prior_back(prior_normed_grad[:n_summary])
    tokens_grad = middle_grad + token_part
    summary_grad = lax.ppermute(
        prior_part.astype(bf16), BOTH, [(i + 1, i) for i in range(total - 1)]
    ).astype(f32)

    def whole(value):
        return value.reshape(total, -1)

    def sliced(value):
        mine = value.reshape(columns, -1)
        full = jnp.zeros((total, mine.shape[1]), f32)
        return lax.dynamic_update_slice_in_dim(full, mine, me * columns, 0)

    pieces = [
        whole(gain_token + gain_prior),
        whole(bias_token + bias_prior),
        sliced(query_off_grad),
        sliced(value_off_grad),
        whole(out_off_grad),
        whole(gain_two_grad),
        whole(bias_two_grad),
        sliced(up_off_grad),
        whole(down_off_grad),
    ]
    share = scatter_small(jnp.concatenate(pieces, 1))
    outs = []
    at = 0
    for piece in pieces:
        outs.append(share[at : at + piece.shape[1]])
        at += piece.shape[1]
    return (
        output,
        tokens_grad,
        summary_grad[None],
        outs[0],
        outs[1],
        query_mat_grad,
        outs[2],
        key_mat_grad,
        value_mat_grad,
        outs[3],
        out_grad,
        outs[4],
        outs[5],
        outs[6],
        up_grad,
        outs[7],
        down_grad,
        outs[8],
    )


def solution(mesh):
    rows, rows2, rows3 = P(BOTH), P(BOTH, None), P(BOTH, None, None)
    return jax.shard_map(
        shards,
        mesh=mesh,
        in_specs=(
            rows2, rows3, rows2, P(), rows, rows, rows2, rows, rows2, rows2, rows, rows2, rows,
            rows, rows, rows2, rows, rows2, rows, rows2,
        ),
        out_specs=(
            rows2, rows2, rows3, rows, rows, rows2, rows, rows2, rows2, rows, rows2, rows, rows,
            rows, rows2, rows, rows2, rows,
        ),
        check_vma=False,
    )
```

time: 3150 us -> 1110 us (0.35)
  waiting for transfers between devices: 2700 us -> 492 us
  local copies, waits for them, and re-layouts: 37.8 us -> 187 us
  starting transfers between devices: 4.18 us -> 90.7 us
  blocking collectives: 84 us -> 0 us
  other arithmetic: 28.9 us -> 79.9 us
  matrix products: 276 us -> 228 us
    reduce_scatter x6 -> x4, waiting for transfers between devices: 2150 us -> 94 us  [scatter_dp(): return lax.psum_scatter(value, 'dp', scatter_dimension=axis, tiled=True)]
    all_gather x6 -> x4, waiting for transfers between devices: 539 us -> 0.05 us  [gather_dp(): return lax.all_gather(value, 'dp', axis=axis, tiled=True)]
    ppermute x2 -> x54, waiting for transfers between devices: 0.01 us -> 397 us  [the longest x39 331 us: swap(): return lax.ppermute(value, 'fsdp', [(i, i ^ rel) for i in range(count)])]
    ppermute x2 -> x54, starting transfers between devices: 3.66 us -> 90.3 us  [the longest x39 55.6 us: swap(): return lax.ppermute(value, 'fsdp', [(i, i ^ rel) for i in range(count)])]
    reshape x0 -> x28, local copies, waits for them, and re-layouts: none -> 46.6 us  [the longest x12 27.1 us: heads_of(): return value.reshape(members, rows, my_heads, head_size)]
    dynamic_update_slice x0 -> x13, local copies, waits for them, and re-layouts: none -> 45.2 us  [the longest x10 45.2 us: trade_blocks(): out = lax.dynamic_update_slice_in_dim(out, swap(theirs, rel), me ^ rel, 0)]
    unnamed x1 -> x0, blocking collectives: 42.8 us -> none
    all_gather x1 -> x0, blocking collectives: 41.2 us -> none  [fetch_ffn(): lax.all_gather(up_off, ('fsdp', 'dp'), axis=0, tiled=True)]
  transfers between devices with their start and end apart: 15 -> 62, of which waited for: 11 -> 33; matrix products, arithmetic and copies ran while one was open for 7% -> 29% of each run, Pallas kernels for 0% -> 0%
where the time goes in v1:
time: 1110 us; the launch traced here: 1090 us
  waiting for transfers between devices  492 us (44%)
  matrix products  228 us (21%)
  local copies, waits for them, and re-layouts  187 us (17%)
  starting transfers between devices  90.7 us (8%)
  other arithmetic  79.9 us (7%)
  between operations  16.3 us (1%)
    ppermute x39, waiting for transfers between devices, swap(): return lax.ppermute(value, 'fsdp', [(i, i ^ rel) for i in range(count)])  331 us
    reduce_scatter x4, waiting for transfers between devices, scatter_dp(): return lax.psum_scatter(value, 'dp', scatter_dimension=axis, tiled=True)  94 us
    dot_general x5, matrix products, contract_cols(): lax.dot_general(left, right, (((1,), (1,)), ((), ())), preferred_element_...  67.6 us
    dot_general x5, matrix products, dot(): return jnp.dot(left, right, preferred_element_type=jnp.float32)  62.2 us
    dot_general x5, matrix products, contract_rows(): lax.dot_general(left, right, (((0,), (0,)), ((), ())), preferred_element_...  60.8 us
    ppermute x39, starting transfers between devices, swap(): return lax.ppermute(value, 'fsdp', [(i, i ^ rel) for i in range(count)])  55.6 us
    ppermute x5, waiting for transfers between devices, gather_small(): came = lax.ppermute(row, BOTH, [(i, i ^ step) for i in range(total)])  46.4 us
    dynamic_update_slice x10, local copies, waits for them, and re-layouts, trade_blocks(): out = lax.dynamic_update_slice_in_dim(out, swap(theirs, rel), me ^ rel, 0)  45.2 us
  transfers between devices with their start and end apart: 62, of which 33 were waited for; matrix products, arithmetic and copies ran while one was open for 29% of the time, Pallas kernels for 0%

profile of v1, /device:TPU:0, one launch (start us, length us, event | category | flops | bytes accessed | tf_op | source)
XLA Modules:
  0.0 1093.6 jit_solution(7194274176358766644)
XLA Ops:
  16.8 8.5 collective-permute-done.8
  25.3 7.2 dynamic_update_slice.45
  34.4 7.2 dynamic_update_slice.46
  41.7 5.6 dynamic_update_slice.47
  55.1 11.4 %collective-permute-done.21 = bf16[1,64,2048]{2,0,1:T(2,128)(2,1)S(1)} collective-permute-done((bf16[1,64,2048]{2,0,1:T(2,128)(2,1)S(1)}, bf16[1,64,2048]{2,0,1:T(2,128)(2,1)S(1)}, u32[]{:S(2)}, u32[]{:S(2)}) %collective-permute-start.21) | collective-permute-done | bytes 262176 | tf_op jit(solution)/shard_map/ppermute | solution.py:42
  67.3 7.8 dynamic_update_slice.48
  75.1 7.9 dynamic_update_slice.49
  83.1 7.9 dynamic_update_slice.50
  109.1 37.3 %collective-permute-done.6 = bf16[8,818]{1,0:T(8,128)(2,1)S(1)} collective-permute-done((bf16[8,818]{1,0:T(8,128)(2,1)S(1)}, bf16[8,818]{1,0:T(8,128)(2,1)S(1)}, u32[]{:S(2)}, u32[]{:S(2)}) %collective-permute-start.6) | collective-permute-done | bytes 13120 | tf_op jit(solution)/shard_map/ppermute | solution.py:71
  156.4 5.9 collective-permute-done.12
  181.4 3.8 convert_reduce_fusion
  185.2 5.5 fusion.4
  190.8 4.1 copy.124
  194.9 11.9 %fusion.20 = bf16[1280,1536]{1,0:T(8,128)(2,1)S(1)} fusion(bf16[2048,1536]{1,0:T(8,128)(2,1)S(1)} %bitcast.116, f32[1536]{0:T(1024)S(1)} %copy-done.62, f32[2048]{0:T(1024)S(1)} %copy-done.50, f32[2048]{0:T(1024)S(1)} %reshape.399, f32[1280]{0:T(1024)S(1)} %add_rsqrt_fusion, f32[1280]{0:T(1024)S(1)} %broadcast_multiply_fusion, ...), kind=kOutput, calls=%fused_computation.34 | convolution fusion | flops 8091074560 | bytes 15499264 | tf_op jit(solution)/shard_map/dot_general | solution.py:35
  210.7 4.2 copy.130
  217.3 4.6 copy.132
  233.5 6.2 fusion.135
  239.7 4.1 fusion
  246.6 5.3 fusion.56
  254.5 7.7 fusion.136
  264.2 4.0 collective-permute-start.15
  271.9 26.2 %collective-permute-done.15 = bf16[320,2048]{1,0:T(8,128)(2,1)S(1)} collective-permute-done((bf16[320,2048]{1,0:T(8,128)(2,1)}, bf16[320,2048]{1,0:T(8,128)(2,1)S(1)}, u32[]{:S(2)}, u32[]{:S(2)}) %collective-permute-start.15) | collective-permute-done | bytes 1310752 | tf_op jit(solution)/shard_map/ppermute | solution.py:42
  299.5 28.7 %collective-permute-done.16 = bf16[320,2048]{1,0:T(8,128)(2,1)S(1)} collective-permute-done((bf16[320,2048]{1,0:T(8,128)(2,1)}, bf16[320,2048]{1,0:T(8,128)(2,1)S(1)}, u32[]{:S(2)}, u32[]{:S(2)}) %collective-permute-start.16) | collective-permute-done | bytes 1310752 | tf_op jit(solution)/shard_map/ppermute | solution.py:42
  329.3 5.0 fusion.126
  336.9 17.5 %collective-permute-done.27 = bf16[320,2048]{1,0:T(8,128)(2,1)} collective-permute-done((bf16[320,2048]{1,0:T(8,128)(2,1)}, bf16[320,2048]{1,0:T(8,128)(2,1)}, u32[]{:S(2)}, u32[]{:S(2)}) %collective-permute-start.27) | collective-permute-done | bytes 1310752 | tf_op jit(solution)/shard_map/ppermute | solution.py:42
  361.0 23.5 %collective-permute-done.28 = bf16[320,2048]{1,0:T(8,128)(2,1)} collective-permute-done((bf16[320,2048]{1,0:T(8,128)(2,1)}, bf16[320,2048]{1,0:T(8,128)(2,1)}, u32[]{:S(2)}, u32[]{:S(2)}) %collective-permute-start.28) | collective-permute-done | bytes 1310752 | tf_op jit(solution)/shard_map/ppermute | solution.py:42
  389.6 11.3 %copy.134 = bf16[4,512,2048]{2,1,0:T(8,128)(2,1)} copy(bf16[4,512,2048]{2,0,1:T(4,128)(2,1)} %all-gather.9.cloned.1.call-done) | data formatting | bytes 16777216 | tf_op jit(solution)/shard_map/all_gather | solution.py:93
  400.9 9.7 collective-permute-done.18
  410.6 21.4 %collective-permute-done.20 = bf16[320,2048]{1,0:T(8,128)(2,1)} collective-permute-done((bf16[320,2048]{1,0:T(8,128)(2,1)}, bf16[320,2048]{1,0:T(8,128)(2,1)}, u32[]{:S(2)}, u32[]{:S(2)}) %collective-permute-start.20) | collective-permute-done | bytes 1310752 | tf_op jit(solution)/shard_map/ppermute | solution.py:42
  432.1 19.2 %fusion.68 = f32[1280,2048]{1,0:T(8,128)} fusion(bf16[2048,2048]{1,0:T(8,128)(2,1)} %bitcast.113, bf16[320,2048]{1,0:T(8,128)(2,1)} %collective-permute-done.20, bf16[320,2048]{1,0:T(8,128)(2,1)} %collective-permute-done.19, bf16[320,2048]{1,0:T(8,128)(2,1)} %collective-permute-done.18, bf16[320,2048]{1,0:T(8,128)(2,1)} %add_convert_fusion), kind=kOutput, calls=%fused_computation.111 | convolution fusion | flops 10758389760 | bytes 24117248 | tf_op jit(solution)/shard_map/dot_general | solution.py:35
  451.3 25.3 %convert_reduce_fusion.1 = (f32[2048]{0:T(1024)}, bf16[1280,2048]{1,0:T(8,128)(2,1)}) fusion(f32[1280,2048]{1,0:T(8,128)} %fusion.68, f32[2048]{0:T(1024)S(1)} %dynamic_slice.55, bf16[1280,2048]{1,0:T(8,128)(2,1)} %constant_dynamic-update-slice_fusion, bf16[2048,2048]{1,0:T(8,128)(2,1)} %all-gather.11.cloned.1.call-done), kind=kOutput, calls=%fused_computation.26 | convolution fusion | flops 10797709312 | bytes 29376512 | tf_op jit(solution)/shard_map/dot_general | solution.py:29
  476.6 16.6 %fusion.137 = (bf16[1280,2048]{1,0:T(8,128)(2,1)}, f32[1280,2048]{1,0:T(8,128)}) fusion(bf16[1280,2048]{1,0:T(8,128)(2,1)} %get-tuple-element.120, bf16[2048,2048]{1,0:T(8,128)(2,1)S(1)} %bitcast.114), kind=kOutput, calls=%fused_computation.288 | convolution fusion | flops 10740039680 | bytes 29360128 | tf_op jit(solution)/shard_map/dot_general | solution.py:29
  493.3 4.0 fusion.129
  500.8 19.8 %fusion.138 = (bf16[1280,2048]{1,0:T(8,128)(2,1)S(1)}, f32[1280,2048]{1,0:T(8,128)}) fusion(bf16[2048,2048]{1,0:T(8,128)(2,1)} %all-gather.11.cloned.1.call-done, f32[1280,2048]{1,0:T(8,128)} %fusion.68, f32[2048]{0:T(1024)S(1)} %dynamic_slice.55), kind=kOutput, calls=%fused_computation.289 | convolution fusion | flops 10766254080 | bytes 34611200 | tf_op jit(solution)/shard_map/dot_general | solution.py:35
  524.8 4.3 collective-permute-done.30
  530.9 26.3 %collective-permute-done.31 = bf16[320,2048]{1,0:T(8,128)(2,1)} collective-permute-done((bf16[320,2048]{1,0:T(8,128)(2,1)}, bf16[320,2048]{1,0:T(8,128)(2,1)}, u32[]{:S(2)}, u32[]{:S(2)}) %collective-permute-start.31) | collective-permute-done | bytes 1310752 | tf_op jit(solution)/shard_map/ppermute | solution.py:42
  557.3 5.1 multiply_reduce_fusion.1
  562.4 22.9 %collective-permute-done.24 = bf16[320,2048]{1,0:T(8,128)(2,1)} collective-permute-done((bf16[320,2048]{1,0:T(8,128)(2,1)}, bf16[320,2048]{1,0:T(8,128)(2,1)}, u32[]{:S(2)}, u32[]{:S(2)}) %collective-permute-start.24) | collective-permute-done | bytes 1310752 | tf_op jit(solution)/shard_map/ppermute | solution.py:42
  585.4 21.3 %collective-permute-done.25 = bf16[320,2048]{1,0:T(8,128)(2,1)} collective-permute-done((bf16[320,2048]{1,0:T(8,128)(2,1)}, bf16[320,2048]{1,0:T(8,128)(2,1)}, u32[]{:S(2)}, u32[]{:S(2)}) %collective-permute-start.25) | collective-permute-done | bytes 1310752 | tf_op jit(solution)/shard_map/ppermute | solution.py:42
  606.7 5.5 fusion.124
  619.1 28.2 %collective-permute-done.33 = bf16[320,2048]{1,0:T(8,128)(2,1)S(1)} collective-permute-done((bf16[320,2048]{1,0:T(8,128)(2,1)S(1)}, bf16[320,2048]{1,0:T(8,128)(2,1)S(1)}, u32[]{:S(2)}, u32[]{:S(2)}) %collective-permute-start.33) | collective-permute-done | bytes 1310752 | tf_op jit(solution)/shard_map/ppermute | solution.py:42
  647.3 19.1 %collective-permute-done.34 = bf16[320,2048]{1,0:T(8,128)(2,1)S(1)} collective-permute-done((bf16[320,2048]{1,0:T(8,128)(2,1)S(1)}, bf16[320,2048]{1,0:T(8,128)(2,1)S(1)}, u32[]{:S(2)}, u32[]{:S(2)}) %collective-permute-start.34) | collective-permute-done | bytes 1310752 | tf_op jit(solution)/shard_map/ppermute | solution.py:42
  669.3 6.5 convolution_convert_fusion.3
  681.6 7.7 convert_reduce_fusion.4
  689.3 13.0 %multiply_reduce_fusion = (f32[4,8,320]{2,1,0:T(8,128)S(1)}, f32[4,8,320,384]{3,2,1,0:T(8,128)}) fusion(f32[4,8,320,384]{3,2,1,0:T(8,128)} %copy-done, f32[4,8,320]{2,1,0:T(8,128)S(1)} %log_add_fusion, bf16[4,320,8,64]{1,3,2,0:T(8,128)(2,1)S(1)} %copy.136, bf16[4,64,8,64]{1,3,2,0:T(8,128)(2,1)S(1)} %copy-done.27, bf16[4,320,8,64]{1,3,2,0:T(8,128)(2,1)S(1)} %copy-done.11), kind=kOutput, calls=%fused_computation.2 | convolution fusion | flops 518248448 | bytes 34422784 | tf_op jit(solution)/shard_map/sqhd,skhd->shqk/dot_general | solution.py:263
  702.4 11.6 %multiply_convert_fusion = bf16[4,8,320,384]{3,2,1,0:T(8,128)(2,1)S(1)} fusion(f32[4,8,320,384]{3,2,1,0:T(8,128)} %get-tuple-element.208, f32[4,8,320,384]{3,2,1,0:T(8,128)} %copy-done, f32[4,8,320]{2,1,0:T(8,128)S(1)} %get-tuple-element.207, f32[4,8,320]{2,1,0:T(8,128)S(1)} %log_add_fusion), kind=kLoop, calls=%fused_computation.1 | loop fusion | flops 15728640 | bytes 39403520 | tf_op jit(solution)/shard_map/convert_element_type | solution.py:267
  734.2 4.0 reshape.390
  740.6 3.9 reshape.389
  751.0 13.7 %fusion.114 = f32[2048,1536]{1,0:T(8,128)} fusion(bf16[1280,1536]{0,1:T(8,128)(2,1)S(1)} %constant_dynamic-update-slice_fusion.4, f32[2048]{0:T(1024)S(1)} %copy-done.51, f32[2048]{0:T(1024)S(1)} %copy-done.45, f32[1280]{0:T(1024)S(1)} %copy-done.64, f32[1280]{0:T(1024)S(1)} %copy-done.54, bf16[320,2048]{1,0:T(8,128)(2,1)} %collective-permute-done.2, ...), kind=kOutput, calls=%fused_computation.273 | convolution fusion | flops 8087142400 | bytes 21784576 | tf_op jit(solution)/shard_map/dot_general | solution.py:23
  767.4 5.2 fusion.15
  777.2 5.7 convolution_convert_fusion.2
  783.0 16.7 %convolution_convert_fusion.1 = bf16[2048,2048]{1,0:T(8,128)(2,1)} fusion(bf16[1280,2048]{1,0:T(8,128)(2,1)} %get-tuple-element.120, bf16[320,2048]{1,0:T(8,128)(2,1)} %collective-permute-done.20, bf16[320,2048]{1,0:T(8,128)(2,1)} %collective-permute-done.19, bf16[320,2048]{1,0:T(8,128)(2,1)} %collective-permute-done.18, bf16[320,2048]{1,0:T(8,128)(2,1)} %add_convert_fusion), kind=kOutput, calls=%fused_computation.36 | convolution fusion | flops 10762584064 | bytes 18874368 | tf_op jit(solution)/shard_map/dot_general | solution.py:23
  799.7 19.5 %convolution_convert_fusion = bf16[2048,2048]{1,0:T(8,128)(2,1)} fusion(bf16[1280,2048]{1,0:T(8,128)(2,1)} %constant_dynamic-update-slice_fusion, f32[1280,2048]{1,0:T(8,128)} %fusion.68, f32[2048]{0:T(1024)S(1)} %dynamic_slice.55), kind=kOutput, calls=%fused_computation.35 | convolution fusion | flops 10767826944 | bytes 24125440 | tf_op jit(solution)/shard_map/dot_general | solution.py:23
  819.7 14.4 %fusion.139 = (bf16[1280,2048]{1,0:T(8,128)(2,1)S(1)}, f32[1280,2048]{1,0:T(8,128)}) fusion(bf16[1280,1536]{0,1:T(8,128)(2,1)} %copy-done.43, bf16[2048,1536]{1,0:T(8,128)(2,1)} %bitcast.118), kind=kOutput, calls=%fused_computation.290 | convolution fusion | flops 8055685120 | bytes 25952256 | tf_op jit(solution)/shard_map/dot_general | solution.py:29
  839.7 4.8 fusion.140
  848.8 47.1 %collective-permute-done.39 = bf16[64,2048]{1,0:T(8,128)(2,1)} collective-permute-done((bf16[64,2048]{1,0:T(8,128)(2,1)}, bf16[64,2048]{1,0:T(8,128)(2,1)}, u32[]{:S(2)}, u32[]{:S(2)}) %collective-permute-start.39) | collective-permute-done | bytes 262176 | tf_op jit(solution)/shard_map/ppermute | solution.py:42
  897.3 6.0 collective-permute-done.41
  904.8 5.4 fusion.118
  913.3 5.8 convert_reduce_fusion.3
  919.4 4.1 collective-permute-done.43
  927.4 19.1 %collective-permute-start.45 = (f32[4,768]{1,0:T(4,128)S(1)}, f32[4,768]{1,0:T(4,128)S(1)}, u32[]{:S(2)}, u32[]{:S(2)}) collective-permute-start(f32[4,768]{1,0:T(4,128)S(1)} %slice_select_fusion.2), channel_id=1, source_target_pairs={{0,4},{1,5},{2,6},{3,7},{4,0},{5,1},{6,2},{7,3},{8,12},{9,13},{10,... | collective-permute-start | bytes 36872 | tf_op jit(solution)/shard_map/ppermute | solution.py:86
  955.7 7.1 collective-permute-start.48
  971.8 19.7 %reduce-scatter.9.cloned.1.call-done = bf16[4,64,2048]{2,1,0:T(8,128)(2,1)} async-done(((bf16[4,512,2048]{2,1,0:T(8,128)(2,1)}), bf16[4,64,2048]{2,1,0:T(8,128)(2,1)}) %reduce-scatter.9.cloned.1.call-update) | async-done | bytes 1048592 | tf_op jit(solution)/shard_map/reduce_scatter | solution.py:97
  1007.5 74.2 %reduce-scatter.11.cloned.1.call-done = bf16[256,2048]{1,0:T(8,128)(2,1)} async-done(((bf16[2048,2048]{1,0:T(8,128)(2,1)}), bf16[256,2048]{1,0:T(8,128)(2,1)}) %reduce-scatter.11.cloned.1.call-update) | async-done | bytes 1048592 | tf_op jit(solution)/shard_map/reduce_scatter | solution.py:97
  (443 shorter events, 232.8 us)
Async XLA Ops:
  7.2 183.6 %all-gather.5.cloned.1.call-start = ((), (), s32[]{:S(2)}) async-start(), calls=%async_computation.4 | async-start | bytes 7077888 | tf_op jit(solution)/shard_map/all_gather | solution.py:93
  12.3 13.1 %collective-permute-start.8 = (bf16[1,64,1536]{2,0,1:T(2,128)(2,1)S(1)}, bf16[1,64,1536]{2,0,1:T(2,128)(2,1)}, u32[]{:S(2)}, u32[]{:S(2)}) collective-permute-start(bf16[1,64,1536]{2,0,1:T(2,128)(2,1)S(1)} %get-tuple-element.168), channel_id=1, source_target_pairs={{0,8},{8,0},{16,24},{24,16},{1,9},{9,1},{17,25},{25,17},{2,10},{10... | collective-permute-start | bytes 589832 | tf_op jit(solution)/shard_map/ppermute | solution.py:42
  15.3 19.1 %collective-permute-start.9 = (bf16[1,64,1536]{2,0,1:T(2,128)(2,1)S(1)}, bf16[1,64,1536]{2,0,1:T(2,128)(2,1)}, u32[]{:S(2)}, u32[]{:S(2)}) collective-permute-start(bf16[1,64,1536]{2,0,1:T(2,128)(2,1)S(1)} %get-tuple-element.167), channel_id=1, source_target_pairs={{0,16},{8,24},{16,0},{24,8},{1,17},{9,25},{17,1},{25,9},{2,18},{10... | collective-permute-start | bytes 589832 | tf_op jit(solution)/shard_map/ppermute | solution.py:42
  16.8 24.8 %collective-permute-start.10 = (bf16[1,64,1536]{2,0,1:T(2,128)(2,1)S(1)}, bf16[1,64,1536]{2,0,1:T(2,128)(2,1)S(1)}, u32[]{:S(2)}, u32[]{:S(2)}) collective-permute-start(bf16[1,64,1536]{2,0,1:T(2,128)(2,1)S(1)} %get-tuple-element.166), channel_id=1, source_target_pairs={{0,24},{8,16},{16,8},{24,0},{1,25},{9,17},{17,9},{25,1},{2,26},{10... | collective-permute-start | bytes 589832 | tf_op jit(solution)/shard_map/ppermute | solution.py:42
  48.2 206.3 %all-gather.7.cloned.1.call-start = ((), (), s32[]{:S(2)}) async-start(), calls=%async_computation.5 | async-start | bytes 2359296 | tf_op jit(solution)/shard_map/all_gather | solution.py:93
  48.9 340.7 %all-gather.9.cloned.1.call-start = ((), (), s32[]{:S(2)}) async-start(), calls=%async_computation.6 | async-start | bytes 9437184 | tf_op jit(solution)/shard_map/all_gather | solution.py:93
  51.5 14.9 %collective-permute-start.21 = (bf16[1,64,2048]{2,0,1:T(2,128)(2,1)S(1)}, bf16[1,64,2048]{2,0,1:T(2,128)(2,1)S(1)}, u32[]{:S(2)}, u32[]{:S(2)}) collective-permute-start(bf16[1,64,2048]{2,0,1:T(2,128)(2,1)S(1)} %get-tuple-element.159), channel_id=1, source_target_pairs={{0,8},{8,0},{16,24},{24,16},{1,9},{9,1},{17,25},{25,17},{2,10},{10... | collective-permute-start | bytes 786440 | tf_op jit(solution)/shard_map/ppermute | solution.py:42
  51.9 23.2 %collective-permute-start.22 = (bf16[1,64,2048]{2,0,1:T(2,128)(2,1)S(1)}, bf16[1,64,2048]{2,0,1:T(2,128)(2,1)}, u32[]{:S(2)}, u32[]{:S(2)}) collective-permute-start(bf16[1,64,2048]{2,0,1:T(2,128)(2,1)S(1)} %get-tuple-element.158), channel_id=1, source_target_pairs={{0,16},{8,24},{16,0},{24,8},{1,17},{9,25},{17,1},{25,9},{2,18},{10... | collective-permute-start | bytes 786440 | tf_op jit(solution)/shard_map/ppermute | solution.py:42
  53.7 29.4 %collective-permute-start.23 = (bf16[1,64,2048]{2,0,1:T(2,128)(2,1)S(1)}, bf16[1,64,2048]{2,0,1:T(2,128)(2,1)}, u32[]{:S(2)}, u32[]{:S(2)}) collective-permute-start(bf16[1,64,2048]{2,0,1:T(2,128)(2,1)S(1)} %get-tuple-element.157), channel_id=1, source_target_pairs={{0,24},{8,16},{16,8},{24,0},{1,25},{9,17},{17,9},{25,1},{2,26},{10... | collective-permute-start | bytes 786440 | tf_op jit(solution)/shard_map/ppermute | solution.py:42
  92.0 359.4 %all-gather.11.cloned.1.call-start = ((), (), s32[]{:S(2)}) async-start(), calls=%async_computation.7 | async-start | bytes 9437184 | tf_op jit(solution)/shard_map/all_gather | solution.py:93
  92.0 89.4 %collective-permute-start = (bf16[320,2048]{1,0:T(8,128)(2,1)S(1)}, bf16[320,2048]{1,0:T(8,128)(2,1)S(1)}, u32[]{:S(2)}, u32[]{:S(2)}) collective-permute-start(bf16[320,2048]{1,0:T(8,128)(2,1)S(1)} %copy-done.1), channel_id=1, source_target_pairs={{0,8},{8,0},{16,24},{24,16},{1,9},{9,1},{17,25},{25,17},{2,10},{10... | collective-permute-start | bytes 3932168 | tf_op jit(solution)/shard_map/ppermute | solution.py:42
  92.4 89.0 %collective-permute-start.1 = (bf16[320,2048]{1,0:T(8,128)(2,1)S(1)}, bf16[320,2048]{1,0:T(8,128)(2,1)}, u32[]{:S(2)}, u32[]{:S(2)}) collective-permute-start(bf16[320,2048]{1,0:T(8,128)(2,1)S(1)} %copy-done.1), channel_id=1, source_target_pairs={{0,16},{8,24},{16,0},{24,8},{1,17},{9,25},{17,1},{25,9},{2,18},{10... | collective-permute-start | bytes 3932168 | tf_op jit(solution)/shard_map/ppermute | solution.py:42
  94.2 87.2 %collective-permute-start.2 = (bf16[320,2048]{1,0:T(8,128)(2,1)S(1)}, bf16[320,2048]{1,0:T(8,128)(2,1)}, u32[]{:S(2)}, u32[]{:S(2)}) collective-permute-start(bf16[320,2048]{1,0:T(8,128)(2,1)S(1)} %copy-done.1), channel_id=1, source_target_pairs={{0,24},{8,16},{16,8},{24,0},{1,25},{9,17},{17,9},{25,1},{2,26},{10... | collective-permute-start | bytes 3932168 | tf_op jit(solution)/shard_map/ppermute | solution.py:42
  95.8 3.5 collective-permute-start.3
  96.6 56.9 %collective-permute-start.11 = (bf16[64,2048]{1,0:T(8,128)(2,1)}, bf16[64,2048]{1,0:T(8,128)(2,1)S(1)}, u32[]{:S(2)}, u32[]{:S(2)}) collective-permute-start(bf16[64,2048]{1,0:T(8,128)(2,1)} %pad.9), channel_id=1, source_target_pairs={{0,1},{1,2},{2,3},{3,4},{4,5},{5,6},{6,7},{7,8},{8,9},{9,10},{10,1... | collective-permute-start | bytes 786440 | tf_op jit(solution)/shard_map/ppermute | solution.py:169
  99.0 855.8 %reduce-scatter.5.cloned.1.call-start = ((), (), s32[]{:S(2)}) async-start(), calls=%async_computation.8 | async-start | bytes 7077888 | tf_op jit(solution)/shard_map/reduce_scatter | solution.py:97
  99.4 4.6 collective-permute-start.4
  104.0 4.9 collective-permute-start.5
  109.0 37.4 %collective-permute-start.6 = (bf16[8,818]{1,0:T(8,128)(2,1)S(1)}, bf16[8,818]{1,0:T(8,128)(2,1)S(1)}, u32[]{:S(2)}, u32[]{:S(2)}) collective-permute-start(bf16[8,818]{1,0:T(8,128)(2,1)S(1)} %pad_maximum_fusion.17), channel_id=1, source_target_pairs={{0,8},{1,9},{2,10},{3,11},{4,12},{5,13},{6,14},{7,15},{8,0},{9,1},... | collective-permute-start | bytes 39272 | tf_op jit(solution)/shard_map/ppermute | solution.py:71
  146.4 3.9 collective-permute-start.7
  150.3 11.9 %collective-permute-start.12 = (bf16[64,2048]{1,0:T(8,128)(2,1)}, bf16[64,2048]{1,0:T(8,128)(2,1)S(1)}, u32[]{:S(2)}, u32[]{:S(2)}) collective-permute-start(bf16[64,2048]{1,0:T(8,128)(2,1)} %pad.9), channel_id=1, source_target_pairs={{7,0},{8,1},{9,2},{10,3},{11,4},{12,5},{13,6},{14,7},{0,9},{1,10},... | collective-permute-start | bytes 786440 | tf_op jit(solution)/shard_map/ppermute | solution.py:169
  153.5 68.4 %copy-start.5 = (bf16[64,2048]{1,0:T(8,128)(2,1)}, bf16[64,2048]{1,0:T(8,128)(2,1)S(1)}, u32[]{:S(2)}) copy-start(bf16[64,2048]{1,0:T(8,128)(2,1)S(1)} %collective-permute-done.11) | copy-start | bytes 786436
  153.5 23.1 %collective-permute-start.13 = (bf16[64,2048]{1,0:T(8,128)(2,1)}, bf16[64,2048]{1,0:T(8,128)(2,1)S(1)}, u32[]{:S(2)}, u32[]{:S(2)}) collective-permute-start(bf16[64,2048]{1,0:T(8,128)(2,1)} %pad.9), channel_id=1, source_target_pairs={{15,0},{16,1},{17,2},{18,3},{19,4},{20,5},{21,6},{22,7},{23,8},{24... | collective-permute-start | bytes 786440 | tf_op jit(solution)/shard_map/ppermute | solution.py:169
  162.3 16.5 %collective-permute-start.14 = (bf16[64,2048]{1,0:T(8,128)(2,1)}, bf16[64,2048]{1,0:T(8,128)(2,1)}, u32[]{:S(2)}, u32[]{:S(2)}) collective-permute-start(bf16[64,2048]{1,0:T(8,128)(2,1)} %pad.9), channel_id=1, source_target_pairs={{23,0},{24,1},{25,2},{26,3},{27,4},{28,5},{29,6},{30,7},{15,8},{16... | collective-permute-start | bytes 786440 | tf_op jit(solution)/shard_map/ppermute | solution.py:169
  264.2 33.9 %collective-permute-start.15 = (bf16[320,2048]{1,0:T(8,128)(2,1)}, bf16[320,2048]{1,0:T(8,128)(2,1)S(1)}, u32[]{:S(2)}, u32[]{:S(2)}) collective-permute-start(bf16[320,2048]{1,0:T(8,128)(2,1)} %get-tuple-element.141), channel_id=1, source_target_pairs={{0,8},{8,0},{16,24},{24,16},{1,9},{9,1},{17,25},{25,17},{2,10},{10... | collective-permute-start | bytes 3932168 | tf_op jit(solution)/shard_map/ppermute | solution.py:42
  268.2 60.0 %collective-permute-start.16 = (bf16[320,2048]{1,0:T(8,128)(2,1)}, bf16[320,2048]{1,0:T(8,128)(2,1)S(1)}, u32[]{:S(2)}, u32[]{:S(2)}) collective-permute-start(bf16[320,2048]{1,0:T(8,128)(2,1)} %get-tuple-element.143), channel_id=1, source_target_pairs={{0,16},{8,24},{16,0},{24,8},{1,17},{9,25},{17,1},{25,9},{2,18},{10... | collective-permute-start | bytes 3932168 | tf_op jit(solution)/shard_map/ppermute | solution.py:42
  268.2 60.0 %collective-permute-start.17 = (bf16[320,2048]{1,0:T(8,128)(2,1)}, bf16[320,2048]{1,0:T(8,128)(2,1)}, u32[]{:S(2)}, u32[]{:S(2)}) collective-permute-start(bf16[320,2048]{1,0:T(8,128)(2,1)} %get-tuple-element.142), channel_id=1, source_target_pairs={{0,24},{8,16},{16,8},{24,0},{1,25},{9,17},{17,9},{25,1},{2,26},{10... | collective-permute-start | bytes 3932168 | tf_op jit(solution)/shard_map/ppermute | solution.py:42
  269.7 84.8 %collective-permute-start.27 = (bf16[320,2048]{1,0:T(8,128)(2,1)}, bf16[320,2048]{1,0:T(8,128)(2,1)}, u32[]{:S(2)}, u32[]{:S(2)}) collective-permute-start(bf16[320,2048]{1,0:T(8,128)(2,1)} %param.39), channel_id=1, source_target_pairs={{0,8},{8,0},{16,24},{24,16},{1,9},{9,1},{17,25},{25,17},{2,10},{10... | collective-permute-start | bytes 3932168 | tf_op jit(solution)/shard_map/ppermute | solution.py:42
  271.7 112.8 %collective-permute-start.28 = (bf16[320,2048]{1,0:T(8,128)(2,1)}, bf16[320,2048]{1,0:T(8,128)(2,1)}, u32[]{:S(2)}, u32[]{:S(2)}) collective-permute-start(bf16[320,2048]{1,0:T(8,128)(2,1)} %param.39), channel_id=1, source_target_pairs={{0,16},{8,24},{16,0},{24,8},{1,17},{9,25},{17,1},{25,9},{2,18},{10... | collective-permute-start | bytes 3932168 | tf_op jit(solution)/shard_map/ppermute | solution.py:42
  298.1 88.9 %collective-permute-start.29 = (bf16[320,2048]{1,0:T(8,128)(2,1)}, bf16[320,2048]{1,0:T(8,128)(2,1)}, u32[]{:S(2)}, u32[]{:S(2)}) collective-permute-start(bf16[320,2048]{1,0:T(8,128)(2,1)} %param.39), channel_id=1, source_target_pairs={{0,24},{8,16},{16,8},{24,0},{1,25},{9,17},{17,9},{25,1},{2,26},{10... | collective-permute-start | bytes 3932168 | tf_op jit(solution)/shard_map/ppermute | solution.py:42
  336.3 74.3 %collective-permute-start.18 = (bf16[320,2048]{1,0:T(8,128)(2,1)}, bf16[320,2048]{1,0:T(8,128)(2,1)}, u32[]{:S(2)}, u32[]{:S(2)}) collective-permute-start(bf16[320,2048]{1,0:T(8,128)(2,1)} %add_convert_fusion), channel_id=1, source_target_pairs={{0,8},{8,0},{16,24},{24,16},{1,9},{9,1},{17,25},{25,17},{2,10},{10... | collective-permute-start | bytes 3932168 | tf_op jit(solution)/shard_map/ppermute | solution.py:42
  336.3 74.3 %collective-permute-start.19 = (bf16[320,2048]{1,0:T(8,128)(2,1)}, bf16[320,2048]{1,0:T(8,128)(2,1)}, u32[]{:S(2)}, u32[]{:S(2)}) collective-permute-start(bf16[320,2048]{1,0:T(8,128)(2,1)} %add_convert_fusion), channel_id=1, source_target_pairs={{0,16},{8,24},{16,0},{24,8},{1,17},{9,25},{17,1},{25,9},{2,18},{10... | collective-permute-start | bytes 3932168 | tf_op jit(solution)/shard_map/ppermute | solution.py:42
  354.4 77.7 %collective-permute-start.20 = (bf16[320,2048]{1,0:T(8,128)(2,1)}, bf16[320,2048]{1,0:T(8,128)(2,1)}, u32[]{:S(2)}, u32[]{:S(2)}) collective-permute-start(bf16[320,2048]{1,0:T(8,128)(2,1)} %add_convert_fusion), channel_id=1, source_target_pairs={{0,24},{8,16},{16,8},{24,0},{1,25},{9,17},{17,9},{25,1},{2,26},{10... | collective-permute-start | bytes 3932168 | tf_op jit(solution)/shard_map/ppermute | solution.py:42
  497.3 31.8 %collective-permute-start.30 = (bf16[320,2048]{1,0:T(8,128)(2,1)S(1)}, bf16[320,2048]{1,0:T(8,128)(2,1)}, u32[]{:S(2)}, u32[]{:S(2)}) collective-permute-start(bf16[320,2048]{1,0:T(8,128)(2,1)S(1)} %get-tuple-element.135), channel_id=1, source_target_pairs={{0,8},{8,0},{16,24},{24,16},{1,9},{9,1},{17,25},{25,17},{2,10},{10... | collective-permute-start | bytes 3932168 | tf_op jit(solution)/shard_map/ppermute | solution.py:42
  498.2 59.0 %collective-permute-start.31 = (bf16[320,2048]{1,0:T(8,128)(2,1)}, bf16[320,2048]{1,0:T(8,128)(2,1)}, u32[]{:S(2)}, u32[]{:S(2)}) collective-permute-start(bf16[320,2048]{1,0:T(8,128)(2,1)} %get-tuple-element.137), channel_id=1, source_target_pairs={{0,16},{8,24},{16,0},{24,8},{1,17},{9,25},{17,1},{25,9},{2,18},{10... | collective-permute-start | bytes 3932168 | tf_op jit(solution)/shard_map/ppermute | solution.py:42
  499.6 57.8 %collective-permute-start.32 = (bf16[320,2048]{1,0:T(8,128)(2,1)}, bf16[320,2048]{1,0:T(8,128)(2,1)}, u32[]{:S(2)}, u32[]{:S(2)}) collective-permute-start(bf16[320,2048]{1,0:T(8,128)(2,1)} %get-tuple-element.136), channel_id=1, source_target_pairs={{0,24},{8,16},{16,8},{24,0},{1,25},{9,17},{17,9},{25,1},{2,26},{10... | collective-permute-start | bytes 3932168 | tf_op jit(solution)/shard_map/ppermute | solution.py:42
  522.6 62.8 %collective-permute-start.24 = (bf16[320,2048]{1,0:T(8,128)(2,1)}, bf16[320,2048]{1,0:T(8,128)(2,1)}, u32[]{:S(2)}, u32[]{:S(2)}) collective-permute-start(bf16[320,2048]{1,0:T(8,128)(2,1)} %get-tuple-element.138), channel_id=1, source_target_pairs={{0,8},{8,0},{16,24},{24,16},{1,9},{9,1},{17,25},{25,17},{2,10},{10... | collective-permute-start | bytes 3932168 | tf_op jit(solution)/shard_map/ppermute | solution.py:42
  523.4 83.2 %collective-permute-start.25 = (bf16[320,2048]{1,0:T(8,128)(2,1)}, bf16[320,2048]{1,0:T(8,128)(2,1)}, u32[]{:S(2)}, u32[]{:S(2)}) collective-permute-start(bf16[320,2048]{1,0:T(8,128)(2,1)} %get-tuple-element.140), channel_id=1, source_target_pairs={{0,16},{8,24},{16,0},{24,8},{1,17},{9,25},{17,1},{25,9},{2,18},{10... | collective-permute-start | bytes 3932168 | tf_op jit(solution)/shard_map/ppermute | solution.py:42
  529.1 77.5 %collective-permute-start.26 = (bf16[320,2048]{1,0:T(8,128)(2,1)}, bf16[320,2048]{1,0:T(8,128)(2,1)}, u32[]{:S(2)}, u32[]{:S(2)}) collective-permute-start(bf16[320,2048]{1,0:T(8,128)(2,1)} %get-tuple-element.139), channel_id=1, source_target_pairs={{0,24},{8,16},{16,8},{24,0},{1,25},{9,17},{17,9},{25,1},{2,26},{10... | collective-permute-start | bytes 3932168 | tf_op jit(solution)/shard_map/ppermute | solution.py:42
  615.6 31.7 %collective-permute-start.33 = (bf16[320,2048]{1,0:T(8,128)(2,1)S(1)}, bf16[320,2048]{1,0:T(8,128)(2,1)S(1)}, u32[]{:S(2)}, u32[]{:S(2)}) collective-permute-start(bf16[320,2048]{1,0:T(8,128)(2,1)S(1)} %get-tuple-element.122), channel_id=1, source_target_pairs={{0,8},{8,0},{16,24},{24,16},{1,9},{9,1},{17,25},{25,17},{2,10},{10... | collective-permute-start | bytes 3932168 | tf_op jit(solution)/shard_map/ppermute | solution.py:42
  617.3 49.1 %collective-permute-start.34 = (bf16[320,2048]{1,0:T(8,128)(2,1)S(1)}, bf16[320,2048]{1,0:T(8,128)(2,1)S(1)}, u32[]{:S(2)}, u32[]{:S(2)}) collective-permute-start(bf16[320,2048]{1,0:T(8,128)(2,1)S(1)} %get-tuple-element.122), channel_id=1, source_target_pairs={{0,16},{8,24},{16,0},{24,8},{1,17},{9,25},{17,1},{25,9},{2,18},{10... | collective-permute-start | bytes 3932168 | tf_op jit(solution)/shard_map/ppermute | solution.py:42
  617.6 50.6 %collective-permute-start.35 = (bf16[320,2048]{1,0:T(8,128)(2,1)S(1)}, bf16[320,2048]{1,0:T(8,128)(2,1)S(1)}, u32[]{:S(2)}, u32[]{:S(2)}) collective-permute-start(bf16[320,2048]{1,0:T(8,128)(2,1)S(1)} %get-tuple-element.122), channel_id=1, source_target_pairs={{0,24},{8,16},{16,8},{24,0},{1,25},{9,17},{17,9},{25,1},{2,26},{10... | collective-permute-start | bytes 3932168 | tf_op jit(solution)/shard_map/ppermute | solution.py:42
  775.9 187.5 %reduce-scatter.7.cloned.1.call-start = ((), (), s32[]{:S(2)}) async-start(), calls=%async_computation.9 | async-start | bytes 2359296 | tf_op jit(solution)/shard_map/reduce_scatter | solution.py:97
  782.9 208.6 %reduce-scatter.9.cloned.1.call-start = ((), (), s32[]{:S(2)}) async-start(), calls=%async_computation.10 | async-start | bytes 9437184 | tf_op jit(solution)/shard_map/reduce_scatter | solution.py:97
  799.7 282.1 %reduce-scatter.11.cloned.1.call-start = ((), (), s32[]{:S(2)}) async-start(), calls=%async_computation.11 | async-start | bytes 9437184 | tf_op jit(solution)/shard_map/reduce_scatter | solution.py:97
  836.1 68.7 %collective-permute-start.36 = (bf16[320,2048]{1,0:T(8,128)(2,1)}, bf16[320,2048]{1,0:T(8,128)(2,1)S(1)}, u32[]{:S(2)}, u32[]{:S(2)}) collective-permute-start(bf16[320,2048]{1,0:T(8,128)(2,1)} %get-tuple-element.132), channel_id=1, source_target_pairs={{0,8},{8,0},{16,24},{24,16},{1,9},{9,1},{17,25},{25,17},{2,10},{10... | collective-permute-start | bytes 3932168 | tf_op jit(solution)/shard_map/ppermute | solution.py:42
  837.8 67.1 %collective-permute-start.37 = (bf16[320,2048]{1,0:T(8,128)(2,1)}, bf16[320,2048]{1,0:T(8,128)(2,1)}, u32[]{:S(2)}, u32[]{:S(2)}) collective-permute-start(bf16[320,2048]{1,0:T(8,128)(2,1)} %get-tuple-element.134), channel_id=1, source_target_pairs={{0,16},{8,24},{16,0},{24,8},{1,17},{9,25},{17,1},{25,9},{2,18},{10... | collective-permute-start | bytes 3932168 | tf_op jit(solution)/shard_map/ppermute | solution.py:42
  839.5 65.3 %collective-permute-start.38 = (bf16[320,2048]{1,0:T(8,128)(2,1)}, bf16[320,2048]{1,0:T(8,128)(2,1)}, u32[]{:S(2)}, u32[]{:S(2)}) collective-permute-start(bf16[320,2048]{1,0:T(8,128)(2,1)} %get-tuple-element.133), channel_id=1, source_target_pairs={{0,24},{8,16},{16,8},{24,0},{1,25},{9,17},{17,9},{25,1},{2,26},{10... | collective-permute-start | bytes 3932168 | tf_op jit(solution)/shard_map/ppermute | solution.py:42
  845.3 50.6 %collective-permute-start.39 = (bf16[64,2048]{1,0:T(8,128)(2,1)}, bf16[64,2048]{1,0:T(8,128)(2,1)}, u32[]{:S(2)}, u32[]{:S(2)}) collective-permute-start(bf16[64,2048]{1,0:T(8,128)(2,1)} %get-tuple-element.154), channel_id=1, source_target_pairs={{0,8},{8,0},{16,24},{24,16},{1,9},{9,1},{17,25},{25,17},{2,10},{10... | collective-permute-start | bytes 786440 | tf_op jit(solution)/shard_map/ppermute | solution.py:42
  847.0 50.3 %collective-permute-start.40 = (bf16[64,2048]{1,0:T(8,128)(2,1)}, bf16[64,2048]{1,0:T(8,128)(2,1)}, u32[]{:S(2)}, u32[]{:S(2)}) collective-permute-start(bf16[64,2048]{1,0:T(8,128)(2,1)} %get-tuple-element.156), channel_id=1, source_target_pairs={{0,16},{8,24},{16,0},{24,8},{1,17},{9,25},{17,1},{25,9},{2,18},{10... | collective-permute-start | bytes 786440 | tf_op jit(solution)/shard_map/ppermute | solution.py:42
  895.9 7.4 collective-permute-start.41
  919.3 4.2 collective-permute-start.43
  923.5 3.9 collective-permute-start.44
  927.4 21.3 %collective-permute-start.45 = (f32[4,768]{1,0:T(4,128)S(1)}, f32[4,768]{1,0:T(4,128)S(1)}, u32[]{:S(2)}, u32[]{:S(2)}) collective-permute-start(f32[4,768]{1,0:T(4,128)S(1)} %slice_select_fusion.2), channel_id=1, source_target_pairs={{0,4},{1,5},{2,6},{3,7},{4,0},{5,1},{6,2},{7,3},{8,12},{9,13},{10,... | collective-permute-start | bytes 36872 | tf_op jit(solution)/shard_map/ppermute | solution.py:86
  948.7 4.1 collective-permute-start.46
  948.9 4.0 collective-permute-start.42
  952.8 1.3 collective-permute-start.47
  955.7 10.7 collective-permute-start.48
  968.2 25.8 %collective-permute-start.49 = (bf16[1,64,1536]{2,1,0:T(8,128)(2,1)S(1)}, bf16[1,64,1536]{2,1,0:T(8,128)(2,1)S(1)}, u32[]{:S(2)}, u32[]{:S(2)}) collective-permute-start(bf16[1,64,1536]{2,1,0:T(8,128)(2,1)S(1)} %get-tuple-element.164), channel_id=1, source_target_pairs={{0,16},{8,24},{16,0},{24,8},{1,17},{9,25},{17,1},{25,9},{2,18},{10... | collective-permute-start | bytes 589832 | tf_op jit(solution)/shard_map/ppermute | solution.py:42
  971.8 22.9 %collective-permute-start.50 = (bf16[1,64,1536]{2,1,0:T(8,128)(2,1)S(1)}, bf16[1,64,1536]{2,1,0:T(8,128)(2,1)S(1)}, u32[]{:S(2)}, u32[]{:S(2)}) collective-permute-start(bf16[1,64,1536]{2,1,0:T(8,128)(2,1)S(1)} %get-tuple-element.163), channel_id=1, source_target_pairs={{0,24},{8,16},{16,8},{24,0},{1,25},{9,17},{17,9},{25,1},{2,26},{10... | collective-permute-start | bytes 589832 | tf_op jit(solution)/shard_map/ppermute | solution.py:42
  992.4 6.4 collective-permute-start.51
  1000.7 83.8 %collective-permute-start.52 = (bf16[1,64,2048]{2,1,0:T(8,128)(2,1)S(1)}, bf16[1,64,2048]{2,1,0:T(8,128)(2,1)S(1)}, u32[]{:S(2)}, u32[]{:S(2)}) collective-permute-start(bf16[1,64,2048]{2,1,0:T(8,128)(2,1)S(1)} %get-tuple-element.152), channel_id=1, source_target_pairs={{0,16},{8,24},{16,0},{24,8},{1,17},{9,25},{17,1},{25,9},{2,18},{10... | collective-permute-start | bytes 786440 | tf_op jit(solution)/shard_map/ppermute | solution.py:42
  1002.2 82.4 %collective-permute-start.53 = (bf16[1,64,2048]{2,1,0:T(8,128)(2,1)S(1)}, bf16[1,64,2048]{2,1,0:T(8,128)(2,1)S(1)}, u32[]{:S(2)}, u32[]{:S(2)}) collective-permute-start(bf16[1,64,2048]{2,1,0:T(8,128)(2,1)S(1)} %get-tuple-element.151), channel_id=1, source_target_pairs={{0,24},{8,16},{16,8},{24,0},{1,25},{9,17},{17,9},{25,1},{2,26},{10... | collective-permute-start | bytes 786440 | tf_op jit(solution)/shard_map/ppermute | solution.py:42
  1005.8 78.7 %copy-start.21 = (bf16[4,64,2048]{2,1,0:T(8,128)(2,1)S(1)}, bf16[4,64,2048]{2,1,0:T(8,128)(2,1)}, u32[]{:S(2)}) copy-start(bf16[4,64,2048]{2,1,0:T(8,128)(2,1)} %get-tuple-element.153) | copy-start | bytes 3145732
  (82 other events, 1513.9 us)
Sparse Core Ops, SparseCore 0:
  48.3 68.0 all-gather.4
  118.0 26.9 all-gather.6
  146.5 88.5 all-gather.8
  236.6 80.3 all-gather.10
  776.0 85.1 reduce-scatter.4
  863.9 33.8 reduce-scatter.6
  900.1 91.3 reduce-scatter.8
  993.8 87.9 reduce-scatter.10

commit v2 on v1

v2 whole, which is shorter than its diff:
```python
import jax
import jax.numpy as jnp
from jax import lax
from jax.experimental import pallas as pl
from jax.experimental.pallas import tpu as pltpu
from jax.sharding import PartitionSpec as P

F32, BF16 = jnp.float32, jnp.bfloat16
HEADS = 32
BOTH = ("fsdp", "dp")
HEAD = 64
PAIR = 2 * HEAD
PRIOR_ROWS = 64
NORM_ROWS = 64
MASKED = -1e30
GELU_A, GELU_B = 0.7978845608028654, 0.044715
VMEM_LIMIT = 60 * 1024 * 1024
VMEM = pl.BlockSpec(memory_space=pltpu.VMEM)
HBM = pl.BlockSpec(memory_space=pl.ANY)


def dot(left, right):
    return jnp.dot(left, right, preferred_element_type=F32)


def dot_t(left, right):
    return lax.dot_general(left, right, (((1,), (1,)), ((), ())), preferred_element_type=F32)


def t_dot(left, right):
    return lax.dot_general(left, right, (((0,), (0,)), ((), ())), preferred_element_type=F32)


def norm_parts(values):
    centre = values - jnp.mean(values, axis=-1, keepdims=True)
    spread = jnp.mean(centre * centre, axis=-1, keepdims=True)
    return centre, lax.rsqrt(spread + 1e-05)


def norm_apply(values, norm_gain, norm_bias):
    centre, inverse = norm_parts(values)
    return centre * inverse * norm_gain + norm_bias


def in_pair(half, rows):
    lane = lax.broadcasted_iota(jnp.int32, (rows, PAIR), 1)
    return (lane >= HEAD) if half else (lane < HEAD)


def pair_at(base, pair):
    return pl.ds(pl.multiple_of(base + pair * PAIR, PAIR), PAIR)


def load_blocks(hbm, scratch, sems):
    copies = [
        pltpu.make_async_copy(hbm.at[:, block], scratch.at[block], sems.at[block])
        for block in range(scratch.shape[0])
    ]
    for copy in copies:
        copy.start()
    return copies


def load_rows(parts, scratch, sems):
    copies = []
    at = 0
    for index, part in enumerate(parts):
        rows = part.shape[0]
        copies.append(
            pltpu.make_async_copy(part, scratch.at[pl.ds(at, rows)], sems.at[index])
        )
        at += rows
    for copy in copies:
        copy.start()
    return copies


def wait_all(copies):
    for copy in copies:
        copy.wait()


def rows_of(ref, columns):
    value = ref[:, :, :, columns]
    return value.reshape(-1, value.shape[-1])


def block_of(ref, block, columns):
    value = ref[block, :, :, columns]
    return value.reshape(-1, value.shape[-1])


COST = 230_000_000


def kernel_params(cost):
    return dict(
        compiler_params=pltpu.CompilerParams(vmem_limit_bytes=VMEM_LIMIT),
        cost_estimate=pl.CostEstimate(flops=cost * COST, bytes_accessed=1, transcendentals=0),
    )


def shape_of(rows, columns, dtype=BF16):
    return jax.ShapeDtypeStruct((rows, columns), dtype)


def attn_forward_kernel(
    x_ref, prior_ref, gain_ref, bias_ref, off_ref, ok_ref, attn_hbm,
    low_ref, qkv_ref, lse_ref, mixed_ref, part_ref, weights, mask, sems,
):
    members = weights.shape[0]
    cols = mixed_ref.shape[1]
    seg = x_ref.shape[0]
    keys = low_ref.shape[0]
    copies = load_blocks(attn_hbm, weights, sems)
    row = lax.broadcasted_iota(jnp.int32, (seg, keys), 0)
    col = lax.broadcasted_iota(jnp.int32, (seg, keys), 1)
    mask[...] = jnp.where(jnp.logical_or(col <= row, ok_ref[...] > 0.5), 0.0, MASKED)
    gain, bias = gain_ref[...], bias_ref[...]

    def norm_rows(block, _):
        at = pl.ds(pl.multiple_of(block * NORM_ROWS, NORM_ROWS), NORM_ROWS)
        low_ref[at, :] = norm_apply(x_ref[at, :].astype(F32), gain, bias).astype(BF16)
        return _

    lax.fori_loop(0, seg // NORM_ROWS, norm_rows, 0)
    low_ref[seg:, :] = norm_apply(prior_ref[...].astype(F32), gain, bias).astype(BF16)
    wait_all(copies)

    def project(part, _):
        at = pl.ds(pl.multiple_of(part * cols, PAIR), cols)
        qkv_ref[:, at] = (dot(low_ref[...], rows_of(weights, at)) + off_ref[:, at]).astype(BF16)
        return _

    lax.fori_loop(0, 3, project, 0)
    lane = lax.broadcasted_iota(jnp.int32, (seg, PAIR), 1)

    def attend(pair, _):
        query = qkv_ref[:seg, pair_at(0, pair)] * jnp.asarray(HEAD**-0.5, BF16)
        key = qkv_ref[:, pair_at(cols, pair)]
        value = qkv_ref[:, pair_at(2 * cols, pair)]
        merged = None
        for half in range(2):
            inside = in_pair(half, seg)
            scores = dot_t(jnp.where(inside, query, jnp.zeros_like(query)), key) + mask[...]
            row_max = jnp.max(scores, axis=-1, keepdims=True)
            expo = jnp.exp(scores - row_max)
            row_total = jnp.sum(expo, axis=-1, keepdims=True)
            log_total = row_max + jnp.log(row_total)
            lse_ref[...] = jnp.where(lane == 2 * pair + half, log_total, lse_ref[...])
            mixed = dot((expo * (1.0 / row_total)).astype(BF16), value)
            merged = mixed if merged is None else jnp.where(inside, mixed, merged)
        mixed_ref[:, pair_at(0, pair)] = merged.astype(BF16)
        return _

    lse_ref[...] = jnp.zeros_like(lse_ref)
    lax.fori_loop(0, cols // PAIR, attend, 0)

    def project_out(block, _):
        at = pl.ds(pl.multiple_of(block * cols, PAIR), cols)
        weight = block_of(weights, block, pl.ds(3 * cols, cols))
        part_ref[:, at] = dot(mixed_ref[...], weight).astype(part_ref.dtype)
        return _

    lax.fori_loop(0, members, project_out, 0)


def attn_forward(x, prior, gain, bias, off, ok_row, attn_w, part_type):
    seg, width = x.shape
    keys = seg + PRIOR_ROWS
    columns, members, share, wide = attn_w.shape
    cols = wide // 4
    return pl.pallas_call(
        attn_forward_kernel,
        out_shape=(
            shape_of(keys, width),
            shape_of(keys, 3 * cols),
            shape_of(seg, PAIR, F32),
            shape_of(seg, cols),
            shape_of(seg, width, part_type),
        ),
        in_specs=[VMEM] * 6 + [HBM],
        out_specs=(VMEM,) * 5,
        scratch_shapes=[
            pltpu.VMEM((members, columns, share, wide), BF16),
            pltpu.VMEM((seg, keys), F32),
            pltpu.SemaphoreType.DMA((members,)),
        ],
        name="attn_forward",
        **kernel_params(15),
    )(x, prior, gain, bias, off, ok_row, attn_w)


def attn_backward_kernel(
    branch_ref, qkv_ref, lse_ref, ok_ref, attn_hbm,
    grads_ref, sums_ref, joined_ref, weights, mask, lse_t, mixed_grad, sems,
):
    members = weights.shape[0]
    cols = mixed_grad.shape[1]
    seg = branch_ref.shape[0]
    keys = qkv_ref.shape[0]
    copies = load_blocks(attn_hbm, weights, sems)
    row = lax.broadcasted_iota(jnp.int32, (keys, seg), 0)
    col = lax.broadcasted_iota(jnp.int32, (keys, seg), 1)
    mask[...] = jnp.where(jnp.logical_or(row <= col, ok_ref[:, :1] > 0.5), 0.0, MASKED)
    lse_t[...] = lse_ref[...].T
    grads_ref[seg:, :cols] = jnp.zeros((keys - seg, cols), BF16)
    total = 0.0
    for block in range(members):
        copies[block].wait()
        weight = block_of(weights, block, pl.ds(3 * cols, cols))
        total = total + dot_t(branch_ref[:, block * cols : (block + 1) * cols], weight)
    mixed_grad[...] = total.astype(BF16)

    def attend(pair, _):
        query = qkv_ref[:seg, pair_at(0, pair)]
        scaled = query * jnp.asarray(HEAD**-0.5, BF16)
        key = qkv_ref[:, pair_at(cols, pair)]
        value = qkv_ref[:, pair_at(2 * cols, pair)]
        mixed = mixed_grad[:, pair_at(0, pair)]
        query_grad = key_grad = value_grad = 0.0
        for half in range(2):
            inside, inside_key = in_pair(half, seg), in_pair(half, keys)
            zero = jnp.zeros_like(query)
            scores = dot_t(key, jnp.where(inside, scaled, zero)) + mask[...]
            probs = jnp.exp(scores - lse_t[pl.ds(2 * pair + half, 1), :])
            mixed_half = jnp.where(inside, mixed, zero)
            prob_grad = dot_t(value, mixed_half)
            value_grad = value_grad + dot(probs.astype(BF16), mixed_half)
            delta = jnp.sum(prob_grad * probs, axis=0, keepdims=True)
            score_grad = (probs * (prob_grad - delta)).astype(BF16)
            key_grad = key_grad + dot(score_grad, jnp.where(inside, query, zero))
            key_half = jnp.where(inside_key, key, jnp.zeros_like(key))
            query_grad = query_grad + t_dot(score_grad, key_half)
        grads_ref[:seg, pair_at(0, pair)] = (query_grad * HEAD**-0.5).astype(BF16)
        grads_ref[:, pair_at(cols, pair)] = (key_grad * HEAD**-0.5).astype(BF16)
        grads_ref[:, pair_at(2 * cols, pair)] = value_grad.astype(BF16)
        return _

    lax.fori_loop(0, cols // PAIR, attend, 0)

    def back(block, _):
        weight = block_of(weights, block, pl.ds(0, 3 * cols))
        at = pl.ds(pl.multiple_of(block * cols, PAIR), cols)
        joined_ref[:, at] = dot_t(grads_ref[...], weight).astype(joined_ref.dtype)
        return _

    lax.fori_loop(0, members, back, 0)
    sums_ref[...] = jnp.sum(grads_ref[...].astype(F32), axis=0, keepdims=True)


def attn_backward(branch, qkv, lse, ok_col, attn_w, joined_type):
    seg, width = branch.shape
    keys = qkv.shape[0]
    columns, members, share, wide = attn_w.shape
    cols = wide // 4
    return pl.pallas_call(
        attn_backward_kernel,
        out_shape=(
            shape_of(keys, 3 * cols),
            shape_of(1, 3 * cols, F32),
            shape_of(keys, width, joined_type),
        ),
        in_specs=[VMEM] * 4 + [HBM],
        out_specs=(VMEM,) * 3,
        scratch_shapes=[
            pltpu.VMEM((members, columns, share, wide), BF16),
            pltpu.VMEM((keys, seg), F32),
            pltpu.VMEM((PAIR, seg), F32),
            pltpu.VMEM((seg, cols), BF16),
            pltpu.SemaphoreType.DMA((members,)),
        ],
        name="attn_backward",
        **kernel_params(14),
    )(branch, qkv, lse, ok_col, attn_w)


def ffn_hidden(seconds, off, up_w):
    count = len(seconds)
    seg, width = seconds[0].shape
    columns, members, share, wide = up_w.shape
    step = 512

    def kernel(*refs):
        off_ref, up_hbm, hidden_ref, slope_ref, second, up, sems = refs[count:]
        copies = load_blocks(up_hbm, up, sems) + load_rows(refs[:count], second, sems.at[pl.ds(members, count)])
        wait_all(copies)

        def hidden(block, _):
            at = pl.ds(pl.multiple_of(block * step, step), step)
            weight = rows_of(up, at)
            for index in range(count):
                rows = pl.ds(index * seg, seg)
                pre = dot(second[rows, :], weight) + off_ref[:, at]
                square = pre * pre
                bent = jnp.tanh(GELU_A * pre * (1.0 + GELU_B * square))
                gate = 0.5 * (1.0 + bent)
                hidden_ref[rows, at] = (pre * gate).astype(BF16)
                rise = 0.5 * pre * (1.0 - bent * bent) * (GELU_A * (1.0 + 3.0 * GELU_B * square))
                slope_ref[rows, at] = (gate + rise).astype(BF16)
            return _

        lax.fori_loop(0, wide // step, hidden, 0)

    return pl.pallas_call(
        kernel,
        out_shape=(shape_of(count * seg, wide), shape_of(count * seg, wide)),
        in_specs=[HBM] * count + [VMEM, HBM],
        out_specs=(VMEM,) * 2,
        scratch_shapes=[
            pltpu.VMEM((count * seg, width), BF16),
            pltpu.VMEM((members, columns, share, wide), BF16),
            pltpu.SemaphoreType.DMA((members + count,)),
        ],
        name="ffn_hidden",
        **kernel_params(24),
    )(*seconds, off, up_w)


def ffn_back(cots, slope, start, up_w, down_w, types):
    count = len(cots)
    seg, width = cots[0].shape
    columns, members, share, wide = up_w.shape
    step = 512
    rows = count * seg

    def kernel(*refs):
        slope_hbm, up_hbm, down_hbm, pre_ref, sums_ref = refs[count : count + 5]
        backs = refs[count + 5 : 2 * count + 5]
        cot, slope_here, up, down, sems = refs[2 * count + 5 :]
        first = load_rows(refs[:count], cot, sems)
        first += load_rows([slope_hbm.at[pl.ds(start, rows)]], slope_here, sems.at[pl.ds(count, 1)])
        first += load_rows([down_hbm], down, sems.at[pl.ds(count + 1, 1)])
        later = load_blocks(up_hbm, up, sems.at[pl.ds(count + 2, members)])
        wait_all(first)

        def grad(block, _):
            at = pl.ds(pl.multiple_of(block * step, step), step)
            value = dot_t(cot[...], down[at, :]) * slope_here[:, at].astype(F32)
            value = value.astype(BF16)
            pre_ref[:, at] = value
            sums_ref[:, at] = jnp.sum(value.astype(F32), axis=0, keepdims=True)
            return _

        lax.fori_loop(0, wide // step, grad, 0)
        wait_all(later)
        deep = columns * share

        def back(block, _):
            at = pl.ds(pl.multiple_of(block * deep, PAIR), deep)
            value = dot_t(pre_ref[...], up[block].reshape(deep, wide))
            for index in range(count):
                backs[index][:, at] = value[index * seg : (index + 1) * seg].astype(types[index])
            return _

        lax.fori_loop(0, members, back, 0)

    return pl.pallas_call(
        kernel,
        out_shape=(
            shape_of(rows, wide),
            shape_of(1, wide, F32),
            *[shape_of(seg, width, dtype) for dtype in types],
        ),
        in_specs=[HBM] * (count + 3),
        out_specs=(VMEM,) * (2 + count),
        scratch_shapes=[
            pltpu.VMEM((rows, width), BF16),
            pltpu.VMEM((rows, wide), BF16),
            pltpu.VMEM((members, columns, share, wide), BF16),
            pltpu.VMEM((wide, width), BF16),
            pltpu.SemaphoreType.DMA((count + 2 + members,)),
        ],
        name="ffn_back",
        **kernel_params(19),
    )(*cots, slope, up_w, down_w)


def ffn_out(hidden, down_w, types):
    count = len(types)
    rows, wide = hidden.shape
    seg = rows // count
    width = down_w.shape[1]
    step = 512

    def kernel(hidden_ref, down_ref, *outs):
        def block(part, _):
            at = pl.ds(pl.multiple_of(part * step, step), step)
            value = dot(hidden_ref[...], down_ref[:, at])
            for index in range(count):
                outs[index][:, at] = value[index * seg : (index + 1) * seg].astype(types[index])
            return _

        lax.fori_loop(0, width // step, block, 0)

    return pl.pallas_call(
        kernel,
        out_shape=tuple(shape_of(seg, width, dtype) for dtype in types),
        in_specs=[VMEM] * 2,
        out_specs=(VMEM,) * count,
        name="ffn_out",
        **kernel_params(15),
    )(hidden, down_w)


GRAD_ROWS = 256


def weight_grad(lefts, rights):
    tall, wide = lefts[0].shape[1], rights[0].shape[1]
    deep = sum(left.shape[0] for left in lefts)
    counts = len(lefts), len(rights)
    both = sum(counts)

    def kernel(*refs):
        out_ref, left, right, sems = refs[both:]
        step = pl.program_id(0)

        @pl.when(step == 0)
        def _():
            copies = load_rows(refs[: counts[0]], left, sems)
            wait_all(copies + load_rows(refs[counts[0] : both], right, sems.at[pl.ds(counts[0], counts[1])]))

        at = pl.ds(pl.multiple_of(step * GRAD_ROWS, GRAD_ROWS), GRAD_ROWS)
        out_ref[...] = t_dot(left[:, at], right[...]).astype(BF16)

    return pl.pallas_call(
        kernel,
        grid=(tall // GRAD_ROWS,),
        out_shape=shape_of(tall, wide),
        in_specs=[HBM] * both,
        out_specs=pl.BlockSpec((GRAD_ROWS, wide), lambda i: (i, 0)),
        scratch_shapes=[
            pltpu.VMEM((deep, tall), BF16),
            pltpu.VMEM((deep, wide), BF16),
            pltpu.SemaphoreType.DMA((both,)),
        ],
        name="weight_grad",
        **kernel_params(17),
    )(*lefts, *rights)


def attn_weight_grad(lows, grads, mixeds, branches):
    count = len(lows)
    keys, width = lows[0].shape
    seg, cols = mixeds[0].shape
    halves = cols // GRAD_ROWS

    def kernel(*refs):
        out_ref, low, grad, mixed, branch, sems = refs[4 * count :]
        step = pl.program_id(0)

        @pl.when(step == 0)
        def _():
            copies = []
            for index, scratch in enumerate((low, grad, mixed, branch)):
                some = refs[index * count : (index + 1) * count]
                copies += load_rows(some, scratch, sems.at[pl.ds(index * count, count)])
            wait_all(copies)

        at = pl.ds(pl.multiple_of(step * GRAD_ROWS, GRAD_ROWS), GRAD_ROWS)
        out_ref[:, : 3 * cols] = t_dot(low[:, at], grad[...]).astype(BF16)
        half = pl.ds(pl.multiple_of((step % halves) * GRAD_ROWS, GRAD_ROWS), GRAD_ROWS)
        block = pl.ds(pl.multiple_of((step // halves) * cols, PAIR), cols)
        out_ref[:, 3 * cols :] = t_dot(mixed[:, half], branch[:, block]).astype(BF16)

    return pl.pallas_call(
        kernel,
        grid=(width // GRAD_ROWS,),
        out_shape=shape_of(width, 4 * cols),
        in_specs=[HBM] * (4 * count),
        out_specs=pl.BlockSpec((GRAD_ROWS, 4 * cols), lambda i: (i, 0)),
        scratch_shapes=[
            pltpu.VMEM((count * keys, width), BF16),
            pltpu.VMEM((count * keys, 3 * cols), BF16),
            pltpu.VMEM((count * seg, cols), BF16),
            pltpu.VMEM((count * seg, width), BF16),
            pltpu.SemaphoreType.DMA((4 * count,)),
        ],
        name="attn_weight_grad",
        **kernel_params(21),
    )(*lows, *grads, *mixeds, *branches)


def swap(value, rel):
    if rel == 0:
        return value
    count = lax.axis_size("fsdp")
    return lax.ppermute(value, "fsdp", [(i, i ^ rel) for i in range(count)])


def after(value, *others):
    return lax.optimization_barrier((value, *others))[0]


def trade_blocks(blocks):
    return lax.all_to_all(blocks, "fsdp", 0, 0, tiled=True)


def gather_small(row):
    total = lax.axis_size("fsdp") * lax.axis_size("dp")
    place = lax.axis_index(BOTH)
    step = 1
    while step < total:
        came = lax.ppermute(row, BOTH, [(i, i ^ step) for i in range(total)])
        high = (place & step) != 0
        row = jnp.concatenate([jnp.where(high, came, row), jnp.where(high, row, came)], 0)
        step *= 2
    return row


def scatter_small(rows):
    total = lax.axis_size("fsdp") * lax.axis_size("dp")
    place = lax.axis_index(BOTH)
    step = total // 2
    while step >= 1:
        high = (place & step) != 0
        lower, upper = rows[:step], rows[step:]
        sent = jnp.where(high, lower, upper)
        came = lax.ppermute(sent, BOTH, [(i, i ^ step) for i in range(total)])
        rows = jnp.where(high, upper, lower) + came
        step //= 2
    return rows[0]


def gather_dp(value):
    return lax.all_gather(value, "dp", axis=0, tiled=True)


def scatter_dp(value, axis):
    return lax.psum_scatter(value, "dp", scatter_dimension=axis, tiled=True)


def shards(
    tokens,
    summaries,
    presence,
    seg_counts,
    ln1_gain,
    ln1_bias,
    w_query,
    query_bias,
    w_key,
    w_value,
    value_bias,
    w_out,
    out_bias,
    ln2_gain,
    ln2_bias,
    w_up,
    up_bias,
    w_down,
    down_bias,
    cotangent,
):
    members = lax.axis_size("fsdp")
    columns = lax.axis_size("dp")
    total = members * columns
    me = lax.axis_index("fsdp")
    seg_len, width = tokens.shape
    n_summary = summaries.shape[1]
    my_cols = width // members
    my_ff = w_up.shape[1] // members
    row_share = w_query.shape[0]
    rels = list(range(members))
    own_last = rels[::-1]

    def blocks_of(weight):
        return weight.reshape(row_share, members, -1).swapaxes(0, 1)

    def gathered(blocks):
        rows = blocks.reshape(members * row_share, -1)
        return gather_dp(rows).reshape(columns, members, row_share, -1)

    qkv_blocks = jnp.concatenate([blocks_of(w_query), blocks_of(w_key), blocks_of(w_value)], 2)
    qkv_blocks = trade_blocks(qkv_blocks)
    up_blocks = trade_blocks(after(blocks_of(w_up), qkv_blocks))
    attn_w = gathered(jnp.concatenate([qkv_blocks, blocks_of(w_out)], 2))
    up_w = gathered(up_blocks)
    down_w = gather_dp(w_down)

    group_tokens = [swap(tokens, rel) for rel in rels]
    prior_own = jnp.pad(summaries[0], ((0, PRIOR_ROWS - n_summary), (0, 0)))
    priors = []
    for rel in rels:
        pairs = [((((i // columns) ^ rel) * columns + i % columns) - 1, i) for i in range(total)]
        priors.append(lax.ppermute(prior_own, BOTH, [pair for pair in pairs if pair[0] >= 0]))

    small_parts = (
        ln1_gain, ln1_bias, query_bias, value_bias, out_bias, ln2_gain, ln2_bias, up_bias,
        down_bias, presence[0].astype(BF16),
    )
    packed = gather_small(jnp.concatenate(small_parts)[None])
    smalls = []
    at = 0
    for part in small_parts:
        smalls.append(packed[:, at : at + part.shape[0]].astype(F32))
        at += part.shape[0]
    gain_one, bias_one, query_off, value_off, out_off, gain_two, bias_two, up_off, down_off = [
        part.reshape(1, -1) for part in smalls[:-1]
    ]
    present_all = smalls[-1]
    query_off = lax.dynamic_slice_in_dim(query_off, me * my_cols, my_cols, 1)
    value_off = lax.dynamic_slice_in_dim(value_off, me * my_cols, my_cols, 1)
    up_off = lax.dynamic_slice_in_dim(up_off, me * my_ff, my_ff, 1)
    qkv_off = jnp.concatenate([query_off, jnp.zeros_like(query_off), value_off], 1)

    starts = jnp.cumsum(seg_counts) - seg_counts
    group_places = (me ^ jnp.arange(members)) * columns + lax.axis_index("dp")
    has_prev = jnp.all(group_places[:, None] != starts[None, :], axis=1)
    summary_ok = jnp.logical_and(present_all[group_places] == 1, has_prev[:, None]).astype(F32)
    ok_rows = jnp.pad(summary_ok, ((0, 0), (seg_len, PRIOR_ROWS - n_summary)))
    ok_cols = jnp.broadcast_to(ok_rows[:, :, None], (*ok_rows.shape, PAIR))

    group_cot = [swap(cotangent, rel) for rel in rels]

    def part_type(rel):
        return BF16 if rel else F32

    attn = {}
    middle_parts = {}
    previous = None
    for rel in own_last:
        x = group_tokens[rel]
        if previous is not None:
            x = after(x, previous)
        low, qkv, lse, mixed, part = attn_forward(
            x, priors[rel], gain_one, bias_one, qkv_off, ok_rows[rel : rel + 1], attn_w,
            part_type(rel),
        )
        attn[rel] = (low, qkv, lse, mixed)
        middle_parts[rel] = swap(part, rel).astype(F32)
        previous = lse
    token_vals = tokens.astype(F32)
    middle = token_vals + sum(middle_parts[rel] for rel in rels) + out_off
    second_own = norm_apply(middle, gain_two, bias_two).astype(BF16)
    group_second = [swap(second_own, rel) for rel in rels]

    def ordered(values):
        return [values[rel] for rel in own_last]

    hidden, slope = ffn_hidden(ordered(group_second), up_off, up_w)
    down_partial = weight_grad([hidden], ordered(group_cot))
    down_grad = scatter_dp(down_partial, 0).astype(F32)
    pre, up_sums, second_parts = [], [], {}
    half = (members + 1) // 2
    for at in range(0, members, half):
        some = own_last[at : at + half]
        cots = [group_cot[rel] for rel in some]
        cots[0] = after(cots[0], *(pre[-1:] or [down_partial]))
        pre_some, sums, *backs = ffn_back(
            cots, slope, at * seg_len, up_w, down_w, [part_type(rel) for rel in some]
        )
        pre.append(pre_some)
        up_sums.append(sums)
        for rel, back in zip(some, backs):
            second_parts[rel] = swap(back, rel)
    up_partial = weight_grad(ordered(group_second), pre)
    output_parts = ffn_out(after(hidden, up_partial), down_w, [part_type(rel) for rel in own_last])
    output_parts = {rel: swap(part, rel) for rel, part in zip(own_last, output_parts)}

    def to_row_blocks(grad):
        return scatter_dp(grad.reshape(members, columns * row_share, -1), 1)

    up_share = to_row_blocks(up_partial)
    up_grad = trade_blocks(up_share).swapaxes(0, 1).reshape(row_share, members * my_ff).astype(F32)
    second_parts = after(second_parts, up_partial)
    cot_vals = cotangent.astype(F32)
    second_grad = sum(second_parts[rel].astype(F32) for rel in rels)
    _, second_back = jax.vjp(norm_apply, middle, gain_two, bias_two)
    middle_part, gain_two_grad, bias_two_grad = second_back(second_grad)
    middle_grad = cot_vals + middle_part
    branch_low = middle_grad.astype(BF16)
    group_branch = [swap(branch_low, rel) for rel in rels]
    output_sum = sum(output_parts[rel].astype(F32) for rel in rels)
    output = (middle + output_sum + down_off).astype(BF16)

    grads, qkv_sums, joined_parts = {}, {}, {}
    previous = None
    for rel in rels:
        x = group_branch[rel]
        if previous is not None:
            x = after(x, previous)
        _, qkv, lse, _ = attn[rel]
        grads[rel], qkv_sums[rel], joined = attn_backward(
            x, qkv, lse, ok_cols[rel], attn_w, part_type(rel)
        )
        joined_parts[rel] = swap(joined, rel)
        previous = qkv_sums[rel]
    attn_partial = attn_weight_grad(
        [attn[rel][0] for rel in rels],
        [grads[rel] for rel in rels],
        [attn[rel][3] for rel in rels],
        group_branch,
    )
    attn_share = to_row_blocks(attn_partial)
    joined_parts = after(joined_parts, attn_partial)
    out_grad = (
        attn_share[:, :, 3 * my_cols :].swapaxes(0, 1).reshape(row_share, width).astype(F32)
    )
    qkv_shares = trade_blocks(attn_share[:, :, : 3 * my_cols])
    query_mat_grad, key_mat_grad, value_mat_grad = [
        qkv_shares[:, :, part * my_cols : (part + 1) * my_cols]
        .swapaxes(0, 1)
        .reshape(row_share, width)
        .astype(F32)
        for part in range(3)
    ]
    joined_grad = sum(joined_parts[rel].astype(F32) for rel in rels)
    _, first_back = jax.vjp(norm_apply, token_vals, gain_one, bias_one)
    token_part, gain_token, bias_token = first_back(joined_grad[:seg_len])
    prior_vals = priors[0][:n_summary].astype(F32)
    _, prior_back = jax.vjp(norm_apply, prior_vals, gain_one, bias_one)
    prior_part, gain_prior, bias_prior = prior_back(joined_grad[seg_len : seg_len + n_summary])
    tokens_grad = middle_grad + token_part
    summary_grad = lax.ppermute(
        prior_part.astype(BF16), BOTH, [(i + 1, i) for i in range(total - 1)]
    ).astype(F32)

    def whole(value):
        return value.reshape(total, -1)

    def sliced(value):
        mine = value.reshape(columns, -1)
        full = jnp.zeros((total, mine.shape[1]), F32)
        return lax.dynamic_update_slice_in_dim(full, mine, me * columns, 0)

    qkv_sum = sum(qkv_sums[rel] for rel in rels)
    pieces = [
        whole(gain_token + gain_prior),
        whole(bias_token + bias_prior),
        sliced(qkv_sum[:, :my_cols]),
        sliced(qkv_sum[:, 2 * my_cols :]),
        whole(jnp.sum(branch_low.astype(F32), axis=0)),
        whole(gain_two_grad),
        whole(bias_two_grad),
        sliced(sum(up_sums)),
        whole(jnp.sum(cot_vals, axis=0)),
    ]
    share = scatter_small(jnp.concatenate(pieces, 1))
    outs = []
    at = 0
    for piece in pieces:
        outs.append(share[at : at + piece.shape[1]])
        at += piece.shape[1]
    return (
        output,
        tokens_grad,
        summary_grad[None],
        outs[0],
        outs[1],
        query_mat_grad,
        outs[2],
        key_mat_grad,
        value_mat_grad,
        outs[3],
        out_grad,
        outs[4],
        outs[5],
        outs[6],
        up_grad,
        outs[7],
        down_grad,
        outs[8],
    )


def solution(mesh):
    rows, rows2, rows3 = P(BOTH), P(BOTH, None), P(BOTH, None, None)
    return jax.shard_map(
        shards,
        mesh=mesh,
        in_specs=(
            rows2, rows3, rows2, P(), rows, rows, rows2, rows, rows2, rows2, rows, rows2, rows,
            rows, rows, rows2, rows, rows2, rows, rows2,
        ),
        out_specs=(
            rows2, rows2, rows3, rows, rows, rows2, rows, rows2, rows2, rows, rows2, rows, rows,
            rows, rows2, rows, rows2, rows,
        ),
        check_vma=False,
    )
```

time: 1110 us -> 812 us (0.73)
  Pallas kernels: 0 us -> 273 us
  matrix products: 228 us -> 0 us
  waiting for transfers between devices: 492 us -> 331 us
  local copies, waits for them, and re-layouts: 187 us -> 33.3 us
  other arithmetic: 79.9 us -> 39.1 us
  blocking collectives: 0 us -> 16.9 us
    pallas_call x0 -> x15, Pallas kernels: none -> 273 us  [the longest x4 62.4 us: attn_forward(): pl.pallas_call(attn_forward_kernel, out_shape=(shape_of(keys, width), sha...]
    dot_general x21 -> x0, matrix products: 228 us -> none  [the longest x5 67.6 us: contract_cols(): lax.dot_general(left, right, (((1,), (1,)), ((), ())), preferred_element_...]
    reduce_scatter x4 -> x3, waiting for transfers between devices: 94 us -> 0.02 us  [scatter_dp(): return lax.psum_scatter(value, 'dp', scatter_dimension=axis, tiled=True)]
    ppermute x39 -> x24, waiting for transfers between devices: 331 us -> 268 us  [swap(): return lax.ppermute(value, 'fsdp', [(i, i ^ rel) for i in range(count)])]
    dynamic_update_slice x10 -> x0, local copies, waits for them, and re-layouts: 45.2 us -> none  [trade_blocks(): out = lax.dynamic_update_slice_in_dim(out, swap(theirs, rel), me ^ rel, 0)]
    reshape x19 -> x4, local copies, waits for them, and re-layouts: 42.1 us -> 1.51 us  [shards(): part.reshape(1, -1)]
    slice x15 -> x3, local copies, waits for them, and re-layouts: 28.1 us -> 2.68 us  [the longest x1 2.07 us: shards(): qkv_shares = trade_blocks(attn_share[:, :, :3 * my_cols])]
    all_to_all x0 -> x3, waiting for transfers between devices: none -> 23.6 us  [trade_blocks(): return lax.all_to_all(blocks, 'fsdp', 0, 0, tiled=True)]
  transfers between devices with their start and end apart: 62 -> 48, of which waited for: 33 -> 29; matrix products, arithmetic and copies ran while one was open for 29% -> 7% of each run, Pallas kernels for 0% -> 26%
where the time goes in v2:
time: 812 us; the launch traced here: 803 us
  waiting for transfers between devices  331 us (41%)
  Pallas kernels  273 us (34%)
  starting transfers between devices  94.4 us (12%)
  other arithmetic  39.1 us (5%)
  local copies, waits for them, and re-layouts  33.3 us (4%)
  blocking collectives  16.9 us (2%)
  between operations  15.5 us (2%)
    ppermute x24, waiting for transfers between devices, swap(): return lax.ppermute(value, 'fsdp', [(i, i ^ rel) for i in range(count)])  268 us
    pallas_call x4, Pallas kernels, attn_forward(): pl.pallas_call(attn_forward_kernel, out_shape=(shape_of(keys, width), sha...  62.4 us
    pallas_call x4, Pallas kernels, attn_backward(): pl.pallas_call(attn_backward_kernel, out_shape=(shape_of(keys, 3 * cols),...  58.5 us
    pallas_call x2, Pallas kernels, ffn_back(): pl.pallas_call(kernel, out_shape=(shape_of(rows, wide), shape_of(1, wide,...  48.7 us
    pallas_call x2, Pallas kernels, weight_grad(): pl.pallas_call(kernel, grid=(tall // GRAD_ROWS,), out_shape=shape_of(tall...  35.6 us
    ppermute x24, starting transfers between devices, swap(): return lax.ppermute(value, 'fsdp', [(i, i ^ rel) for i in range(count)])  33.9 us
    ppermute x5, starting transfers between devices, scatter_small(): came = lax.ppermute(sent, BOTH, [(i, i ^ step) for i in range(total)])  27.9 us
    ppermute x5, waiting for transfers between devices, gather_small(): came = lax.ppermute(row, BOTH, [(i, i ^ step) for i in range(total)])  27.5 us
  transfers between devices with their start and end apart: 48, of which 29 were waited for; matrix products, arithmetic and copies ran while one was open for 7% of the time, Pallas kernels for 26%

profile of v2, /device:TPU:0, one launch (start us, length us, event | category | flops | bytes accessed | tf_op | source)
XLA Modules:
  0.0 802.8 jit_solution(2065831643532795844)
XLA Ops:
  12.0 5.3 all-to-all-start
  17.6 10.6 %all-to-all-done = bf16[4,64,1536]{2,1,0:T(8,128)(2,1)S(1)} async-done(((bf16[4,64,1536]{2,1,0:T(8,128)(2,1)}), bf16[4,64,1536]{2,1,0:T(8,128)(2,1)S(1)}, u32[]{:S(2)}, u32[]{:S(2)}) %all-to-all-start) | async-done | bytes 786464 | tf_op jit(solution)/shard_map/all_to_all | solution.py:497
  30.9 16.9 %all_to_all.20 = bf16[4,64,2048]{2,1,0:T(8,128)(2,1)} all-to-all(bf16[4,64,2048]{2,1,0:T(8,128)(2,1)S(1)} %copy.63), channel_id=1, replica_groups=mesh['fsdp'=4,'dp'=8] {'fsdp'}, dimensions={0} | all-to-all | bytes 2097152 | tf_op jit(solution)/shard_map/all_to_all | solution.py:497
  48.6 1.9 collective-permute-start.10
  50.5 5.0 collective-permute-start.3
  60.8 2.1 collective-permute-done.5
  62.9 2.6 collective-permute-start.6
  65.8 2.1 collective-permute-done.6
  69.0 19.8 %collective-permute-done.7 = bf16[8,818]{1,0:T(8,128)(2,1)S(1)} collective-permute-done((bf16[8,818]{1,0:T(8,128)(2,1)S(1)}, bf16[8,818]{1,0:T(8,128)(2,1)S(1)}, u32[]{:S(2)}, u32[]{:S(2)}) %collective-permute-start.7) | collective-permute-done | bytes 13120 | tf_op jit(solution)/shard_map/ppermute | solution.py:505
  90.3 2.6 collective-permute-done.8
  92.8 1.9 collective-permute-start.2
  98.2 1.9 collective-permute-start.9
  100.1 25.3 %collective-permute-done.2.x_ref = bf16[320,2048]{1,0:T(8,128)(2,1)} collective-permute-done((bf16[320,2048]{1,0:T(8,128)(2,1)S(1)}, bf16[320,2048]{1,0:T(8,128)(2,1)}, u32[]{:S(2)}, u32[]{:S(2)}) %collective-permute-start.2) | collective-permute-done | bytes 1310752 | tf_op jit(solution)/shard_map/ppermute | solution.py:489
  125.4 16.2 %attn_forward.4 = (bf16[384,2048]{1,0:T(8,128)(2,1)}, bf16[384,1536]{1,0:T(8,128)(2,1)}, f32[320,128]{1,0:T(8,128)}, bf16[320,512]{1,0:T(8,128)(2,1)}, bf16[320,2048]{1,0:T(8,128)(2,1)}) custom-call(bf16[320,2048]{1,0:T(8,128)(2,1)} %collective-permute-done.2.x_ref, bf16[64,2048]{1,0:T(8,128)(2,1)} %copy-done.34, f32[1,2048]{1,0:T(1,128)} %reshape.299.gain_ref, ...), custom_call_target="tpu_custom_call" | custom-call | flops 3449999872 | bytes 1 | tf_op jit(solution)/shard_map/attn_forward/pallas_call | solution.py:173
  141.7 3.4 collective-permute-start.14
  145.1 15.2 %attn_forward.5 = (bf16[384,2048]{1,0:T(8,128)(2,1)}, bf16[384,1536]{1,0:T(8,128)(2,1)}, f32[320,128]{1,0:T(8,128)}, bf16[320,512]{1,0:T(8,128)(2,1)}, bf16[320,2048]{1,0:T(8,128)(2,1)}) custom-call(bf16[320,2048]{1,0:T(8,128)(2,1)} %collective-permute-done.1.x_ref, bf16[64,2048]{1,0:T(8,128)(2,1)} %collective-permute-done.9.prior_ref, ...), custom_call_target="tpu_custom_call" | custom-call | flops 3449999872 | bytes 1 | tf_op jit(solution)/shard_map/attn_forward/pallas_call | solution.py:173
  161.8 15.3 %attn_forward.6 = (bf16[384,2048]{1,0:T(8,128)(2,1)}, bf16[384,1536]{1,0:T(8,128)(2,1)}, f32[320,128]{1,0:T(8,128)}, bf16[320,512]{1,0:T(8,128)(2,1)}, bf16[320,2048]{1,0:T(8,128)(2,1)}) custom-call(bf16[320,2048]{1,0:T(8,128)(2,1)} %collective-permute-done.x_ref, bf16[64,2048]{1,0:T(8,128)(2,1)} %copy-done.33, f32[1,2048]{1,0:T(1,128)} %reshape.299.gain_ref, ...), custom_call_target="tpu_custom_call" | custom-call | flops 3449999872 | bytes 1 | tf_op jit(solution)/shard_map/attn_forward/pallas_call | solution.py:173
  180.4 15.7 %attn_forward.7 = (bf16[384,2048]{1,0:T(8,128)(2,1)}, bf16[384,1536]{1,0:T(8,128)(2,1)}, f32[320,128]{1,0:T(8,128)}, bf16[320,512]{1,0:T(8,128)(2,1)}, f32[320,2048]{1,0:T(8,128)}) custom-call(bf16[320,2048]{1,0:T(8,128)(2,1)} %x_ref, bf16[64,2048]{1,0:T(8,128)(2,1)} %copy-done.5, f32[1,2048]{1,0:T(1,128)} %reshape.299.gain_ref, ...), custom_call_target="tpu_custom_call" | custom-call | flops 3449999872 | bytes 1 | tf_op jit(solution)/shard_map/attn_forward/pallas_call | solution.py:173
  196.1 7.2 collective-permute-done.13
  203.3 5.9 collective-permute-done.12
  209.2 5.0 fusion.46
  216.2 3.9 collective-permute-start.17
  224.8 25.3 %collective-permute-done.17.refs_2_ = bf16[320,2048]{1,0:T(8,128)(2,1)} collective-permute-done((bf16[320,2048]{1,0:T(8,128)(2,1)}, bf16[320,2048]{1,0:T(8,128)(2,1)}, u32[]{:S(2)}, u32[]{:S(2)}) %collective-permute-start.17) | collective-permute-done | bytes 1310752 | tf_op jit(solution)/shard_map/ppermute | solution.py:489
  250.0 2.7 collective-permute-start.18
  253.5 26.2 %collective-permute-done.16.refs_1_ = bf16[320,2048]{1,0:T(8,128)(2,1)} collective-permute-done((bf16[320,2048]{1,0:T(8,128)(2,1)}, bf16[320,2048]{1,0:T(8,128)(2,1)}, u32[]{:S(2)}, u32[]{:S(2)}) %collective-permute-start.16) | collective-permute-done | bytes 1310752 | tf_op jit(solution)/shard_map/ppermute | solution.py:489
  280.6 26.8 %ffn_hidden.1 = (bf16[1280,2048]{1,0:T(8,128)(2,1)}, bf16[1280,2048]{1,0:T(8,128)(2,1)}) custom-call(bf16[320,2048]{1,0:T(8,128)(2,1)} %collective-permute-done.15.refs_0_, bf16[320,2048]{1,0:T(8,128)(2,1)} %collective-permute-done.16.refs_1_, bf16[320,2048]{1,0:T(8,128)(2,1)} %collective-permute-done.17.refs_2_, ...), custom_call_target="tpu_custom_call" | custom-call | flops 5520000000 | bytes 1 | tf_op jit(solution)/shard_map/ffn_hidden/pallas_call | solution.py:305
  307.4 25.2 %collective-permute-done.19.refs_2_.refs_1_ = bf16[320,2048]{1,0:T(8,128)(2,1)} collective-permute-done((bf16[320,2048]{1,0:T(8,128)(2,1)}, bf16[320,2048]{1,0:T(8,128)(2,1)}, u32[]{:S(2)}, u32[]{:S(2)}) %collective-permute-start.19) | collective-permute-done | bytes 1310752 | tf_op jit(solution)/shard_map/ppermute | solution.py:489
  332.6 17.7 %weight_grad.2 = bf16[2048,2048]{1,0:T(8,128)(2,1)} custom-call(bf16[1280,2048]{1,0:T(8,128)(2,1)} %get-tuple-element.99.refs_0_.hidden_ref, bf16[320,2048]{1,0:T(8,128)(2,1)} %collective-permute-done.18.refs_1_.refs_0_, bf16[320,2048]{1,0:T(8,128)(2,1)} %collective-permute-done.19.refs_2_.refs_1_, ...), custom_call_target="tpu_custom_call" | custom-call | flops 3910000128 | bytes 1 | tf_op jit(solution)/shard_map/weight_grad/pallas_call | solution.py:427
  350.3 19.0 %ffn_back.2 = (bf16[640,2048]{1,0:T(8,128)(2,1)}, f32[1,2048]{1,0:T(1,128)}, bf16[320,2048]{1,0:T(8,128)(2,1)}, bf16[320,2048]{1,0:T(8,128)(2,1)}) custom-call(bf16[320,2048]{1,0:T(8,128)(2,1)} %collective-permute-done.18.refs_1_.refs_0_, bf16[320,2048]{1,0:T(8,128)(2,1)} %collective-permute-done.19.refs_2_.refs_1_, ...), custom_call_target="tpu_custom_call" | custom-call | flops 4369999872 | bytes 1 | tf_op jit(solution)/shard_map/ffn_back/pallas_call | solution.py:358
  369.3 29.7 %ffn_back.3 = (bf16[640,2048]{1,0:T(8,128)(2,1)}, f32[1,2048]{1,0:T(1,128)}, bf16[320,2048]{1,0:T(8,128)(2,1)}, f32[320,2048]{1,0:T(8,128)}) custom-call(bf16[320,2048]{1,0:T(8,128)(2,1)} %collective-permute-done.20.refs_3_.refs_0_, bf16[320,2048]{1,0:T(8,128)(2,1)} %refs_1_.1, bf16[1280,2048]{1,0:T(8,128)(2,1)} %get-tuple-element.95.refs_2_, ...), custom_call_target="tpu_custom_call" | custom-call | flops 4369999872 | bytes 1 | tf_op jit(solution)/shard_map/ffn_back/pallas_call | solution.py:358
  399.1 17.9 %weight_grad.3 = bf16[2048,2048]{1,0:T(8,128)(2,1)} custom-call(bf16[320,2048]{1,0:T(8,128)(2,1)} %collective-permute-done.15.refs_0_, bf16[320,2048]{1,0:T(8,128)(2,1)} %collective-permute-done.16.refs_1_, bf16[320,2048]{1,0:T(8,128)(2,1)} %collective-permute-done.17.refs_2_, bf16[320,2048]{1,0:T(8,128)(2,1)} %add_convert_fusion.1.refs_3_, ...), custom_call_target="tpu_custom_call" | custom-call | flops 3910000128 | bytes 1 | tf_op jit(solution)/shard_map/weight_grad/pallas_call | solution.py:427
  417.6 1.8 collective-permute-start.24
  421.2 19.0 %ffn_out.1 = (bf16[320,2048]{1,0:T(8,128)(2,1)}, bf16[320,2048]{1,0:T(8,128)(2,1)}, bf16[320,2048]{1,0:T(8,128)(2,1)}, f32[320,2048]{1,0:T(8,128)}) custom-call(bf16[1280,2048]{1,0:T(8,128)(2,1)} %get-tuple-element.99.refs_0_.hidden_ref, bf16[2048,2048]{1,0:T(8,128)(2,1)} %all-gather.8.cloned.1.call-done.refs_4_.down_ref), custom_call_target="tpu_custom_call" | custom-call | flops 3449999872 | bytes 1 | tf_op jit(solution)/shard_map/ffn_out/pallas_call | solution.py:396
  442.3 7.4 collective-permute-done.24
  451.3 28.3 %collective-permute-done.25 = bf16[320,2048]{1,0:T(8,128)(2,1)} collective-permute-done((bf16[320,2048]{1,0:T(8,128)(2,1)}, bf16[320,2048]{1,0:T(8,128)(2,1)}, u32[]{:S(2)}, u32[]{:S(2)}) %collective-permute-start.25) | collective-permute-done | bytes 1310752 | tf_op jit(solution)/shard_map/ppermute | solution.py:489
  479.6 4.6 multiply_reduce_fusion
  484.2 21.7 %collective-permute-done.21 = bf16[320,2048]{1,0:T(8,128)(2,1)} collective-permute-done((bf16[320,2048]{1,0:T(8,128)(2,1)}, bf16[320,2048]{1,0:T(8,128)(2,1)}, u32[]{:S(2)}, u32[]{:S(2)}) %collective-permute-start.21) | collective-permute-done | bytes 1310752 | tf_op jit(solution)/shard_map/ppermute | solution.py:489
  505.9 24.5 %collective-permute-done.22 = bf16[320,2048]{1,0:T(8,128)(2,1)} collective-permute-done((bf16[320,2048]{1,0:T(8,128)(2,1)}, bf16[320,2048]{1,0:T(8,128)(2,1)}, u32[]{:S(2)}, u32[]{:S(2)}) %collective-permute-start.22) | collective-permute-done | bytes 1310752 | tf_op jit(solution)/shard_map/ppermute | solution.py:489
  530.5 1.9 collective-permute-done.23
  532.3 4.8 fusion.45
  537.1 2.8 convert_reduce_fusion.2
  540.4 1.8 collective-permute-start.29
  544.3 15.0 %attn_backward.4 = (bf16[384,1536]{1,0:T(8,128)(2,1)}, f32[1,1536]{1,0:T(1,128)}, f32[384,2048]{1,0:T(8,128)}) custom-call(bf16[320,2048]{1,0:T(8,128)(2,1)} %copy-done.4, bf16[384,1536]{1,0:T(8,128)(2,1)} %get-tuple-element.112.qkv_ref, f32[320,128]{1,0:T(8,128)} %get-tuple-element.113.lse_ref, f32[384,128]{1,0:T(8,128)} %broadcast_in_dim.70.ok_ref, ...), custom_call_target="tpu_custom_call" | custom-call | flops 3220000000 | bytes 1 | tf_op jit(solution)/shard_map/attn_backward/pallas_call | solution.py:257
  559.2 12.5 %collective-permute-done.27.branch_ref.refs_13_ = bf16[320,2048]{1,0:T(8,128)(2,1)S(1)} collective-permute-done((bf16[320,2048]{1,0:T(8,128)(2,1)S(1)}, bf16[320,2048]{1,0:T(8,128)(2,1)S(1)}, u32[]{:S(2)}, u32[]{:S(2)}) %collective-permute-start.27) | collective-permute-done | bytes 1310752 | tf_op jit(solution)/shard_map/ppermute | solution.py:489
  572.8 14.7 %attn_backward.5 = (bf16[384,1536]{1,0:T(8,128)(2,1)}, f32[1,1536]{1,0:T(1,128)}, bf16[384,2048]{1,0:T(8,128)(2,1)}) custom-call(bf16[320,2048]{1,0:T(8,128)(2,1)} %copy-done.10, bf16[384,1536]{1,0:T(8,128)(2,1)} %get-tuple-element.117.qkv_ref, f32[320,128]{1,0:T(8,128)} %get-tuple-element.86.lse_ref, f32[384,128]{1,0:T(8,128)} %broadcast_in_dim.72.ok_ref, ...), custom_call_target="tpu_custom_call" | custom-call | flops 3220000000 | bytes 1 | tf_op jit(solution)/shard_map/attn_backward/pallas_call | solution.py:257
  587.5 8.7 %collective-permute-done.29.branch_ref.refs_14_ = bf16[320,2048]{1,0:T(8,128)(2,1)S(1)} collective-permute-done((bf16[320,2048]{1,0:T(8,128)(2,1)S(1)}, bf16[320,2048]{1,0:T(8,128)(2,1)S(1)}, u32[]{:S(2)}, u32[]{:S(2)}) %collective-permute-start.29) | collective-permute-done | bytes 1310752 | tf_op jit(solution)/shard_map/ppermute | solution.py:489
  597.3 14.5 %attn_backward.6 = (bf16[384,1536]{1,0:T(8,128)(2,1)}, f32[1,1536]{1,0:T(1,128)}, bf16[384,2048]{1,0:T(8,128)(2,1)}) custom-call(bf16[320,2048]{1,0:T(8,128)(2,1)} %copy-done.11, bf16[384,1536]{1,0:T(8,128)(2,1)} %get-tuple-element.121.qkv_ref, f32[320,128]{1,0:T(8,128)} %get-tuple-element.84.lse_ref, f32[384,128]{1,0:T(8,128)} %broadcast_in_dim.74.ok_ref, ...), custom_call_target="tpu_custom_call" | custom-call | flops 3220000000 | bytes 1 | tf_op jit(solution)/shard_map/attn_backward/pallas_call | solution.py:257
  612.6 14.4 %attn_backward.7 = (bf16[384,1536]{1,0:T(8,128)(2,1)}, f32[1,1536]{1,0:T(1,128)}, bf16[384,2048]{1,0:T(8,128)(2,1)}) custom-call(bf16[320,2048]{1,0:T(8,128)(2,1)} %collective-permute-done.31.branch_ref.refs_15_, bf16[384,1536]{1,0:T(8,128)(2,1)} %get-tuple-element.125.qkv_ref, f32[320,128]{1,0:T(8,128)} %get-tuple-element.82.lse_ref, ...), custom_call_target="tpu_custom_call" | custom-call | flops 3220000000 | bytes 1 | tf_op jit(solution)/shard_map/attn_backward/pallas_call | solution.py:257
  627.0 21.8 %attn_weight_grad.1 = bf16[2048,2048]{1,0:T(8,128)(2,1)} custom-call(bf16[384,2048]{1,0:T(8,128)(2,1)} %get-tuple-element.127.refs_0_, bf16[384,2048]{1,0:T(8,128)(2,1)} %get-tuple-element.128.refs_1_, bf16[384,2048]{1,0:T(8,128)(2,1)} %get-tuple-element.129.refs_2_, bf16[384,2048]{1,0:T(8,128)(2,1)} %get-tuple-element.130.refs_3_, ...), custom_call_target="tpu_custom_call" | custom-call | flops 4830000128 | bytes 1 | tf_op jit(solution)/shard_map/attn_weight_grad/pallas_call | solution.py:467
  657.3 31.1 %collective-permute-done.32 = bf16[384,2048]{1,0:T(8,128)(2,1)S(1)} collective-permute-done((bf16[384,2048]{1,0:T(8,128)(2,1)}, bf16[384,2048]{1,0:T(8,128)(2,1)S(1)}, u32[]{:S(2)}, u32[]{:S(2)}) %collective-permute-start.32) | collective-permute-done | bytes 1572896 | tf_op jit(solution)/shard_map/ppermute | solution.py:489
  688.4 16.2 %collective-permute-done.30 = bf16[384,2048]{1,0:T(8,128)(2,1)S(1)} collective-permute-done((bf16[384,2048]{1,0:T(8,128)(2,1)}, bf16[384,2048]{1,0:T(8,128)(2,1)S(1)}, u32[]{:S(2)}, u32[]{:S(2)}) %collective-permute-start.30) | collective-permute-done | bytes 1572896 | tf_op jit(solution)/shard_map/ppermute | solution.py:489
  705.8 4.4 convert_add_fusion.2
  712.8 4.0 convert_reduce_fusion.1
  721.0 3.7 collective-permute-done.34
  726.4 2.2 collective-permute-done.35
  728.6 4.5 collective-permute-start.36
  733.4 2.0 collective-permute-done.36
  735.4 21.9 %collective-permute-start.37 = (f32[2,768]{1,0:T(2,128)S(1)}, f32[2,768]{1,0:T(2,128)S(1)}, u32[]{:S(2)}, u32[]{:S(2)}) collective-permute-start(f32[2,768]{1,0:T(2,128)S(1)} %broadcast_select_fusion.10), channel_id=1, source_target_pairs={{0,2},{1,3},{2,0},{3,1},{4,6},{5,7},{6,4},{7,5},{8,10},{9,11},{10,... | collective-permute-start | bytes 18440 | tf_op jit(solution)/shard_map/ppermute | solution.py:520
  760.4 5.1 all-to-all-start.3
  767.9 2.8 convert_element_type.173
  770.7 2.1 slice.258
  772.8 6.3 all-to-all-done.3
  779.1 3.5 all-to-all-start.2
  786.1 6.7 all-to-all-done.2
  (254 shorter events, 74.8 us)
Async XLA Ops:
  12.0 16.1 %all-to-all-start = ((bf16[4,64,1536]{2,1,0:T(8,128)(2,1)}), bf16[4,64,1536]{2,1,0:T(8,128)(2,1)S(1)}, u32[]{:S(2)}, u32[]{:S(2)}) async-start(bf16[4,64,1536]{2,1,0:T(8,128)(2,1)} %copy.61), calls=%async_computation | async-start | bytes 1572864 | tf_op jit(solution)/shard_map/all_to_all | solution.py:497
  17.3 108.1 %all-gather.4.cloned.1.call-start = ((), (), s32[]{:S(2)}) async-start(), calls=%async_computation.7 | async-start | bytes 9437184 | tf_op jit(solution)/shard_map/all_gather | solution.py:527
  29.3 224.2 %all-gather.6.cloned.1.call-start = ((), (), s32[]{:S(2)}) async-start(), calls=%async_computation.8 | async-start | bytes 9437184 | tf_op jit(solution)/shard_map/all_gather | solution.py:527
  30.7 24.8 %copy-start.2 = (bf16[320,2048]{1,0:T(8,128)(2,1)S(1)}, bf16[320,2048]{1,0:T(8,128)(2,1)}, u32[]{:S(2)}) copy-start(bf16[320,2048]{1,0:T(8,128)(2,1)} %x_ref) | copy-start | bytes 3932164
  30.8 26.9 %copy-start.35 = (s32[1,50]{1,0:T(1,128)S(1)}, s32[1,50]{1,0:T(1,128)}, u32[]{:S(2)}) copy-start(s32[1,50]{1,0:T(1,128)} %param.22) | copy-start | bytes 604
  30.8 26.9 %copy-start.24 = (bf16[64]{0:T(256)(128)(2,1)S(1)}, bf16[64]{0:T(256)(128)(2,1)}, u32[]{:S(2)}) copy-start(bf16[64]{0:T(256)(128)(2,1)} %param.24) | copy-start | bytes 388
  30.8 26.9 %copy-start.25 = (bf16[64]{0:T(256)(128)(2,1)S(1)}, bf16[64]{0:T(256)(128)(2,1)}, u32[]{:S(2)}) copy-start(bf16[64]{0:T(256)(128)(2,1)} %param.25) | copy-start | bytes 388
  30.8 26.9 %copy-start.26 = (bf16[64]{0:T(256)(128)(2,1)S(1)}, bf16[64]{0:T(256)(128)(2,1)}, u32[]{:S(2)}) copy-start(bf16[64]{0:T(256)(128)(2,1)} %param.27) | copy-start | bytes 388
  30.8 26.9 %copy-start.27 = (bf16[64]{0:T(256)(128)(2,1)S(1)}, bf16[64]{0:T(256)(128)(2,1)}, u32[]{:S(2)}) copy-start(bf16[64]{0:T(256)(128)(2,1)} %param.30) | copy-start | bytes 388
  30.8 26.9 %copy-start.28 = (bf16[64]{0:T(256)(128)(2,1)S(1)}, bf16[64]{0:T(256)(128)(2,1)}, u32[]{:S(2)}) copy-start(bf16[64]{0:T(256)(128)(2,1)} %param.32) | copy-start | bytes 388
  30.8 26.9 %copy-start.29 = (bf16[64]{0:T(256)(128)(2,1)S(1)}, bf16[64]{0:T(256)(128)(2,1)}, u32[]{:S(2)}) copy-start(bf16[64]{0:T(256)(128)(2,1)} %param.33) | copy-start | bytes 388
  30.8 26.9 %copy-start.30 = (bf16[64]{0:T(256)(128)(2,1)S(1)}, bf16[64]{0:T(256)(128)(2,1)}, u32[]{:S(2)}) copy-start(bf16[64]{0:T(256)(128)(2,1)} %param.34) | copy-start | bytes 388
  30.9 26.9 %copy-start.31 = (bf16[256]{0:T(256)(128)(2,1)S(1)}, bf16[256]{0:T(256)(128)(2,1)}, u32[]{:S(2)}) copy-start(bf16[256]{0:T(256)(128)(2,1)} %param.36) | copy-start | bytes 1540
  30.9 26.9 %copy-start.32 = (bf16[64]{0:T(256)(128)(2,1)S(1)}, bf16[64]{0:T(256)(128)(2,1)}, u32[]{:S(2)}) copy-start(bf16[64]{0:T(256)(128)(2,1)} %param.38) | copy-start | bytes 388
  30.9 27.1 %copy-start.36 = (s32[8]{0:T(128)S(1)}, s32[8]{0:T(128)}, u32[]{:S(2)}) copy-start(s32[8]{0:T(128)} %param.23) | copy-start | bytes 100
  47.8 302.5 %all-gather.8.cloned.1.call-start = ((), (), s32[]{:S(2)}) async-start(), calls=%async_computation.9 | async-start | bytes 9437184 | tf_op jit(solution)/shard_map/all_gather | solution.py:527
  48.5 711.8 %reduce-scatter.6.cloned.1.call-start = ((), (), s32[]{:S(2)}) async-start(), calls=%async_computation.11 | async-start | bytes 9437184 | tf_op jit(solution)/shard_map/reduce_scatter | solution.py:531
  48.6 112.5 %collective-permute-start.10 = (bf16[64,2048]{1,0:T(8,128)(2,1)S(1)}, bf16[64,2048]{1,0:T(8,128)(2,1)S(1)}, u32[]{:S(2)}, u32[]{:S(2)}) collective-permute-start(bf16[64,2048]{1,0:T(8,128)(2,1)S(1)} %pad.11), channel_id=1, source_target_pairs={{7,0},{8,1},{9,2},{10,3},{11,4},{12,5},{13,6},{14,7},{0,9},{1,10},... | collective-permute-start | bytes 786440 | tf_op jit(solution)/shard_map/ppermute | solution.py:587
  50.5 47.7 %collective-permute-start.3 = (bf16[64,2048]{1,0:T(8,128)(2,1)S(1)}, bf16[64,2048]{1,0:T(8,128)(2,1)S(1)}, u32[]{:S(2)}, u32[]{:S(2)}) collective-permute-start(bf16[64,2048]{1,0:T(8,128)(2,1)S(1)} %pad.11), channel_id=1, source_target_pairs={{23,0},{24,1},{25,2},{26,3},{27,4},{28,5},{29,6},{30,7},{15,8},{16... | collective-permute-start | bytes 786440 | tf_op jit(solution)/shard_map/ppermute | solution.py:587
  55.6 86.1 %collective-permute-start.1 = (bf16[320,2048]{1,0:T(8,128)(2,1)S(1)}, bf16[320,2048]{1,0:T(8,128)(2,1)}, u32[]{:S(2)}, u32[]{:S(2)}) collective-permute-start(bf16[320,2048]{1,0:T(8,128)(2,1)S(1)} %copy-done.2), channel_id=1, source_target_pairs={{0,16},{8,24},{16,0},{24,8},{1,17},{9,25},{17,1},{25,9},{2,18},{10... | collective-permute-start | bytes 3932168 | tf_op jit(solution)/shard_map/ppermute | solution.py:489
  56.8 103.6 %collective-permute-start = (bf16[320,2048]{1,0:T(8,128)(2,1)S(1)}, bf16[320,2048]{1,0:T(8,128)(2,1)}, u32[]{:S(2)}, u32[]{:S(2)}) collective-permute-start(bf16[320,2048]{1,0:T(8,128)(2,1)S(1)} %copy-done.2), channel_id=1, source_target_pairs={{0,8},{8,0},{16,24},{24,16},{1,9},{9,1},{17,25},{25,17},{2,10},{10... | collective-permute-start | bytes 3932168 | tf_op jit(solution)/shard_map/ppermute | solution.py:489
  57.9 1.2 collective-permute-start.4
  59.1 3.8 collective-permute-start.5
  62.9 4.9 collective-permute-start.6
  67.9 21.0 %collective-permute-start.7 = (bf16[8,818]{1,0:T(8,128)(2,1)S(1)}, bf16[8,818]{1,0:T(8,128)(2,1)S(1)}, u32[]{:S(2)}, u32[]{:S(2)}) collective-permute-start(bf16[8,818]{1,0:T(8,128)(2,1)S(1)} %pad_maximum_fusion.3), channel_id=1, source_target_pairs={{0,8},{1,9},{2,10},{3,11},{4,12},{5,13},{6,14},{7,15},{8,0},{9,1},... | collective-permute-start | bytes 39272 | tf_op jit(solution)/shard_map/ppermute | solution.py:505
  88.9 3.9 collective-permute-start.8
  92.8 32.6 %collective-permute-start.2 = (bf16[320,2048]{1,0:T(8,128)(2,1)S(1)}, bf16[320,2048]{1,0:T(8,128)(2,1)}, u32[]{:S(2)}, u32[]{:S(2)}) collective-permute-start(bf16[320,2048]{1,0:T(8,128)(2,1)S(1)} %copy-done.2), channel_id=1, source_target_pairs={{0,24},{8,16},{16,8},{24,0},{1,25},{9,17},{17,9},{25,1},{2,26},{10... | collective-permute-start | bytes 3932168 | tf_op jit(solution)/shard_map/ppermute | solution.py:489
  98.2 27.2 %copy-start.34 = (bf16[64,2048]{1,0:T(8,128)(2,1)}, bf16[64,2048]{1,0:T(8,128)(2,1)S(1)}, u32[]{:S(2)}) copy-start(bf16[64,2048]{1,0:T(8,128)(2,1)S(1)} %collective-permute-done.3.prior_ref) | copy-start | bytes 786436
  98.2 46.9 %collective-permute-start.9 = (bf16[64,2048]{1,0:T(8,128)(2,1)S(1)}, bf16[64,2048]{1,0:T(8,128)(2,1)}, u32[]{:S(2)}, u32[]{:S(2)}) collective-permute-start(bf16[64,2048]{1,0:T(8,128)(2,1)S(1)} %pad.11), channel_id=1, source_target_pairs={{15,0},{16,1},{17,2},{18,3},{19,4},{20,5},{21,6},{22,7},{23,8},{24... | collective-permute-start | bytes 786440 | tf_op jit(solution)/shard_map/ppermute | solution.py:587
  141.7 54.4 %collective-permute-start.14 = (bf16[320,2048]{1,0:T(8,128)(2,1)}, bf16[320,2048]{1,0:T(8,128)(2,1)S(1)}, u32[]{:S(2)}, u32[]{:S(2)}) collective-permute-start(bf16[320,2048]{1,0:T(8,128)(2,1)} %get-tuple-element.91), channel_id=1, source_target_pairs={{0,24},{8,16},{16,8},{24,0},{1,25},{9,17},{17,9},{25,1},{2,26},{10... | collective-permute-start | bytes 3932168 | tf_op jit(solution)/shard_map/ppermute | solution.py:489
  160.3 43.0 %collective-permute-start.13 = (bf16[320,2048]{1,0:T(8,128)(2,1)}, bf16[320,2048]{1,0:T(8,128)(2,1)}, u32[]{:S(2)}, u32[]{:S(2)}) collective-permute-start(bf16[320,2048]{1,0:T(8,128)(2,1)} %get-tuple-element.90), channel_id=1, source_target_pairs={{0,16},{8,24},{16,0},{24,8},{1,17},{9,25},{17,1},{25,9},{2,18},{10... | collective-permute-start | bytes 3932168 | tf_op jit(solution)/shard_map/ppermute | solution.py:489
  177.1 32.1 %collective-permute-start.12 = (bf16[320,2048]{1,0:T(8,128)(2,1)}, bf16[320,2048]{1,0:T(8,128)(2,1)}, u32[]{:S(2)}, u32[]{:S(2)}) collective-permute-start(bf16[320,2048]{1,0:T(8,128)(2,1)} %get-tuple-element.89), channel_id=1, source_target_pairs={{0,8},{8,0},{16,24},{24,16},{1,9},{9,1},{17,25},{25,17},{2,10},{10... | collective-permute-start | bytes 3932168 | tf_op jit(solution)/shard_map/ppermute | solution.py:489
  177.3 2.4 collective-permute-start.11
  216.2 33.9 %collective-permute-start.17 = (bf16[320,2048]{1,0:T(8,128)(2,1)}, bf16[320,2048]{1,0:T(8,128)(2,1)}, u32[]{:S(2)}, u32[]{:S(2)}) collective-permute-start(bf16[320,2048]{1,0:T(8,128)(2,1)} %add_convert_fusion.1.refs_3_), channel_id=1, source_target_pairs={{0,8},{8,0},{16,24},{24,16},{1,9},{9,1},{17,25},{25,17},{2,10},{10... | collective-permute-start | bytes 3932168 | tf_op jit(solution)/shard_map/ppermute | solution.py:489
  220.0 59.7 %collective-permute-start.16 = (bf16[320,2048]{1,0:T(8,128)(2,1)}, bf16[320,2048]{1,0:T(8,128)(2,1)}, u32[]{:S(2)}, u32[]{:S(2)}) collective-permute-start(bf16[320,2048]{1,0:T(8,128)(2,1)} %add_convert_fusion.1.refs_3_), channel_id=1, source_target_pairs={{0,16},{8,24},{16,0},{24,8},{1,17},{9,25},{17,1},{25,9},{2,18},{10... | collective-permute-start | bytes 3932168 | tf_op jit(solution)/shard_map/ppermute | solution.py:489
  221.3 59.3 %collective-permute-start.15 = (bf16[320,2048]{1,0:T(8,128)(2,1)}, bf16[320,2048]{1,0:T(8,128)(2,1)}, u32[]{:S(2)}, u32[]{:S(2)}) collective-permute-start(bf16[320,2048]{1,0:T(8,128)(2,1)} %add_convert_fusion.1.refs_3_), channel_id=1, source_target_pairs={{0,24},{8,16},{16,8},{24,0},{1,25},{9,17},{17,9},{25,1},{2,26},{10... | collective-permute-start | bytes 3932168 | tf_op jit(solution)/shard_map/ppermute | solution.py:489
  222.4 85.0 %collective-permute-start.20 = (bf16[320,2048]{1,0:T(8,128)(2,1)}, bf16[320,2048]{1,0:T(8,128)(2,1)}, u32[]{:S(2)}, u32[]{:S(2)}) collective-permute-start(bf16[320,2048]{1,0:T(8,128)(2,1)} %refs_1_.1), channel_id=1, source_target_pairs={{0,8},{8,0},{16,24},{24,16},{1,9},{9,1},{17,25},{25,17},{2,10},{10... | collective-permute-start | bytes 3932168 | tf_op jit(solution)/shard_map/ppermute | solution.py:489
  223.5 109.1 %collective-permute-start.19 = (bf16[320,2048]{1,0:T(8,128)(2,1)}, bf16[320,2048]{1,0:T(8,128)(2,1)}, u32[]{:S(2)}, u32[]{:S(2)}) collective-permute-start(bf16[320,2048]{1,0:T(8,128)(2,1)} %refs_1_.1), channel_id=1, source_target_pairs={{0,16},{8,24},{16,0},{24,8},{1,17},{9,25},{17,1},{25,9},{2,18},{10... | collective-permute-start | bytes 3932168 | tf_op jit(solution)/shard_map/ppermute | solution.py:489
  250.0 82.5 %collective-permute-start.18 = (bf16[320,2048]{1,0:T(8,128)(2,1)}, bf16[320,2048]{1,0:T(8,128)(2,1)}, u32[]{:S(2)}, u32[]{:S(2)}) collective-permute-start(bf16[320,2048]{1,0:T(8,128)(2,1)} %refs_1_.1), channel_id=1, source_target_pairs={{0,24},{8,16},{16,8},{24,0},{1,25},{9,17},{17,9},{25,1},{2,26},{10... | collective-permute-start | bytes 3932168 | tf_op jit(solution)/shard_map/ppermute | solution.py:489
  417.0 350.9 %reduce-scatter.8.cloned.1.call-start = ((), (), s32[]{:S(2)}) async-start(), calls=%async_computation.12 | async-start | bytes 9437184 | tf_op jit(solution)/shard_map/reduce_scatter | solution.py:531
  417.6 353.1 %reduce-scatter.4.cloned.1.call-start = ((), (), s32[]{:S(2)}) async-start(), calls=%async_computation.10 | async-start | bytes 9437184 | tf_op jit(solution)/shard_map/reduce_scatter | solution.py:531
  417.6 32.1 %collective-permute-start.24 = (bf16[320,2048]{1,0:T(8,128)(2,1)}, bf16[320,2048]{1,0:T(8,128)(2,1)}, u32[]{:S(2)}, u32[]{:S(2)}) collective-permute-start(bf16[320,2048]{1,0:T(8,128)(2,1)} %get-tuple-element.105), channel_id=1, source_target_pairs={{0,8},{8,0},{16,24},{24,16},{1,9},{9,1},{17,25},{25,17},{2,10},{10... | collective-permute-start | bytes 3932168 | tf_op jit(solution)/shard_map/ppermute | solution.py:489
  419.5 60.1 %collective-permute-start.25 = (bf16[320,2048]{1,0:T(8,128)(2,1)}, bf16[320,2048]{1,0:T(8,128)(2,1)}, u32[]{:S(2)}, u32[]{:S(2)}) collective-permute-start(bf16[320,2048]{1,0:T(8,128)(2,1)} %get-tuple-element.106), channel_id=1, source_target_pairs={{0,16},{8,24},{16,0},{24,8},{1,17},{9,25},{17,1},{25,9},{2,18},{10... | collective-permute-start | bytes 3932168 | tf_op jit(solution)/shard_map/ppermute | solution.py:489
  419.8 59.8 %collective-permute-start.26 = (bf16[320,2048]{1,0:T(8,128)(2,1)}, bf16[320,2048]{1,0:T(8,128)(2,1)}, u32[]{:S(2)}, u32[]{:S(2)}) collective-permute-start(bf16[320,2048]{1,0:T(8,128)(2,1)} %get-tuple-element.107), channel_id=1, source_target_pairs={{0,24},{8,16},{16,8},{24,0},{1,25},{9,17},{17,9},{25,1},{2,26},{10... | collective-permute-start | bytes 3932168 | tf_op jit(solution)/shard_map/ppermute | solution.py:489
  440.2 65.7 %collective-permute-start.21 = (bf16[320,2048]{1,0:T(8,128)(2,1)}, bf16[320,2048]{1,0:T(8,128)(2,1)}, u32[]{:S(2)}, u32[]{:S(2)}) collective-permute-start(bf16[320,2048]{1,0:T(8,128)(2,1)} %get-tuple-element.101), channel_id=1, source_target_pairs={{0,8},{8,0},{16,24},{24,16},{1,9},{9,1},{17,25},{25,17},{2,10},{10... | collective-permute-start | bytes 3932168 | tf_op jit(solution)/shard_map/ppermute | solution.py:489
  442.0 88.5 %collective-permute-start.22 = (bf16[320,2048]{1,0:T(8,128)(2,1)}, bf16[320,2048]{1,0:T(8,128)(2,1)}, u32[]{:S(2)}, u32[]{:S(2)}) collective-permute-start(bf16[320,2048]{1,0:T(8,128)(2,1)} %get-tuple-element.102), channel_id=1, source_target_pairs={{0,16},{8,24},{16,0},{24,8},{1,17},{9,25},{17,1},{25,9},{2,18},{10... | collective-permute-start | bytes 3932168 | tf_op jit(solution)/shard_map/ppermute | solution.py:489
  449.7 82.6 %collective-permute-start.23 = (bf16[320,2048]{1,0:T(8,128)(2,1)}, bf16[320,2048]{1,0:T(8,128)(2,1)}, u32[]{:S(2)}, u32[]{:S(2)}) collective-permute-start(bf16[320,2048]{1,0:T(8,128)(2,1)} %get-tuple-element.103), channel_id=1, source_target_pairs={{0,24},{8,16},{16,8},{24,0},{1,25},{9,17},{17,9},{25,1},{2,26},{10... | collective-permute-start | bytes 3932168 | tf_op jit(solution)/shard_map/ppermute | solution.py:489
  479.6 52.8 %copy-start.7 = (f32[320,2048]{1,0:T(8,128)S(1)}, f32[320,2048]{1,0:T(8,128)}, u32[]{:S(2)}) copy-start(f32[320,2048]{1,0:T(8,128)} %get-tuple-element.100) | copy-start | bytes 7864324
  539.9 31.8 %collective-permute-start.27 = (bf16[320,2048]{1,0:T(8,128)(2,1)S(1)}, bf16[320,2048]{1,0:T(8,128)(2,1)S(1)}, u32[]{:S(2)}, u32[]{:S(2)}) collective-permute-start(bf16[320,2048]{1,0:T(8,128)(2,1)S(1)} %get-tuple-element.236.branch_ref.refs_12_), channel_id=1, source_target_pairs={{0,8},{8,0},{16,24},{24,16},{1,9},{9,1},{17,25},{25,17},{2,10},{10... | collective-permute-start | bytes 3932168 | tf_op jit(solution)/shard_map/ppermute | solution.py:489
  540.4 55.8 %collective-permute-start.29 = (bf16[320,2048]{1,0:T(8,128)(2,1)S(1)}, bf16[320,2048]{1,0:T(8,128)(2,1)S(1)}, u32[]{:S(2)}, u32[]{:S(2)}) collective-permute-start(bf16[320,2048]{1,0:T(8,128)(2,1)S(1)} %get-tuple-element.236.branch_ref.refs_12_), channel_id=1, source_target_pairs={{0,16},{8,24},{16,0},{24,8},{1,17},{9,25},{17,1},{25,9},{2,18},{10... | collective-permute-start | bytes 3932168 | tf_op jit(solution)/shard_map/ppermute | solution.py:489
  542.2 69.6 %collective-permute-start.31 = (bf16[320,2048]{1,0:T(8,128)(2,1)S(1)}, bf16[320,2048]{1,0:T(8,128)(2,1)}, u32[]{:S(2)}, u32[]{:S(2)}) collective-permute-start(bf16[320,2048]{1,0:T(8,128)(2,1)S(1)} %get-tuple-element.236.branch_ref.refs_12_), channel_id=1, source_target_pairs={{0,24},{8,16},{16,8},{24,0},{1,25},{9,17},{17,9},{25,1},{2,26},{10... | collective-permute-start | bytes 3932168 | tf_op jit(solution)/shard_map/ppermute | solution.py:489
  649.9 38.5 %collective-permute-start.32 = (bf16[384,2048]{1,0:T(8,128)(2,1)}, bf16[384,2048]{1,0:T(8,128)(2,1)S(1)}, u32[]{:S(2)}, u32[]{:S(2)}) collective-permute-start(bf16[384,2048]{1,0:T(8,128)(2,1)} %get-tuple-element.126), channel_id=1, source_target_pairs={{0,24},{8,16},{16,8},{24,0},{1,25},{9,17},{17,9},{25,1},{2,26},{10... | collective-permute-start | bytes 4718600 | tf_op jit(solution)/shard_map/ppermute | solution.py:489
  651.4 53.3 %collective-permute-start.30 = (bf16[384,2048]{1,0:T(8,128)(2,1)}, bf16[384,2048]{1,0:T(8,128)(2,1)S(1)}, u32[]{:S(2)}, u32[]{:S(2)}) collective-permute-start(bf16[384,2048]{1,0:T(8,128)(2,1)} %get-tuple-element.122), channel_id=1, source_target_pairs={{0,16},{8,24},{16,0},{24,8},{1,17},{9,25},{17,1},{25,9},{2,18},{10... | collective-permute-start | bytes 4718600 | tf_op jit(solution)/shard_map/ppermute | solution.py:489
  653.1 51.6 %collective-permute-start.28 = (bf16[384,2048]{1,0:T(8,128)(2,1)}, bf16[384,2048]{1,0:T(8,128)(2,1)}, u32[]{:S(2)}, u32[]{:S(2)}) collective-permute-start(bf16[384,2048]{1,0:T(8,128)(2,1)} %get-tuple-element.118), channel_id=1, source_target_pairs={{0,8},{8,0},{16,24},{24,16},{1,9},{9,1},{17,25},{25,17},{2,10},{10... | collective-permute-start | bytes 4718600 | tf_op jit(solution)/shard_map/ppermute | solution.py:489
  653.7 56.5 %copy-start.23 = (f32[50]{0:T(128)}, f32[50]{0:T(128)S(1)}, u32[]{:S(2)}) copy-start(f32[50]{0:T(128)S(1)} %fusion.14) | copy-start | bytes 604
  657.3 55.0 %copy-start.16 = (f32[32,64]{1,0:T(8,128)}, f32[32,64]{1,0:T(8,128)S(1)}, u32[]{:S(2)}) copy-start(f32[32,64]{1,0:T(8,128)S(1)} %constant_dynamic-update-slice_fusion.2) | copy-start | bytes 24580
  720.5 4.2 collective-permute-start.34
  724.7 3.9 collective-permute-start.35
  728.6 6.7 collective-permute-start.36
  735.4 23.5 %collective-permute-start.37 = (f32[2,768]{1,0:T(2,128)S(1)}, f32[2,768]{1,0:T(2,128)S(1)}, u32[]{:S(2)}, u32[]{:S(2)}) collective-permute-start(f32[2,768]{1,0:T(2,128)S(1)} %broadcast_select_fusion.10), channel_id=1, source_target_pairs={{0,2},{1,3},{2,0},{3,1},{4,6},{5,7},{6,4},{7,5},{8,10},{9,11},{10,... | collective-permute-start | bytes 18440 | tf_op jit(solution)/shard_map/ppermute | solution.py:520
  758.9 6.6 collective-permute-start.38
  759.0 7.7 collective-permute-start.33
  760.4 18.7 %all-to-all-start.3 = ((bf16[4,64,2048]{2,1,0:T(8,128)(2,1)}), bf16[4,64,2048]{2,1,0:T(8,128)(2,1)S(1)}, u32[]{:S(2)}, u32[]{:S(2)}) async-start(bf16[4,64,2048]{2,1,0:T(8,128)(2,1)} %reduce-scatter.6.cloned.1.call-done), calls=%async_computation.5 | async-start | bytes 2097152 | tf_op jit(solution)/shard_map/all_to_all | solution.py:497
  779.1 13.7 %all-to-all-start.2 = ((bf16[4,64,1536]{2,1,0:T(8,128)(2,1)}), bf16[4,64,1536]{2,1,0:T(8,128)(2,1)S(1)}, u32[]{:S(2)}, u32[]{:S(2)}) async-start(bf16[4,64,1536]{2,1,0:T(8,128)(2,1)} %slice.258), calls=%async_computation.3 | async-start | bytes 1572864 | tf_op jit(solution)/shard_map/all_to_all | solution.py:497
  (21 other events, 129.2 us)
Sparse Core Ops, SparseCore 0:
  29.4 90.9 all-gather.3
  122.0 82.3 all-gather.5
  206.0 80.4 all-gather.7
  417.1 93.3 reduce-scatter.5
  512.6 87.9 reduce-scatter.7
  649.0 94.4 reduce-scatter.3

commit v3 on v2

--- a/solution.py
+++ b/solution.py
@@ -1,3 +1,4 @@
+import functools
 import jax
 import jax.numpy as jnp
 from jax import lax
@@ -90,7 +91,7 @@
     return value.reshape(-1, value.shape[-1])
 
 
-COST = 230_000_000
+COST = 1_000_000
 
 
 def kernel_params(cost):
@@ -105,26 +106,27 @@
 
 
 def attn_forward_kernel(
-    x_ref, prior_ref, gain_ref, bias_ref, off_ref, ok_ref, attn_hbm,
-    low_ref, qkv_ref, lse_ref, mixed_ref, part_ref, weights, mask, sems,
+    count, *refs,
 ):
+    gain_ref, bias_ref, off_ref, ok_ref, attn_hbm = refs[count : count + 5]
+    low_ref, qkv_ref, lse_ref, mixed_ref, part_ref, x_ref, weights, mask, sems = refs[count + 5 :]
     members = weights.shape[0]
-    cols = mixed_ref.shape[1]
-    seg = x_ref.shape[0]
+    seg, cols = mixed_ref.shape
     keys = low_ref.shape[0]
+    x_copies = load_rows(refs[:count], x_ref, sems.at[pl.ds(members, count)])
     copies = load_blocks(attn_hbm, weights, sems)
     row = lax.broadcasted_iota(jnp.int32, (seg, keys), 0)
     col = lax.broadcasted_iota(jnp.int32, (seg, keys), 1)
     mask[...] = jnp.where(jnp.logical_or(col <= row, ok_ref[...] > 0.5), 0.0, MASKED)
     gain, bias = gain_ref[...], bias_ref[...]
+    wait_all(x_copies)
 
     def norm_rows(block, _):
         at = pl.ds(pl.multiple_of(block * NORM_ROWS, NORM_ROWS), NORM_ROWS)
         low_ref[at, :] = norm_apply(x_ref[at, :].astype(F32), gain, bias).astype(BF16)
         return _
 
-    lax.fori_loop(0, seg // NORM_ROWS, norm_rows, 0)
-    low_ref[seg:, :] = norm_apply(prior_ref[...].astype(F32), gain, bias).astype(BF16)
+    lax.fori_loop(0, keys // NORM_ROWS, norm_rows, 0)
     wait_all(copies)
 
     def project(part, _):
@@ -165,13 +167,13 @@
     lax.fori_loop(0, members, project_out, 0)
 
 
-def attn_forward(x, prior, gain, bias, off, ok_row, attn_w, part_type):
-    seg, width = x.shape
-    keys = seg + PRIOR_ROWS
+def attn_forward(x, gain, bias, off, ok_row, attn_w, part_type):
+    keys, width = sum(piece.shape[0] for piece in x), x[0].shape[1]
+    seg = keys - PRIOR_ROWS
     columns, members, share, wide = attn_w.shape
     cols = wide // 4
     return pl.pallas_call(
-        attn_forward_kernel,
+        functools.partial(attn_forward_kernel, len(x)),
         out_shape=(
             shape_of(keys, width),
             shape_of(keys, 3 * cols),
@@ -179,26 +181,29 @@
             shape_of(seg, cols),
             shape_of(seg, width, part_type),
         ),
-        in_specs=[VMEM] * 6 + [HBM],
+        in_specs=[HBM] * len(x) + [VMEM] * 4 + [HBM],
         out_specs=(VMEM,) * 5,
         scratch_shapes=[
+            pltpu.VMEM((keys, width), BF16),
             pltpu.VMEM((members, columns, share, wide), BF16),
             pltpu.VMEM((seg, keys), F32),
-            pltpu.SemaphoreType.DMA((members,)),
+            pltpu.SemaphoreType.DMA((members + len(x),)),
         ],
         name="attn_forward",
         **kernel_params(15),
-    )(x, prior, gain, bias, off, ok_row, attn_w)
+    )(*x, gain, bias, off, ok_row, attn_w)
 
 
 def attn_backward_kernel(
-    branch_ref, qkv_ref, lse_ref, ok_ref, attn_hbm,
-    grads_ref, sums_ref, joined_ref, weights, mask, lse_t, mixed_grad, sems,
+    count, *refs,
 ):
+    qkv_ref, lse_ref, ok_ref, attn_hbm, grads_ref, sums_ref, joined_ref = refs[count : count + 7]
+    branch_ref, weights, mask, lse_t, mixed_grad, sems = refs[count + 7 :]
     members = weights.shape[0]
     cols = mixed_grad.shape[1]
     seg = branch_ref.shape[0]
     keys = qkv_ref.shape[0]
+    branch_copies = load_rows(refs[:count], branch_ref, sems.at[pl.ds(members, count)])
     copies = load_blocks(attn_hbm, weights, sems)
     row = lax.broadcasted_iota(jnp.int32, (keys, seg), 0)
     col = lax.broadcasted_iota(jnp.int32, (keys, seg), 1)
@@ -206,6 +211,7 @@
     lse_t[...] = lse_ref[...].T
     grads_ref[seg:, :cols] = jnp.zeros((keys - seg, cols), BF16)
     total = 0.0
+    wait_all(branch_copies)
     for block in range(members):
         copies[block].wait()
         weight = block_of(weights, block, pl.ds(3 * cols, cols))
@@ -250,93 +256,102 @@
 
 
 def attn_backward(branch, qkv, lse, ok_col, attn_w, joined_type):
-    seg, width = branch.shape
+    seg, width = sum(piece.shape[0] for piece in branch), branch[0].shape[1]
     keys = qkv.shape[0]
     columns, members, share, wide = attn_w.shape
     cols = wide // 4
     return pl.pallas_call(
-        attn_backward_kernel,
+        functools.partial(attn_backward_kernel, len(branch)),
         out_shape=(
             shape_of(keys, 3 * cols),
             shape_of(1, 3 * cols, F32),
             shape_of(keys, width, joined_type),
         ),
-        in_specs=[VMEM] * 4 + [HBM],
+        in_specs=[HBM] * len(branch) + [VMEM] * 3 + [HBM],
         out_specs=(VMEM,) * 3,
         scratch_shapes=[
+            pltpu.VMEM((seg, width), BF16),
             pltpu.VMEM((members, columns, share, wide), BF16),
             pltpu.VMEM((keys, seg), F32),
             pltpu.VMEM((PAIR, seg), F32),
             pltpu.VMEM((seg, cols), BF16),
-            pltpu.SemaphoreType.DMA((members,)),
+            pltpu.SemaphoreType.DMA((members + len(branch),)),
         ],
         name="attn_backward",
         **kernel_params(14),
-    )(branch, qkv, lse, ok_col, attn_w)
+    )(*branch, qkv, lse, ok_col, attn_w)
 
 
 def ffn_hidden(seconds, off, up_w):
+    pieces = flat_list(seconds)
+    given = len(pieces)
+    width = pieces[0].shape[1]
     count = len(seconds)
-    seg, width = seconds[0].shape
+    seg = sum(piece.shape[0] for piece in pieces) // count
     columns, members, share, wide = up_w.shape
     step = 512
 
     def kernel(*refs):
-        off_ref, up_hbm, hidden_ref, slope_ref, second, up, sems = refs[count:]
-        copies = load_blocks(up_hbm, up, sems) + load_rows(refs[:count], second, sems.at[pl.ds(members, count)])
-        wait_all(copies)
+        off_ref, up_hbm = refs[given : given + 2]
+        outs = refs[given + 2 : given + 2 + 2 * count]
+        second, up, sems = refs[given + 2 + 2 * count :]
+        copies = load_blocks(up_hbm, up, sems)
+        wait_all(copies + load_rows(refs[:given], second, sems.at[pl.ds(members, given)]))
 
         def hidden(block, _):
             at = pl.ds(pl.multiple_of(block * step, step), step)
             weight = rows_of(up, at)
             for index in range(count):
-                rows = pl.ds(index * seg, seg)
-                pre = dot(second[rows, :], weight) + off_ref[:, at]
+                pre = dot(second[pl.ds(index * seg, seg), :], weight) + off_ref[:, at]
                 square = pre * pre
                 bent = jnp.tanh(GELU_A * pre * (1.0 + GELU_B * square))
                 gate = 0.5 * (1.0 + bent)
-                hidden_ref[rows, at] = (pre * gate).astype(BF16)
+                outs[index][:, at] = (pre * gate).astype(BF16)
                 rise = 0.5 * pre * (1.0 - bent * bent) * (GELU_A * (1.0 + 3.0 * GELU_B * square))
-                slope_ref[rows, at] = (gate + rise).astype(BF16)
+                outs[count + index][:, at] = (gate + rise).astype(BF16)
             return _
 
         lax.fori_loop(0, wide // step, hidden, 0)
 
-    return pl.pallas_call(
+    outs = pl.pallas_call(
         kernel,
-        out_shape=(shape_of(count * seg, wide), shape_of(count * seg, wide)),
-        in_specs=[HBM] * count + [VMEM, HBM],
-        out_specs=(VMEM,) * 2,
+        out_shape=[shape_of(seg, wide)] * (2 * count),
+        in_specs=[HBM] * given + [VMEM, HBM],
+        out_specs=[VMEM] * (2 * count),
         scratch_shapes=[
             pltpu.VMEM((count * seg, width), BF16),
             pltpu.VMEM((members, columns, share, wide), BF16),
-            pltpu.SemaphoreType.DMA((members + count,)),
+            pltpu.SemaphoreType.DMA((members + given,)),
         ],
         name="ffn_hidden",
-        **kernel_params(24),
-    )(*seconds, off, up_w)
-
-
-def ffn_back(cots, slope, start, up_w, down_w, types):
-    count = len(cots)
-    seg, width = cots[0].shape
+        **kernel_params(6 * count),
+    )(*pieces, off, up_w)
+    return outs[:count], outs[count:]
+
+
+def ffn_back(cots, slopes, up_w, down_w, types):
+    pieces = flat_list(cots)
+    given = len(pieces)
+    count = len(slopes)
+    seg, width = slopes[0].shape[0], pieces[0].shape[1]
     columns, members, share, wide = up_w.shape
     step = 512
     rows = count * seg
+    loads = given + count
 
     def kernel(*refs):
-        slope_hbm, up_hbm, down_hbm, pre_ref, sums_ref = refs[count : count + 5]
-        backs = refs[count + 5 : 2 * count + 5]
-        cot, slope_here, up, down, sems = refs[2 * count + 5 :]
-        first = load_rows(refs[:count], cot, sems)
-        first += load_rows([slope_hbm.at[pl.ds(start, rows)]], slope_here, sems.at[pl.ds(count, 1)])
-        first += load_rows([down_hbm], down, sems.at[pl.ds(count + 1, 1)])
-        later = load_blocks(up_hbm, up, sems.at[pl.ds(count + 2, members)])
+        up_hbm, down_hbm, pre_ref, sums_ref = refs[loads : loads + 4]
+        backs = refs[loads + 4 : loads + 4 + count]
+        cot, slope, up, down, sems = refs[loads + 4 + count :]
+        first = load_rows(refs[:given], cot, sems)
+        first += load_rows([down_hbm], down, sems.at[pl.ds(loads, 1)])
+        first += load_rows(refs[given:loads], slope, sems.at[pl.ds(given, count)])
+        later = load_blocks(up_hbm, up, sems.at[pl.ds(loads + 1, members)])
         wait_all(first)
 
         def grad(block, _):
             at = pl.ds(pl.multiple_of(block * step, step), step)
-            value = dot_t(cot[...], down[at, :]) * slope_here[:, at].astype(F32)
+            value = dot_t(cot[...], down[at, :]) * slope[:, at].astype(F32)
             value = value.astype(BF16)
             pre_ref[:, at] = value
             sums_ref[:, at] = jnp.sum(value.astype(F32), axis=0, keepdims=True)
@@ -362,31 +377,35 @@
             shape_of(1, wide, F32),
             *[shape_of(seg, width, dtype) for dtype in types],
         ),
-        in_specs=[HBM] * (count + 3),
+        in_specs=[HBM] * (loads + 2),
         out_specs=(VMEM,) * (2 + count),
         scratch_shapes=[
             pltpu.VMEM((rows, width), BF16),
             pltpu.VMEM((rows, wide), BF16),
             pltpu.VMEM((members, columns, share, wide), BF16),
             pltpu.VMEM((wide, width), BF16),
-            pltpu.SemaphoreType.DMA((count + 2 + members,)),
+            pltpu.SemaphoreType.DMA((loads + 1 + members,)),
         ],
         name="ffn_back",
-        **kernel_params(19),
-    )(*cots, slope, up_w, down_w)
-
-
-def ffn_out(hidden, down_w, types):
+        **kernel_params(10 * count),
+    )(*pieces, *slopes, up_w, down_w)
+
+
+def ffn_out(hiddens, down_w, types):
     count = len(types)
-    rows, wide = hidden.shape
-    seg = rows // count
+    seg, wide = hiddens[0].shape
     width = down_w.shape[1]
     step = 512
 
-    def kernel(hidden_ref, down_ref, *outs):
+    def kernel(*refs):
+        down_ref = refs[count]
+        outs = refs[count + 1 : 2 * count + 1]
+        hidden, sems = refs[2 * count + 1 :]
+        wait_all(load_rows(refs[:count], hidden, sems))
+
         def block(part, _):
             at = pl.ds(pl.multiple_of(part * step, step), step)
-            value = dot(hidden_ref[...], down_ref[:, at])
+            value = dot(hidden[...], down_ref[:, at])
             for index in range(count):
                 outs[index][:, at] = value[index * seg : (index + 1) * seg].astype(types[index])
             return _
@@ -396,11 +415,15 @@
     return pl.pallas_call(
         kernel,
         out_shape=tuple(shape_of(seg, width, dtype) for dtype in types),
-        in_specs=[VMEM] * 2,
+        in_specs=[HBM] * count + [VMEM],
         out_specs=(VMEM,) * count,
+        scratch_shapes=[
+            pltpu.VMEM((count * seg, wide), BF16),
+            pltpu.SemaphoreType.DMA((count,)),
+        ],
         name="ffn_out",
-        **kernel_params(15),
-    )(hidden, down_w)
+        **kernel_params(18),
+    )(*hiddens, down_w)
 
 
 GRAD_ROWS = 256
@@ -441,21 +464,22 @@
 
 
 def attn_weight_grad(lows, grads, mixeds, branches):
-    count = len(lows)
-    keys, width = lows[0].shape
-    seg, cols = mixeds[0].shape
+    lists = lows, grads, mixeds, branches
+    width, cols = lows[0].shape[1], mixeds[0].shape[1]
     halves = cols // GRAD_ROWS
+    ends = [0]
+    for some in lists:
+        ends.append(ends[-1] + len(some))
 
     def kernel(*refs):
-        out_ref, low, grad, mixed, branch, sems = refs[4 * count :]
+        out_ref, low, grad, mixed, branch, sems = refs[ends[-1] :]
         step = pl.program_id(0)
 
         @pl.when(step == 0)
         def _():
             copies = []
-            for index, scratch in enumerate((low, grad, mixed, branch)):
-                some = refs[index * count : (index + 1) * count]
-                copies += load_rows(some, scratch, sems.at[pl.ds(index * count, count)])
+            for first, last, scratch in zip(ends, ends[1:], (low, grad, mixed, branch)):
+                copies += load_rows(refs[first:last], scratch, sems.at[pl.ds(first, last - first)])
             wait_all(copies)
 
         at = pl.ds(pl.multiple_of(step * GRAD_ROWS, GRAD_ROWS), GRAD_ROWS)
@@ -468,18 +492,147 @@
         kernel,
         grid=(width // GRAD_ROWS,),
         out_shape=shape_of(width, 4 * cols),
-        in_specs=[HBM] * (4 * count),
+        in_specs=[HBM] * ends[-1],
         out_specs=pl.BlockSpec((GRAD_ROWS, 4 * cols), lambda i: (i, 0)),
         scratch_shapes=[
-            pltpu.VMEM((count * keys, width), BF16),
-            pltpu.VMEM((count * keys, 3 * cols), BF16),
-            pltpu.VMEM((count * seg, cols), BF16),
-            pltpu.VMEM((count * seg, width), BF16),
-            pltpu.SemaphoreType.DMA((4 * count,)),
-        ],
+            pltpu.VMEM((sum(one.shape[0] for one in some), some[0].shape[1]), BF16)
+            for some in lists
+        ]
+        + [pltpu.SemaphoreType.DMA((ends[-1],))],
         name="attn_weight_grad",
         **kernel_params(21),
     )(*lows, *grads, *mixeds, *branches)
+
+
+def norm_values(values):
+    centre, inverse = norm_parts(values)
+    return centre * inverse, inverse
+
+
+def norm_back(hat, inverse, grad, gain):
+    hat_grad = grad * gain
+    mean = jnp.mean(hat_grad, axis=-1, keepdims=True)
+    along = jnp.mean(hat_grad * hat, axis=-1, keepdims=True)
+    return inverse * (hat_grad - mean - hat * along)
+
+
+def column_sum(value):
+    return jnp.sum(value, axis=0, keepdims=True)
+
+
+def row_blocks(width, last=None):
+    if last is None:
+        return pl.BlockSpec((NORM_ROWS, width), lambda i: (i, 0))
+    return pl.BlockSpec((NORM_ROWS, width), lambda i: (jnp.minimum(i, last), 0))
+
+
+def kept(rows, width):
+    return pl.BlockSpec((rows, width), lambda i: (0, 0))
+
+
+def sum_parts(parts):
+    total = parts[0][...].astype(F32)
+    for part in parts[1:]:
+        total = total + part[...].astype(F32)
+    return total
+
+
+def middle_norm(tokens, parts, off, gain, bias):
+    seg, width = tokens.shape
+    count = len(parts)
+
+    def kernel(*refs):
+        off_ref, gain_ref, bias_ref, middle_ref, second_ref = refs[count + 1 :]
+        total = sum_parts(refs[: count + 1]) + off_ref[...]
+        middle_ref[...] = total
+        second_ref[...] = norm_apply(total, gain_ref[...], bias_ref[...]).astype(BF16)
+
+    return pl.pallas_call(
+        kernel,
+        grid=(seg // NORM_ROWS,),
+        out_shape=(shape_of(seg, width, F32), shape_of(seg, width)),
+        in_specs=[row_blocks(width)] * (count + 1) + [kept(1, width)] * 3,
+        out_specs=(row_blocks(width),) * 2,
+        name="middle_norm",
+        **kernel_params(5),
+    )(tokens, *parts, off, gain, bias)
+
+
+def middle_back(middle, cot, parts, gain):
+    seg, width = middle.shape
+    count = len(parts)
+
+    def kernel(*refs):
+        middle_ref, cot_ref, gain_ref, grad_ref, branch_ref, sums_ref = refs[count:]
+
+        @pl.when(pl.program_id(0) == 0)
+        def _():
+            sums_ref[...] = jnp.zeros_like(sums_ref)
+
+        grad = sum_parts(refs[:count])
+        hat, inverse = norm_values(middle_ref[...])
+        cots = cot_ref[...].astype(F32)
+        total = cots + norm_back(hat, inverse, grad, gain_ref[...])
+        low = total.astype(BF16)
+        grad_ref[...] = total
+        branch_ref[...] = low
+        sums_ref[0:1, :] += column_sum(grad * hat)
+        sums_ref[1:2, :] += column_sum(grad)
+        sums_ref[2:3, :] += column_sum(low.astype(F32))
+        sums_ref[3:4, :] += column_sum(cots)
+
+    return pl.pallas_call(
+        kernel,
+        grid=(seg // NORM_ROWS,),
+        out_shape=(shape_of(seg, width, F32), shape_of(seg, width), shape_of(4, width, F32)),
+        in_specs=[row_blocks(width)] * (count + 2) + [kept(1, width)],
+        out_specs=(row_blocks(width), row_blocks(width), kept(4, width)),
+        name="middle_back",
+        **kernel_params(5),
+    )(*parts, middle, cot, gain)
+
+
+def first_back(joined, parts, middle_grad, gain):
+    seg, width = middle_grad.shape
+    keys = joined.shape[0]
+    count = len(parts)
+    last = seg // NORM_ROWS - 1
+
+    def kernel(*refs):
+        joined_ref, middle_ref, gain_ref, tokens_ref, prior_ref, sums_ref = refs[count:]
+        step = pl.program_id(0)
+
+        @pl.when(step == 0)
+        def _():
+            sums_ref[...] = jnp.zeros_like(sums_ref)
+
+        grad = sum_parts(refs[:count])
+        hat, inverse = norm_values(joined_ref[...].astype(F32))
+        sums_ref[0:1, :] += column_sum(grad * hat)
+        sums_ref[1:2, :] += column_sum(grad)
+        back = norm_back(hat, inverse, grad, gain_ref[...])
+
+        @pl.when(step <= last)
+        def _():
+            tokens_ref[...] = middle_ref[...] + back
+
+        @pl.when(step > last)
+        def _():
+            prior_ref[...] = back.astype(BF16)
+
+    return pl.pallas_call(
+        kernel,
+        grid=(keys // NORM_ROWS,),
+        out_shape=(
+            shape_of(seg, width, F32),
+            shape_of(keys - seg, width),
+            shape_of(2, width, F32),
+        ),
+        in_specs=[row_blocks(width)] * (count + 1) + [row_blocks(width, last), kept(1, width)],
+        out_specs=(row_blocks(width, last), kept(keys - seg, width), kept(2, width)),
+        name="first_back",
+        **kernel_params(500_000),
+    )(*parts, joined, middle_grad, gain)
 
 
 def swap(value, rel):
@@ -489,6 +642,24 @@
     return lax.ppermute(value, "fsdp", [(i, i ^ rel) for i in range(count)])
 
 
+def spread_near(value):
+    return [swap(value, rel) for rel in range(1, min(lax.axis_size("fsdp"), 3))]
+
+
+def spread_far(value, near, *others):
+    members = lax.axis_size("fsdp")
+    near = list(lax.optimization_barrier((*near, others))[: len(near)])
+    pieces = [[value]] + [[one] for one in near]
+    if members > 3:
+        rows = value.shape[0] // 2
+        pieces.append([swap(near[0][:rows], 2), swap(near[1][rows:], 1)])
+    return pieces + [[swap(value, rel)] for rel in range(4, members)]
+
+
+def flat_list(lists):
+    return [piece for some in lists for piece in some]
+
+
 def after(value, *others):
     return lax.optimization_barrier((value, *others))[0]
 
@@ -497,30 +668,20 @@
     return lax.all_to_all(blocks, "fsdp", 0, 0, tiled=True)
 
 
-def gather_small(row):
-    total = lax.axis_size("fsdp") * lax.axis_size("dp")
-    place = lax.axis_index(BOTH)
+def doubled(rows, axis):
+    size = lax.axis_size(axis)
+    place = lax.axis_index(axis)
     step = 1
-    while step < total:
-        came = lax.ppermute(row, BOTH, [(i, i ^ step) for i in range(total)])
+    while step < size:
+        came = lax.ppermute(rows, axis, [(i, i ^ step) for i in range(size)])
         high = (place & step) != 0
-        row = jnp.concatenate([jnp.where(high, came, row), jnp.where(high, row, came)], 0)
+        rows = jnp.concatenate([jnp.where(high, came, rows), jnp.where(high, rows, came)], 0)
         step *= 2
-    return row
+    return rows
 
 
 def scatter_small(rows):
-    total = lax.axis_size("fsdp") * lax.axis_size("dp")
-    place = lax.axis_index(BOTH)
-    step = total // 2
-    while step >= 1:
-        high = (place & step) != 0
-        lower, upper = rows[:step], rows[step:]
-        sent = jnp.where(high, lower, upper)
-        came = lax.ppermute(sent, BOTH, [(i, i ^ step) for i in range(total)])
-        rows = jnp.where(high, upper, lower) + came
-        step //= 2
-    return rows[0]
+    return jnp.sum(lax.all_to_all(rows, BOTH, 0, 0, tiled=True), axis=0)
 
 
 def gather_dp(value):
@@ -572,25 +733,29 @@
         rows = blocks.reshape(members * row_share, -1)
         return gather_dp(rows).reshape(columns, members, row_share, -1)
 
-    qkv_blocks = jnp.concatenate([blocks_of(w_query), blocks_of(w_key), blocks_of(w_value)], 2)
-    qkv_blocks = trade_blocks(qkv_blocks)
-    up_blocks = trade_blocks(after(blocks_of(w_up), qkv_blocks))
-    attn_w = gathered(jnp.concatenate([qkv_blocks, blocks_of(w_out)], 2))
-    up_w = gathered(up_blocks)
-    down_w = gather_dp(w_down)
-
-    group_tokens = [swap(tokens, rel) for rel in rels]
-    prior_own = jnp.pad(summaries[0], ((0, PRIOR_ROWS - n_summary), (0, 0)))
-    priors = []
-    for rel in rels:
-        pairs = [((((i // columns) ^ rel) * columns + i % columns) - 1, i) for i in range(total)]
-        priors.append(lax.ppermute(prior_own, BOTH, [pair for pair in pairs if pair[0] >= 0]))
-
     small_parts = (
         ln1_gain, ln1_bias, query_bias, value_bias, out_bias, ln2_gain, ln2_bias, up_bias,
         down_bias, presence[0].astype(BF16),
     )
-    packed = gather_small(jnp.concatenate(small_parts)[None])
+    packed = doubled(jnp.concatenate(small_parts)[None], "fsdp")
+    prior = jnp.pad(summaries[0], ((0, PRIOR_ROWS - n_summary), (0, 0)))
+    prior = lax.ppermute(prior, BOTH, [(i, i + 1) for i in range(total - 1)])
+    joined = jnp.concatenate([tokens, prior], 0)
+
+    qkv_blocks = jnp.concatenate([blocks_of(w_query), blocks_of(w_key), blocks_of(w_value)], 2)
+    qkv_blocks = trade_blocks(qkv_blocks)
+    up_blocks, packed = lax.optimization_barrier((blocks_of(w_up), packed, qkv_blocks, joined))[:2]
+    up_blocks = trade_blocks(up_blocks)
+    attn_w = gathered(jnp.concatenate([qkv_blocks, blocks_of(w_out)], 2))
+    up_w = gathered(up_blocks)
+    down_w = gather_dp(w_down)
+
+    joined_near = spread_near(after(joined, up_blocks))
+    group_joined = spread_far(joined, joined_near)
+    cot_near = spread_near(after(cotangent, *flat_list(group_joined[1:])))
+    packed = doubled(packed, "dp").reshape(columns, members, -1).swapaxes(0, 1)
+    packed = packed.reshape(total, -1)
+
     smalls = []
     at = 0
     for part in small_parts:
@@ -612,89 +777,102 @@
     ok_rows = jnp.pad(summary_ok, ((0, 0), (seg_len, PRIOR_ROWS - n_summary)))
     ok_cols = jnp.broadcast_to(ok_rows[:, :, None], (*ok_rows.shape, PAIR))
 
-    group_cot = [swap(cotangent, rel) for rel in rels]
 
     def part_type(rel):
         return BF16 if rel else F32
 
     attn = {}
     middle_parts = {}
-    previous = None
+    previous = []
     for rel in own_last:
-        x = group_tokens[rel]
-        if previous is not None:
-            x = after(x, previous)
+        x = group_joined[rel]
+        if rel == 0:
+            previous = previous + cot_near
+        x = [after(x[0], *previous), *x[1:]]
         low, qkv, lse, mixed, part = attn_forward(
-            x, priors[rel], gain_one, bias_one, qkv_off, ok_rows[rel : rel + 1], attn_w,
-            part_type(rel),
+            x, gain_one, bias_one, qkv_off, ok_rows[rel : rel + 1], attn_w, part_type(rel)
         )
         attn[rel] = (low, qkv, lse, mixed)
-        middle_parts[rel] = swap(part, rel).astype(F32)
-        previous = lse
-    token_vals = tokens.astype(F32)
-    middle = token_vals + sum(middle_parts[rel] for rel in rels) + out_off
-    second_own = norm_apply(middle, gain_two, bias_two).astype(BF16)
-    group_second = [swap(second_own, rel) for rel in rels]
-
+        middle_parts[rel] = swap(part, rel)
+        previous = [lse]
+    middle, second_own = middle_norm(
+        tokens, [middle_parts[rel] for rel in rels], out_off, gain_two, bias_two
+    )
     def ordered(values):
         return [values[rel] for rel in own_last]
 
-    hidden, slope = ffn_hidden(ordered(group_second), up_off, up_w)
-    down_partial = weight_grad([hidden], ordered(group_cot))
-    down_grad = scatter_dp(down_partial, 0).astype(F32)
+    second_near = spread_near(second_own)
+    hidden_own, slope_own = ffn_hidden([[second_own]], up_off, up_w)
+    group_second = spread_far(second_own, second_near, hidden_own)
+    group_cot = spread_far(cotangent, cot_near, hidden_own, second_near)
+    hidden, slope = {0: hidden_own[0]}, {0: slope_own[0]}
+    previous = hidden_own
+    cuts = [1, members - 1, members] if members > 2 else [1, members]
+    for low_rel, high_rel in zip(cuts, cuts[1:]):
+        some = rels[low_rel:high_rel]
+        seconds = [group_second[rel] for rel in some]
+        seconds[0] = [after(seconds[0][0], *previous), *seconds[0][1:]]
+        hiddens, slopes = ffn_hidden(seconds, up_off, up_w)
+        for rel, one, other in zip(some, hiddens, slopes):
+            hidden[rel], slope[rel] = one, other
+        previous = hiddens[:1]
+    down_partial = weight_grad(ordered(hidden), flat_list(ordered(group_cot)))
+    down_share = scatter_dp(down_partial, 0)
+    down_grad = down_share.astype(F32)
     pre, up_sums, second_parts = [], [], {}
-    half = (members + 1) // 2
-    for at in range(0, members, half):
-        some = own_last[at : at + half]
+    for some in (own_last[:-1], [0]):
+        if not some:
+            continue
         cots = [group_cot[rel] for rel in some]
-        cots[0] = after(cots[0], *(pre[-1:] or [down_partial]))
+        cots[0] = [after(cots[0][0], *(pre[-1:] or [down_partial])), *cots[0][1:]]
         pre_some, sums, *backs = ffn_back(
-            cots, slope, at * seg_len, up_w, down_w, [part_type(rel) for rel in some]
+            cots, [slope[rel] for rel in some], up_w, down_w, [part_type(rel) for rel in some]
         )
         pre.append(pre_some)
         up_sums.append(sums)
         for rel, back in zip(some, backs):
             second_parts[rel] = swap(back, rel)
-    up_partial = weight_grad(ordered(group_second), pre)
-    output_parts = ffn_out(after(hidden, up_partial), down_w, [part_type(rel) for rel in own_last])
-    output_parts = {rel: swap(part, rel) for rel, part in zip(own_last, output_parts)}
-
+    up_partial = weight_grad(flat_list(ordered(group_second)), pre)
     def to_row_blocks(grad):
         return scatter_dp(grad.reshape(members, columns * row_share, -1), 1)
 
-    up_share = to_row_blocks(up_partial)
-    up_grad = trade_blocks(up_share).swapaxes(0, 1).reshape(row_share, members * my_ff).astype(F32)
-    second_parts = after(second_parts, up_partial)
-    cot_vals = cotangent.astype(F32)
-    second_grad = sum(second_parts[rel].astype(F32) for rel in rels)
-    _, second_back = jax.vjp(norm_apply, middle, gain_two, bias_two)
-    middle_part, gain_two_grad, bias_two_grad = second_back(second_grad)
-    middle_grad = cot_vals + middle_part
-    branch_low = middle_grad.astype(BF16)
-    group_branch = [swap(branch_low, rel) for rel in rels]
-    output_sum = sum(output_parts[rel].astype(F32) for rel in rels)
-    output = (middle + output_sum + down_off).astype(BF16)
-
+    hiddens = ordered(hidden)
+    hiddens[0] = after(hiddens[0], up_partial)
+    output_parts = ffn_out(hiddens, down_w, [part_type(rel) for rel in own_last])
+    second_parts = after(second_parts, output_parts)
+    up_share = to_row_blocks(after(up_partial, second_parts))
+    middle_grad, branch_low, middle_sums = middle_back(
+        middle, cotangent, [second_parts[rel] for rel in rels], gain_two
+    )
+
+    branch_near = spread_near(branch_low)
     grads, qkv_sums, joined_parts = {}, {}, {}
-    previous = None
-    for rel in rels:
-        x = group_branch[rel]
-        if previous is not None:
-            x = after(x, previous)
+
+    def back_of(rel, x, *others):
         _, qkv, lse, _ = attn[rel]
-        grads[rel], qkv_sums[rel], joined = attn_backward(
+        x = [after(x[0], *others), *x[1:]]
+        grads[rel], qkv_sums[rel], part = attn_backward(
             x, qkv, lse, ok_cols[rel], attn_w, part_type(rel)
         )
-        joined_parts[rel] = swap(joined, rel)
-        previous = qkv_sums[rel]
+        joined_parts[rel] = swap(part, rel)
+
+    back_of(0, [branch_low], down_share)
+    group_branch = spread_far(branch_low, branch_near, qkv_sums[0])
+    order = [0] + ([1, 3, 2] if members == 4 else rels[1:])
+    for last, rel in zip(order, order[1:]):
+        back_of(rel, group_branch[rel], qkv_sums[last])
     attn_partial = attn_weight_grad(
         [attn[rel][0] for rel in rels],
         [grads[rel] for rel in rels],
         [attn[rel][3] for rel in rels],
-        group_branch,
+        flat_list(group_branch),
     )
-    attn_share = to_row_blocks(attn_partial)
     joined_parts = after(joined_parts, attn_partial)
+    attn_share = to_row_blocks(after(attn_partial, up_share))
+    output_parts = {
+        rel: swap(part, rel)
+        for rel, part in zip(own_last, after(output_parts, joined_parts))
+    }
     out_grad = (
         attn_share[:, :, 3 * my_cols :].swapaxes(0, 1).reshape(row_share, width).astype(F32)
     )
@@ -706,17 +884,12 @@
         .astype(F32)
         for part in range(3)
     ]
-    joined_grad = sum(joined_parts[rel].astype(F32) for rel in rels)
-    _, first_back = jax.vjp(norm_apply, token_vals, gain_one, bias_one)
-    token_part, gain_token, bias_token = first_back(joined_grad[:seg_len])
-    prior_vals = priors[0][:n_summary].astype(F32)
-    _, prior_back = jax.vjp(norm_apply, prior_vals, gain_one, bias_one)
-    prior_part, gain_prior, bias_prior = prior_back(joined_grad[seg_len : seg_len + n_summary])
-    tokens_grad = middle_grad + token_part
+    tokens_grad, prior_part, first_sums = first_back(
+        joined, [joined_parts[rel] for rel in rels], middle_grad, gain_one
+    )
     summary_grad = lax.ppermute(
-        prior_part.astype(BF16), BOTH, [(i + 1, i) for i in range(total - 1)]
+        prior_part[:n_summary], BOTH, [(i + 1, i) for i in range(total - 1)]
     ).astype(F32)
-
     def whole(value):
         return value.reshape(total, -1)
 
@@ -727,17 +900,21 @@
 
     qkv_sum = sum(qkv_sums[rel] for rel in rels)
     pieces = [
-        whole(gain_token + gain_prior),
-        whole(bias_token + bias_prior),
+        whole(first_sums[0]),
+        whole(first_sums[1]),
         sliced(qkv_sum[:, :my_cols]),
         sliced(qkv_sum[:, 2 * my_cols :]),
-        whole(jnp.sum(branch_low.astype(F32), axis=0)),
-        whole(gain_two_grad),
-        whole(bias_two_grad),
+        whole(middle_sums[2]),
+        whole(middle_sums[0]),
+        whole(middle_sums[1]),
         sliced(sum(up_sums)),
-        whole(jnp.sum(cot_vals, axis=0)),
+        whole(middle_sums[3]),
     ]
-    share = scatter_small(jnp.concatenate(pieces, 1))
+    share = scatter_small(after(jnp.concatenate(pieces, 1), output_parts))
+    up_blocks = trade_blocks(after(up_share, share))
+    up_grad = up_blocks.swapaxes(0, 1).reshape(row_share, members * my_ff).astype(F32)
+    output_sum = sum(output_parts[rel].astype(F32) for rel in rels)
+    output = (middle + output_sum + down_off).astype(BF16)
     outs = []
     at = 0
     for piece in pieces:

time: 812 us -> 658 us (0.81)
  waiting for transfers between devices: 331 us -> 201 us
  starting transfers between devices: 94.4 us -> 56.3 us
  Pallas kernels: 273 us -> 300 us
  other arithmetic: 39.1 us -> 12.3 us
  local copies, waits for them, and re-layouts: 33.3 us -> 48.6 us
    ppermute x24 -> x28, waiting for transfers between devices: 268 us -> 160 us  [swap(): return lax.ppermute(value, 'fsdp', [(i, i ^ rel) for i in range(count)])]
    ppermute x15 -> x7, starting transfers between devices: 46.4 us -> 7.38 us  [the longest x5 4.79 us: doubled(): came = lax.ppermute(rows, axis, [(i, i ^ step) for i in range(size)])]
    pallas_call x9 -> x14, Pallas kernels: 148 us -> 183 us  [the longest x4 61.8 us: attn_forward(): pl.pallas_call(functools.partial(attn_forward_kernel, len(x)), out_shape=...]
    ppermute x15 -> x7, waiting for transfers between devices: 37.7 us -> 11.6 us  [the longest x5 11.6 us: doubled(): came = lax.ppermute(rows, axis, [(i, i ^ step) for i in range(size)])]
    reduce_sum x12 -> x1, other arithmetic: 25 us -> 0.08 us  [scatter_small(): return jnp.sum(lax.all_to_all(rows, BOTH, 0, 0, tiled=True), axis=0)]
    slice x0 -> x11, local copies, waits for them, and re-layouts: none -> 11.9 us  [the longest x8 10 us: spread_far(): pieces.append([swap(near[0][:rows], 2), swap(near[1][rows:], 1)])]
    pallas_call x2, Pallas kernels: 48.7 us -> 38.9 us  [ffn_back(): pl.pallas_call(kernel, out_shape=(shape_of(rows, wide), shape_of(1, wide,...]
    ppermute x24 -> x28, starting transfers between devices: 33.9 us -> 30.3 us  [swap(): return lax.ppermute(value, 'fsdp', [(i, i ^ rel) for i in range(count)])]
  transfers between devices with their start and end apart: 48 -> 45, of which waited for: 29 -> 20; matrix products, arithmetic and copies ran while one was open for 7% -> 7% of each run, Pallas kernels for 26% -> 46%
where the time goes in v3:
time: 658 us; the launch traced here: 652 us
  Pallas kernels  300 us (46%)
  waiting for transfers between devices  201 us (31%)
  starting transfers between devices  56.3 us (9%)
  local copies, waits for them, and re-layouts  48.6 us (7%)
  blocking collectives  18.8 us (3%)
  between operations  15.3 us (2%)
  other arithmetic  12.3 us (2%)
    ppermute x28, waiting for transfers between devices, swap(): return lax.ppermute(value, 'fsdp', [(i, i ^ rel) for i in range(count)])  160 us
    pallas_call x4, Pallas kernels, attn_forward(): pl.pallas_call(functools.partial(attn_forward_kernel, len(x)), out_shape=...  61.8 us
    pallas_call x4, Pallas kernels, attn_backward(): pl.pallas_call(functools.partial(attn_backward_kernel, len(branch)), out_...  59 us
    pallas_call x2, Pallas kernels, ffn_back(): pl.pallas_call(kernel, out_shape=(shape_of(rows, wide), shape_of(1, wide,...  38.9 us
    pallas_call x3, Pallas kernels, ffn_hidden(): pl.pallas_call(kernel, out_shape=[shape_of(seg, wide)] * (2 * count), in_...  37.7 us
    pallas_call x2, Pallas kernels, weight_grad(): pl.pallas_call(kernel, grid=(tall // GRAD_ROWS,), out_shape=shape_of(tall...  36 us
    ppermute x28, starting transfers between devices, swap(): return lax.ppermute(value, 'fsdp', [(i, i ^ rel) for i in range(count)])  30.3 us
    all_to_all x3, waiting for transfers between devices, trade_blocks(): return lax.all_to_all(blocks, 'fsdp', 0, 0, tiled=True)  22.2 us
  transfers between devices with their start and end apart: 45, of which 20 were waited for; matrix products, arithmetic and copies ran while one was open for 7% of the time, Pallas kernels for 46%

profile of v3, /device:TPU:0, one launch (start us, length us, event | category | flops | bytes accessed | tf_op | source)
XLA Modules:
  0.0 651.8 jit_solution(10430884566277043573)
XLA Ops:
  12.0 5.2 all-to-all-start
  17.5 10.4 %all-to-all-done = bf16[4,64,1536]{2,1,0:T(8,128)(2,1)S(1)} async-done(((bf16[4,64,1536]{2,1,0:T(8,128)(2,1)}), bf16[4,64,1536]{2,1,0:T(8,128)(2,1)S(1)}, u32[]{:S(2)}, u32[]{:S(2)}) %all-to-all-start) | async-done | bytes 786464 | tf_op jit(solution)/shard_map/all_to_all | solution.py:668
  29.4 1.5 collective-permute-start.1
  30.9 1.3 collective-permute-start
  33.1 1.5 collective-permute-start.2
  34.7 1.8 reshape.206
  37.4 18.8 %all_to_all.29 = bf16[4,64,2048]{2,1,0:T(8,128)(2,1)} all-to-all(bf16[4,64,2048]{2,1,0:T(8,128)(2,1)S(1)} %copy.73), channel_id=1, replica_groups=mesh['fsdp'=4,'dp'=8] {'fsdp'}, dimensions={0} | all-to-all | bytes 2097152 | tf_op jit(solution)/shard_map/all_to_all | solution.py:668
  59.0 1.6 collective-permute-start.8
  60.7 5.3 collective-permute-done.8
  66.1 5.3 collective-permute-done.9
  71.8 22.6 %collective-permute-done.4.refs_0_ = bf16[384,2048]{1,0:T(8,128)(2,1)} collective-permute-done((bf16[384,2048]{1,0:T(8,128)(2,1)S(1)}, bf16[384,2048]{1,0:T(8,128)(2,1)}, u32[]{:S(2)}, u32[]{:S(2)}) %collective-permute-start.4) | collective-permute-done | bytes 1572896 | tf_op jit(solution)/shard_map/ppermute | solution.py:642
  98.0 1.5 collective-permute-start.5
  102.8 13.7 %collective-permute-done.6.refs_1_ = bf16[192,2048]{1,0:T(8,128)(2,1)} collective-permute-done((bf16[192,2048]{1,0:T(8,128)(2,1)S(1)}, bf16[192,2048]{1,0:T(8,128)(2,1)}, u32[]{:S(2)}, u32[]{:S(2)}) %collective-permute-start.6) | collective-permute-done | bytes 786464 | tf_op jit(solution)/shard_map/ppermute | solution.py:642
  116.8 1.4 collective-permute-start.11
  119.3 16.0 %attn_forward.4 = (bf16[384,2048]{1,0:T(8,128)(2,1)}, bf16[384,1536]{1,0:T(8,128)(2,1)}, f32[320,128]{1,0:T(8,128)}, bf16[320,512]{1,0:T(8,128)(2,1)}, bf16[320,2048]{1,0:T(8,128)(2,1)}) custom-call(bf16[192,2048]{1,0:T(8,128)(2,1)} %collective-permute-done.5.refs_0_, bf16[192,2048]{1,0:T(8,128)(2,1)} %collective-permute-done.6.refs_1_, ...), custom_call_target="tpu_custom_call" | custom-call | flops 15000000 | bytes 1 | tf_op jit(solution)/shard_map/attn_forward/pallas_call | solution.py:175
  136.4 15.1 %attn_forward.5 = (bf16[384,2048]{1,0:T(8,128)(2,1)}, bf16[384,1536]{1,0:T(8,128)(2,1)}, f32[320,128]{1,0:T(8,128)}, bf16[320,512]{1,0:T(8,128)(2,1)}, bf16[320,2048]{1,0:T(8,128)(2,1)}) custom-call(bf16[384,2048]{1,0:T(8,128)(2,1)} %collective-permute-done.4.refs_0_, f32[1,2048]{1,0:T(1,128)} %reshape.241.refs_2_.refs_1_.refs_6_, ...), custom_call_target="tpu_custom_call" | custom-call | flops 15000000 | bytes 1 | tf_op jit(solution)/shard_map/attn_forward/pallas_call | solution.py:175
  151.6 1.6 collective-permute-start.13
  153.2 15.1 %attn_forward.6 = (bf16[384,2048]{1,0:T(8,128)(2,1)}, bf16[384,1536]{1,0:T(8,128)(2,1)}, f32[320,128]{1,0:T(8,128)}, bf16[320,512]{1,0:T(8,128)(2,1)}, bf16[320,2048]{1,0:T(8,128)(2,1)}) custom-call(bf16[384,2048]{1,0:T(8,128)(2,1)} %collective-permute-done.3.refs_0_, f32[1,2048]{1,0:T(1,128)} %reshape.241.refs_2_.refs_1_.refs_6_, ...), custom_call_target="tpu_custom_call" | custom-call | flops 15000000 | bytes 1 | tf_op jit(solution)/shard_map/attn_forward/pallas_call | solution.py:175
  171.3 15.6 %attn_forward.7 = (bf16[384,2048]{1,0:T(8,128)(2,1)}, bf16[384,1536]{1,0:T(8,128)(2,1)}, f32[320,128]{1,0:T(8,128)}, bf16[320,512]{1,0:T(8,128)(2,1)}, f32[320,2048]{1,0:T(8,128)}) custom-call(bf16[384,2048]{1,0:T(8,128)(2,1)} %copy-done.6, f32[1,2048]{1,0:T(1,128)} %reshape.241.refs_2_.refs_1_.refs_6_, f32[1,2048]{1,0:T(1,128)} %reshape.243.refs_3_.refs_2_, ...), custom_call_target="tpu_custom_call" | custom-call | flops 15000000 | bytes 1 | tf_op jit(solution)/shard_map/attn_forward/pallas_call | solution.py:175
  186.9 16.3 %collective-permute-done.13.refs_3_ = bf16[320,2048]{1,0:T(8,128)(2,1)} collective-permute-done((bf16[320,2048]{1,0:T(8,128)(2,1)}, bf16[320,2048]{1,0:T(8,128)(2,1)}, u32[]{:S(2)}, u32[]{:S(2)}) %collective-permute-start.13) | collective-permute-done | bytes 1310752 | tf_op jit(solution)/shard_map/ppermute | solution.py:642
  203.2 7.4 %middle_norm.1 = (f32[320,2048]{1,0:T(8,128)}, bf16[320,2048]{1,0:T(8,128)(2,1)}) custom-call(bf16[320,2048]{1,0:T(8,128)(2,1)} %refs_0_.1, f32[320,2048]{1,0:T(8,128)} %get-tuple-element.130.refs_1_, bf16[320,2048]{1,0:T(8,128)(2,1)} %collective-permute-done.12.refs_2_, bf16[320,2048]{1,0:T(8,128)(2,1)} %collective-permute-done.13.refs_3_, ...), custom_call_target="tpu_custom_call" | custom-call | flops 5000000 | bytes 1 | tf_op jit(solution)/shard_map/middle_norm/pallas_call | solution.py:550
  210.5 1.3 collective-permute-start.16
  213.8 10.9 %ffn_hidden.3 = (bf16[320,2048]{1,0:T(8,128)(2,1)}, bf16[320,2048]{1,0:T(8,128)(2,1)}) custom-call(bf16[320,2048]{1,0:T(8,128)(2,1)} %get-tuple-element.135.refs_0_.refs_4_, f32[1,2048]{1,0:T(1,128)} %constant_dynamic-slice_fusion.refs_1_.refs_2_, bf16[8,4,64,2048]{3,2,1,0:T(8,128)(2,1)} %bitcast.58), custom_call_target="tpu_custom_call" | custom-call | flops 6000000 | bytes 1 | tf_op jit(solution)/shard_map/ffn_hidden/pallas_call | solution.py:316
  224.7 16.7 %collective-permute-done.16.refs_1_.refs_2_ = bf16[320,2048]{1,0:T(8,128)(2,1)S(1)} collective-permute-done((bf16[320,2048]{1,0:T(8,128)(2,1)}, bf16[320,2048]{1,0:T(8,128)(2,1)S(1)}, u32[]{:S(2)}, u32[]{:S(2)}) %collective-permute-start.16) | collective-permute-done | bytes 1310752 | tf_op jit(solution)/shard_map/ppermute | solution.py:642
  241.3 1.3 collective-permute-done.15.refs_0_.refs_3_
  242.6 2.0 slice.159
  246.1 1.5 collective-permute-start.18
  247.6 2.0 slice.161
  251.0 1.4 collective-permute-start.19
  252.4 15.9 %ffn_hidden.4 = (bf16[320,2048]{1,0:T(8,128)(2,1)}, bf16[320,2048]{1,0:T(8,128)(2,1)}, bf16[320,2048]{1,0:T(8,128)(2,1)}, bf16[320,2048]{1,0:T(8,128)(2,1)}) custom-call(bf16[320,2048]{1,0:T(8,128)(2,1)} %collective-permute-done.15.refs_0_.refs_3_, bf16[320,2048]{1,0:T(8,128)(2,1)} %copy-done.3, f32[1,2048]{1,0:T(1,128)} %constant_dynamic-slice_fusion.refs_1_.refs_2_, ...), custom_call_target="tpu_custom_call" | custom-call | flops 12000000 | bytes 1 | tf_op jit(solution)/shard_map/ffn_hidden/pallas_call | solution.py:316
  269.2 10.9 %ffn_hidden.5 = (bf16[320,2048]{1,0:T(8,128)(2,1)}, bf16[320,2048]{1,0:T(8,128)(2,1)}) custom-call(bf16[160,2048]{1,0:T(8,128)(2,1)} %copy-done.11, bf16[160,2048]{1,0:T(8,128)(2,1)} %collective-permute-done.18.refs_1_, f32[1,2048]{1,0:T(1,128)} %constant_dynamic-slice_fusion.refs_1_.refs_2_, bf16[8,4,64,2048]{3,2,1,0:T(8,128)(2,1)} %bitcast.60), custom_call_target="tpu_custom_call" | custom-call | flops 6000000 | bytes 1 | tf_op jit(solution)/shard_map/ffn_hidden/pallas_call | solution.py:316
  281.1 18.0 %weight_grad.2 = bf16[2048,2048]{1,0:T(8,128)(2,1)} custom-call(bf16[320,2048]{1,0:T(8,128)(2,1)} %get-tuple-element.154.refs_0_, bf16[320,2048]{1,0:T(8,128)(2,1)} %get-tuple-element.144.refs_1_, bf16[320,2048]{1,0:T(8,128)(2,1)} %get-tuple-element.140.refs_2_, bf16[320,2048]{1,0:T(8,128)(2,1)} %get-tuple-element.136.refs_3_, bf16[160,2048]{1,0:T(8,128)(2,1)} %copy-done.9, ...), custom_call_target="tpu_custom_call" | custom-call | flops 17000000 | bytes 1 | tf_op jit(solution)/shard_map/weight_grad/pallas_call | solution.py:450
  299.3 26.0 %ffn_back.2 = (bf16[960,2048]{1,0:T(8,128)(2,1)}, f32[1,2048]{1,0:T(1,128)}, bf16[320,2048]{1,0:T(8,128)(2,1)}, bf16[320,2048]{1,0:T(8,128)(2,1)}, bf16[320,2048]{1,0:T(8,128)(2,1)}) custom-call(bf16[160,2048]{1,0:T(8,128)(2,1)} %copy-done.9, bf16[160,2048]{1,0:T(8,128)(2,1)} %copy-done.8, bf16[320,2048]{1,0:T(8,128)(2,1)} %copy-done.2, ...), custom_call_target="tpu_custom_call" | custom-call | flops 30000000 | bytes 1 | tf_op jit(solution)/shard_map/ffn_back/pallas_call | solution.py:373
  327.3 1.5 collective-permute-start.23
  328.8 12.9 %ffn_back.3 = (bf16[320,2048]{1,0:T(8,128)(2,1)}, f32[1,2048]{1,0:T(1,128)}, f32[320,2048]{1,0:T(8,128)}) custom-call(bf16[320,2048]{1,0:T(8,128)(2,1)} %refs_5_.1, bf16[320,2048]{1,0:T(8,128)(2,1)} %get-tuple-element.152.refs_1_, bf16[8,4,64,2048]{3,2,1,0:T(8,128)(2,1)} %bitcast.62, bf16[2048,2048]{1,0:T(8,128)(2,1)} %all-gather.8.cloned.1.call-done.refs_8_.refs_3_.refs_4_), custom_call_target="tpu_custom_call" | custom-call | flops 10000000 | bytes 1 | tf_op jit(solution)/shard_map/ffn_back/pallas_call | solution.py:373
  341.7 17.9 %weight_grad.3 = bf16[2048,2048]{1,0:T(8,128)(2,1)} custom-call(bf16[160,2048]{1,0:T(8,128)(2,1)} %copy-done.11, bf16[160,2048]{1,0:T(8,128)(2,1)} %collective-permute-done.18.refs_1_, bf16[320,2048]{1,0:T(8,128)(2,1)} %copy-done.3, bf16[320,2048]{1,0:T(8,128)(2,1)} %collective-permute-done.15.refs_0_.refs_3_, ...), custom_call_target="tpu_custom_call" | custom-call | flops 17000000 | bytes 1 | tf_op jit(solution)/shard_map/weight_grad/pallas_call | solution.py:450
  359.6 20.1 %ffn_out.1 = (bf16[320,2048]{1,0:T(8,128)(2,1)}, bf16[320,2048]{1,0:T(8,128)(2,1)}, bf16[320,2048]{1,0:T(8,128)(2,1)}, f32[320,2048]{1,0:T(8,128)}) custom-call(bf16[320,2048]{1,0:T(8,128)(2,1)} %get-tuple-element.154.refs_0_, bf16[320,2048]{1,0:T(8,128)(2,1)} %get-tuple-element.144.refs_1_, bf16[320,2048]{1,0:T(8,128)(2,1)} %get-tuple-element.140.refs_2_, ...), custom_call_target="tpu_custom_call" | custom-call | flops 18000000 | bytes 1 | tf_op jit(solution)/shard_map/ffn_out/pallas_call | solution.py:415
  379.8 3.0 collective-permute-done.22.refs_2_
  383.8 8.3 %middle_back.1 = (f32[320,2048]{1,0:T(8,128)}, bf16[320,2048]{1,0:T(8,128)(2,1)}, f32[4,2048]{1,0:T(4,128)}) custom-call(f32[320,2048]{1,0:T(8,128)} %get-tuple-element.163.refs_0_, bf16[320,2048]{1,0:T(8,128)(2,1)} %copy-done.12, bf16[320,2048]{1,0:T(8,128)(2,1)} %copy-done.13, bf16[320,2048]{1,0:T(8,128)(2,1)} %collective-permute-done.23.refs_3_, ...), custom_call_target="tpu_custom_call" | custom-call | flops 5000000 | bytes 1 | tf_op jit(solution)/shard_map/middle_back/pallas_call | solution.py:584
  394.4 15.1 %attn_backward.4 = (bf16[384,1536]{1,0:T(8,128)(2,1)}, f32[1,1536]{1,0:T(1,128)}, f32[384,2048]{1,0:T(8,128)}) custom-call(bf16[320,2048]{1,0:T(8,128)(2,1)} %get-tuple-element.168.refs_0_.refs_12_, bf16[384,1536]{1,0:T(8,128)(2,1)} %get-tuple-element.169.refs_1_, f32[320,128]{1,0:T(8,128)} %get-tuple-element.170.refs_2_, ...), custom_call_target="tpu_custom_call" | custom-call | flops 14000000 | bytes 1 | tf_op jit(solution)/shard_map/attn_backward/pallas_call | solution.py:263
  409.5 10.6 %collective-permute-done.25.refs_0_.refs_14_ = bf16[320,2048]{1,0:T(8,128)(2,1)S(1)} collective-permute-done((bf16[320,2048]{1,0:T(8,128)(2,1)}, bf16[320,2048]{1,0:T(8,128)(2,1)S(1)}, u32[]{:S(2)}, u32[]{:S(2)}) %collective-permute-start.25) | collective-permute-done | bytes 1310752 | tf_op jit(solution)/shard_map/ppermute | solution.py:642
  424.7 14.5 %attn_backward.5 = (bf16[384,1536]{1,0:T(8,128)(2,1)}, f32[1,1536]{1,0:T(1,128)}, bf16[384,2048]{1,0:T(8,128)(2,1)}) custom-call(bf16[320,2048]{1,0:T(8,128)(2,1)} %copy-done.5, bf16[384,1536]{1,0:T(8,128)(2,1)} %get-tuple-element.175.refs_1_, f32[320,128]{1,0:T(8,128)} %get-tuple-element.127.refs_2_, f32[384,128]{1,0:T(8,128)} %broadcast_in_dim.44.refs_3_, ...), custom_call_target="tpu_custom_call" | custom-call | flops 14000000 | bytes 1 | tf_op jit(solution)/shard_map/attn_backward/pallas_call | solution.py:263
  441.2 14.5 %attn_backward.6 = (bf16[384,1536]{1,0:T(8,128)(2,1)}, f32[1,1536]{1,0:T(1,128)}, bf16[384,2048]{1,0:T(8,128)(2,1)}) custom-call(bf16[160,2048]{1,0:T(8,128)(2,1)} %copy-done.10, bf16[160,2048]{1,0:T(8,128)(2,1)} %collective-permute-done.28.refs_1_.refs_16_, bf16[384,1536]{1,0:T(8,128)(2,1)} %get-tuple-element.180.refs_2_, ...), custom_call_target="tpu_custom_call" | custom-call | flops 14000000 | bytes 1 | tf_op jit(solution)/shard_map/attn_backward/pallas_call | solution.py:263
  456.6 14.8 %attn_backward.7 = (bf16[384,1536]{1,0:T(8,128)(2,1)}, f32[1,1536]{1,0:T(1,128)}, bf16[384,2048]{1,0:T(8,128)(2,1)}) custom-call(bf16[320,2048]{1,0:T(8,128)(2,1)} %copy-done.4, bf16[384,1536]{1,0:T(8,128)(2,1)} %get-tuple-element.183.refs_1_, f32[320,128]{1,0:T(8,128)} %get-tuple-element.125.refs_2_, f32[384,128]{1,0:T(8,128)} %broadcast_in_dim.48.refs_3_, ...), custom_call_target="tpu_custom_call" | custom-call | flops 14000000 | bytes 1 | tf_op jit(solution)/shard_map/attn_backward/pallas_call | solution.py:263
  472.5 1.3 collective-permute-start.30
  478.6 1.6 convert_element_type.106
  480.9 21.7 %attn_weight_grad.1 = bf16[2048,2048]{1,0:T(8,128)(2,1)} custom-call(bf16[384,2048]{1,0:T(8,128)(2,1)} %get-tuple-element.186.refs_0_, bf16[384,2048]{1,0:T(8,128)(2,1)} %get-tuple-element.187.refs_1_, bf16[384,2048]{1,0:T(8,128)(2,1)} %get-tuple-element.188.refs_2_, bf16[384,2048]{1,0:T(8,128)(2,1)} %get-tuple-element.189.refs_3_, ...), custom_call_target="tpu_custom_call" | custom-call | flops 21000000 | bytes 1 | tf_op jit(solution)/shard_map/attn_weight_grad/pallas_call | solution.py:491
  503.9 31.9 %collective-permute-done.29.refs_2_ = bf16[384,2048]{1,0:T(8,128)(2,1)S(1)} collective-permute-done((bf16[384,2048]{1,0:T(8,128)(2,1)}, bf16[384,2048]{1,0:T(8,128)(2,1)S(1)}, u32[]{:S(2)}, u32[]{:S(2)}) %collective-permute-start.29) | collective-permute-done | bytes 1572896 | tf_op jit(solution)/shard_map/ppermute | solution.py:642
  535.8 1.7 collective-permute-start.31
  538.1 1.2 collective-permute-start.33
  539.4 8.9 %first_back.1 = (f32[320,2048]{1,0:T(8,128)}, bf16[64,2048]{1,0:T(8,128)(2,1)}, f32[2,2048]{1,0:T(2,128)}) custom-call(f32[384,2048]{1,0:T(8,128)} %get-tuple-element.198.refs_0_, bf16[384,2048]{1,0:T(8,128)(2,1)} %collective-permute-done.26.refs_1_, bf16[384,2048]{1,0:T(8,128)(2,1)} %copy-done.39, bf16[384,2048]{1,0:T(8,128)(2,1)} %collective-permute-done.30.refs_3_, ...), custom_call_target="tpu_custom_call" | custom-call | flops 499999997952 | bytes 1 | tf_op jit(solution)/shard_map/first_back/pallas_call | solution.py:623
  549.2 1.3 collective-permute-start.34
  552.4 15.4 %collective-permute-done.31 = bf16[320,2048]{1,0:T(8,128)(2,1)} collective-permute-done((bf16[320,2048]{1,0:T(8,128)(2,1)}, bf16[320,2048]{1,0:T(8,128)(2,1)}, u32[]{:S(2)}, u32[]{:S(2)}) %collective-permute-start.31) | collective-permute-done | bytes 1310752 | tf_op jit(solution)/shard_map/ppermute | solution.py:642
  567.9 27.4 %collective-permute-done.32 = bf16[320,2048]{1,0:T(8,128)(2,1)} collective-permute-done((bf16[320,2048]{1,0:T(8,128)(2,1)}, bf16[320,2048]{1,0:T(8,128)(2,1)}, u32[]{:S(2)}, u32[]{:S(2)}) %collective-permute-start.32) | collective-permute-done | bytes 1310752 | tf_op jit(solution)/shard_map/ppermute | solution.py:642
  596.0 5.6 all-to-all-start.2
  602.8 6.5 %all-to-all-done.2 = f32[32,1,768]{2,1,0:T(1,128)S(1)} async-done(((f32[32,1,768]{2,1,0:T(1,128)}), f32[32,1,768]{2,1,0:T(1,128)S(1)}, u32[]{:S(2)}, u32[]{:S(2)}) %all-to-all-start.2) | async-done | bytes 98336 | tf_op jit(solution)/shard_map/all_to_all | solution.py:684
  609.4 4.3 all-to-all-start.4
  613.7 5.0 add_convert_fusion
  619.9 2.1 slice.207
  622.0 6.0 all-to-all-done.4
  628.0 3.5 all-to-all-start.3
  631.5 1.5 convert_bitcast_fusion
  633.0 1.5 copy.86
  636.3 5.8 all-to-all-done.3
  (243 shorter events, 62.3 us)
Async XLA Ops:
  12.0 16.0 %all-to-all-start = ((bf16[4,64,1536]{2,1,0:T(8,128)(2,1)}), bf16[4,64,1536]{2,1,0:T(8,128)(2,1)S(1)}, u32[]{:S(2)}, u32[]{:S(2)}) async-start(bf16[4,64,1536]{2,1,0:T(8,128)(2,1)} %copy.72), calls=%async_computation | async-start | bytes 1572864 | tf_op jit(solution)/shard_map/all_to_all | solution.py:668
  17.1 102.2 %all-gather.4.cloned.1.call-start = ((), (), s32[]{:S(2)}) async-start(), calls=%async_computation.8 | async-start | bytes 9437184 | tf_op jit(solution)/shard_map/all_gather | solution.py:688
  17.4 11.8 %copy-start.30 = (bf16[64]{0:T(256)(128)(2,1)S(1)}, bf16[64]{0:T(256)(128)(2,1)}, u32[]{:S(2)}) copy-start(bf16[64]{0:T(256)(128)(2,1)} %param.24) | copy-start | bytes 388
  17.4 11.8 %copy-start.31 = (bf16[64]{0:T(256)(128)(2,1)S(1)}, bf16[64]{0:T(256)(128)(2,1)}, u32[]{:S(2)}) copy-start(bf16[64]{0:T(256)(128)(2,1)} %param.25) | copy-start | bytes 388
  17.4 11.8 %copy-start.32 = (bf16[64]{0:T(256)(128)(2,1)S(1)}, bf16[64]{0:T(256)(128)(2,1)}, u32[]{:S(2)}) copy-start(bf16[64]{0:T(256)(128)(2,1)} %param.27) | copy-start | bytes 388
  17.5 13.3 %copy-start.16 = (bf16[1,50,2048]{2,1,0:T(8,128)(2,1)S(1)}, bf16[1,50,2048]{2,1,0:T(8,128)(2,1)}, u32[]{:S(2)}) copy-start(bf16[1,50,2048]{2,1,0:T(8,128)(2,1)} %param.21) | copy-start | bytes 614404
  17.5 17.1 %copy-start.7 = (bf16[320,2048]{1,0:T(8,128)(2,1)S(1)}, bf16[320,2048]{1,0:T(8,128)(2,1)}, u32[]{:S(2)}) copy-start(bf16[320,2048]{1,0:T(8,128)(2,1)} %refs_0_.1) | copy-start | bytes 3932164
  29.1 184.6 %all-gather.6.cloned.1.call-start = ((), (), s32[]{:S(2)}) async-start(), calls=%async_computation.9 | async-start | bytes 9437184 | tf_op jit(solution)/shard_map/all_gather | solution.py:688
  29.4 3.7 collective-permute-start.1
  30.9 5.9 collective-permute-start
  33.1 3.7 collective-permute-start.2
  36.8 21.6 %copy-start.6 = (bf16[384,2048]{1,0:T(8,128)(2,1)}, bf16[384,2048]{1,0:T(8,128)(2,1)S(1)}, u32[]{:S(2)}) copy-start(bf16[384,2048]{1,0:T(8,128)(2,1)S(1)} %constant_dynamic-update-slice_fusion.refs_0_.refs_4_) | copy-start | bytes 4718596
  56.2 243.1 %all-gather.8.cloned.1.call-start = ((), (), s32[]{:S(2)}) async-start(), calls=%async_computation.10 | async-start | bytes 9437184 | tf_op jit(solution)/shard_map/all_gather | solution.py:688
  56.9 336.7 %reduce-scatter.4.cloned.1.call-start = ((), (), s32[]{:S(2)}) async-start(), calls=%async_computation.11 | async-start | bytes 9437184 | tf_op jit(solution)/shard_map/reduce_scatter | solution.py:692
  57.2 1.8 collective-permute-start.7
  57.4 37.0 %collective-permute-start.4 = (bf16[384,2048]{1,0:T(8,128)(2,1)S(1)}, bf16[384,2048]{1,0:T(8,128)(2,1)}, u32[]{:S(2)}, u32[]{:S(2)}) collective-permute-start(bf16[384,2048]{1,0:T(8,128)(2,1)S(1)} %constant_dynamic-update-slice_fusion.refs_0_.refs_4_), channel_id=1, source_target_pairs={{0,16},{8,24},{16,0},{24,8},{1,17},{9,25},{17,1},{25,9},{2,18},{10... | collective-permute-start | bytes 4718600 | tf_op jit(solution)/shard_map/ppermute | solution.py:642
  58.4 36.6 %collective-permute-start.3 = (bf16[384,2048]{1,0:T(8,128)(2,1)S(1)}, bf16[384,2048]{1,0:T(8,128)(2,1)}, u32[]{:S(2)}, u32[]{:S(2)}) collective-permute-start(bf16[384,2048]{1,0:T(8,128)(2,1)S(1)} %constant_dynamic-update-slice_fusion.refs_0_.refs_4_), channel_id=1, source_target_pairs={{0,8},{8,0},{16,24},{24,16},{1,9},{9,1},{17,25},{25,17},{2,10},{10... | collective-permute-start | bytes 4718600 | tf_op jit(solution)/shard_map/ppermute | solution.py:642
  59.0 6.9 %collective-permute-start.8 = (bf16[8,818]{1,0:T(8,128)(2,1)S(1)}, bf16[8,818]{1,0:T(8,128)(2,1)S(1)}, u32[]{:S(2)}, u32[]{:S(2)}) collective-permute-start(bf16[8,818]{1,0:T(8,128)(2,1)S(1)} %pad_maximum_fusion.4), channel_id=1, source_target_pairs={{0,2},{1,3},{2,0},{3,1},{4,6},{5,7},{6,4},{7,5},{8,10},{9,11},{10,... | collective-permute-start | bytes 39272 | tf_op jit(solution)/shard_map/ppermute | solution.py:676
  66.0 5.5 collective-permute-start.9
  71.8 45.0 %copy-start = (bf16[320,2048]{1,0:T(8,128)(2,1)S(1)}, bf16[320,2048]{1,0:T(8,128)(2,1)}, u32[]{:S(2)}) copy-start(bf16[320,2048]{1,0:T(8,128)(2,1)} %refs_5_.1) | copy-start | bytes 3932164
  97.4 19.1 %collective-permute-start.6 = (bf16[192,2048]{1,0:T(8,128)(2,1)S(1)}, bf16[192,2048]{1,0:T(8,128)(2,1)}, u32[]{:S(2)}, u32[]{:S(2)}) collective-permute-start(bf16[192,2048]{1,0:T(8,128)(2,1)S(1)} %slice.145), channel_id=1, source_target_pairs={{0,8},{8,0},{16,24},{24,16},{1,9},{9,1},{17,25},{25,17},{2,10},{10... | collective-permute-start | bytes 2359304 | tf_op jit(solution)/shard_map/ppermute | solution.py:642
  98.0 18.7 %collective-permute-start.5 = (bf16[192,2048]{1,0:T(8,128)(2,1)S(1)}, bf16[192,2048]{1,0:T(8,128)(2,1)}, u32[]{:S(2)}, u32[]{:S(2)}) collective-permute-start(bf16[192,2048]{1,0:T(8,128)(2,1)S(1)} %slice.144), channel_id=1, source_target_pairs={{0,16},{8,24},{16,0},{24,8},{1,17},{9,25},{17,1},{25,9},{2,18},{10... | collective-permute-start | bytes 2359304 | tf_op jit(solution)/shard_map/ppermute | solution.py:642
  116.8 54.5 %collective-permute-start.11 = (bf16[320,2048]{1,0:T(8,128)(2,1)S(1)}, bf16[320,2048]{1,0:T(8,128)(2,1)S(1)}, u32[]{:S(2)}, u32[]{:S(2)}) collective-permute-start(bf16[320,2048]{1,0:T(8,128)(2,1)S(1)} %copy-done), channel_id=1, source_target_pairs={{0,16},{8,24},{16,0},{24,8},{1,17},{9,25},{17,1},{25,9},{2,18},{10... | collective-permute-start | bytes 3932168 | tf_op jit(solution)/shard_map/ppermute | solution.py:642
  118.2 53.1 %collective-permute-start.10 = (bf16[320,2048]{1,0:T(8,128)(2,1)S(1)}, bf16[320,2048]{1,0:T(8,128)(2,1)}, u32[]{:S(2)}, u32[]{:S(2)}) collective-permute-start(bf16[320,2048]{1,0:T(8,128)(2,1)S(1)} %copy-done), channel_id=1, source_target_pairs={{0,8},{8,0},{16,24},{24,16},{1,9},{9,1},{17,25},{25,17},{2,10},{10... | collective-permute-start | bytes 3932168 | tf_op jit(solution)/shard_map/ppermute | solution.py:642
  135.3 51.6 %collective-permute-start.14 = (bf16[320,2048]{1,0:T(8,128)(2,1)}, bf16[320,2048]{1,0:T(8,128)(2,1)}, u32[]{:S(2)}, u32[]{:S(2)}) collective-permute-start(bf16[320,2048]{1,0:T(8,128)(2,1)} %get-tuple-element.133), channel_id=1, source_target_pairs={{0,24},{8,16},{16,8},{24,0},{1,25},{9,17},{17,9},{25,1},{2,26},{10... | collective-permute-start | bytes 3932168 | tf_op jit(solution)/shard_map/ppermute | solution.py:642
  151.6 51.6 %collective-permute-start.13 = (bf16[320,2048]{1,0:T(8,128)(2,1)}, bf16[320,2048]{1,0:T(8,128)(2,1)}, u32[]{:S(2)}, u32[]{:S(2)}) collective-permute-start(bf16[320,2048]{1,0:T(8,128)(2,1)} %get-tuple-element.132), channel_id=1, source_target_pairs={{0,16},{8,24},{16,0},{24,8},{1,17},{9,25},{17,1},{25,9},{2,18},{10... | collective-permute-start | bytes 3932168 | tf_op jit(solution)/shard_map/ppermute | solution.py:642
  168.3 34.8 %collective-permute-start.12 = (bf16[320,2048]{1,0:T(8,128)(2,1)}, bf16[320,2048]{1,0:T(8,128)(2,1)}, u32[]{:S(2)}, u32[]{:S(2)}) collective-permute-start(bf16[320,2048]{1,0:T(8,128)(2,1)} %get-tuple-element.131), channel_id=1, source_target_pairs={{0,8},{8,0},{16,24},{24,16},{1,9},{9,1},{17,25},{25,17},{2,10},{10... | collective-permute-start | bytes 3932168 | tf_op jit(solution)/shard_map/ppermute | solution.py:642
  171.3 78.3 %copy-start.2 = (bf16[320,2048]{1,0:T(8,128)(2,1)}, bf16[320,2048]{1,0:T(8,128)(2,1)S(1)}, u32[]{:S(2)}) copy-start(bf16[320,2048]{1,0:T(8,128)(2,1)S(1)} %collective-permute-done.11.refs_6_.refs_2_) | copy-start | bytes 3932164
  210.5 30.8 %collective-permute-start.16 = (bf16[320,2048]{1,0:T(8,128)(2,1)}, bf16[320,2048]{1,0:T(8,128)(2,1)S(1)}, u32[]{:S(2)}, u32[]{:S(2)}) collective-permute-start(bf16[320,2048]{1,0:T(8,128)(2,1)} %get-tuple-element.135.refs_0_.refs_4_), channel_id=1, source_target_pairs={{0,16},{8,24},{16,0},{24,8},{1,17},{9,25},{17,1},{25,9},{2,18},{10... | collective-permute-start | bytes 3932168 | tf_op jit(solution)/shard_map/ppermute | solution.py:642
  211.8 30.7 %collective-permute-start.15 = (bf16[320,2048]{1,0:T(8,128)(2,1)}, bf16[320,2048]{1,0:T(8,128)(2,1)}, u32[]{:S(2)}, u32[]{:S(2)}) collective-permute-start(bf16[320,2048]{1,0:T(8,128)(2,1)} %get-tuple-element.135.refs_0_.refs_4_), channel_id=1, source_target_pairs={{0,8},{8,0},{16,24},{24,16},{1,9},{9,1},{17,25},{25,17},{2,10},{10... | collective-permute-start | bytes 3932168 | tf_op jit(solution)/shard_map/ppermute | solution.py:642
  244.6 23.7 %collective-permute-start.17 = (bf16[160,2048]{1,0:T(8,128)(2,1)}, bf16[160,2048]{1,0:T(8,128)(2,1)S(1)}, u32[]{:S(2)}, u32[]{:S(2)}) collective-permute-start(bf16[160,2048]{1,0:T(8,128)(2,1)} %slice.159), channel_id=1, source_target_pairs={{0,16},{8,24},{16,0},{24,8},{1,17},{9,25},{17,1},{25,9},{2,18},{10... | collective-permute-start | bytes 1966088 | tf_op jit(solution)/shard_map/ppermute | solution.py:642
  246.1 22.3 %collective-permute-start.18 = (bf16[160,2048]{1,0:T(8,128)(2,1)}, bf16[160,2048]{1,0:T(8,128)(2,1)}, u32[]{:S(2)}, u32[]{:S(2)}) collective-permute-start(bf16[160,2048]{1,0:T(8,128)(2,1)} %slice.160), channel_id=1, source_target_pairs={{0,8},{8,0},{16,24},{24,16},{1,9},{9,1},{17,25},{25,17},{2,10},{10... | collective-permute-start | bytes 1966088 | tf_op jit(solution)/shard_map/ppermute | solution.py:642
  250.5 29.6 %collective-permute-start.20 = (bf16[160,2048]{1,0:T(8,128)(2,1)}, bf16[160,2048]{1,0:T(8,128)(2,1)S(1)}, u32[]{:S(2)}, u32[]{:S(2)}) collective-permute-start(bf16[160,2048]{1,0:T(8,128)(2,1)} %slice.162), channel_id=1, source_target_pairs={{0,8},{8,0},{16,24},{24,16},{1,9},{9,1},{17,25},{25,17},{2,10},{10... | collective-permute-start | bytes 1966088 | tf_op jit(solution)/shard_map/ppermute | solution.py:642
  251.0 29.1 %collective-permute-start.19 = (bf16[160,2048]{1,0:T(8,128)(2,1)}, bf16[160,2048]{1,0:T(8,128)(2,1)S(1)}, u32[]{:S(2)}, u32[]{:S(2)}) collective-permute-start(bf16[160,2048]{1,0:T(8,128)(2,1)} %slice.161), channel_id=1, source_target_pairs={{0,16},{8,24},{16,0},{24,8},{1,17},{9,25},{17,1},{25,9},{2,18},{10... | collective-permute-start | bytes 1966088 | tf_op jit(solution)/shard_map/ppermute | solution.py:642
  299.2 204.7 %reduce-scatter.6.cloned.1.call-start = ((), (), s32[]{:S(2)}) async-start(), calls=%async_computation.12 | async-start | bytes 9437184 | tf_op jit(solution)/shard_map/reduce_scatter | solution.py:692
  325.2 54.5 %collective-permute-start.21 = (bf16[320,2048]{1,0:T(8,128)(2,1)}, bf16[320,2048]{1,0:T(8,128)(2,1)S(1)}, u32[]{:S(2)}, u32[]{:S(2)}) collective-permute-start(bf16[320,2048]{1,0:T(8,128)(2,1)} %get-tuple-element.160), channel_id=1, source_target_pairs={{0,8},{8,0},{16,24},{24,16},{1,9},{9,1},{17,25},{25,17},{2,10},{10... | collective-permute-start | bytes 3932168 | tf_op jit(solution)/shard_map/ppermute | solution.py:642
  326.4 56.3 %collective-permute-start.22 = (bf16[320,2048]{1,0:T(8,128)(2,1)}, bf16[320,2048]{1,0:T(8,128)(2,1)S(1)}, u32[]{:S(2)}, u32[]{:S(2)}) collective-permute-start(bf16[320,2048]{1,0:T(8,128)(2,1)} %get-tuple-element.161), channel_id=1, source_target_pairs={{0,16},{8,24},{16,0},{24,8},{1,17},{9,25},{17,1},{25,9},{2,18},{10... | collective-permute-start | bytes 3932168 | tf_op jit(solution)/shard_map/ppermute | solution.py:642
  327.3 55.5 %collective-permute-start.23 = (bf16[320,2048]{1,0:T(8,128)(2,1)}, bf16[320,2048]{1,0:T(8,128)(2,1)}, u32[]{:S(2)}, u32[]{:S(2)}) collective-permute-start(bf16[320,2048]{1,0:T(8,128)(2,1)} %get-tuple-element.162), channel_id=1, source_target_pairs={{0,24},{8,16},{16,8},{24,0},{1,25},{9,17},{17,9},{25,1},{2,26},{10... | collective-permute-start | bytes 3932168 | tf_op jit(solution)/shard_map/ppermute | solution.py:642
  383.8 236.1 %reduce-scatter.8.cloned.1.call-start = ((), (), s32[]{:S(2)}) async-start(), calls=%async_computation.13 | async-start | bytes 9437184 | tf_op jit(solution)/shard_map/reduce_scatter | solution.py:692
  392.2 27.9 %collective-permute-start.25 = (bf16[320,2048]{1,0:T(8,128)(2,1)}, bf16[320,2048]{1,0:T(8,128)(2,1)S(1)}, u32[]{:S(2)}, u32[]{:S(2)}) collective-permute-start(bf16[320,2048]{1,0:T(8,128)(2,1)} %get-tuple-element.168.refs_0_.refs_12_), channel_id=1, source_target_pairs={{0,16},{8,24},{16,0},{24,8},{1,17},{9,25},{17,1},{25,9},{2,18},{10... | collective-permute-start | bytes 3932168 | tf_op jit(solution)/shard_map/ppermute | solution.py:642
  393.2 26.9 %collective-permute-start.24 = (bf16[320,2048]{1,0:T(8,128)(2,1)}, bf16[320,2048]{1,0:T(8,128)(2,1)S(1)}, u32[]{:S(2)}, u32[]{:S(2)}) collective-permute-start(bf16[320,2048]{1,0:T(8,128)(2,1)} %get-tuple-element.168.refs_0_.refs_12_), channel_id=1, source_target_pairs={{0,8},{8,0},{16,24},{24,16},{1,9},{9,1},{17,25},{25,17},{2,10},{10... | collective-permute-start | bytes 3932168 | tf_op jit(solution)/shard_map/ppermute | solution.py:642
  420.1 19.1 %copy-start.4 = (bf16[320,2048]{1,0:T(8,128)(2,1)}, bf16[320,2048]{1,0:T(8,128)(2,1)S(1)}, u32[]{:S(2)}) copy-start(bf16[320,2048]{1,0:T(8,128)(2,1)S(1)} %collective-permute-done.25.refs_0_.refs_14_) | copy-start | bytes 3932164
  421.1 19.2 %collective-permute-start.27 = (bf16[160,2048]{1,0:T(8,128)(2,1)}, bf16[160,2048]{1,0:T(8,128)(2,1)S(1)}, u32[]{:S(2)}, u32[]{:S(2)}) collective-permute-start(bf16[160,2048]{1,0:T(8,128)(2,1)} %slice.163), channel_id=1, source_target_pairs={{0,16},{8,24},{16,0},{24,8},{1,17},{9,25},{17,1},{25,9},{2,18},{10... | collective-permute-start | bytes 1966088 | tf_op jit(solution)/shard_map/ppermute | solution.py:642
  422.9 17.4 %collective-permute-start.28 = (bf16[160,2048]{1,0:T(8,128)(2,1)}, bf16[160,2048]{1,0:T(8,128)(2,1)}, u32[]{:S(2)}, u32[]{:S(2)}) collective-permute-start(bf16[160,2048]{1,0:T(8,128)(2,1)} %slice.164), channel_id=1, source_target_pairs={{0,8},{8,0},{16,24},{24,16},{1,9},{9,1},{17,25},{25,17},{2,10},{10... | collective-permute-start | bytes 1966088 | tf_op jit(solution)/shard_map/ppermute | solution.py:642
  439.2 64.7 %collective-permute-start.26 = (bf16[384,2048]{1,0:T(8,128)(2,1)}, bf16[384,2048]{1,0:T(8,128)(2,1)}, u32[]{:S(2)}, u32[]{:S(2)}) collective-permute-start(bf16[384,2048]{1,0:T(8,128)(2,1)} %get-tuple-element.176), channel_id=1, source_target_pairs={{0,8},{8,0},{16,24},{24,16},{1,9},{9,1},{17,25},{25,17},{2,10},{10... | collective-permute-start | bytes 4718600 | tf_op jit(solution)/shard_map/ppermute | solution.py:642
  456.6 18.0 %copy-start.24 = (f32[1,2048]{1,0:T(1,128)S(1)}, f32[1,2048]{1,0:T(1,128)}, u32[]{:S(2)}) copy-start(f32[1,2048]{1,0:T(1,128)} %get-tuple-element.212) | copy-start | bytes 24580
  456.6 18.0 %copy-start.25 = (f32[1,2048]{1,0:T(1,128)S(1)}, f32[1,2048]{1,0:T(1,128)}, u32[]{:S(2)}) copy-start(f32[1,2048]{1,0:T(1,128)} %get-tuple-element.213) | copy-start | bytes 24580
  456.6 19.2 %copy-start.21 = (f32[4,2048]{1,0:T(4,128)S(1)}, f32[4,2048]{1,0:T(4,128)}, u32[]{:S(2)}) copy-start(f32[4,2048]{1,0:T(4,128)} %get-tuple-element.211) | copy-start | bytes 98308
  456.6 22.0 %copy-start.14 = (bf16[256,2048]{1,0:T(8,128)(2,1)S(1)}, bf16[256,2048]{1,0:T(8,128)(2,1)}, u32[]{:S(2)}) copy-start(bf16[256,2048]{1,0:T(8,128)(2,1)} %reduce-scatter.4.cloned.1.call-done) | copy-start | bytes 3145732
  471.3 64.5 %collective-permute-start.29 = (bf16[384,2048]{1,0:T(8,128)(2,1)}, bf16[384,2048]{1,0:T(8,128)(2,1)S(1)}, u32[]{:S(2)}, u32[]{:S(2)}) collective-permute-start(bf16[384,2048]{1,0:T(8,128)(2,1)} %get-tuple-element.184), channel_id=1, source_target_pairs={{0,16},{8,24},{16,0},{24,8},{1,17},{9,25},{17,1},{25,9},{2,18},{10... | collective-permute-start | bytes 4718600 | tf_op jit(solution)/shard_map/ppermute | solution.py:642
  472.5 63.3 %collective-permute-start.30 = (bf16[384,2048]{1,0:T(8,128)(2,1)}, bf16[384,2048]{1,0:T(8,128)(2,1)}, u32[]{:S(2)}, u32[]{:S(2)}) collective-permute-start(bf16[384,2048]{1,0:T(8,128)(2,1)} %get-tuple-element.185), channel_id=1, source_target_pairs={{0,24},{8,16},{16,8},{24,0},{1,25},{9,17},{17,9},{25,1},{2,26},{10... | collective-permute-start | bytes 4718600 | tf_op jit(solution)/shard_map/ppermute | solution.py:642
  535.8 32.0 %collective-permute-start.31 = (bf16[320,2048]{1,0:T(8,128)(2,1)}, bf16[320,2048]{1,0:T(8,128)(2,1)}, u32[]{:S(2)}, u32[]{:S(2)}) collective-permute-start(bf16[320,2048]{1,0:T(8,128)(2,1)} %get-tuple-element.203), channel_id=1, source_target_pairs={{0,8},{8,0},{16,24},{24,16},{1,9},{9,1},{17,25},{25,17},{2,10},{10... | collective-permute-start | bytes 3932168 | tf_op jit(solution)/shard_map/ppermute | solution.py:642
  537.6 57.7 %collective-permute-start.32 = (bf16[320,2048]{1,0:T(8,128)(2,1)}, bf16[320,2048]{1,0:T(8,128)(2,1)}, u32[]{:S(2)}, u32[]{:S(2)}) collective-permute-start(bf16[320,2048]{1,0:T(8,128)(2,1)} %get-tuple-element.204), channel_id=1, source_target_pairs={{0,16},{8,24},{16,0},{24,8},{1,17},{9,25},{17,1},{25,9},{2,18},{10... | collective-permute-start | bytes 3932168 | tf_op jit(solution)/shard_map/ppermute | solution.py:642
  538.1 57.2 %collective-permute-start.33 = (bf16[320,2048]{1,0:T(8,128)(2,1)}, bf16[320,2048]{1,0:T(8,128)(2,1)}, u32[]{:S(2)}, u32[]{:S(2)}) collective-permute-start(bf16[320,2048]{1,0:T(8,128)(2,1)} %get-tuple-element.205), channel_id=1, source_target_pairs={{0,24},{8,16},{16,8},{24,0},{1,25},{9,17},{17,9},{25,1},{2,26},{10... | collective-permute-start | bytes 3932168 | tf_op jit(solution)/shard_map/ppermute | solution.py:642
  539.3 12.2 %copy-start.17 = (f32[32,64]{1,0:T(8,128)S(1)}, f32[32,64]{1,0:T(8,128)}, u32[]{:S(2)}) copy-start(f32[32,64]{1,0:T(8,128)} %reshape_squeeze.23) | copy-start | bytes 24580
  539.3 12.2 %copy-start.18 = (f32[32,64]{1,0:T(8,128)S(1)}, f32[32,64]{1,0:T(8,128)}, u32[]{:S(2)}) copy-start(f32[32,64]{1,0:T(8,128)} %reshape_squeeze.22) | copy-start | bytes 24580
  539.3 12.2 %copy-start.19 = (f32[32,64]{1,0:T(8,128)S(1)}, f32[32,64]{1,0:T(8,128)}, u32[]{:S(2)}) copy-start(f32[32,64]{1,0:T(8,128)} %reshape_squeeze.21) | copy-start | bytes 24580
  539.4 12.2 %copy-start.20 = (f32[32,64]{1,0:T(8,128)S(1)}, f32[32,64]{1,0:T(8,128)}, u32[]{:S(2)}) copy-start(f32[32,64]{1,0:T(8,128)} %reshape_squeeze.20) | copy-start | bytes 24580
  549.2 52.3 %collective-permute-start.34 = (bf16[50,2048]{1,0:T(8,128)(2,1)S(1)}, bf16[50,2048]{1,0:T(8,128)(2,1)S(1)}, u32[]{:S(2)}, u32[]{:S(2)}) collective-permute-start(bf16[50,2048]{1,0:T(8,128)(2,1)S(1)} %slice.166), channel_id=1, source_target_pairs={{1,0},{2,1},{3,2},{4,3},{5,4},{6,5},{7,6},{8,7},{9,8},{10,9},{11,1... | collective-permute-start | bytes 614408 | tf_op jit(solution)/shard_map/ppermute | solution.py:890
  596.0 13.3 %all-to-all-start.2 = ((f32[32,1,768]{2,1,0:T(1,128)}), f32[32,1,768]{2,1,0:T(1,128)S(1)}, u32[]{:S(2)}, u32[]{:S(2)}) async-start(f32[32,1,768]{2,1,0:T(1,128)} %all_to_all.20), calls=%async_computation.3 | async-start | bytes 196608 | tf_op jit(solution)/shard_map/all_to_all | solution.py:684
  601.6 12.1 %copy-start.1 = (f32[320,2048]{1,0:T(8,128)S(1)}, f32[320,2048]{1,0:T(8,128)}, u32[]{:S(2)}) copy-start(f32[320,2048]{1,0:T(8,128)} %get-tuple-element.134.refs_4_) | copy-start | bytes 7864324
  601.6 12.1 %copy-start.22 = (f32[2048]{0:T(1024)S(1)}, f32[2048]{0:T(1024)}, u32[]{:S(2)}) copy-start(f32[2048]{0:T(1024)} %reshape.256) | copy-start | bytes 24580
  609.4 18.6 %all-to-all-start.4 = ((bf16[4,64,2048]{2,1,0:T(8,128)(2,1)}), bf16[4,64,2048]{2,1,0:T(8,128)(2,1)}, u32[]{:S(2)}, u32[]{:S(2)}) async-start(bf16[4,64,2048]{2,1,0:T(8,128)(2,1)} %reduce-scatter.6.cloned.1.call-done), calls=%async_computation.7 | async-start | bytes 2097152 | tf_op jit(solution)/shard_map/all_to_all | solution.py:668
  628.0 14.1 %all-to-all-start.3 = ((bf16[4,64,1536]{2,1,0:T(8,128)(2,1)}), bf16[4,64,1536]{2,1,0:T(8,128)(2,1)S(1)}, u32[]{:S(2)}, u32[]{:S(2)}) async-start(bf16[4,64,1536]{2,1,0:T(8,128)(2,1)} %slice.207), calls=%async_computation.6 | async-start | bytes 1572864 | tf_op jit(solution)/shard_map/all_to_all | solution.py:668
  (23 other events, 131.0 us)
Sparse Core Ops, SparseCore 0:
  29.2 83.5 all-gather.3
  114.4 80.4 all-gather.5
  196.5 80.6 all-gather.7
  299.3 88.9 reduce-scatter.3
  390.4 87.9 reduce-scatter.5
  504.1 91.4 reduce-scatter.7

commit v4 on v3

--- a/solution.py
+++ b/solution.py
@@ -76,6 +76,10 @@
     return copies
 
 
+def flat_list(lists):
+    return [piece for some in lists for piece in some]
+
+
 def wait_all(copies):
     for copy in copies:
         copy.wait()
@@ -105,181 +109,207 @@
     return jax.ShapeDtypeStruct((rows, columns), dtype)
 
 
-def attn_forward_kernel(
-    count, *refs,
-):
-    gain_ref, bias_ref, off_ref, ok_ref, attn_hbm = refs[count : count + 5]
-    low_ref, qkv_ref, lse_ref, mixed_ref, part_ref, x_ref, weights, mask, sems = refs[count + 5 :]
-    members = weights.shape[0]
-    seg, cols = mixed_ref.shape
-    keys = low_ref.shape[0]
-    x_copies = load_rows(refs[:count], x_ref, sems.at[pl.ds(members, count)])
-    copies = load_blocks(attn_hbm, weights, sems)
-    row = lax.broadcasted_iota(jnp.int32, (seg, keys), 0)
-    col = lax.broadcasted_iota(jnp.int32, (seg, keys), 1)
-    mask[...] = jnp.where(jnp.logical_or(col <= row, ok_ref[...] > 0.5), 0.0, MASKED)
-    gain, bias = gain_ref[...], bias_ref[...]
-    wait_all(x_copies)
-
-    def norm_rows(block, _):
-        at = pl.ds(pl.multiple_of(block * NORM_ROWS, NORM_ROWS), NORM_ROWS)
-        low_ref[at, :] = norm_apply(x_ref[at, :].astype(F32), gain, bias).astype(BF16)
-        return _
-
-    lax.fori_loop(0, keys // NORM_ROWS, norm_rows, 0)
-    wait_all(copies)
-
-    def project(part, _):
-        at = pl.ds(pl.multiple_of(part * cols, PAIR), cols)
-        qkv_ref[:, at] = (dot(low_ref[...], rows_of(weights, at)) + off_ref[:, at]).astype(BF16)
-        return _
-
-    lax.fori_loop(0, 3, project, 0)
-    lane = lax.broadcasted_iota(jnp.int32, (seg, PAIR), 1)
-
-    def attend(pair, _):
-        query = qkv_ref[:seg, pair_at(0, pair)] * jnp.asarray(HEAD**-0.5, BF16)
-        key = qkv_ref[:, pair_at(cols, pair)]
-        value = qkv_ref[:, pair_at(2 * cols, pair)]
-        merged = None
-        for half in range(2):
-            inside = in_pair(half, seg)
-            scores = dot_t(jnp.where(inside, query, jnp.zeros_like(query)), key) + mask[...]
-            row_max = jnp.max(scores, axis=-1, keepdims=True)
-            expo = jnp.exp(scores - row_max)
-            row_total = jnp.sum(expo, axis=-1, keepdims=True)
-            log_total = row_max + jnp.log(row_total)
-            lse_ref[...] = jnp.where(lane == 2 * pair + half, log_total, lse_ref[...])
-            mixed = dot((expo * (1.0 / row_total)).astype(BF16), value)
-            merged = mixed if merged is None else jnp.where(inside, mixed, merged)
-        mixed_ref[:, pair_at(0, pair)] = merged.astype(BF16)
-        return _
-
-    lse_ref[...] = jnp.zeros_like(lse_ref)
-    lax.fori_loop(0, cols // PAIR, attend, 0)
-
-    def project_out(block, _):
-        at = pl.ds(pl.multiple_of(block * cols, PAIR), cols)
-        weight = block_of(weights, block, pl.ds(3 * cols, cols))
-        part_ref[:, at] = dot(mixed_ref[...], weight).astype(part_ref.dtype)
-        return _
-
-    lax.fori_loop(0, members, project_out, 0)
-
-
-def attn_forward(x, gain, bias, off, ok_row, attn_w, part_type):
-    keys, width = sum(piece.shape[0] for piece in x), x[0].shape[1]
+def attn_forward(xs, gain, bias, off, ok_rows, attn_w, types):
+    count = len(xs)
+    pieces = flat_list(xs)
+    given = len(pieces)
+    keys, width = sum(piece.shape[0] for piece in xs[0]), pieces[0].shape[1]
     seg = keys - PRIOR_ROWS
     columns, members, share, wide = attn_w.shape
     cols = wide // 4
-    return pl.pallas_call(
-        functools.partial(attn_forward_kernel, len(x)),
-        out_shape=(
+
+    def kernel(*refs):
+        gain_ref, bias_ref, off_ref, ok_ref, attn_hbm = refs[given : given + 5]
+        outs = refs[given + 5 : given + 5 + 5 * count]
+        x_all, weights, mask, sems = refs[given + 5 + 5 * count :]
+        x_copies = load_rows(refs[:given], x_all, sems.at[pl.ds(members, given)])
+        copies = load_blocks(attn_hbm, weights, sems)
+        gain, bias = gain_ref[...], bias_ref[...]
+        wait_all(x_copies)
+        for index in range(count):
+            low_ref = outs[5 * index]
+
+            def norm_rows(block, _):
+                start = pl.multiple_of(block * NORM_ROWS, NORM_ROWS)
+                values = x_all[pl.ds(index * keys + start, NORM_ROWS), :].astype(F32)
+                low_ref[pl.ds(start, NORM_ROWS), :] = norm_apply(values, gain, bias).astype(BF16)
+                return _
+
+            lax.fori_loop(0, keys // NORM_ROWS, norm_rows, 0)
+        wait_all(copies)
+        for index in range(count):
+            attend_segment(ok_ref[index : index + 1, :], off_ref, weights, mask, outs[5 * index : 5 * index + 5])
+
+    def attend_segment(ok_row, off_ref, weights, mask, refs):
+        low_ref, qkv_ref, lse_ref, mixed_ref, part_ref = refs
+        row = lax.broadcasted_iota(jnp.int32, (seg, keys), 0)
+        col = lax.broadcasted_iota(jnp.int32, (seg, keys), 1)
+        mask[...] = jnp.where(jnp.logical_or(col <= row, ok_row > 0.5), 0.0, MASKED)
+
+        def project(part, _):
+            at = pl.ds(pl.multiple_of(part * cols, PAIR), cols)
+            value = dot(low_ref[...], rows_of(weights, at)) + off_ref[:, at]
+            qkv_ref[:, at] = value.astype(BF16)
+            return _
+
+        lax.fori_loop(0, 3, project, 0)
+        lane = lax.broadcasted_iota(jnp.int32, (seg, PAIR), 1)
+
+        def attend(pair, _):
+            query = qkv_ref[:seg, pair_at(0, pair)] * jnp.asarray(HEAD**-0.5, BF16)
+            key = qkv_ref[:, pair_at(cols, pair)]
+            value = qkv_ref[:, pair_at(2 * cols, pair)]
+            merged = None
+            for half in range(2):
+                inside = in_pair(half, seg)
+                scores = dot_t(jnp.where(inside, query, jnp.zeros_like(query)), key) + mask[...]
+                row_max = jnp.max(scores, axis=-1, keepdims=True)
+                expo = jnp.exp(scores - row_max)
+                row_total = jnp.sum(expo, axis=-1, keepdims=True)
+                log_total = row_max + jnp.log(row_total)
+                lse_ref[...] = jnp.where(lane == 2 * pair + half, log_total, lse_ref[...])
+                mixed = dot((expo * (1.0 / row_total)).astype(BF16), value)
+                merged = mixed if merged is None else jnp.where(inside, mixed, merged)
+            mixed_ref[:, pair_at(0, pair)] = merged.astype(BF16)
+            return _
+
+        lse_ref[...] = jnp.zeros_like(lse_ref)
+        lax.fori_loop(0, cols // PAIR, attend, 0)
+
+        def project_out(block, _):
+            at = pl.ds(pl.multiple_of(block * cols, PAIR), cols)
+            weight = block_of(weights, block, pl.ds(3 * cols, cols))
+            part_ref[:, at] = dot(mixed_ref[...], weight).astype(part_ref.dtype)
+            return _
+
+        lax.fori_loop(0, members, project_out, 0)
+
+    shapes = []
+    for dtype in types:
+        shapes += [
             shape_of(keys, width),
             shape_of(keys, 3 * cols),
             shape_of(seg, PAIR, F32),
             shape_of(seg, cols),
-            shape_of(seg, width, part_type),
-        ),
-        in_specs=[HBM] * len(x) + [VMEM] * 4 + [HBM],
-        out_specs=(VMEM,) * 5,
+            shape_of(seg, width, dtype),
+        ]
+    outs = pl.pallas_call(
+        kernel,
+        out_shape=shapes,
+        in_specs=[HBM] * given + [VMEM] * 4 + [HBM],
+        out_specs=[VMEM] * len(shapes),
         scratch_shapes=[
-            pltpu.VMEM((keys, width), BF16),
+            pltpu.VMEM((count * keys, width), BF16),
             pltpu.VMEM((members, columns, share, wide), BF16),
             pltpu.VMEM((seg, keys), F32),
-            pltpu.SemaphoreType.DMA((members + len(x),)),
+            pltpu.SemaphoreType.DMA((members + given,)),
         ],
         name="attn_forward",
-        **kernel_params(15),
-    )(*x, gain, bias, off, ok_row, attn_w)
-
-
-def attn_backward_kernel(
-    count, *refs,
-):
-    qkv_ref, lse_ref, ok_ref, attn_hbm, grads_ref, sums_ref, joined_ref = refs[count : count + 7]
-    branch_ref, weights, mask, lse_t, mixed_grad, sems = refs[count + 7 :]
-    members = weights.shape[0]
-    cols = mixed_grad.shape[1]
-    seg = branch_ref.shape[0]
-    keys = qkv_ref.shape[0]
-    branch_copies = load_rows(refs[:count], branch_ref, sems.at[pl.ds(members, count)])
-    copies = load_blocks(attn_hbm, weights, sems)
-    row = lax.broadcasted_iota(jnp.int32, (keys, seg), 0)
-    col = lax.broadcasted_iota(jnp.int32, (keys, seg), 1)
-    mask[...] = jnp.where(jnp.logical_or(row <= col, ok_ref[:, :1] > 0.5), 0.0, MASKED)
-    lse_t[...] = lse_ref[...].T
-    grads_ref[seg:, :cols] = jnp.zeros((keys - seg, cols), BF16)
-    total = 0.0
-    wait_all(branch_copies)
-    for block in range(members):
-        copies[block].wait()
-        weight = block_of(weights, block, pl.ds(3 * cols, cols))
-        total = total + dot_t(branch_ref[:, block * cols : (block + 1) * cols], weight)
-    mixed_grad[...] = total.astype(BF16)
-
-    def attend(pair, _):
-        query = qkv_ref[:seg, pair_at(0, pair)]
-        scaled = query * jnp.asarray(HEAD**-0.5, BF16)
-        key = qkv_ref[:, pair_at(cols, pair)]
-        value = qkv_ref[:, pair_at(2 * cols, pair)]
-        mixed = mixed_grad[:, pair_at(0, pair)]
-        query_grad = key_grad = value_grad = 0.0
-        for half in range(2):
-            inside, inside_key = in_pair(half, seg), in_pair(half, keys)
-            zero = jnp.zeros_like(query)
-            scores = dot_t(key, jnp.where(inside, scaled, zero)) + mask[...]
-            probs = jnp.exp(scores - lse_t[pl.ds(2 * pair + half, 1), :])
-            mixed_half = jnp.where(inside, mixed, zero)
-            prob_grad = dot_t(value, mixed_half)
-            value_grad = value_grad + dot(probs.astype(BF16), mixed_half)
-            delta = jnp.sum(prob_grad * probs, axis=0, keepdims=True)
-            score_grad = (probs * (prob_grad - delta)).astype(BF16)
-            key_grad = key_grad + dot(score_grad, jnp.where(inside, query, zero))
-            key_half = jnp.where(inside_key, key, jnp.zeros_like(key))
-            query_grad = query_grad + t_dot(score_grad, key_half)
-        grads_ref[:seg, pair_at(0, pair)] = (query_grad * HEAD**-0.5).astype(BF16)
-        grads_ref[:, pair_at(cols, pair)] = (key_grad * HEAD**-0.5).astype(BF16)
-        grads_ref[:, pair_at(2 * cols, pair)] = value_grad.astype(BF16)
-        return _
-
-    lax.fori_loop(0, cols // PAIR, attend, 0)
-
-    def back(block, _):
-        weight = block_of(weights, block, pl.ds(0, 3 * cols))
-        at = pl.ds(pl.multiple_of(block * cols, PAIR), cols)
-        joined_ref[:, at] = dot_t(grads_ref[...], weight).astype(joined_ref.dtype)
-        return _
-
-    lax.fori_loop(0, members, back, 0)
-    sums_ref[...] = jnp.sum(grads_ref[...].astype(F32), axis=0, keepdims=True)
-
-
-def attn_backward(branch, qkv, lse, ok_col, attn_w, joined_type):
-    seg, width = sum(piece.shape[0] for piece in branch), branch[0].shape[1]
-    keys = qkv.shape[0]
+        **kernel_params(12 * count),
+    )(*pieces, gain, bias, off, ok_rows, attn_w)
+    return [outs[5 * index : 5 * index + 5] for index in range(count)]
+
+
+def attn_backward(branches, qkvs, lses, ok_cols, attn_w, types):
+    count = len(branches)
+    pieces = flat_list(branches)
+    given = len(pieces)
+    seg, width = sum(piece.shape[0] for piece in branches[0]), pieces[0].shape[1]
+    keys = qkvs[0].shape[0]
     columns, members, share, wide = attn_w.shape
     cols = wide // 4
-    return pl.pallas_call(
-        functools.partial(attn_backward_kernel, len(branch)),
-        out_shape=(
+
+    def kernel(*refs):
+        ins = refs[given : given + 3 * count]
+        attn_hbm = refs[given + 3 * count]
+        outs = refs[given + 3 * count + 1 : given + 6 * count + 1]
+        branch_all, weights, mask, lse_t, mixed_grad, sems = refs[given + 6 * count + 1 :]
+        branch_copies = load_rows(refs[:given], branch_all, sems.at[pl.ds(members, given)])
+        copies = load_blocks(attn_hbm, weights, sems)
+        wait_all(branch_copies)
+        for index in range(count):
+            branch = branch_all.at[pl.ds(index * seg, seg)]
+            some_in = [ins[index], ins[count + index], ins[2 * count + index]]
+            some_out = outs[3 * index : 3 * index + 3]
+            waits = copies if index == 0 else []
+            back_segment(branch, *some_in, *some_out, weights, mask, lse_t, mixed_grad, waits)
+
+    def back_segment(
+        branch_ref, qkv_ref, lse_ref, ok_ref, grads_ref, sums_ref, joined_ref,
+        weights, mask, lse_t, mixed_grad, waits,
+    ):
+        row = lax.broadcasted_iota(jnp.int32, (keys, seg), 0)
+        col = lax.broadcasted_iota(jnp.int32, (keys, seg), 1)
+        mask[...] = jnp.where(jnp.logical_or(row <= col, ok_ref[:, :1] > 0.5), 0.0, MASKED)
+        lse_t[...] = lse_ref[...].T
+        grads_ref[seg:, :cols] = jnp.zeros((keys - seg, cols), BF16)
+        total = 0.0
+        for block in range(members):
+            wait_all(waits[block : block + 1])
+            weight = block_of(weights, block, pl.ds(3 * cols, cols))
+            total = total + dot_t(branch_ref[:, block * cols : (block + 1) * cols], weight)
+        mixed_grad[...] = total.astype(BF16)
+
+        def attend(pair, _):
+            query = qkv_ref[:seg, pair_at(0, pair)]
+            scaled = query * jnp.asarray(HEAD**-0.5, BF16)
+            key = qkv_ref[:, pair_at(cols, pair)]
+            value = qkv_ref[:, pair_at(2 * cols, pair)]
+            mixed = mixed_grad[:, pair_at(0, pair)]
+            query_grad = key_grad = value_grad = 0.0
+            for half in range(2):
+                inside, inside_key = in_pair(half, seg), in_pair(half, keys)
+                zero = jnp.zeros_like(query)
+                scores = dot_t(key, jnp.where(inside, scaled, zero)) + mask[...]
+                probs = jnp.exp(scores - lse_t[pl.ds(2 * pair + half, 1), :])
+                mixed_half = jnp.where(inside, mixed, zero)
+                prob_grad = dot_t(value, mixed_half)
+                value_grad = value_grad + dot(probs.astype(BF16), mixed_half)
+                delta = jnp.sum(prob_grad * probs, axis=0, keepdims=True)
+                score_grad = (probs * (prob_grad - delta)).astype(BF16)
+                key_grad = key_grad + dot(score_grad, jnp.where(inside, query, zero))
+                key_half = jnp.where(inside_key, key, jnp.zeros_like(key))
+                query_grad = query_grad + t_dot(score_grad, key_half)
+            grads_ref[:seg, pair_at(0, pair)] = (query_grad * HEAD**-0.5).astype(BF16)
+            grads_ref[:, pair_at(cols, pair)] = (key_grad * HEAD**-0.5).astype(BF16)
+            grads_ref[:, pair_at(2 * cols, pair)] = value_grad.astype(BF16)
+            return _
+
+        lax.fori_loop(0, cols // PAIR, attend, 0)
+
+        def back(block, _):
+            weight = block_of(weights, block, pl.ds(0, 3 * cols))
+            at = pl.ds(pl.multiple_of(block * cols, PAIR), cols)
+            joined_ref[:, at] = dot_t(grads_ref[...], weight).astype(joined_ref.dtype)
+            return _
+
+        lax.fori_loop(0, members, back, 0)
+        sums_ref[...] = jnp.sum(grads_ref[...].astype(F32), axis=0, keepdims=True)
+
+    shapes = []
+    for dtype in types:
+        shapes += [
             shape_of(keys, 3 * cols),
             shape_of(1, 3 * cols, F32),
-            shape_of(keys, width, joined_type),
-        ),
-        in_specs=[HBM] * len(branch) + [VMEM] * 3 + [HBM],
-        out_specs=(VMEM,) * 3,
+            shape_of(keys, width, dtype),
+        ]
+    outs = pl.pallas_call(
+        kernel,
+        out_shape=shapes,
+        in_specs=[HBM] * given + [VMEM] * (3 * count) + [HBM],
+        out_specs=[VMEM] * len(shapes),
         scratch_shapes=[
-            pltpu.VMEM((seg, width), BF16),
+            pltpu.VMEM((count * seg, width), BF16),
             pltpu.VMEM((members, columns, share, wide), BF16),
             pltpu.VMEM((keys, seg), F32),
             pltpu.VMEM((PAIR, seg), F32),
             pltpu.VMEM((seg, cols), BF16),
-            pltpu.SemaphoreType.DMA((members + len(branch),)),
+            pltpu.SemaphoreType.DMA((members + given,)),
         ],
         name="attn_backward",
-        **kernel_params(14),
-    )(*branch, qkv, lse, ok_col, attn_w)
+        **kernel_params(12 * count),
+    )(*pieces, *qkvs, *lses, *ok_cols, attn_w)
+    return [outs[3 * index : 3 * index + 3] for index in range(count)]
 
 
 def ffn_hidden(seconds, off, up_w):
@@ -394,29 +424,31 @@
 def ffn_out(hiddens, down_w, types):
     count = len(types)
     seg, wide = hiddens[0].shape
+    rows = seg // 2
     width = down_w.shape[1]
     step = 512
 
     def kernel(*refs):
         down_ref = refs[count]
-        outs = refs[count + 1 : 2 * count + 1]
-        hidden, sems = refs[2 * count + 1 :]
+        outs = refs[count + 1 : 3 * count + 1]
+        hidden, sems = refs[3 * count + 1 :]
         wait_all(load_rows(refs[:count], hidden, sems))
 
         def block(part, _):
             at = pl.ds(pl.multiple_of(part * step, step), step)
             value = dot(hidden[...], down_ref[:, at])
-            for index in range(count):
-                outs[index][:, at] = value[index * seg : (index + 1) * seg].astype(types[index])
+            for index in range(2 * count):
+                half = value[index * rows : (index + 1) * rows]
+                outs[index][:, at] = half.astype(types[index // 2])
             return _
 
         lax.fori_loop(0, width // step, block, 0)
 
-    return pl.pallas_call(
+    outs = pl.pallas_call(
         kernel,
-        out_shape=tuple(shape_of(seg, width, dtype) for dtype in types),
+        out_shape=[shape_of(rows, width, types[index // 2]) for index in range(2 * count)],
         in_specs=[HBM] * count + [VMEM],
-        out_specs=(VMEM,) * count,
+        out_specs=[VMEM] * (2 * count),
         scratch_shapes=[
             pltpu.VMEM((count * seg, wide), BF16),
             pltpu.SemaphoreType.DMA((count,)),
@@ -424,6 +456,7 @@
         name="ffn_out",
         **kernel_params(18),
     )(*hiddens, down_w)
+    return [outs[2 * index : 2 * index + 2] for index in range(count)]
 
 
 GRAD_ROWS = 256
@@ -520,10 +553,18 @@
     return jnp.sum(value, axis=0, keepdims=True)
 
 
-def row_blocks(width, last=None):
+def row_blocks(width, last=None, rows=NORM_ROWS):
     if last is None:
-        return pl.BlockSpec((NORM_ROWS, width), lambda i: (i, 0))
-    return pl.BlockSpec((NORM_ROWS, width), lambda i: (jnp.minimum(i, last), 0))
+        return pl.BlockSpec((rows, width), lambda i: (i, 0))
+    return pl.BlockSpec((rows, width), lambda i: (jnp.minimum(i, last), 0))
+
+
+def store_half(refs, value):
+    for half, ref in enumerate(refs):
+
+        @pl.when(pl.program_id(0) == half)
+        def _(ref=ref):
+            ref[...] = value
 
 
 def kept(rows, width):
@@ -541,18 +582,20 @@
     seg, width = tokens.shape
     count = len(parts)
 
+    rows = seg // 2
+
     def kernel(*refs):
-        off_ref, gain_ref, bias_ref, middle_ref, second_ref = refs[count + 1 :]
+        off_ref, gain_ref, bias_ref, middle_ref, *seconds = refs[count + 1 :]
         total = sum_parts(refs[: count + 1]) + off_ref[...]
         middle_ref[...] = total
-        second_ref[...] = norm_apply(total, gain_ref[...], bias_ref[...]).astype(BF16)
+        store_half(seconds, norm_apply(total, gain_ref[...], bias_ref[...]).astype(BF16))
 
     return pl.pallas_call(
         kernel,
-        grid=(seg // NORM_ROWS,),
-        out_shape=(shape_of(seg, width, F32), shape_of(seg, width)),
-        in_specs=[row_blocks(width)] * (count + 1) + [kept(1, width)] * 3,
-        out_specs=(row_blocks(width),) * 2,
+        grid=(2,),
+        out_shape=(shape_of(seg, width, F32), shape_of(rows, width), shape_of(rows, width)),
+        in_specs=[row_blocks(width, rows=rows)] * (count + 1) + [kept(1, width)] * 3,
+        out_specs=(row_blocks(width, rows=rows), kept(rows, width), kept(rows, width)),
         name="middle_norm",
         **kernel_params(5),
     )(tokens, *parts, off, gain, bias)
@@ -561,9 +604,10 @@
 def middle_back(middle, cot, parts, gain):
     seg, width = middle.shape
     count = len(parts)
+    rows = seg // 2
 
     def kernel(*refs):
-        middle_ref, cot_ref, gain_ref, grad_ref, branch_ref, sums_ref = refs[count:]
+        middle_ref, cot_ref, gain_ref, grad_ref, top_ref, bottom_ref, sums_ref = refs[count:]
 
         @pl.when(pl.program_id(0) == 0)
         def _():
@@ -575,7 +619,7 @@
         total = cots + norm_back(hat, inverse, grad, gain_ref[...])
         low = total.astype(BF16)
         grad_ref[...] = total
-        branch_ref[...] = low
+        store_half([top_ref, bottom_ref], low)
         sums_ref[0:1, :] += column_sum(grad * hat)
         sums_ref[1:2, :] += column_sum(grad)
         sums_ref[2:3, :] += column_sum(low.astype(F32))
@@ -583,10 +627,20 @@
 
     return pl.pallas_call(
         kernel,
-        grid=(seg // NORM_ROWS,),
-        out_shape=(shape_of(seg, width, F32), shape_of(seg, width), shape_of(4, width, F32)),
-        in_specs=[row_blocks(width)] * (count + 2) + [kept(1, width)],
-        out_specs=(row_blocks(width), row_blocks(width), kept(4, width)),
+        grid=(2,),
+        out_shape=(
+            shape_of(seg, width, F32),
+            shape_of(rows, width),
+            shape_of(rows, width),
+            shape_of(4, width, F32),
+        ),
+        in_specs=[row_blocks(width, rows=rows)] * (count + 2) + [kept(1, width)],
+        out_specs=(
+            row_blocks(width, rows=rows),
+            kept(rows, width),
+            kept(rows, width),
+            kept(4, width),
+        ),
         name="middle_back",
         **kernel_params(5),
     )(*parts, middle, cot, gain)
@@ -642,26 +696,34 @@
     return lax.ppermute(value, "fsdp", [(i, i ^ rel) for i in range(count)])
 
 
-def spread_near(value):
-    return [swap(value, rel) for rel in range(1, min(lax.axis_size("fsdp"), 3))]
-
-
-def spread_far(value, near, *others):
+def halves_of(value):
+    rows = value.shape[0] // 2
+    return [value[:rows], value[rows:]]
+
+
+def spread_near(halves):
+    near = range(1, min(lax.axis_size("fsdp"), 3))
+    return [[swap(half, rel) for half in halves] for rel in near]
+
+
+def spread_far(halves, near, *others):
     members = lax.axis_size("fsdp")
-    near = list(lax.optimization_barrier((*near, others))[: len(near)])
-    pieces = [[value]] + [[one] for one in near]
+    near = lax.optimization_barrier((near, others))[0]
+    pieces = [halves, *near]
     if members > 3:
-        rows = value.shape[0] // 2
-        pieces.append([swap(near[0][:rows], 2), swap(near[1][rows:], 1)])
-    return pieces + [[swap(value, rel)] for rel in range(4, members)]
-
-
-def flat_list(lists):
-    return [piece for some in lists for piece in some]
+        top, bottom = near[0][0], near[1][-1]
+        if len(halves) == 1:
+            top, bottom = halves_of(top)[0], halves_of(bottom)[1]
+        pieces.append([swap(top, 2), swap(bottom, 1)])
+    return pieces + [[swap(half, rel) for half in halves] for rel in range(4, members)]
 
 
 def after(value, *others):
     return lax.optimization_barrier((value, *others))[0]
+
+
+def add_low(left, right):
+    return (left.astype(F32) + right.astype(F32)).astype(BF16)
 
 
 def trade_blocks(blocks):
@@ -750,9 +812,11 @@
     up_w = gathered(up_blocks)
     down_w = gather_dp(w_down)
 
-    joined_near = spread_near(after(joined, up_blocks))
-    group_joined = spread_far(joined, joined_near)
-    cot_near = spread_near(after(cotangent, *flat_list(group_joined[1:])))
+    joined_rows = [joined]
+    joined_near = spread_near(after(joined_rows, up_blocks))
+    group_joined = spread_far(joined_rows, joined_near)
+    cot_rows = [cotangent]
+    cot_near = spread_near(after(cot_rows, group_joined))
     packed = doubled(packed, "dp").reshape(columns, members, -1).swapaxes(0, 1)
     packed = packed.reshape(total, -1)
 
@@ -784,27 +848,28 @@
     attn = {}
     middle_parts = {}
     previous = []
-    for rel in own_last:
-        x = group_joined[rel]
-        if rel == 0:
-            previous = previous + cot_near
-        x = [after(x[0], *previous), *x[1:]]
-        low, qkv, lse, mixed, part = attn_forward(
-            x, gain_one, bias_one, qkv_off, ok_rows[rel : rel + 1], attn_w, part_type(rel)
+    for some in ([[3], [1, 2], [0]] if members == 4 else [[rel] for rel in own_last]):
+        xs = [group_joined[rel] for rel in some]
+        if some == [0]:
+            previous = previous + flat_list(cot_near)
+        xs[0] = [after(xs[0][0], *previous), *xs[0][1:]]
+        oks = jnp.concatenate([ok_rows[rel : rel + 1] for rel in some], 0)
+        outs = attn_forward(
+            xs, gain_one, bias_one, qkv_off, oks, attn_w, [part_type(rel) for rel in some]
         )
-        attn[rel] = (low, qkv, lse, mixed)
-        middle_parts[rel] = swap(part, rel)
-        previous = [lse]
-    middle, second_own = middle_norm(
+        for rel, (low, qkv, lse, mixed, part) in zip(some, outs):
+            attn[rel] = (low, qkv, lse, mixed)
+            middle_parts[rel] = swap(part, rel)
+            previous = [lse]
+    middle, *second_own = middle_norm(
         tokens, [middle_parts[rel] for rel in rels], out_off, gain_two, bias_two
     )
     def ordered(values):
         return [values[rel] for rel in own_last]
 
     second_near = spread_near(second_own)
-    hidden_own, slope_own = ffn_hidden([[second_own]], up_off, up_w)
+    hidden_own, slope_own = ffn_hidden([second_own], up_off, up_w)
     group_second = spread_far(second_own, second_near, hidden_own)
-    group_cot = spread_far(cotangent, cot_near, hidden_own, second_near)
     hidden, slope = {0: hidden_own[0]}, {0: slope_own[0]}
     previous = hidden_own
     cuts = [1, members - 1, members] if members > 2 else [1, members]
@@ -816,9 +881,10 @@
         for rel, one, other in zip(some, hiddens, slopes):
             hidden[rel], slope[rel] = one, other
         previous = hiddens[:1]
+        if low_rel == 1:
+            group_cot = spread_far(cot_rows, cot_near, previous)
     down_partial = weight_grad(ordered(hidden), flat_list(ordered(group_cot)))
     down_share = scatter_dp(down_partial, 0)
-    down_grad = down_share.astype(F32)
     pre, up_sums, second_parts = [], [], {}
     for some in (own_last[:-1], [0]):
         if not some:
@@ -839,40 +905,50 @@
     hiddens = ordered(hidden)
     hiddens[0] = after(hiddens[0], up_partial)
     output_parts = ffn_out(hiddens, down_w, [part_type(rel) for rel in own_last])
+    output_parts = dict(zip(own_last, output_parts))
     second_parts = after(second_parts, output_parts)
     up_share = to_row_blocks(after(up_partial, second_parts))
-    middle_grad, branch_low, middle_sums = middle_back(
+    middle_grad, *branch_low, middle_sums = middle_back(
         middle, cotangent, [second_parts[rel] for rel in rels], gain_two
     )
 
     branch_near = spread_near(branch_low)
     grads, qkv_sums, joined_parts = {}, {}, {}
 
-    def back_of(rel, x, *others):
-        _, qkv, lse, _ = attn[rel]
-        x = [after(x[0], *others), *x[1:]]
-        grads[rel], qkv_sums[rel], part = attn_backward(
-            x, qkv, lse, ok_cols[rel], attn_w, part_type(rel)
+    def back_of(some, branches, *others):
+        first = [after(branches[0][0], *others), *branches[0][1:]]
+        outs = attn_backward(
+            [first, *branches[1:]],
+            [attn[rel][1] for rel in some],
+            [attn[rel][2] for rel in some],
+            [ok_cols[rel] for rel in some],
+            attn_w,
+            [part_type(rel) for rel in some],
         )
-        joined_parts[rel] = swap(part, rel)
-
-    back_of(0, [branch_low], down_share)
+        for rel, (grad, sums, part) in zip(some, outs):
+            grads[rel], qkv_sums[rel] = grad, sums
+            joined_parts[rel] = swap(part, rel)
+
+    back_of([0], [branch_low], down_share)
     group_branch = spread_far(branch_low, branch_near, qkv_sums[0])
-    order = [0] + ([1, 3, 2] if members == 4 else rels[1:])
-    for last, rel in zip(order, order[1:]):
-        back_of(rel, group_branch[rel], qkv_sums[last])
+    output_over = []
+    if members > 3:
+        far = after(output_parts.pop(3), qkv_sums[0])
+        output_over = [swap(far[0], 1), swap(far[1], 2)]
+    last = 0
+    for some in ([[1, 2], [3]] if members == 4 else [[rel] for rel in rels[1:]]):
+        others = output_over if some == [3] else []
+        back_of(some, [group_branch[rel] for rel in some], qkv_sums[last], *others)
+        last = some[-1]
     attn_partial = attn_weight_grad(
         [attn[rel][0] for rel in rels],
         [grads[rel] for rel in rels],
         [attn[rel][3] for rel in rels],
         flat_list(group_branch),
     )
-    joined_parts = after(joined_parts, attn_partial)
+    up_blocks = trade_blocks(after(up_share, attn_partial))
+    joined_parts = after(joined_parts, attn_partial, up_blocks)
     attn_share = to_row_blocks(after(attn_partial, up_share))
-    output_parts = {
-        rel: swap(part, rel)
-        for rel, part in zip(own_last, after(output_parts, joined_parts))
-    }
     out_grad = (
         attn_share[:, :, 3 * my_cols :].swapaxes(0, 1).reshape(row_share, width).astype(F32)
     )
@@ -898,6 +974,7 @@
         full = jnp.zeros((total, mine.shape[1]), F32)
         return lax.dynamic_update_slice_in_dim(full, mine, me * columns, 0)
 
+    qkv_sums, middle_sums, up_sums = after((qkv_sums, middle_sums, up_sums), first_sums)
     qkv_sum = sum(qkv_sums[rel] for rel in rels)
     pieces = [
         whole(first_sums[0]),
@@ -910,10 +987,20 @@
         sliced(sum(up_sums)),
         whole(middle_sums[3]),
     ]
-    share = scatter_small(after(jnp.concatenate(pieces, 1), output_parts))
-    up_blocks = trade_blocks(after(up_share, share))
+    share = scatter_small(jnp.concatenate(pieces, 1))
+    output_parts = after(output_parts, share)
+    if output_over:
+        two, one = output_parts[2], output_parts[1]
+        output_parts[2] = [add_low(two[0], output_over[0]), two[1]]
+        output_parts[1] = [one[0], add_low(one[1], output_over[1])]
+    output_parts = {
+        rel: [swap(half, rel) for half in halves] for rel, halves in output_parts.items()
+    }
+    down_grad = after(down_share, share).astype(F32)
     up_grad = up_blocks.swapaxes(0, 1).reshape(row_share, members * my_ff).astype(F32)
-    output_sum = sum(output_parts[rel].astype(F32) for rel in rels)
+    output_sum = jnp.concatenate(
+        [sum(halves[half].astype(F32) for halves in output_parts.values()) for half in range(2)], 0
+    )
     output = (middle + output_sum + down_off).astype(BF16)
     outs = []
     at = 0

time: 658 us -> 618 us (0.939)
  waiting for transfers between devices: 201 us -> 178 us
  local copies, waits for them, and re-layouts: 48.6 us -> 36.6 us
  Pallas kernels: 300 us -> 289 us
    ppermute x28 -> x35, waiting for transfers between devices: 160 us -> 109 us  [swap(): return lax.ppermute(value, 'fsdp', [(i, i ^ rel) for i in range(count)])]
    all_to_all x3, waiting for transfers between devices: 22.2 us -> 43.8 us  [trade_blocks(): return lax.all_to_all(blocks, 'fsdp', 0, 0, tiled=True)]
    pallas_call x11 -> x9, Pallas kernels: 157 us -> 146 us  [the longest x3 57.7 us: attn_forward(): pl.pallas_call(kernel, out_shape=shapes, in_specs=[HBM] * given + [VMEM]...]
    ppermute x28 -> x35, starting transfers between devices: 30.3 us -> 37.4 us  [swap(): return lax.ppermute(value, 'fsdp', [(i, i ^ rel) for i in range(count)])]
  transfers between devices with their start and end apart: 45 -> 52, of which waited for: 20 -> 27; matrix products, arithmetic and copies ran while one was open for 7% -> 6% of each run, Pallas kernels for 46% -> 47%
where the time goes in v4:
time: 618 us; the launch traced here: 613 us
  Pallas kernels  289 us (47%)
  waiting for transfers between devices  178 us (29%)
  starting transfers between devices  61 us (10%)
  local copies, waits for them, and re-layouts  36.6 us (6%)
  blocking collectives  18.8 us (3%)
  between operations  15.4 us (2%)
  other arithmetic  14.6 us (2%)
    ppermute x35, waiting for transfers between devices, swap(): return lax.ppermute(value, 'fsdp', [(i, i ^ rel) for i in range(count)])  109 us
    pallas_call x3, Pallas kernels, attn_forward(): pl.pallas_call(kernel, out_shape=shapes, in_specs=[HBM] * given + [VMEM]...  57.7 us
    pallas_call x3, Pallas kernels, attn_backward(): pl.pallas_call(kernel, out_shape=shapes, in_specs=[HBM] * given + [VMEM]...  53.6 us
    all_to_all x3, waiting for transfers between devices, trade_blocks(): return lax.all_to_all(blocks, 'fsdp', 0, 0, tiled=True)  43.8 us
    pallas_call x2, Pallas kernels, ffn_back(): pl.pallas_call(kernel, out_shape=(shape_of(rows, wide), shape_of(1, wide,...  38.7 us
    pallas_call x3, Pallas kernels, ffn_hidden(): pl.pallas_call(kernel, out_shape=[shape_of(seg, wide)] * (2 * count), in_...  37.9 us
    ppermute x35, starting transfers between devices, swap(): return lax.ppermute(value, 'fsdp', [(i, i ^ rel) for i in range(count)])  37.4 us
    pallas_call x2, Pallas kernels, weight_grad(): pl.pallas_call(kernel, grid=(tall // GRAD_ROWS,), out_shape=shape_of(tall...  35.8 us
  transfers between devices with their start and end apart: 52, of which 27 were waited for; matrix products, arithmetic and copies ran while one was open for 6% of the time, Pallas kernels for 47%

profile of v4, /device:TPU:0, one launch (start us, length us, event | category | flops | bytes accessed | tf_op | source)
XLA Modules:
  0.0 613.0 jit_solution(2670834143762211403)
XLA Ops:
  12.0 5.2 all-to-all-start
  17.5 10.4 %all-to-all-done = bf16[4,64,1536]{2,1,0:T(8,128)(2,1)S(1)} async-done(((bf16[4,64,1536]{2,1,0:T(8,128)(2,1)}), bf16[4,64,1536]{2,1,0:T(8,128)(2,1)S(1)}, u32[]{:S(2)}, u32[]{:S(2)}) %all-to-all-start) | async-done | bytes 786464 | tf_op jit(solution)/shard_map/all_to_all | solution.py:730
  29.4 1.5 collective-permute-start.1
  30.9 1.3 collective-permute-start
  33.1 1.5 collective-permute-start.2
  34.7 1.8 reshape.206
  37.4 18.8 %all_to_all.29 = bf16[4,64,2048]{2,1,0:T(8,128)(2,1)} all-to-all(bf16[4,64,2048]{2,1,0:T(8,128)(2,1)S(1)} %copy.73), channel_id=1, replica_groups=mesh['fsdp'=4,'dp'=8] {'fsdp'}, dimensions={0} | all-to-all | bytes 2097152 | tf_op jit(solution)/shard_map/all_to_all | solution.py:730
  59.0 1.6 collective-permute-start.8
  60.7 5.2 collective-permute-done.8
  66.1 5.3 collective-permute-done.9
  72.2 22.2 %collective-permute-done.4.refs_1_ = bf16[384,2048]{1,0:T(8,128)(2,1)} collective-permute-done((bf16[384,2048]{1,0:T(8,128)(2,1)S(1)}, bf16[384,2048]{1,0:T(8,128)(2,1)}, u32[]{:S(2)}, u32[]{:S(2)}) %collective-permute-start.4) | collective-permute-done | bytes 1572896 | tf_op jit(solution)/shard_map/ppermute | solution.py:696
  98.1 1.5 collective-permute-start.5
  103.0 13.5 %collective-permute-done.6.refs_1_ = bf16[192,2048]{1,0:T(8,128)(2,1)} collective-permute-done((bf16[192,2048]{1,0:T(8,128)(2,1)S(1)}, bf16[192,2048]{1,0:T(8,128)(2,1)}, u32[]{:S(2)}, u32[]{:S(2)}) %collective-permute-start.6) | collective-permute-done | bytes 786464 | tf_op jit(solution)/shard_map/ppermute | solution.py:696
  116.8 1.4 collective-permute-start.11
  119.3 16.0 %attn_forward.3 = (bf16[384,2048]{1,0:T(8,128)(2,1)}, bf16[384,1536]{1,0:T(8,128)(2,1)}, f32[320,128]{1,0:T(8,128)}, bf16[320,512]{1,0:T(8,128)(2,1)}, bf16[320,2048]{1,0:T(8,128)(2,1)}) custom-call(bf16[192,2048]{1,0:T(8,128)(2,1)} %collective-permute-done.5.refs_0_, bf16[192,2048]{1,0:T(8,128)(2,1)} %collective-permute-done.6.refs_1_, ...), custom_call_target="tpu_custom_call" | custom-call | flops 12000000 | bytes 1 | tf_op jit(solution)/shard_map/attn_forward/pallas_call | solution.py:196
  136.5 26.2 %attn_forward.4 = (bf16[384,2048]{1,0:T(8,128)(2,1)}, bf16[384,1536]{1,0:T(8,128)(2,1)}, f32[320,128]{1,0:T(8,128)}, bf16[320,512]{1,0:T(8,128)(2,1)}, bf16[320,...) custom-call(bf16[384,2048]{1,0:T(8,128)(2,1)} %collective-permute-do, ...), custom_call_target="tpu_custom_call" | custom-call | flops 24000000 | bytes 1 | tf_op jit(solution)/shard_map/attn_forward/pallas_call | solution.py:196
  162.7 1.6 collective-permute-start.12
  167.1 15.5 %attn_forward.5 = (bf16[384,2048]{1,0:T(8,128)(2,1)}, bf16[384,1536]{1,0:T(8,128)(2,1)}, f32[320,128]{1,0:T(8,128)}, bf16[320,512]{1,0:T(8,128)(2,1)}, f32[320,2048]{1,0:T(8,128)}) custom-call(bf16[384,2048]{1,0:T(8,128)(2,1)} %copy-done.3, f32[1,2048]{1,0:T(1,128)} %reshape.241.refs_2_.refs_1_.refs_6_, f32[1,2048]{1,0:T(1,128)} %reshape.243.refs_3_.refs_2_, ...), custom_call_target="tpu_custom_call" | custom-call | flops 12000000 | bytes 1 | tf_op jit(solution)/shard_map/attn_forward/pallas_call | solution.py:196
  182.7 20.4 %collective-permute-done.12.refs_2_ = bf16[320,2048]{1,0:T(8,128)(2,1)} collective-permute-done((bf16[320,2048]{1,0:T(8,128)(2,1)}, bf16[320,2048]{1,0:T(8,128)(2,1)}, u32[]{:S(2)}, u32[]{:S(2)}) %collective-permute-start.12) | collective-permute-done | bytes 1310752 | tf_op jit(solution)/shard_map/ppermute | solution.py:696
  203.2 6.7 %middle_norm.1 = (f32[320,2048]{1,0:T(8,128)}, bf16[160,2048]{1,0:T(8,128)(2,1)}, bf16[160,2048]{1,0:T(8,128)(2,1)}) custom-call(bf16[320,2048]{1,0:T(8,128)(2,1)} %refs_0_.1, f32[320,2048]{1,0:T(8,128)} %get-tuple-element.147.refs_1_, bf16[320,2048]{1,0:T(8,128)(2,1)} %collective-permute-done.12.refs_2_, bf16[320,2048]{1,0:T(8,128)(2,1)} %collective-permute-done.13.refs_3_, ...), custom_call_target="tpu_custom_call" | custom-call | flops 5000000 | bytes 1 | tf_op jit(solution)/shard_map/middle_norm/pallas_call | solution.py:593
  209.8 1.5 collective-permute-start.17
  214.7 10.8 %ffn_hidden.3 = (bf16[320,2048]{1,0:T(8,128)(2,1)}, bf16[320,2048]{1,0:T(8,128)(2,1)}) custom-call(bf16[160,2048]{1,0:T(8,128)(2,1)} %get-tuple-element.152.refs_0_.refs_6_, bf16[160,2048]{1,0:T(8,128)(2,1)} %get-tuple-element.153.refs_1_.refs_7_, f32[1,2048]{1,0:T(1,128)} %constant_dynamic-slice_fusion.refs_2_.refs_4_, bf16[8,4,64,2048]{3,2,1,0:T(8,128)(2,1)} %bitcast.56), custom_call_target="tpu_custom_call" | custom-call | flops 6000000 | bytes 1 | tf_op jit(solution)/shard_map/ffn_hidden/pallas_call | solution.py:346
  225.5 2.2 collective-permute-done.17.refs_2_
  227.7 1.5 collective-permute-done.15.refs_0_.refs_4_
  229.2 11.6 %collective-permute-done.18.refs_3_ = bf16[160,2048]{1,0:T(8,128)(2,1)S(1)} collective-permute-done((bf16[160,2048]{1,0:T(8,128)(2,1)}, bf16[160,2048]{1,0:T(8,128)(2,1)S(1)}, u32[]{:S(2)}, u32[]{:S(2)}) %collective-permute-start.18) | collective-permute-done | bytes 655392 | tf_op jit(solution)/shard_map/ppermute | solution.py:696
  240.8 1.3 collective-permute-done.16.refs_1_.refs_5_
  242.7 1.5 collective-permute-start.20
  244.2 15.8 %ffn_hidden.4 = (bf16[320,2048]{1,0:T(8,128)(2,1)}, bf16[320,2048]{1,0:T(8,128)(2,1)}, bf16[320,2048]{1,0:T(8,128)(2,1)}, bf16[320,2048]{1,0:T(8,128)(2,1)}) custom-call(bf16[160,2048]{1,0:T(8,128)(2,1)} %copy-done.8, bf16[160,2048]{1,0:T(8,128)(2,1)} %collective-permute-done.16.refs_1_.refs_5_, bf16[160,2048]{1,0:T(8,128)(2,1)} %copy-done.7, ...), custom_call_target="tpu_custom_call" | custom-call | flops 12000000 | bytes 1 | tf_op jit(solution)/shard_map/ffn_hidden/pallas_call | solution.py:346
  262.6 1.5 collective-permute-start.21
  264.1 11.2 %ffn_hidden.5 = (bf16[320,2048]{1,0:T(8,128)(2,1)}, bf16[320,2048]{1,0:T(8,128)(2,1)}) custom-call(bf16[160,2048]{1,0:T(8,128)(2,1)} %collective-permute-done.19.refs_0_, bf16[160,2048]{1,0:T(8,128)(2,1)} %collective-permute-done.20.refs_1_, f32[1,2048]{1,0:T(1,128)} %constant_dynamic-slice_fusion.refs_2_.refs_4_, bf16[8,4,64,2048]{3,2,1,0:T(8,128)(2,1)} %bitcast.58), custom_call_target="tpu_custom_call" | custom-call | flops 6000000 | bytes 1 | tf_op jit(solution)/shard_map/ffn_hidden/pallas_call | solution.py:346
  275.3 2.0 collective-permute-done.22.refs_5_.refs_1_
  278.4 17.8 %weight_grad.2 = bf16[2048,2048]{1,0:T(8,128)(2,1)} custom-call(bf16[320,2048]{1,0:T(8,128)(2,1)} %get-tuple-element.174.refs_0_, bf16[320,2048]{1,0:T(8,128)(2,1)} %get-tuple-element.164.refs_1_, bf16[320,2048]{1,0:T(8,128)(2,1)} %get-tuple-element.160.refs_2_, bf16[320,2048]{1,0:T(8,128)(2,1)} %get-tuple-element.154.refs_3_, bf16[160,2048]{1,0:T(8,128)(2,1)} %copy-done.15, ...), custom_call_target="tpu_custom_call" | custom-call | flops 17000000 | bytes 1 | tf_op jit(solution)/shard_map/weight_grad/pallas_call | solution.py:483
  296.4 25.8 %ffn_back.2 = (bf16[960,2048]{1,0:T(8,128)(2,1)}, f32[1,2048]{1,0:T(1,128)}, bf16[320,2048]{1,0:T(8,128)(2,1)}, bf16[320,2048]{1,0:T(8,128)(2,1)}, bf16[320,2048]{1,0:T(8,128)(2,1)}) custom-call(bf16[160,2048]{1,0:T(8,128)(2,1)} %copy-done.15, bf16[160,2048]{1,0:T(8,128)(2,1)} %copy-done.14, bf16[320,2048]{1,0:T(8,128)(2,1)} %copy-done.2, ...), custom_call_target="tpu_custom_call" | custom-call | flops 30000000 | bytes 1 | tf_op jit(solution)/shard_map/ffn_back/pallas_call | solution.py:403
  325.7 12.9 %ffn_back.3 = (bf16[320,2048]{1,0:T(8,128)(2,1)}, f32[1,2048]{1,0:T(1,128)}, f32[320,2048]{1,0:T(8,128)}) custom-call(bf16[320,2048]{1,0:T(8,128)(2,1)} %refs_5_.1, bf16[320,2048]{1,0:T(8,128)(2,1)} %get-tuple-element.172.refs_1_, bf16[8,4,64,2048]{3,2,1,0:T(8,128)(2,1)} %bitcast.60, bf16[2048,2048]{1,0:T(8,128)(2,1)} %all-gather.8.cloned.1.call-done.refs_8_.refs_3_.refs_4_), custom_call_target="tpu_custom_call" | custom-call | flops 10000000 | bytes 1 | tf_op jit(solution)/shard_map/ffn_back/pallas_call | solution.py:403
  338.6 18.0 %weight_grad.3 = bf16[2048,2048]{1,0:T(8,128)(2,1)} custom-call(bf16[160,2048]{1,0:T(8,128)(2,1)} %collective-permute-done.19.refs_0_, bf16[160,2048]{1,0:T(8,128)(2,1)} %collective-permute-done.20.refs_1_, bf16[160,2048]{1,0:T(8,128)(2,1)} %copy-done.7, bf16[160,2048]{1,0:T(8,128)(2,1)} %copy-done.9, bf16[160,2048]{1,0:T(8,128)(2,1)} %copy-done.8, ...), custom_call_target="tpu_custom_call" | custom-call | flops 17000000 | bytes 1 | tf_op jit(solution)/shard_map/weight_grad/pallas_call | solution.py:483
  356.6 19.9 %ffn_out.1 = (bf16[160,2048]{1,0:T(8,128)(2,1)}, bf16[160,2048]{1,0:T(8,128)(2,1)}, bf16[160,2048]{1,0:T(8,128)(2,1)}, bf16[160,2048]{1,0:T(8,128)(2,1)}, bf16[1...) custom-call(bf16[320,2048]{1,0:T(8,128)(2,1)} %get-tuple-element.174.refs_0_, ...), custom_call_target="tpu_custom_call" | custom-call | flops 18000000 | bytes 1 | tf_op jit(solution)/shard_map/ffn_out/pallas_call | solution.py:447
  376.6 2.9 collective-permute-done.24.refs_2_
  380.5 7.6 %middle_back.1 = (f32[320,2048]{1,0:T(8,128)}, bf16[160,2048]{1,0:T(8,128)(2,1)}, bf16[160,2048]{1,0:T(8,128)(2,1)}, f32[4,2048]{1,0:T(4,128)}) custom-call(f32[320,2048]{1,0:T(8,128)} %get-tuple-element.187.refs_0_, bf16[320,2048]{1,0:T(8,128)(2,1)} %copy-done.17, bf16[320,2048]{1,0:T(8,128)(2,1)} %copy-done.18, ...), custom_call_target="tpu_custom_call" | custom-call | flops 5000000 | bytes 1 | tf_op jit(solution)/shard_map/middle_back/pallas_call | solution.py:628
  393.0 15.1 %attn_backward.3 = (bf16[384,1536]{1,0:T(8,128)(2,1)}, f32[1,1536]{1,0:T(1,128)}, f32[384,2048]{1,0:T(8,128)}) custom-call(bf16[160,2048]{1,0:T(8,128)(2,1)} %get-tuple-element.192.refs_0_.refs_12_, bf16[160,2048]{1,0:T(8,128)(2,1)} %get-tuple-element.193.refs_1_.refs_13_, bf16[384,1536]{1,0:T(8,128)(2,1)} %get-tuple-element.194.refs_2_, ...), custom_call_target="tpu_custom_call" | custom-call | flops 12000000 | bytes 1 | tf_op jit(solution)/shard_map/attn_backward/pallas_call | solution.py:296
  408.1 8.5 %collective-permute-done.29.refs_3_.refs_17_ = bf16[160,2048]{1,0:T(8,128)(2,1)S(1)} collective-permute-done((bf16[160,2048]{1,0:T(8,128)(2,1)}, bf16[160,2048]{1,0:T(8,128)(2,1)S(1)}, u32[]{:S(2)}, u32[]{:S(2)}) %collective-permute-start.29) | collective-permute-done | bytes 655392 | tf_op jit(solution)/shard_map/ppermute | solution.py:696
  423.1 24.1 %attn_backward.4 = (bf16[384,1536]{1,0:T(8,128)(2,1)}, f32[1,1536]{1,0:T(1,128)}, bf16[384,2048]{1,0:T(8,128)(2,1)}, bf16[384,1536]{1,0:T(8,128)(2,1)}, f32[1,1536]{1,0:T(1,128)}, /*index=5*/bf16[384,2048]{1,0:T(8,128)(2,1)}) custom-call(bf16[160,2048]{1,0:T(8,128)(2,1)} %copy-done.11, bf16[160,2048]{1,0:T(8,128)(2,1)} %copy-done.13, ...), custom_call_target="tpu_custom_call" | custom-call | flops 24000000 | bytes 1 | tf_op jit(solution)/shard_map/attn_backward/pallas_call | solution.py:296
  449.8 14.5 %attn_backward.5 = (bf16[384,1536]{1,0:T(8,128)(2,1)}, f32[1,1536]{1,0:T(1,128)}, bf16[384,2048]{1,0:T(8,128)(2,1)}) custom-call(bf16[160,2048]{1,0:T(8,128)(2,1)} %copy-done.16, bf16[160,2048]{1,0:T(8,128)(2,1)} %collective-permute-done.35.refs_1_.refs_19_, bf16[384,1536]{1,0:T(8,128)(2,1)} %get-tuple-element.212.refs_2_, ...), custom_call_target="tpu_custom_call" | custom-call | flops 12000000 | bytes 1 | tf_op jit(solution)/shard_map/attn_backward/pallas_call | solution.py:296
  464.3 1.8 collective-permute-start.36
  466.1 22.0 %attn_weight_grad.1 = bf16[2048,2048]{1,0:T(8,128)(2,1)} custom-call(bf16[384,2048]{1,0:T(8,128)(2,1)} %get-tuple-element.214.refs_0_, bf16[384,2048]{1,0:T(8,128)(2,1)} %get-tuple-element.215.refs_1_, bf16[384,2048]{1,0:T(8,128)(2,1)} %get-tuple-element.216.refs_2_, bf16[384,2048]{1,0:T(8,128)(2,1)} %get-tuple-element.217.refs_3_, ...), custom_call_target="tpu_custom_call" | custom-call | flops 21000000 | bytes 1 | tf_op jit(solution)/shard_map/attn_weight_grad/pallas_call | solution.py:524
  488.1 3.5 all-to-all-start.2
  492.4 29.7 %all-to-all-done.2 = bf16[4,64,2048]{2,1,0:T(8,128)(2,1)S(1)} async-done(((bf16[4,64,2048]{2,1,0:T(8,128)(2,1)}), bf16[4,64,2048]{2,1,0:T(8,128)(2,1)S(1)}, u32[]{:S(2)}, u32[]{:S(2)}) %all-to-all-start.2) | async-done | bytes 1048608 | tf_op jit(solution)/shard_map/all_to_all | solution.py:730
  523.3 9.0 %first_back.1 = (f32[320,2048]{1,0:T(8,128)}, bf16[64,2048]{1,0:T(8,128)(2,1)}, f32[2,2048]{1,0:T(2,128)}) custom-call(f32[384,2048]{1,0:T(8,128)} %get-tuple-element.228.refs_0_, bf16[384,2048]{1,0:T(8,128)(2,1)} %collective-permute-done.30.refs_1_, bf16[384,2048]{1,0:T(8,128)(2,1)} %collective-permute-done.31.refs_2_, bf16[384,2048]{1,0:T(8,128)(2,1)} %copy-done.44, ...), custom_call_target="tpu_custom_call" | custom-call | flops 499999997952 | bytes 1 | tf_op jit(solution)/shard_map/first_back/pallas_call | solution.py:677
  534.7 3.5 all-to-all-start.3
  538.5 1.5 copy.86
  540.0 1.4 collective-permute-start.41
  541.5 5.9 all-to-all-done.3
  549.1 1.3 add_convert_fusion.1
  554.8 1.6 convert_element_type.134
  558.2 7.4 %collective-permute-done.37 = bf16[160,2048]{1,0:T(8,128)(2,1)S(1)} collective-permute-done((bf16[160,2048]{1,0:T(8,128)(2,1)S(1)}, bf16[160,2048]{1,0:T(8,128)(2,1)S(1)}, u32[]{:S(2)}, u32[]{:S(2)}) %collective-permute-start.37) | collective-permute-done | bytes 655392 | tf_op jit(solution)/shard_map/ppermute | solution.py:696
  565.7 2.5 collective-permute-done.38
  568.2 1.3 convert_add_fusion.1
  569.5 10.1 %collective-permute-done.39 = bf16[160,2048]{1,0:T(8,128)(2,1)S(1)} collective-permute-done((bf16[160,2048]{1,0:T(8,128)(2,1)S(1)}, bf16[160,2048]{1,0:T(8,128)(2,1)S(1)}, u32[]{:S(2)}, u32[]{:S(2)}) %collective-permute-start.39) | collective-permute-done | bytes 655392 | tf_op jit(solution)/shard_map/ppermute | solution.py:696
  579.6 1.4 collective-permute-done.40
  581.0 1.3 convert_add_fusion
  582.3 6.2 %reduce-scatter.8.cloned.1.call-done = bf16[4,64,2048]{2,1,0:T(8,128)(2,1)} async-done(((bf16[4,512,2048]{2,1,0:T(8,128)(2,1)}), bf16[4,64,2048]{2,1,0:T(8,128)(2,1)}) %reduce-scatter.8.cloned.1.call-update) | async-done | bytes 1048592 | tf_op jit(solution)/shard_map/reduce_scatter | solution.py:754
  588.6 2.1 slice.192
  590.7 3.7 all-to-all-start.4
  594.4 3.3 fusion.1
  599.5 3.7 all-to-all-done.4
  (270 shorter events, 67.6 us)
Async XLA Ops:
  12.0 16.0 %all-to-all-start = ((bf16[4,64,1536]{2,1,0:T(8,128)(2,1)}), bf16[4,64,1536]{2,1,0:T(8,128)(2,1)S(1)}, u32[]{:S(2)}, u32[]{:S(2)}) async-start(bf16[4,64,1536]{2,1,0:T(8,128)(2,1)} %copy.72), calls=%async_computation | async-start | bytes 1572864 | tf_op jit(solution)/shard_map/all_to_all | solution.py:730
  17.1 102.2 %all-gather.4.cloned.1.call-start = ((), (), s32[]{:S(2)}) async-start(), calls=%async_computation.8 | async-start | bytes 9437184 | tf_op jit(solution)/shard_map/all_gather | solution.py:750
  17.4 11.8 %copy-start.35 = (bf16[64]{0:T(256)(128)(2,1)S(1)}, bf16[64]{0:T(256)(128)(2,1)}, u32[]{:S(2)}) copy-start(bf16[64]{0:T(256)(128)(2,1)} %param.24) | copy-start | bytes 388
  17.5 13.3 %copy-start.25 = (bf16[1,50,2048]{2,1,0:T(8,128)(2,1)S(1)}, bf16[1,50,2048]{2,1,0:T(8,128)(2,1)}, u32[]{:S(2)}) copy-start(bf16[1,50,2048]{2,1,0:T(8,128)(2,1)} %param.21) | copy-start | bytes 614404
  29.1 185.6 %all-gather.6.cloned.1.call-start = ((), (), s32[]{:S(2)}) async-start(), calls=%async_computation.9 | async-start | bytes 9437184 | tf_op jit(solution)/shard_map/all_gather | solution.py:750
  29.4 3.7 collective-permute-start.1
  30.9 5.9 collective-permute-start
  33.1 3.7 collective-permute-start.2
  36.8 21.6 %copy-start.3 = (bf16[384,2048]{1,0:T(8,128)(2,1)}, bf16[384,2048]{1,0:T(8,128)(2,1)S(1)}, u32[]{:S(2)}) copy-start(bf16[384,2048]{1,0:T(8,128)(2,1)S(1)} %constant_dynamic-update-slice_fusion.refs_0_.refs_4_) | copy-start | bytes 4718596
  56.2 240.2 %all-gather.8.cloned.1.call-start = ((), (), s32[]{:S(2)}) async-start(), calls=%async_computation.10 | async-start | bytes 9437184 | tf_op jit(solution)/shard_map/all_gather | solution.py:750
  56.9 335.3 %reduce-scatter.4.cloned.1.call-start = ((), (), s32[]{:S(2)}) async-start(), calls=%async_computation.11 | async-start | bytes 9437184 | tf_op jit(solution)/shard_map/reduce_scatter | solution.py:754
  57.2 1.8 collective-permute-start.7
  57.5 37.0 %collective-permute-start.4 = (bf16[384,2048]{1,0:T(8,128)(2,1)S(1)}, bf16[384,2048]{1,0:T(8,128)(2,1)}, u32[]{:S(2)}, u32[]{:S(2)}) collective-permute-start(bf16[384,2048]{1,0:T(8,128)(2,1)S(1)} %constant_dynamic-update-slice_fusion.refs_0_.refs_4_), channel_id=1, source_target_pairs={{0,16},{8,24},{16,0},{24,8},{1,17},{9,25},{17,1},{25,9},{2,18},{10... | collective-permute-start | bytes 4718600 | tf_op jit(solution)/shard_map/ppermute | solution.py:696
  58.4 36.6 %collective-permute-start.3 = (bf16[384,2048]{1,0:T(8,128)(2,1)S(1)}, bf16[384,2048]{1,0:T(8,128)(2,1)}, u32[]{:S(2)}, u32[]{:S(2)}) collective-permute-start(bf16[384,2048]{1,0:T(8,128)(2,1)S(1)} %constant_dynamic-update-slice_fusion.refs_0_.refs_4_), channel_id=1, source_target_pairs={{0,8},{8,0},{16,24},{24,16},{1,9},{9,1},{17,25},{25,17},{2,10},{10... | collective-permute-start | bytes 4718600 | tf_op jit(solution)/shard_map/ppermute | solution.py:696
  59.0 6.9 %collective-permute-start.8 = (bf16[8,818]{1,0:T(8,128)(2,1)S(1)}, bf16[8,818]{1,0:T(8,128)(2,1)S(1)}, u32[]{:S(2)}, u32[]{:S(2)}) collective-permute-start(bf16[8,818]{1,0:T(8,128)(2,1)S(1)} %pad_maximum_fusion.4), channel_id=1, source_target_pairs={{0,2},{1,3},{2,0},{3,1},{4,6},{5,7},{6,4},{7,5},{8,10},{9,11},{10,... | collective-permute-start | bytes 39272 | tf_op jit(solution)/shard_map/ppermute | solution.py:738
  66.0 5.5 collective-permute-start.9
  72.2 44.6 %copy-start = (bf16[320,2048]{1,0:T(8,128)(2,1)S(1)}, bf16[320,2048]{1,0:T(8,128)(2,1)}, u32[]{:S(2)}) copy-start(bf16[320,2048]{1,0:T(8,128)(2,1)} %refs_5_.1) | copy-start | bytes 3932164
  97.4 19.1 %collective-permute-start.6 = (bf16[192,2048]{1,0:T(8,128)(2,1)S(1)}, bf16[192,2048]{1,0:T(8,128)(2,1)}, u32[]{:S(2)}, u32[]{:S(2)}) collective-permute-start(bf16[192,2048]{1,0:T(8,128)(2,1)S(1)} %slice.134), channel_id=1, source_target_pairs={{0,8},{8,0},{16,24},{24,16},{1,9},{9,1},{17,25},{25,17},{2,10},{10... | collective-permute-start | bytes 2359304 | tf_op jit(solution)/shard_map/ppermute | solution.py:696
  98.1 18.7 %collective-permute-start.5 = (bf16[192,2048]{1,0:T(8,128)(2,1)S(1)}, bf16[192,2048]{1,0:T(8,128)(2,1)}, u32[]{:S(2)}, u32[]{:S(2)}) collective-permute-start(bf16[192,2048]{1,0:T(8,128)(2,1)S(1)} %slice.133), channel_id=1, source_target_pairs={{0,16},{8,24},{16,0},{24,8},{1,17},{9,25},{17,1},{25,9},{2,18},{10... | collective-permute-start | bytes 2359304 | tf_op jit(solution)/shard_map/ppermute | solution.py:696
  116.8 50.4 %collective-permute-start.11 = (bf16[320,2048]{1,0:T(8,128)(2,1)S(1)}, bf16[320,2048]{1,0:T(8,128)(2,1)S(1)}, u32[]{:S(2)}, u32[]{:S(2)}) collective-permute-start(bf16[320,2048]{1,0:T(8,128)(2,1)S(1)} %copy-done), channel_id=1, source_target_pairs={{0,16},{8,24},{16,0},{24,8},{1,17},{9,25},{17,1},{25,9},{2,18},{10... | collective-permute-start | bytes 3932168 | tf_op jit(solution)/shard_map/ppermute | solution.py:696
  118.2 48.9 %collective-permute-start.10 = (bf16[320,2048]{1,0:T(8,128)(2,1)S(1)}, bf16[320,2048]{1,0:T(8,128)(2,1)}, u32[]{:S(2)}, u32[]{:S(2)}) collective-permute-start(bf16[320,2048]{1,0:T(8,128)(2,1)S(1)} %copy-done), channel_id=1, source_target_pairs={{0,8},{8,0},{16,24},{24,16},{1,9},{9,1},{17,25},{25,17},{2,10},{10... | collective-permute-start | bytes 3932168 | tf_op jit(solution)/shard_map/ppermute | solution.py:696
  135.3 47.4 %collective-permute-start.14 = (bf16[320,2048]{1,0:T(8,128)(2,1)}, bf16[320,2048]{1,0:T(8,128)(2,1)}, u32[]{:S(2)}, u32[]{:S(2)}) collective-permute-start(bf16[320,2048]{1,0:T(8,128)(2,1)} %get-tuple-element.150), channel_id=1, source_target_pairs={{0,24},{8,16},{16,8},{24,0},{1,25},{9,17},{17,9},{25,1},{2,26},{10... | collective-permute-start | bytes 3932168 | tf_op jit(solution)/shard_map/ppermute | solution.py:696
  162.7 40.5 %collective-permute-start.12 = (bf16[320,2048]{1,0:T(8,128)(2,1)}, bf16[320,2048]{1,0:T(8,128)(2,1)}, u32[]{:S(2)}, u32[]{:S(2)}) collective-permute-start(bf16[320,2048]{1,0:T(8,128)(2,1)} %get-tuple-element.148), channel_id=1, source_target_pairs={{0,8},{8,0},{16,24},{24,16},{1,9},{9,1},{17,25},{25,17},{2,10},{10... | collective-permute-start | bytes 3932168 | tf_op jit(solution)/shard_map/ppermute | solution.py:696
  164.3 38.9 %collective-permute-start.13 = (bf16[320,2048]{1,0:T(8,128)(2,1)}, bf16[320,2048]{1,0:T(8,128)(2,1)}, u32[]{:S(2)}, u32[]{:S(2)}) collective-permute-start(bf16[320,2048]{1,0:T(8,128)(2,1)} %get-tuple-element.149), channel_id=1, source_target_pairs={{0,16},{8,24},{16,0},{24,8},{1,17},{9,25},{17,1},{25,9},{2,18},{10... | collective-permute-start | bytes 3932168 | tf_op jit(solution)/shard_map/ppermute | solution.py:696
  167.1 94.1 %copy-start.2 = (bf16[320,2048]{1,0:T(8,128)(2,1)}, bf16[320,2048]{1,0:T(8,128)(2,1)S(1)}, u32[]{:S(2)}) copy-start(bf16[320,2048]{1,0:T(8,128)(2,1)S(1)} %collective-permute-done.11.refs_6_.refs_2_) | copy-start | bytes 3932164
  209.8 17.9 %collective-permute-start.17 = (bf16[160,2048]{1,0:T(8,128)(2,1)}, bf16[160,2048]{1,0:T(8,128)(2,1)S(1)}, u32[]{:S(2)}, u32[]{:S(2)}) collective-permute-start(bf16[160,2048]{1,0:T(8,128)(2,1)} %get-tuple-element.152.refs_0_.refs_6_), channel_id=1, source_target_pairs={{0,16},{8,24},{16,0},{24,8},{1,17},{9,25},{17,1},{25,9},{2,18},{10... | collective-permute-start | bytes 1966088 | tf_op jit(solution)/shard_map/ppermute | solution.py:696
  211.4 17.8 %collective-permute-start.15 = (bf16[160,2048]{1,0:T(8,128)(2,1)}, bf16[160,2048]{1,0:T(8,128)(2,1)S(1)}, u32[]{:S(2)}, u32[]{:S(2)}) collective-permute-start(bf16[160,2048]{1,0:T(8,128)(2,1)} %get-tuple-element.152.refs_0_.refs_6_), channel_id=1, source_target_pairs={{0,8},{8,0},{16,24},{24,16},{1,9},{9,1},{17,25},{25,17},{2,10},{10... | collective-permute-start | bytes 1966088 | tf_op jit(solution)/shard_map/ppermute | solution.py:696
  212.6 28.3 %collective-permute-start.18 = (bf16[160,2048]{1,0:T(8,128)(2,1)}, bf16[160,2048]{1,0:T(8,128)(2,1)S(1)}, u32[]{:S(2)}, u32[]{:S(2)}) collective-permute-start(bf16[160,2048]{1,0:T(8,128)(2,1)} %get-tuple-element.153.refs_1_.refs_7_), channel_id=1, source_target_pairs={{0,16},{8,24},{16,0},{24,8},{1,17},{9,25},{17,1},{25,9},{2,18},{10... | collective-permute-start | bytes 1966088 | tf_op jit(solution)/shard_map/ppermute | solution.py:696
  213.4 28.7 %collective-permute-start.16 = (bf16[160,2048]{1,0:T(8,128)(2,1)}, bf16[160,2048]{1,0:T(8,128)(2,1)}, u32[]{:S(2)}, u32[]{:S(2)}) collective-permute-start(bf16[160,2048]{1,0:T(8,128)(2,1)} %get-tuple-element.153.refs_1_.refs_7_), channel_id=1, source_target_pairs={{0,8},{8,0},{16,24},{24,16},{1,9},{9,1},{17,25},{25,17},{2,10},{10... | collective-permute-start | bytes 1966088 | tf_op jit(solution)/shard_map/ppermute | solution.py:696
  227.7 16.6 %copy-start.7 = (bf16[160,2048]{1,0:T(8,128)(2,1)}, bf16[160,2048]{1,0:T(8,128)(2,1)S(1)}, u32[]{:S(2)}) copy-start(bf16[160,2048]{1,0:T(8,128)(2,1)S(1)} %collective-permute-done.17.refs_2_) | copy-start | bytes 1966084
  229.2 15.0 %copy-start.8 = (bf16[160,2048]{1,0:T(8,128)(2,1)}, bf16[160,2048]{1,0:T(8,128)(2,1)S(1)}, u32[]{:S(2)}) copy-start(bf16[160,2048]{1,0:T(8,128)(2,1)S(1)} %collective-permute-done.15.refs_0_.refs_4_) | copy-start | bytes 1966084
  242.1 22.0 %collective-permute-start.19 = (bf16[160,2048]{1,0:T(8,128)(2,1)S(1)}, bf16[160,2048]{1,0:T(8,128)(2,1)}, u32[]{:S(2)}, u32[]{:S(2)}) collective-permute-start(bf16[160,2048]{1,0:T(8,128)(2,1)S(1)} %collective-permute-done.15.refs_0_.refs_4_), channel_id=1, source_target_pairs={{0,16},{8,24},{16,0},{24,8},{1,17},{9,25},{17,1},{25,9},{2,18},{10... | collective-permute-start | bytes 1966088 | tf_op jit(solution)/shard_map/ppermute | solution.py:696
  242.7 21.4 %collective-permute-start.20 = (bf16[160,2048]{1,0:T(8,128)(2,1)S(1)}, bf16[160,2048]{1,0:T(8,128)(2,1)}, u32[]{:S(2)}, u32[]{:S(2)}) collective-permute-start(bf16[160,2048]{1,0:T(8,128)(2,1)S(1)} %collective-permute-done.18.refs_3_), channel_id=1, source_target_pairs={{0,8},{8,0},{16,24},{24,16},{1,9},{9,1},{17,25},{25,17},{2,10},{10... | collective-permute-start | bytes 1966088 | tf_op jit(solution)/shard_map/ppermute | solution.py:696
  262.1 15.2 %collective-permute-start.22 = (bf16[160,2048]{1,0:T(8,128)(2,1)}, bf16[160,2048]{1,0:T(8,128)(2,1)S(1)}, u32[]{:S(2)}, u32[]{:S(2)}) collective-permute-start(bf16[160,2048]{1,0:T(8,128)(2,1)} %slice.147), channel_id=1, source_target_pairs={{0,8},{8,0},{16,24},{24,16},{1,9},{9,1},{17,25},{25,17},{2,10},{10... | collective-permute-start | bytes 1966088 | tf_op jit(solution)/shard_map/ppermute | solution.py:696
  262.6 14.8 %collective-permute-start.21 = (bf16[160,2048]{1,0:T(8,128)(2,1)S(1)}, bf16[160,2048]{1,0:T(8,128)(2,1)S(1)}, u32[]{:S(2)}, u32[]{:S(2)}) collective-permute-start(bf16[160,2048]{1,0:T(8,128)(2,1)S(1)} %slice.146), channel_id=1, source_target_pairs={{0,16},{8,24},{16,0},{24,8},{1,17},{9,25},{17,1},{25,9},{2,18},{10... | collective-permute-start | bytes 1966088 | tf_op jit(solution)/shard_map/ppermute | solution.py:696
  296.3 191.8 %reduce-scatter.6.cloned.1.call-start = ((), (), s32[]{:S(2)}) async-start(), calls=%async_computation.12 | async-start | bytes 9437184 | tf_op jit(solution)/shard_map/reduce_scatter | solution.py:754
  322.2 54.4 %collective-permute-start.23 = (bf16[320,2048]{1,0:T(8,128)(2,1)}, bf16[320,2048]{1,0:T(8,128)(2,1)S(1)}, u32[]{:S(2)}, u32[]{:S(2)}) collective-permute-start(bf16[320,2048]{1,0:T(8,128)(2,1)} %get-tuple-element.182), channel_id=1, source_target_pairs={{0,8},{8,0},{16,24},{24,16},{1,9},{9,1},{17,25},{25,17},{2,10},{10... | collective-permute-start | bytes 3932168 | tf_op jit(solution)/shard_map/ppermute | solution.py:696
  323.5 56.0 %collective-permute-start.24 = (bf16[320,2048]{1,0:T(8,128)(2,1)}, bf16[320,2048]{1,0:T(8,128)(2,1)S(1)}, u32[]{:S(2)}, u32[]{:S(2)}) collective-permute-start(bf16[320,2048]{1,0:T(8,128)(2,1)} %get-tuple-element.183), channel_id=1, source_target_pairs={{0,16},{8,24},{16,0},{24,8},{1,17},{9,25},{17,1},{25,9},{2,18},{10... | collective-permute-start | bytes 3932168 | tf_op jit(solution)/shard_map/ppermute | solution.py:696
  324.5 54.9 %collective-permute-start.25 = (bf16[320,2048]{1,0:T(8,128)(2,1)}, bf16[320,2048]{1,0:T(8,128)(2,1)}, u32[]{:S(2)}, u32[]{:S(2)}) collective-permute-start(bf16[320,2048]{1,0:T(8,128)(2,1)} %get-tuple-element.184), channel_id=1, source_target_pairs={{0,24},{8,16},{16,8},{24,0},{1,25},{9,17},{17,9},{25,1},{2,26},{10... | collective-permute-start | bytes 3932168 | tf_op jit(solution)/shard_map/ppermute | solution.py:696
  388.1 20.0 %collective-permute-start.28 = (bf16[160,2048]{1,0:T(8,128)(2,1)}, bf16[160,2048]{1,0:T(8,128)(2,1)S(1)}, u32[]{:S(2)}, u32[]{:S(2)}) collective-permute-start(bf16[160,2048]{1,0:T(8,128)(2,1)} %get-tuple-element.192.refs_0_.refs_12_), channel_id=1, source_target_pairs={{0,16},{8,24},{16,0},{24,8},{1,17},{9,25},{17,1},{25,9},{2,18},{10... | collective-permute-start | bytes 1966088 | tf_op jit(solution)/shard_map/ppermute | solution.py:696
  389.2 18.9 %collective-permute-start.26 = (bf16[160,2048]{1,0:T(8,128)(2,1)}, bf16[160,2048]{1,0:T(8,128)(2,1)S(1)}, u32[]{:S(2)}, u32[]{:S(2)}) collective-permute-start(bf16[160,2048]{1,0:T(8,128)(2,1)} %get-tuple-element.192.refs_0_.refs_12_), channel_id=1, source_target_pairs={{0,8},{8,0},{16,24},{24,16},{1,9},{9,1},{17,25},{25,17},{2,10},{10... | collective-permute-start | bytes 1966088 | tf_op jit(solution)/shard_map/ppermute | solution.py:696
  390.1 26.5 %collective-permute-start.29 = (bf16[160,2048]{1,0:T(8,128)(2,1)}, bf16[160,2048]{1,0:T(8,128)(2,1)S(1)}, u32[]{:S(2)}, u32[]{:S(2)}) collective-permute-start(bf16[160,2048]{1,0:T(8,128)(2,1)} %get-tuple-element.193.refs_1_.refs_13_), channel_id=1, source_target_pairs={{0,16},{8,24},{16,0},{24,8},{1,17},{9,25},{17,1},{25,9},{2,18},{10... | collective-permute-start | bytes 1966088 | tf_op jit(solution)/shard_map/ppermute | solution.py:696
  391.1 26.3 %collective-permute-start.27 = (bf16[160,2048]{1,0:T(8,128)(2,1)}, bf16[160,2048]{1,0:T(8,128)(2,1)S(1)}, u32[]{:S(2)}, u32[]{:S(2)}) collective-permute-start(bf16[160,2048]{1,0:T(8,128)(2,1)} %get-tuple-element.193.refs_1_.refs_13_), channel_id=1, source_target_pairs={{0,8},{8,0},{16,24},{24,16},{1,9},{9,1},{17,25},{25,17},{2,10},{10... | collective-permute-start | bytes 1966088 | tf_op jit(solution)/shard_map/ppermute | solution.py:696
  408.1 15.0 %copy-start.10 = (bf16[160,2048]{1,0:T(8,128)(2,1)}, bf16[160,2048]{1,0:T(8,128)(2,1)S(1)}, u32[]{:S(2)}) copy-start(bf16[160,2048]{1,0:T(8,128)(2,1)S(1)} %collective-permute-done.28.refs_2_.refs_16_) | copy-start | bytes 1966084
  408.1 14.9 %copy-start.11 = (bf16[160,2048]{1,0:T(8,128)(2,1)}, bf16[160,2048]{1,0:T(8,128)(2,1)S(1)}, u32[]{:S(2)}) copy-start(bf16[160,2048]{1,0:T(8,128)(2,1)S(1)} %collective-permute-done.26.refs_0_.refs_14_) | copy-start | bytes 1966084
  417.4 30.7 %collective-permute-start.32 = (bf16[160,2048]{1,0:T(8,128)(2,1)S(1)}, bf16[160,2048]{1,0:T(8,128)(2,1)S(1)}, u32[]{:S(2)}, u32[]{:S(2)}) collective-permute-start(bf16[160,2048]{1,0:T(8,128)(2,1)S(1)} %collective-permute-done.26.refs_0_.refs_14_), channel_id=1, source_target_pairs={{0,16},{8,24},{16,0},{24,8},{1,17},{9,25},{17,1},{25,9},{2,18},{10... | collective-permute-start | bytes 1966088 | tf_op jit(solution)/shard_map/ppermute | solution.py:696
  418.2 30.8 %collective-permute-start.33 = (bf16[160,2048]{1,0:T(8,128)(2,1)}, bf16[160,2048]{1,0:T(8,128)(2,1)}, u32[]{:S(2)}, u32[]{:S(2)}) collective-permute-start(bf16[160,2048]{1,0:T(8,128)(2,1)} %get-tuple-element.209), channel_id=1, source_target_pairs={{0,8},{8,0},{16,24},{24,16},{1,9},{9,1},{17,25},{25,17},{2,10},{10... | collective-permute-start | bytes 1966088 | tf_op jit(solution)/shard_map/ppermute | solution.py:696
  419.2 29.8 %collective-permute-start.34 = (bf16[160,2048]{1,0:T(8,128)(2,1)}, bf16[160,2048]{1,0:T(8,128)(2,1)}, u32[]{:S(2)}, u32[]{:S(2)}) collective-permute-start(bf16[160,2048]{1,0:T(8,128)(2,1)} %get-tuple-element.210), channel_id=1, source_target_pairs={{0,16},{8,24},{16,0},{24,8},{1,17},{9,25},{17,1},{25,9},{2,18},{10... | collective-permute-start | bytes 1966088 | tf_op jit(solution)/shard_map/ppermute | solution.py:696
  420.4 28.6 %collective-permute-start.35 = (bf16[160,2048]{1,0:T(8,128)(2,1)S(1)}, bf16[160,2048]{1,0:T(8,128)(2,1)}, u32[]{:S(2)}, u32[]{:S(2)}) collective-permute-start(bf16[160,2048]{1,0:T(8,128)(2,1)S(1)} %collective-permute-done.29.refs_3_.refs_17_), channel_id=1, source_target_pairs={{0,8},{8,0},{16,24},{24,16},{1,9},{9,1},{17,25},{25,17},{2,10},{10... | collective-permute-start | bytes 1966088 | tf_op jit(solution)/shard_map/ppermute | solution.py:696
  447.2 45.2 %collective-permute-start.30 = (bf16[384,2048]{1,0:T(8,128)(2,1)}, bf16[384,2048]{1,0:T(8,128)(2,1)}, u32[]{:S(2)}, u32[]{:S(2)}) collective-permute-start(bf16[384,2048]{1,0:T(8,128)(2,1)} %get-tuple-element.206), channel_id=1, source_target_pairs={{0,8},{8,0},{16,24},{24,16},{1,9},{9,1},{17,25},{25,17},{2,10},{10... | collective-permute-start | bytes 4718600 | tf_op jit(solution)/shard_map/ppermute | solution.py:696
  448.1 44.2 %collective-permute-start.31 = (bf16[384,2048]{1,0:T(8,128)(2,1)}, bf16[384,2048]{1,0:T(8,128)(2,1)}, u32[]{:S(2)}, u32[]{:S(2)}) collective-permute-start(bf16[384,2048]{1,0:T(8,128)(2,1)} %get-tuple-element.207), channel_id=1, source_target_pairs={{0,16},{8,24},{16,0},{24,8},{1,17},{9,25},{17,1},{25,9},{2,18},{10... | collective-permute-start | bytes 4718600 | tf_op jit(solution)/shard_map/ppermute | solution.py:696
  464.3 57.7 %collective-permute-start.36 = (bf16[384,2048]{1,0:T(8,128)(2,1)}, bf16[384,2048]{1,0:T(8,128)(2,1)S(1)}, u32[]{:S(2)}, u32[]{:S(2)}) collective-permute-start(bf16[384,2048]{1,0:T(8,128)(2,1)} %get-tuple-element.213), channel_id=1, source_target_pairs={{0,24},{8,16},{16,8},{24,0},{1,25},{9,17},{17,9},{25,1},{2,26},{10... | collective-permute-start | bytes 4718600 | tf_op jit(solution)/shard_map/ppermute | solution.py:696
  488.1 34.0 %all-to-all-start.2 = ((bf16[4,64,2048]{2,1,0:T(8,128)(2,1)}), bf16[4,64,2048]{2,1,0:T(8,128)(2,1)S(1)}, u32[]{:S(2)}, u32[]{:S(2)}) async-start(bf16[4,64,2048]{2,1,0:T(8,128)(2,1)} %reduce-scatter.6.cloned.1.call-done), calls=%async_computation.4 | async-start | bytes 2097152 | tf_op jit(solution)/shard_map/all_to_all | solution.py:730
  491.6 96.9 %reduce-scatter.8.cloned.1.call-start = ((), (), s32[]{:S(2)}) async-start(), calls=%async_computation.13 | async-start | bytes 9437184 | tf_op jit(solution)/shard_map/reduce_scatter | solution.py:754
  534.7 12.6 %all-to-all-start.3 = ((f32[32,1,768]{2,1,0:T(1,128)}), f32[32,1,768]{2,1,0:T(1,128)S(1)}, u32[]{:S(2)}, u32[]{:S(2)}) async-start(f32[32,1,768]{2,1,0:T(1,128)} %all_to_all.21), calls=%async_computation.5 | async-start | bytes 196608 | tf_op jit(solution)/shard_map/all_to_all | solution.py:746
  540.0 17.0 %collective-permute-start.41 = (bf16[50,2048]{1,0:T(8,128)(2,1)S(1)}, bf16[50,2048]{1,0:T(8,128)(2,1)S(1)}, u32[]{:S(2)}, u32[]{:S(2)}) collective-permute-start(bf16[50,2048]{1,0:T(8,128)(2,1)S(1)} %slice.159), channel_id=1, source_target_pairs={{1,0},{2,1},{3,2},{4,3},{5,4},{6,5},{7,6},{8,7},{9,8},{10,9},{11,1... | collective-permute-start | bytes 614408 | tf_op jit(solution)/shard_map/ppermute | solution.py:966
  548.0 17.6 %collective-permute-start.37 = (bf16[160,2048]{1,0:T(8,128)(2,1)S(1)}, bf16[160,2048]{1,0:T(8,128)(2,1)S(1)}, u32[]{:S(2)}, u32[]{:S(2)}) collective-permute-start(bf16[160,2048]{1,0:T(8,128)(2,1)S(1)} %copy-done.46), channel_id=1, source_target_pairs={{0,8},{8,0},{16,24},{24,16},{1,9},{9,1},{17,25},{25,17},{2,10},{10... | collective-permute-start | bytes 1966088 | tf_op jit(solution)/shard_map/ppermute | solution.py:696
  550.5 17.7 %collective-permute-start.38 = (bf16[160,2048]{1,0:T(8,128)(2,1)S(1)}, bf16[160,2048]{1,0:T(8,128)(2,1)S(1)}, u32[]{:S(2)}, u32[]{:S(2)}) collective-permute-start(bf16[160,2048]{1,0:T(8,128)(2,1)S(1)} %add_convert_fusion.1), channel_id=1, source_target_pairs={{0,16},{8,24},{16,0},{24,8},{1,17},{9,25},{17,1},{25,9},{2,18},{10... | collective-permute-start | bytes 1966088 | tf_op jit(solution)/shard_map/ppermute | solution.py:696
  552.7 26.9 %collective-permute-start.39 = (bf16[160,2048]{1,0:T(8,128)(2,1)S(1)}, bf16[160,2048]{1,0:T(8,128)(2,1)S(1)}, u32[]{:S(2)}, u32[]{:S(2)}) collective-permute-start(bf16[160,2048]{1,0:T(8,128)(2,1)S(1)} %add_convert_fusion), channel_id=1, source_target_pairs={{0,8},{8,0},{16,24},{24,16},{1,9},{9,1},{17,25},{25,17},{2,10},{10... | collective-permute-start | bytes 1966088 | tf_op jit(solution)/shard_map/ppermute | solution.py:696
  553.9 27.1 %collective-permute-start.40 = (bf16[160,2048]{1,0:T(8,128)(2,1)S(1)}, bf16[160,2048]{1,0:T(8,128)(2,1)S(1)}, u32[]{:S(2)}, u32[]{:S(2)}) collective-permute-start(bf16[160,2048]{1,0:T(8,128)(2,1)S(1)} %copy-done.45), channel_id=1, source_target_pairs={{0,16},{8,24},{16,0},{24,8},{1,17},{9,25},{17,1},{25,9},{2,18},{10... | collective-permute-start | bytes 1966088 | tf_op jit(solution)/shard_map/ppermute | solution.py:696
  558.2 22.8 %copy-start.19 = (f32[160,2048]{1,0:T(8,128)S(1)}, f32[160,2048]{1,0:T(8,128)}, u32[]{:S(2)}) copy-start(f32[160,2048]{1,0:T(8,128)} %get-tuple-element.249) | copy-start | bytes 3932164
  582.3 12.0 %copy-start.1 = (f32[320,2048]{1,0:T(8,128)S(1)}, f32[320,2048]{1,0:T(8,128)}, u32[]{:S(2)}) copy-start(f32[320,2048]{1,0:T(8,128)} %get-tuple-element.151.refs_4_) | copy-start | bytes 7864324
  582.3 12.0 %copy-start.27 = (f32[2048]{0:T(1024)S(1)}, f32[2048]{0:T(1024)}, u32[]{:S(2)}) copy-start(f32[2048]{0:T(1024)} %reshape.256) | copy-start | bytes 24580
  590.7 12.5 %all-to-all-start.4 = ((bf16[4,64,1536]{2,1,0:T(8,128)(2,1)}), bf16[4,64,1536]{2,1,0:T(8,128)(2,1)S(1)}, u32[]{:S(2)}, u32[]{:S(2)}) async-start(bf16[4,64,1536]{2,1,0:T(8,128)(2,1)} %slice.192), calls=%async_computation.7 | async-start | bytes 1572864 | tf_op jit(solution)/shard_map/all_to_all | solution.py:730
  (37 other events, 278.3 us)
Sparse Core Ops, SparseCore 0:
  29.2 83.5 all-gather.3
  114.4 80.4 all-gather.5
  196.5 80.5 all-gather.7
  296.4 89.1 reduce-scatter.3
  387.7 87.9 reduce-scatter.5
  494.4 94.0 reduce-scatter.7

commit v5 on v4

--- a/solution.py
+++ b/solution.py
@@ -15,7 +15,7 @@
 NORM_ROWS = 64
 MASKED = -1e30
 GELU_A, GELU_B = 0.7978845608028654, 0.044715
-VMEM_LIMIT = 60 * 1024 * 1024
+VMEM_LIMIT = 53 * 1024 * 1024
 VMEM = pl.BlockSpec(memory_space=pltpu.VMEM)
 HBM = pl.BlockSpec(memory_space=pl.ANY)
 
@@ -120,14 +120,14 @@
 
     def kernel(*refs):
         gain_ref, bias_ref, off_ref, ok_ref, attn_hbm = refs[given : given + 5]
-        outs = refs[given + 5 : given + 5 + 5 * count]
-        x_all, weights, mask, sems = refs[given + 5 + 5 * count :]
+        outs = refs[given + 5 : given + 5 + 6 * count]
+        x_all, weights, mask, sems = refs[given + 5 + 6 * count :]
         x_copies = load_rows(refs[:given], x_all, sems.at[pl.ds(members, given)])
         copies = load_blocks(attn_hbm, weights, sems)
         gain, bias = gain_ref[...], bias_ref[...]
         wait_all(x_copies)
         for index in range(count):
-            low_ref = outs[5 * index]
+            low_ref = outs[6 * index]
 
             def norm_rows(block, _):
                 start = pl.multiple_of(block * NORM_ROWS, NORM_ROWS)
@@ -138,10 +138,10 @@
             lax.fori_loop(0, keys // NORM_ROWS, norm_rows, 0)
         wait_all(copies)
         for index in range(count):
-            attend_segment(ok_ref[index : index + 1, :], off_ref, weights, mask, outs[5 * index : 5 * index + 5])
+            attend_segment(ok_ref[index : index + 1, :], off_ref, weights, mask, outs[6 * index : 6 * index + 6])
 
     def attend_segment(ok_row, off_ref, weights, mask, refs):
-        low_ref, qkv_ref, lse_ref, mixed_ref, part_ref = refs
+        low_ref, qkv_ref, lse_ref, mixed_ref, *parts = refs
         row = lax.broadcasted_iota(jnp.int32, (seg, keys), 0)
         col = lax.broadcasted_iota(jnp.int32, (seg, keys), 1)
         mask[...] = jnp.where(jnp.logical_or(col <= row, ok_row > 0.5), 0.0, MASKED)
@@ -179,7 +179,9 @@
         def project_out(block, _):
             at = pl.ds(pl.multiple_of(block * cols, PAIR), cols)
             weight = block_of(weights, block, pl.ds(3 * cols, cols))
-            part_ref[:, at] = dot(mixed_ref[...], weight).astype(part_ref.dtype)
+            value = dot(mixed_ref[...], weight)
+            for half, part in enumerate(parts):
+                part[:, at] = value[half * seg // 2 : (half + 1) * seg // 2].astype(part.dtype)
             return _
 
         lax.fori_loop(0, members, project_out, 0)
@@ -191,7 +193,8 @@
             shape_of(keys, 3 * cols),
             shape_of(seg, PAIR, F32),
             shape_of(seg, cols),
-            shape_of(seg, width, dtype),
+            shape_of(seg // 2, width, dtype),
+            shape_of(seg // 2, width, dtype),
         ]
     outs = pl.pallas_call(
         kernel,
@@ -207,7 +210,7 @@
         name="attn_forward",
         **kernel_params(12 * count),
     )(*pieces, gain, bias, off, ok_rows, attn_w)
-    return [outs[5 * index : 5 * index + 5] for index in range(count)]
+    return [outs[6 * index : 6 * index + 6] for index in range(count)]
 
 
 def attn_backward(branches, qkvs, lses, ok_cols, attn_w, types):
@@ -581,24 +584,35 @@
 def middle_norm(tokens, parts, off, gain, bias):
     seg, width = tokens.shape
     count = len(parts)
-
     rows = seg // 2
+    step = 32
 
     def kernel(*refs):
-        off_ref, gain_ref, bias_ref, middle_ref, *seconds = refs[count + 1 :]
-        total = sum_parts(refs[: count + 1]) + off_ref[...]
-        middle_ref[...] = total
-        store_half(seconds, norm_apply(total, gain_ref[...], bias_ref[...]).astype(BF16))
+        tokens_ref, off_ref, gain_ref, bias_ref, middle_ref, *seconds = refs[2 * count :]
+        off, gain, bias = off_ref[...], gain_ref[...], bias_ref[...]
+        for half in range(2):
+
+            def body(block, _):
+                start = pl.multiple_of(block * step, step)
+                at, whole = pl.ds(start, step), pl.ds(half * rows + start, step)
+                total = tokens_ref[whole, :].astype(F32)
+                for index in range(count):
+                    total = total + refs[2 * index + half][at, :].astype(F32)
+                total = total + off
+                middle_ref[whole, :] = total
+                seconds[half][at, :] = norm_apply(total, gain, bias).astype(BF16)
+                return _
+
+            lax.fori_loop(0, rows // step, body, 0)
 
     return pl.pallas_call(
         kernel,
-        grid=(2,),
         out_shape=(shape_of(seg, width, F32), shape_of(rows, width), shape_of(rows, width)),
-        in_specs=[row_blocks(width, rows=rows)] * (count + 1) + [kept(1, width)] * 3,
-        out_specs=(row_blocks(width, rows=rows), kept(rows, width), kept(rows, width)),
+        in_specs=[VMEM] * (2 * count + 4),
+        out_specs=(VMEM,) * 3,
         name="middle_norm",
         **kernel_params(5),
-    )(tokens, *parts, off, gain, bias)
+    )(*flat_list(parts), tokens, off, gain, bias)
 
 
 def middle_back(middle, cot, parts, gain):
@@ -724,6 +738,14 @@
 
 def add_low(left, right):
     return (left.astype(F32) + right.astype(F32)).astype(BF16)
+
+
+def output_halves(rel, halves, over, early):
+    if over and rel == 2:
+        return [add_low(halves[0], over[0]), early[1]], [False, True]
+    if over and rel == 1:
+        return [early[0], add_low(halves[1], over[1])], [True, False]
+    return halves, [False, False]
 
 
 def trade_blocks(blocks):
@@ -857,12 +879,20 @@
         outs = attn_forward(
             xs, gain_one, bias_one, qkv_off, oks, attn_w, [part_type(rel) for rel in some]
         )
-        for rel, (low, qkv, lse, mixed, part) in zip(some, outs):
+        for rel, (low, qkv, lse, mixed, *part) in zip(some, outs):
             attn[rel] = (low, qkv, lse, mixed)
-            middle_parts[rel] = swap(part, rel)
+            middle_parts[rel] = part
             previous = [lse]
+        if members > 3 and some == [3]:
+            over = middle_parts.pop(3)
+            middle_over = [swap(over[0], 1), swap(over[1], 2)]
+    if members > 3:
+        two, one = middle_parts[2], middle_parts[1]
+        middle_parts[2] = [add_low(two[0], middle_over[0]), two[1]]
+        middle_parts[1] = [one[0], add_low(one[1], middle_over[1])]
+    middle_parts = {rel: [swap(half, rel) for half in part] for rel, part in middle_parts.items()}
     middle, *second_own = middle_norm(
-        tokens, [middle_parts[rel] for rel in rels], out_off, gain_two, bias_two
+        tokens, list(middle_parts.values()), out_off, gain_two, bias_two
     )
     def ordered(values):
         return [values[rel] for rel in own_last]
@@ -940,14 +970,17 @@
         others = output_over if some == [3] else []
         back_of(some, [group_branch[rel] for rel in some], qkv_sums[last], *others)
         last = some[-1]
+    output_early = []
+    if members > 3:
+        early = after([output_parts[1][0], output_parts[2][1]], qkv_sums[2])
+        output_early = [swap(early[0], 1), swap(early[1], 2)]
     attn_partial = attn_weight_grad(
         [attn[rel][0] for rel in rels],
         [grads[rel] for rel in rels],
         [attn[rel][3] for rel in rels],
         flat_list(group_branch),
     )
-    up_blocks = trade_blocks(after(up_share, attn_partial))
-    joined_parts = after(joined_parts, attn_partial, up_blocks)
+    joined_parts = after(joined_parts, attn_partial, output_early)
     attn_share = to_row_blocks(after(attn_partial, up_share))
     out_grad = (
         attn_share[:, :, 3 * my_cols :].swapaxes(0, 1).reshape(row_share, width).astype(F32)
@@ -988,13 +1021,14 @@
         whole(middle_sums[3]),
     ]
     share = scatter_small(jnp.concatenate(pieces, 1))
+    up_blocks = trade_blocks(after(up_share, share))
     output_parts = after(output_parts, share)
-    if output_over:
-        two, one = output_parts[2], output_parts[1]
-        output_parts[2] = [add_low(two[0], output_over[0]), two[1]]
-        output_parts[1] = [one[0], add_low(one[1], output_over[1])]
     output_parts = {
-        rel: [swap(half, rel) for half in halves] for rel, halves in output_parts.items()
+        rel: [half if early else swap(half, rel) for half, early in zip(*halves)]
+        for rel, halves in (
+            (rel, (output_halves(rel, halves, output_over, output_early)))
+            for rel, halves in output_parts.items()
+        )
     }
     down_grad = after(down_share, share).astype(F32)
     up_grad = up_blocks.swapaxes(0, 1).reshape(row_share, members * my_ff).astype(F32)

time: 618 us -> 607 us (0.982)
    ppermute x35 -> x38, waiting for transfers between devices: 109 us -> 137 us  [swap(): return lax.ppermute(value, 'fsdp', [(i, i ^ rel) for i in range(count)])]
    all_to_all x3, waiting for transfers between devices: 43.8 us -> 18.2 us  [trade_blocks(): return lax.all_to_all(blocks, 'fsdp', 0, 0, tiled=True)]
    reduce_scatter x3, waiting for transfers between devices: 6.26 us -> 0.02 us  [scatter_dp(): return lax.psum_scatter(value, 'dp', scatter_dimension=axis, tiled=True)]
    ppermute x35 -> x38, starting transfers between devices: 37.4 us -> 38.5 us  [swap(): return lax.ppermute(value, 'fsdp', [(i, i ^ rel) for i in range(count)])]
  transfers between devices with their start and end apart: 52 -> 55, of which waited for: 27 -> 21; matrix products, arithmetic and copies ran while one was open for 6% -> 5% of each run, Pallas kernels for 47% -> 47%
where the time goes in v5:
time: 607 us; the launch traced here: 602 us
  Pallas kernels  283 us (47%)
  waiting for transfers between devices  173 us (29%)
  starting transfers between devices  62.3 us (10%)
  local copies, waits for them, and re-layouts  34.2 us (6%)
  blocking collectives  18.8 us (3%)
  between operations  15.5 us (3%)
  other arithmetic  14.9 us (2%)
    ppermute x38, waiting for transfers between devices, swap(): return lax.ppermute(value, 'fsdp', [(i, i ^ rel) for i in range(count)])  137 us
    pallas_call x3, Pallas kernels, attn_forward(): pl.pallas_call(kernel, out_shape=shapes, in_specs=[HBM] * given + [VMEM]...  55.3 us
    pallas_call x3, Pallas kernels, attn_backward(): pl.pallas_call(kernel, out_shape=shapes, in_specs=[HBM] * given + [VMEM]...  53.8 us
    pallas_call x2, Pallas kernels, ffn_back(): pl.pallas_call(kernel, out_shape=(shape_of(rows, wide), shape_of(1, wide,...  38.6 us
    ppermute x38, starting transfers between devices, swap(): return lax.ppermute(value, 'fsdp', [(i, i ^ rel) for i in range(count)])  38.5 us
    pallas_call x2, Pallas kernels, weight_grad(): pl.pallas_call(kernel, grid=(tall // GRAD_ROWS,), out_shape=shape_of(tall...  35.6 us
    pallas_call x3, Pallas kernels, ffn_hidden(): pl.pallas_call(kernel, out_shape=[shape_of(seg, wide)] * (2 * count), in_...  35.5 us
    pallas_call x1, Pallas kernels, attn_weight_grad(): pl.pallas_call(kernel, grid=(width // GRAD_ROWS,), out_shape=shape_of(wid...  21.5 us
  transfers between devices with their start and end apart: 55, of which 21 were waited for; matrix products, arithmetic and copies ran while one was open for 5% of the time, Pallas kernels for 47%

profile of v5, /device:TPU:0, one launch (start us, length us, event | category | flops | bytes accessed | tf_op | source)
XLA Modules:
  0.0 601.7 jit_solution(7786567577844956111)
XLA Ops:
  12.0 5.2 all-to-all-start
  17.5 10.4 %all-to-all-done = bf16[4,64,1536]{2,1,0:T(8,128)(2,1)S(1)} async-done(((bf16[4,64,1536]{2,1,0:T(8,128)(2,1)}), bf16[4,64,1536]{2,1,0:T(8,128)(2,1)S(1)}, u32[]{:S(2)}, u32[]{:S(2)}) %all-to-all-start) | async-done | bytes 786464 | tf_op jit(solution)/shard_map/all_to_all | solution.py:752
  29.4 1.5 collective-permute-start.1
  30.9 1.3 collective-permute-start
  33.1 1.5 collective-permute-start.2
  34.7 1.8 reshape.206
  37.4 18.8 %all_to_all.29 = bf16[4,64,2048]{2,1,0:T(8,128)(2,1)} all-to-all(bf16[4,64,2048]{2,1,0:T(8,128)(2,1)S(1)} %copy.73), channel_id=1, replica_groups=mesh['fsdp'=4,'dp'=8] {'fsdp'}, dimensions={0} | all-to-all | bytes 2097152 | tf_op jit(solution)/shard_map/all_to_all | solution.py:752
  60.0 1.6 collective-permute-start.8
  61.6 4.2 collective-permute-done.8
  67.9 3.5 collective-permute-done.9
  73.6 21.3 %collective-permute-done.4.refs_1_ = bf16[384,2048]{1,0:T(8,128)(2,1)S(1)} collective-permute-done((bf16[384,2048]{1,0:T(8,128)(2,1)S(1)}, bf16[384,2048]{1,0:T(8,128)(2,1)S(1)}, u32[]{:S(2)}, u32[]{:S(2)}) %collective-permute-start.4) | collective-permute-done | bytes 1572896 | tf_op jit(solution)/shard_map/ppermute | solution.py:710
  95.7 2.1 slice.133
  98.7 1.3 collective-permute-start.5
  105.1 12.5 %collective-permute-done.5.refs_0_ = bf16[192,2048]{1,0:T(8,128)(2,1)S(1)} collective-permute-done((bf16[192,2048]{1,0:T(8,128)(2,1)}, bf16[192,2048]{1,0:T(8,128)(2,1)S(1)}, u32[]{:S(2)}, u32[]{:S(2)}) %collective-permute-start.5) | collective-permute-done | bytes 786464 | tf_op jit(solution)/shard_map/ppermute | solution.py:710
  118.4 15.4 %attn_forward.3 = (bf16[384,2048]{1,0:T(8,128)(2,1)}, bf16[384,1536]{1,0:T(8,128)(2,1)}, f32[320,128]{1,0:T(8,128)S(1)}, bf16[320,512]{1,0:T(8,128)(2,1)S(1)}, b...) custom-call(bf16[192,2048]{1,0:T(8,128)(2,1)} %copy-done.20, bf16[192,2048]{1,0:T(8,128)(2,1)} %collective-permute-done.6.refs_1_, ...), custom_call_target="tpu_custom_call" | custom-call | flops 12000000 | bytes 1 | tf_op jit(solution)/shard_map/attn_forward/pallas_call | solution.py:199
  134.8 1.8 collective-permute-start.17
  137.3 1.3 collective-permute-start.16
  138.6 25.3 %attn_forward.4 = (bf16[384,2048]{1,0:T(8,128)(2,1)}, bf16[384,1536]{1,0:T(8,128)(2,1)}, f32[320,128]{1,0:T(8,128)S(1)}, bf16[320,512]{1,0:T(8,128)(2,1)S(1)}, b...) custom-call(bf16[384,2048]{1,0:T(8,128)(2,1)} %collective-permute-do, ...), custom_call_target="tpu_custom_call" | custom-call | flops 24000000 | bytes 1 | tf_op jit(solution)/shard_map/attn_forward/pallas_call | solution.py:199
  165.3 2.1 add_convert_fusion.3
  169.5 11.0 %collective-permute-done.17.refs_6_.refs_2_ = bf16[320,2048]{1,0:T(8,128)(2,1)S(1)} collective-permute-done((bf16[320,2048]{1,0:T(8,128)(2,1)S(1)}, bf16[320,2048]{1,0:T(8,128)(2,1)S(1)}, u32[]{:S(2)}, u32[]{:S(2)}) %collective-permute-start.17) | collective-permute-done | bytes 1310752 | tf_op jit(solution)/shard_map/ppermute | solution.py:710
  182.7 14.6 %attn_forward.5 = (bf16[384,2048]{1,0:T(8,128)(2,1)}, bf16[384,1536]{1,0:T(8,128)(2,1)}, f32[320,128]{1,0:T(8,128)S(1)}, bf16[320,512]{1,0:T(8,128)(2,1)S(1)}, f32[160,2048]{1,0:T(8,128)}, /*index=5*/f32[160,2048]{1,0:T(8,128)}) custom-call(bf16[384,2048]{1,0:T(8,128)(2,1)} %copy-done.9, f32[1,2048]{1,0:T(1,128)S(1)} %reshape.241.refs_2_.refs_1_.refs_6_, ...), custom_call_target="tpu_custom_call" | custom-call | flops 12000000 | bytes 1 | tf_op jit(solution)/shard_map/attn_forward/pallas_call | solution.py:199
  197.3 9.3 %collective-permute-done.12.refs_1_ = bf16[160,2048]{1,0:T(8,128)(2,1)} collective-permute-done((bf16[160,2048]{1,0:T(8,128)(2,1)}, bf16[160,2048]{1,0:T(8,128)(2,1)}, u32[]{:S(2)}, u32[]{:S(2)}) %collective-permute-start.12) | collective-permute-done | bytes 655392 | tf_op jit(solution)/shard_map/ppermute | solution.py:710
  206.6 7.2 %middle_norm.1 = (f32[320,2048]{1,0:T(8,128)}, bf16[160,2048]{1,0:T(8,128)(2,1)S(1)}, bf16[160,2048]{1,0:T(8,128)(2,1)}) custom-call(bf16[160,2048]{1,0:T(8,128)(2,1)} %copy-done.21, bf16[160,2048]{1,0:T(8,128)(2,1)} %collective-permute-done.12.refs_1_, bf16[160,2048]{1,0:T(8,128)(2,1)} %collective-permute-done.14.refs_2_, ...), custom_call_target="tpu_custom_call" | custom-call | flops 5000000 | bytes 1 | tf_op jit(solution)/shard_map/middle_norm/pallas_call | solution.py:608
  215.3 1.4 collective-permute-start.21
  216.7 1.2 collective-permute-start.19
  218.1 10.1 %ffn_hidden.3 = (bf16[320,2048]{1,0:T(8,128)(2,1)}, bf16[320,2048]{1,0:T(8,128)(2,1)}) custom-call(bf16[160,2048]{1,0:T(8,128)(2,1)S(1)} %get-tuple-element.160.refs_0_.refs_6_, bf16[160,2048]{1,0:T(8,128)(2,1)} %get-tuple-element.161.refs_1_.refs_7_, f32[1,2048]{1,0:T(1,128)S(1)} %constant_dynamic-slice_fusion.refs_2_.refs_4_, bf16[8,4,64,2048]{3,2,1,0:T(8,128)(2,1)} %bitcast.56), custom_call_target="tpu_custom_call" | custom-call | flops 6000000 | bytes 1 | tf_op jit(solution)/shard_map/ffn_hidden/pallas_call | solution.py:349
  228.1 3.4 collective-permute-done.20.refs_2_
  231.9 10.9 %collective-permute-done.21.refs_3_ = bf16[160,2048]{1,0:T(8,128)(2,1)} collective-permute-done((bf16[160,2048]{1,0:T(8,128)(2,1)}, bf16[160,2048]{1,0:T(8,128)(2,1)}, u32[]{:S(2)}, u32[]{:S(2)}) %collective-permute-start.21) | collective-permute-done | bytes 655392 | tf_op jit(solution)/shard_map/ppermute | solution.py:710
  242.8 1.5 collective-permute-start.22
  245.2 15.0 %ffn_hidden.4 = (bf16[320,2048]{1,0:T(8,128)(2,1)}, bf16[320,2048]{1,0:T(8,128)(2,1)}, bf16[320,2048]{1,0:T(8,128)(2,1)}, bf16[320,2048]{1,0:T(8,128)(2,1)}) custom-call(bf16[160,2048]{1,0:T(8,128)(2,1)S(1)} %collective-permute-done.18.refs_0_.refs_4_, bf16[160,2048]{1,0:T(8,128)(2,1)} %collective-permute-done.19.refs_1_.refs_5_, ...), custom_call_target="tpu_custom_call" | custom-call | flops 12000000 | bytes 1 | tf_op jit(solution)/shard_map/ffn_hidden/pallas_call | solution.py:349
  260.2 1.2 slice.146
  264.3 10.5 %ffn_hidden.5 = (bf16[320,2048]{1,0:T(8,128)(2,1)}, bf16[320,2048]{1,0:T(8,128)(2,1)}) custom-call(bf16[160,2048]{1,0:T(8,128)(2,1)S(1)} %collective-permute-done.22.refs_0_, bf16[160,2048]{1,0:T(8,128)(2,1)} %copy-done.16, f32[1,2048]{1,0:T(1,128)S(1)} %constant_dynamic-slice_fusion.refs_2_.refs_4_, bf16[8,4,64,2048]{3,2,1,0:T(8,128)(2,1)} %bitcast.58), custom_call_target="tpu_custom_call" | custom-call | flops 6000000 | bytes 1 | tf_op jit(solution)/shard_map/ffn_hidden/pallas_call | solution.py:349
  275.7 17.6 %weight_grad.2 = bf16[2048,2048]{1,0:T(8,128)(2,1)} custom-call(bf16[320,2048]{1,0:T(8,128)(2,1)} %get-tuple-element.182.refs_0_, bf16[320,2048]{1,0:T(8,128)(2,1)} %get-tuple-element.172.refs_1_, bf16[320,2048]{1,0:T(8,128)(2,1)} %get-tuple-element.168.refs_2_, bf16[320,2048]{1,0:T(8,128)(2,1)} %get-tuple-element.162.refs_3_, ...), custom_call_target="tpu_custom_call" | custom-call | flops 17000000 | bytes 1 | tf_op jit(solution)/shard_map/weight_grad/pallas_call | solution.py:486
  293.4 25.8 %ffn_back.2 = (bf16[960,2048]{1,0:T(8,128)(2,1)}, f32[1,2048]{1,0:T(1,128)S(1)}, bf16[320,2048]{1,0:T(8,128)(2,1)}, bf16[320,2048]{1,0:T(8,128)(2,1)}, bf16[320,2048]{1,0:T(8,128)(2,1)}) custom-call(bf16[160,2048]{1,0:T(8,128)(2,1)S(1)} %collective-permute-done.24.refs_4_.refs_0_, bf16[160,2048]{1,0:T(8,128)(2,1)} %copy-done.13, ...), custom_call_target="tpu_custom_call" | custom-call | flops 30000000 | bytes 1 | tf_op jit(solution)/shard_map/ffn_back/pallas_call | solution.py:406
  320.0 1.6 collective-permute-start.27
  322.8 12.9 %ffn_back.3 = (bf16[320,2048]{1,0:T(8,128)(2,1)}, f32[1,2048]{1,0:T(1,128)S(1)}, f32[320,2048]{1,0:T(8,128)}) custom-call(bf16[320,2048]{1,0:T(8,128)(2,1)} %refs_5_.1, bf16[320,2048]{1,0:T(8,128)(2,1)} %get-tuple-element.180.refs_1_, bf16[8,4,64,2048]{3,2,1,0:T(8,128)(2,1)} %bitcast.60, bf16[2048,2048]{1,0:T(8,128)(2,1)} %all-gather.8.cloned.1.call-done.refs_8_.refs_3_.refs_4_), custom_call_target="tpu_custom_call" | custom-call | flops 10000000 | bytes 1 | tf_op jit(solution)/shard_map/ffn_back/pallas_call | solution.py:406
  335.7 18.0 %weight_grad.3 = bf16[2048,2048]{1,0:T(8,128)(2,1)} custom-call(bf16[160,2048]{1,0:T(8,128)(2,1)S(1)} %collective-permute-done.22.refs_0_, bf16[160,2048]{1,0:T(8,128)(2,1)} %copy-done.16, bf16[160,2048]{1,0:T(8,128)(2,1)} %copy-done.12, bf16[160,2048]{1,0:T(8,128)(2,1)} %collective-permute-done.21.refs_3_, bf16[160,2048]{1,0:T(8,128)(2,1)} %copy-done, ...), custom_call_target="tpu_custom_call" | custom-call | flops 17000000 | bytes 1 | tf_op jit(solution)/shard_map/weight_grad/pallas_call | solution.py:486
  353.7 19.9 %ffn_out.1 = (bf16[160,2048]{1,0:T(8,128)(2,1)S(1)}, bf16[160,2048]{1,0:T(8,128)(2,1)}, bf16[160,2048]{1,0:T(8,128)(2,1)}, bf16[160,2048]{1,0:T(8,128)(2,1)}, bf...) custom-call(bf16[320,2048]{1,0:T(8,128)(2,1)} %get-tuple-element.182.refs_0_, ...), custom_call_target="tpu_custom_call" | custom-call | flops 18000000 | bytes 1 | tf_op jit(solution)/shard_map/ffn_out/pallas_call | solution.py:450
  373.7 7.0 %middle_back.1 = (f32[320,2048]{1,0:T(8,128)}, bf16[160,2048]{1,0:T(8,128)(2,1)S(1)}, bf16[160,2048]{1,0:T(8,128)(2,1)}, f32[4,2048]{1,0:T(4,128)S(1)}) custom-call(f32[320,2048]{1,0:T(8,128)} %get-tuple-element.195.refs_0_, bf16[320,2048]{1,0:T(8,128)(2,1)} %collective-permute-done.26.refs_1_, bf16[320,2048]{1,0:T(8,128)(2,1)} %collective-permute-done.27.refs_2_, ...), custom_call_target="tpu_custom_call" | custom-call | flops 5000000 | bytes 1 | tf_op jit(solution)/shard_map/middle_back/pallas_call | solution.py:642
  380.7 1.5 collective-permute-start.31
  385.0 15.4 %attn_backward.3 = (bf16[384,1536]{1,0:T(8,128)(2,1)}, f32[1,1536]{1,0:T(1,128)S(1)}, f32[384,2048]{1,0:T(8,128)}) custom-call(bf16[160,2048]{1,0:T(8,128)(2,1)} %copy-done.2, bf16[160,2048]{1,0:T(8,128)(2,1)} %get-tuple-element.201.refs_1_.refs_13_, bf16[384,1536]{1,0:T(8,128)(2,1)} %get-tuple-element.202.refs_2_, ...), custom_call_target="tpu_custom_call" | custom-call | flops 12000000 | bytes 1 | tf_op jit(solution)/shard_map/attn_backward/pallas_call | solution.py:299
  400.4 8.1 %collective-permute-done.32.refs_3_.refs_17_ = bf16[160,2048]{1,0:T(8,128)(2,1)} collective-permute-done((bf16[160,2048]{1,0:T(8,128)(2,1)}, bf16[160,2048]{1,0:T(8,128)(2,1)}, u32[]{:S(2)}, u32[]{:S(2)}) %collective-permute-start.32) | collective-permute-done | bytes 655392 | tf_op jit(solution)/shard_map/ppermute | solution.py:710
  408.5 2.3 collective-permute-done.30.refs_1_.refs_15_
  411.9 1.9 collective-permute-start.37
  415.1 23.8 %attn_backward.4 = (bf16[384,1536]{1,0:T(8,128)(2,1)}, f32[1,1536]{1,0:T(1,128)S(1)}, bf16[384,2048]{1,0:T(8,128)(2,1)}, bf16[384,1536]{1,0:T(8,128)(2,1)}, f32[...) custom-call(bf16[160,2048]{1,0:T(8,128)(2,1)} %collective-permute-done.29.refs_0_.refs_14_, ...), custom_call_target="tpu_custom_call" | custom-call | flops 24000000 | bytes 1 | tf_op jit(solution)/shard_map/attn_backward/pallas_call | solution.py:299
  441.2 14.5 %attn_backward.5 = (bf16[384,1536]{1,0:T(8,128)(2,1)}, f32[1,1536]{1,0:T(1,128)S(1)}, bf16[384,2048]{1,0:T(8,128)(2,1)}) custom-call(bf16[160,2048]{1,0:T(8,128)(2,1)} %copy-done.14, bf16[160,2048]{1,0:T(8,128)(2,1)} %copy-done.15, bf16[384,1536]{1,0:T(8,128)(2,1)} %get-tuple-element.220.refs_2_, f32[320,128]{1,0:T(8,128)S(1)} %get-tuple-element.146.refs_3_, ...), custom_call_target="tpu_custom_call" | custom-call | flops 12000000 | bytes 1 | tf_op jit(solution)/shard_map/attn_backward/pallas_call | solution.py:299
  455.7 2.4 collective-permute-start.39
  459.3 21.5 %attn_weight_grad.1 = bf16[2048,2048]{1,0:T(8,128)(2,1)} custom-call(bf16[384,2048]{1,0:T(8,128)(2,1)} %get-tuple-element.222.refs_0_, bf16[384,2048]{1,0:T(8,128)(2,1)} %get-tuple-element.223.refs_1_, bf16[384,2048]{1,0:T(8,128)(2,1)} %get-tuple-element.224.refs_2_, bf16[384,2048]{1,0:T(8,128)(2,1)} %get-tuple-element.225.refs_3_, ...), custom_call_target="tpu_custom_call" | custom-call | flops 21000000 | bytes 1 | tf_op jit(solution)/shard_map/attn_weight_grad/pallas_call | solution.py:527
  480.8 34.4 %collective-permute-done.40 = bf16[160,2048]{1,0:T(8,128)(2,1)S(1)} collective-permute-done((bf16[160,2048]{1,0:T(8,128)(2,1)}, bf16[160,2048]{1,0:T(8,128)(2,1)S(1)}, u32[]{:S(2)}, u32[]{:S(2)}) %collective-permute-start.40) | collective-permute-done | bytes 655392 | tf_op jit(solution)/shard_map/ppermute | solution.py:710
  515.3 9.0 %first_back.1 = (f32[320,2048]{1,0:T(8,128)}, bf16[64,2048]{1,0:T(8,128)(2,1)S(1)}, f32[2,2048]{1,0:T(2,128)S(1)}) custom-call(f32[384,2048]{1,0:T(8,128)} %get-tuple-element.236.refs_0_, bf16[384,2048]{1,0:T(8,128)(2,1)} %collective-permute-done.33.refs_1_, bf16[384,2048]{1,0:T(8,128)(2,1)} %collective-permute-done.34.refs_2_, ...), custom_call_target="tpu_custom_call" | custom-call | flops 499999997952 | bytes 1 | tf_op jit(solution)/shard_map/first_back/pallas_call | solution.py:691
  526.0 3.0 all-to-all-start.2
  529.1 1.4 collective-permute-start.44
  530.5 7.5 %all-to-all-done.2 = f32[32,1,768]{2,1,0:T(1,128)S(1)} async-done(((f32[32,1,768]{2,1,0:T(1,128)}), f32[32,1,768]{2,1,0:T(1,128)S(1)}, u32[]{:S(2)}, u32[]{:S(2)}) %all-to-all-start.2) | async-done | bytes 98336 | tf_op jit(solution)/shard_map/all_to_all | solution.py:768
  538.8 3.5 all-to-all-start.4
  542.6 2.0 collective-permute-start.42
  544.8 1.5 collective-permute-start.43
  546.3 1.6 convert_element_type.158
  549.7 21.5 %collective-permute-done.42 = bf16[160,2048]{1,0:T(8,128)(2,1)S(1)} collective-permute-done((bf16[160,2048]{1,0:T(8,128)(2,1)S(1)}, bf16[160,2048]{1,0:T(8,128)(2,1)S(1)}, u32[]{:S(2)}, u32[]{:S(2)}) %collective-permute-start.42) | collective-permute-done | bytes 655392 | tf_op jit(solution)/shard_map/ppermute | solution.py:710
  571.8 1.5 copy-done.6
  573.3 1.6 fusion.1
  574.9 2.1 slice.192
  577.0 3.6 all-to-all-start.3
  580.9 1.5 copy.86
  584.2 7.7 %all-to-all-done.3 = bf16[4,64,1536]{2,1,0:T(8,128)(2,1)S(1)} async-done(((bf16[4,64,1536]{2,1,0:T(8,128)(2,1)}), bf16[4,64,1536]{2,1,0:T(8,128)(2,1)S(1)}, u32[]{:S(2)}, u32[]{:S(2)}) %all-to-all-start.3) | async-done | bytes 786464 | tf_op jit(solution)/shard_map/all_to_all | solution.py:752
  (286 shorter events, 58.1 us)
Async XLA Ops:
  12.0 16.0 %all-to-all-start = ((bf16[4,64,1536]{2,1,0:T(8,128)(2,1)}), bf16[4,64,1536]{2,1,0:T(8,128)(2,1)S(1)}, u32[]{:S(2)}, u32[]{:S(2)}) async-start(bf16[4,64,1536]{2,1,0:T(8,128)(2,1)} %copy.72), calls=%async_computation | async-start | bytes 1572864 | tf_op jit(solution)/shard_map/all_to_all | solution.py:752
  17.1 100.4 %all-gather.4.cloned.1.call-start = ((), (), s32[]{:S(2)}) async-start(), calls=%async_computation.8 | async-start | bytes 9437184 | tf_op jit(solution)/shard_map/all_gather | solution.py:772
  29.1 188.9 %all-gather.6.cloned.1.call-start = ((), (), s32[]{:S(2)}) async-start(), calls=%async_computation.9 | async-start | bytes 9437184 | tf_op jit(solution)/shard_map/all_gather | solution.py:772
  29.4 3.7 collective-permute-start.1
  30.9 5.9 collective-permute-start
  33.1 3.7 collective-permute-start.2
  36.8 22.6 %copy-start.9 = (bf16[384,2048]{1,0:T(8,128)(2,1)}, bf16[384,2048]{1,0:T(8,128)(2,1)S(1)}, u32[]{:S(2)}) copy-start(bf16[384,2048]{1,0:T(8,128)(2,1)S(1)} %constant_dynamic-update-slice_fusion.refs_0_.refs_4_) | copy-start | bytes 4718596
  56.2 237.2 %all-gather.8.cloned.1.call-start = ((), (), s32[]{:S(2)}) async-start(), calls=%async_computation.10 | async-start | bytes 9437184 | tf_op jit(solution)/shard_map/all_gather | solution.py:772
  56.9 327.9 %reduce-scatter.4.cloned.1.call-start = ((), (), s32[]{:S(2)}) async-start(), calls=%async_computation.11 | async-start | bytes 9437184 | tf_op jit(solution)/shard_map/reduce_scatter | solution.py:776
  57.2 1.2 collective-permute-start.7
  58.4 36.5 %collective-permute-start.4 = (bf16[384,2048]{1,0:T(8,128)(2,1)S(1)}, bf16[384,2048]{1,0:T(8,128)(2,1)S(1)}, u32[]{:S(2)}, u32[]{:S(2)}) collective-permute-start(bf16[384,2048]{1,0:T(8,128)(2,1)S(1)} %constant_dynamic-update-slice_fusion.refs_0_.refs_4_), channel_id=1, source_target_pairs={{0,16},{8,24},{16,0},{24,8},{1,17},{9,25},{17,1},{25,9},{2,18},{10... | collective-permute-start | bytes 4718600 | tf_op jit(solution)/shard_map/ppermute | solution.py:710
  59.4 36.3 %collective-permute-start.3 = (bf16[384,2048]{1,0:T(8,128)(2,1)S(1)}, bf16[384,2048]{1,0:T(8,128)(2,1)}, u32[]{:S(2)}, u32[]{:S(2)}) collective-permute-start(bf16[384,2048]{1,0:T(8,128)(2,1)S(1)} %constant_dynamic-update-slice_fusion.refs_0_.refs_4_), channel_id=1, source_target_pairs={{0,8},{8,0},{16,24},{24,16},{1,9},{9,1},{17,25},{25,17},{2,10},{10... | collective-permute-start | bytes 4718600 | tf_op jit(solution)/shard_map/ppermute | solution.py:710
  60.0 5.9 collective-permute-start.8
  65.9 5.6 collective-permute-start.9
  97.9 19.6 %collective-permute-start.6 = (bf16[192,2048]{1,0:T(8,128)(2,1)S(1)}, bf16[192,2048]{1,0:T(8,128)(2,1)}, u32[]{:S(2)}, u32[]{:S(2)}) collective-permute-start(bf16[192,2048]{1,0:T(8,128)(2,1)S(1)} %slice.134), channel_id=1, source_target_pairs={{0,8},{8,0},{16,24},{24,16},{1,9},{9,1},{17,25},{25,17},{2,10},{10... | collective-permute-start | bytes 2359304 | tf_op jit(solution)/shard_map/ppermute | solution.py:710
  98.7 18.8 %collective-permute-start.5 = (bf16[192,2048]{1,0:T(8,128)(2,1)}, bf16[192,2048]{1,0:T(8,128)(2,1)S(1)}, u32[]{:S(2)}, u32[]{:S(2)}) collective-permute-start(bf16[192,2048]{1,0:T(8,128)(2,1)} %slice.133), channel_id=1, source_target_pairs={{0,16},{8,24},{16,0},{24,8},{1,17},{9,25},{17,1},{25,9},{2,18},{10... | collective-permute-start | bytes 2359304 | tf_op jit(solution)/shard_map/ppermute | solution.py:710
  134.6 30.1 %collective-permute-start.11 = (bf16[160,2048]{1,0:T(8,128)(2,1)}, bf16[160,2048]{1,0:T(8,128)(2,1)S(1)}, u32[]{:S(2)}, u32[]{:S(2)}) collective-permute-start(bf16[160,2048]{1,0:T(8,128)(2,1)} %get-tuple-element.150), channel_id=1, source_target_pairs={{0,16},{8,24},{16,0},{24,8},{1,17},{9,25},{17,1},{25,9},{2,18},{10... | collective-permute-start | bytes 1966088 | tf_op jit(solution)/shard_map/ppermute | solution.py:710
  134.8 45.7 %collective-permute-start.17 = (bf16[320,2048]{1,0:T(8,128)(2,1)S(1)}, bf16[320,2048]{1,0:T(8,128)(2,1)S(1)}, u32[]{:S(2)}, u32[]{:S(2)}) collective-permute-start(bf16[320,2048]{1,0:T(8,128)(2,1)S(1)} %copy-done.5), channel_id=1, source_target_pairs={{0,16},{8,24},{16,0},{24,8},{1,17},{9,25},{17,1},{25,9},{2,18},{10... | collective-permute-start | bytes 3932168 | tf_op jit(solution)/shard_map/ppermute | solution.py:710
  136.6 30.9 %collective-permute-start.13 = (bf16[160,2048]{1,0:T(8,128)(2,1)}, bf16[160,2048]{1,0:T(8,128)(2,1)S(1)}, u32[]{:S(2)}, u32[]{:S(2)}) collective-permute-start(bf16[160,2048]{1,0:T(8,128)(2,1)} %get-tuple-element.152), channel_id=1, source_target_pairs={{0,8},{8,0},{16,24},{24,16},{1,9},{9,1},{17,25},{25,17},{2,10},{10... | collective-permute-start | bytes 1966088 | tf_op jit(solution)/shard_map/ppermute | solution.py:710
  137.3 45.4 %collective-permute-start.16 = (bf16[320,2048]{1,0:T(8,128)(2,1)S(1)}, bf16[320,2048]{1,0:T(8,128)(2,1)}, u32[]{:S(2)}, u32[]{:S(2)}) collective-permute-start(bf16[320,2048]{1,0:T(8,128)(2,1)S(1)} %copy-done.5), channel_id=1, source_target_pairs={{0,8},{8,0},{16,24},{24,16},{1,9},{9,1},{17,25},{25,17},{2,10},{10... | collective-permute-start | bytes 3932168 | tf_op jit(solution)/shard_map/ppermute | solution.py:710
  163.9 33.3 %collective-permute-start.10 = (bf16[160,2048]{1,0:T(8,128)(2,1)}, bf16[160,2048]{1,0:T(8,128)(2,1)S(1)}, u32[]{:S(2)}, u32[]{:S(2)}) collective-permute-start(bf16[160,2048]{1,0:T(8,128)(2,1)} %get-tuple-element.148), channel_id=1, source_target_pairs={{0,8},{8,0},{16,24},{24,16},{1,9},{9,1},{17,25},{25,17},{2,10},{10... | collective-permute-start | bytes 1966088 | tf_op jit(solution)/shard_map/ppermute | solution.py:710
  164.6 32.6 %collective-permute-start.15 = (bf16[160,2048]{1,0:T(8,128)(2,1)}, bf16[160,2048]{1,0:T(8,128)(2,1)}, u32[]{:S(2)}, u32[]{:S(2)}) collective-permute-start(bf16[160,2048]{1,0:T(8,128)(2,1)} %get-tuple-element.153), channel_id=1, source_target_pairs={{0,16},{8,24},{16,0},{24,8},{1,17},{9,25},{17,1},{25,9},{2,18},{10... | collective-permute-start | bytes 1966088 | tf_op jit(solution)/shard_map/ppermute | solution.py:710
  167.4 39.2 %collective-permute-start.12 = (bf16[160,2048]{1,0:T(8,128)(2,1)}, bf16[160,2048]{1,0:T(8,128)(2,1)}, u32[]{:S(2)}, u32[]{:S(2)}) collective-permute-start(bf16[160,2048]{1,0:T(8,128)(2,1)} %add_convert_fusion.3), channel_id=1, source_target_pairs={{0,8},{8,0},{16,24},{24,16},{1,9},{9,1},{17,25},{25,17},{2,10},{10... | collective-permute-start | bytes 1966088 | tf_op jit(solution)/shard_map/ppermute | solution.py:710
  180.5 26.1 %collective-permute-start.14 = (bf16[160,2048]{1,0:T(8,128)(2,1)}, bf16[160,2048]{1,0:T(8,128)(2,1)}, u32[]{:S(2)}, u32[]{:S(2)}) collective-permute-start(bf16[160,2048]{1,0:T(8,128)(2,1)} %add_convert_fusion.2), channel_id=1, source_target_pairs={{0,16},{8,24},{16,0},{24,8},{1,17},{9,25},{17,1},{25,9},{2,18},{10... | collective-permute-start | bytes 1966088 | tf_op jit(solution)/shard_map/ppermute | solution.py:710
  213.8 17.7 %collective-permute-start.20 = (bf16[160,2048]{1,0:T(8,128)(2,1)S(1)}, bf16[160,2048]{1,0:T(8,128)(2,1)S(1)}, u32[]{:S(2)}, u32[]{:S(2)}) collective-permute-start(bf16[160,2048]{1,0:T(8,128)(2,1)S(1)} %get-tuple-element.160.refs_0_.refs_6_), channel_id=1, source_target_pairs={{0,16},{8,24},{16,0},{24,8},{1,17},{9,25},{17,1},{25,9},{2,18},{10... | collective-permute-start | bytes 1966088 | tf_op jit(solution)/shard_map/ppermute | solution.py:710
  214.2 17.7 %collective-permute-start.18 = (bf16[160,2048]{1,0:T(8,128)(2,1)S(1)}, bf16[160,2048]{1,0:T(8,128)(2,1)S(1)}, u32[]{:S(2)}, u32[]{:S(2)}) collective-permute-start(bf16[160,2048]{1,0:T(8,128)(2,1)S(1)} %get-tuple-element.160.refs_0_.refs_6_), channel_id=1, source_target_pairs={{0,8},{8,0},{16,24},{24,16},{1,9},{9,1},{17,25},{25,17},{2,10},{10... | collective-permute-start | bytes 1966088 | tf_op jit(solution)/shard_map/ppermute | solution.py:710
  215.3 27.5 %collective-permute-start.21 = (bf16[160,2048]{1,0:T(8,128)(2,1)}, bf16[160,2048]{1,0:T(8,128)(2,1)}, u32[]{:S(2)}, u32[]{:S(2)}) collective-permute-start(bf16[160,2048]{1,0:T(8,128)(2,1)} %get-tuple-element.161.refs_1_.refs_7_), channel_id=1, source_target_pairs={{0,16},{8,24},{16,0},{24,8},{1,17},{9,25},{17,1},{25,9},{2,18},{10... | collective-permute-start | bytes 1966088 | tf_op jit(solution)/shard_map/ppermute | solution.py:710
  216.7 26.1 %collective-permute-start.19 = (bf16[160,2048]{1,0:T(8,128)(2,1)}, bf16[160,2048]{1,0:T(8,128)(2,1)}, u32[]{:S(2)}, u32[]{:S(2)}) collective-permute-start(bf16[160,2048]{1,0:T(8,128)(2,1)} %get-tuple-element.161.refs_1_.refs_7_), channel_id=1, source_target_pairs={{0,8},{8,0},{16,24},{24,16},{1,9},{9,1},{17,25},{25,17},{2,10},{10... | collective-permute-start | bytes 1966088 | tf_op jit(solution)/shard_map/ppermute | solution.py:710
  231.8 28.3 %copy-start = (bf16[160,2048]{1,0:T(8,128)(2,1)}, bf16[160,2048]{1,0:T(8,128)(2,1)S(1)}, u32[]{:S(2)}) copy-start(bf16[160,2048]{1,0:T(8,128)(2,1)S(1)} %collective-permute-done.18.refs_0_.refs_4_) | copy-start | bytes 1966084
  242.8 20.7 %collective-permute-start.22 = (bf16[160,2048]{1,0:T(8,128)(2,1)S(1)}, bf16[160,2048]{1,0:T(8,128)(2,1)S(1)}, u32[]{:S(2)}, u32[]{:S(2)}) collective-permute-start(bf16[160,2048]{1,0:T(8,128)(2,1)S(1)} %collective-permute-done.18.refs_0_.refs_4_), channel_id=1, source_target_pairs={{0,16},{8,24},{16,0},{24,8},{1,17},{9,25},{17,1},{25,9},{2,18},{10... | collective-permute-start | bytes 1966088 | tf_op jit(solution)/shard_map/ppermute | solution.py:710
  244.3 19.2 %collective-permute-start.23 = (bf16[160,2048]{1,0:T(8,128)(2,1)}, bf16[160,2048]{1,0:T(8,128)(2,1)S(1)}, u32[]{:S(2)}, u32[]{:S(2)}) collective-permute-start(bf16[160,2048]{1,0:T(8,128)(2,1)} %collective-permute-done.21.refs_3_), channel_id=1, source_target_pairs={{0,8},{8,0},{16,24},{24,16},{1,9},{9,1},{17,25},{25,17},{2,10},{10... | collective-permute-start | bytes 1966088 | tf_op jit(solution)/shard_map/ppermute | solution.py:710
  261.8 13.1 %collective-permute-start.25 = (bf16[160,2048]{1,0:T(8,128)(2,1)S(1)}, bf16[160,2048]{1,0:T(8,128)(2,1)S(1)}, u32[]{:S(2)}, u32[]{:S(2)}) collective-permute-start(bf16[160,2048]{1,0:T(8,128)(2,1)S(1)} %slice.147), channel_id=1, source_target_pairs={{0,8},{8,0},{16,24},{24,16},{1,9},{9,1},{17,25},{25,17},{2,10},{10... | collective-permute-start | bytes 1966088 | tf_op jit(solution)/shard_map/ppermute | solution.py:710
  262.9 11.9 %collective-permute-start.24 = (bf16[160,2048]{1,0:T(8,128)(2,1)S(1)}, bf16[160,2048]{1,0:T(8,128)(2,1)S(1)}, u32[]{:S(2)}, u32[]{:S(2)}) collective-permute-start(bf16[160,2048]{1,0:T(8,128)(2,1)S(1)} %slice.146), channel_id=1, source_target_pairs={{0,16},{8,24},{16,0},{24,8},{1,17},{9,25},{17,1},{25,9},{2,18},{10... | collective-permute-start | bytes 1966088 | tf_op jit(solution)/shard_map/ppermute | solution.py:710
  293.4 187.4 %reduce-scatter.6.cloned.1.call-start = ((), (), s32[]{:S(2)}) async-start(), calls=%async_computation.12 | async-start | bytes 9437184 | tf_op jit(solution)/shard_map/reduce_scatter | solution.py:776
  319.2 54.4 %collective-permute-start.26 = (bf16[320,2048]{1,0:T(8,128)(2,1)}, bf16[320,2048]{1,0:T(8,128)(2,1)}, u32[]{:S(2)}, u32[]{:S(2)}) collective-permute-start(bf16[320,2048]{1,0:T(8,128)(2,1)} %get-tuple-element.190), channel_id=1, source_target_pairs={{0,8},{8,0},{16,24},{24,16},{1,9},{9,1},{17,25},{25,17},{2,10},{10... | collective-permute-start | bytes 3932168 | tf_op jit(solution)/shard_map/ppermute | solution.py:710
  320.0 53.5 %collective-permute-start.27 = (bf16[320,2048]{1,0:T(8,128)(2,1)}, bf16[320,2048]{1,0:T(8,128)(2,1)}, u32[]{:S(2)}, u32[]{:S(2)}) collective-permute-start(bf16[320,2048]{1,0:T(8,128)(2,1)} %get-tuple-element.191), channel_id=1, source_target_pairs={{0,16},{8,24},{16,0},{24,8},{1,17},{9,25},{17,1},{25,9},{2,18},{10... | collective-permute-start | bytes 3932168 | tf_op jit(solution)/shard_map/ppermute | solution.py:710
  321.6 52.0 %collective-permute-start.28 = (bf16[320,2048]{1,0:T(8,128)(2,1)}, bf16[320,2048]{1,0:T(8,128)(2,1)}, u32[]{:S(2)}, u32[]{:S(2)}) collective-permute-start(bf16[320,2048]{1,0:T(8,128)(2,1)} %get-tuple-element.192), channel_id=1, source_target_pairs={{0,24},{8,16},{16,8},{24,0},{1,25},{9,17},{17,9},{25,1},{2,26},{10... | collective-permute-start | bytes 3932168 | tf_op jit(solution)/shard_map/ppermute | solution.py:710
  373.6 201.3 %reduce-scatter.8.cloned.1.call-start = ((), (), s32[]{:S(2)}) async-start(), calls=%async_computation.13 | async-start | bytes 9437184 | tf_op jit(solution)/shard_map/reduce_scatter | solution.py:776
  380.7 19.7 %collective-permute-start.31 = (bf16[160,2048]{1,0:T(8,128)(2,1)S(1)}, bf16[160,2048]{1,0:T(8,128)(2,1)}, u32[]{:S(2)}, u32[]{:S(2)}) collective-permute-start(bf16[160,2048]{1,0:T(8,128)(2,1)S(1)} %get-tuple-element.200.refs_0_.refs_12_), channel_id=1, source_target_pairs={{0,16},{8,24},{16,0},{24,8},{1,17},{9,25},{17,1},{25,9},{2,18},{10... | collective-permute-start | bytes 1966088 | tf_op jit(solution)/shard_map/ppermute | solution.py:710
  382.2 18.2 %collective-permute-start.29 = (bf16[160,2048]{1,0:T(8,128)(2,1)S(1)}, bf16[160,2048]{1,0:T(8,128)(2,1)}, u32[]{:S(2)}, u32[]{:S(2)}) collective-permute-start(bf16[160,2048]{1,0:T(8,128)(2,1)S(1)} %get-tuple-element.200.refs_0_.refs_12_), channel_id=1, source_target_pairs={{0,8},{8,0},{16,24},{24,16},{1,9},{9,1},{17,25},{25,17},{2,10},{10... | collective-permute-start | bytes 1966088 | tf_op jit(solution)/shard_map/ppermute | solution.py:710
  383.2 25.3 %collective-permute-start.32 = (bf16[160,2048]{1,0:T(8,128)(2,1)}, bf16[160,2048]{1,0:T(8,128)(2,1)}, u32[]{:S(2)}, u32[]{:S(2)}) collective-permute-start(bf16[160,2048]{1,0:T(8,128)(2,1)} %get-tuple-element.201.refs_1_.refs_13_), channel_id=1, source_target_pairs={{0,16},{8,24},{16,0},{24,8},{1,17},{9,25},{17,1},{25,9},{2,18},{10... | collective-permute-start | bytes 1966088 | tf_op jit(solution)/shard_map/ppermute | solution.py:710
  383.6 27.2 %collective-permute-start.30 = (bf16[160,2048]{1,0:T(8,128)(2,1)}, bf16[160,2048]{1,0:T(8,128)(2,1)}, u32[]{:S(2)}, u32[]{:S(2)}) collective-permute-start(bf16[160,2048]{1,0:T(8,128)(2,1)} %get-tuple-element.201.refs_1_.refs_13_), channel_id=1, source_target_pairs={{0,8},{8,0},{16,24},{24,16},{1,9},{9,1},{17,25},{25,17},{2,10},{10... | collective-permute-start | bytes 1966088 | tf_op jit(solution)/shard_map/ppermute | solution.py:710
  384.9 27.0 %copy-start.50 = (bf16[160,2048]{1,0:T(8,128)(2,1)S(1)}, bf16[160,2048]{1,0:T(8,128)(2,1)}, u32[]{:S(2)}) copy-start(bf16[160,2048]{1,0:T(8,128)(2,1)} %get-tuple-element.218) | copy-start | bytes 1966084
  384.9 30.0 %copy-start.38 = (f32[384]{0:T(512)S(1)}, f32[384]{0:T(512)}, u32[]{:S(2)}) copy-start(f32[384]{0:T(512)} %get-tuple-element.364) | copy-start | bytes 4612
  385.0 30.1 %copy-start.37 = (f32[384]{0:T(512)S(1)}, f32[384]{0:T(512)}, u32[]{:S(2)}) copy-start(f32[384]{0:T(512)} %get-tuple-element.365) | copy-start | bytes 4612
  410.8 29.2 %collective-permute-start.35 = (bf16[160,2048]{1,0:T(8,128)(2,1)}, bf16[160,2048]{1,0:T(8,128)(2,1)S(1)}, u32[]{:S(2)}, u32[]{:S(2)}) collective-permute-start(bf16[160,2048]{1,0:T(8,128)(2,1)} %collective-permute-done.29.refs_0_.refs_14_), channel_id=1, source_target_pairs={{0,16},{8,24},{16,0},{24,8},{1,17},{9,25},{17,1},{25,9},{2,18},{10... | collective-permute-start | bytes 1966088 | tf_op jit(solution)/shard_map/ppermute | solution.py:710
  410.9 29.3 %collective-permute-start.36 = (bf16[160,2048]{1,0:T(8,128)(2,1)S(1)}, bf16[160,2048]{1,0:T(8,128)(2,1)S(1)}, u32[]{:S(2)}, u32[]{:S(2)}) collective-permute-start(bf16[160,2048]{1,0:T(8,128)(2,1)S(1)} %get-tuple-element.217), channel_id=1, source_target_pairs={{0,8},{8,0},{16,24},{24,16},{1,9},{9,1},{17,25},{25,17},{2,10},{10... | collective-permute-start | bytes 1966088 | tf_op jit(solution)/shard_map/ppermute | solution.py:710
  411.9 28.3 %collective-permute-start.37 = (bf16[160,2048]{1,0:T(8,128)(2,1)S(1)}, bf16[160,2048]{1,0:T(8,128)(2,1)S(1)}, u32[]{:S(2)}, u32[]{:S(2)}) collective-permute-start(bf16[160,2048]{1,0:T(8,128)(2,1)S(1)} %copy-done.50), channel_id=1, source_target_pairs={{0,16},{8,24},{16,0},{24,8},{1,17},{9,25},{17,1},{25,9},{2,18},{10... | collective-permute-start | bytes 1966088 | tf_op jit(solution)/shard_map/ppermute | solution.py:710
  413.8 26.4 %collective-permute-start.38 = (bf16[160,2048]{1,0:T(8,128)(2,1)}, bf16[160,2048]{1,0:T(8,128)(2,1)S(1)}, u32[]{:S(2)}, u32[]{:S(2)}) collective-permute-start(bf16[160,2048]{1,0:T(8,128)(2,1)} %collective-permute-done.32.refs_3_.refs_17_), channel_id=1, source_target_pairs={{0,8},{8,0},{16,24},{24,16},{1,9},{9,1},{17,25},{25,17},{2,10},{10... | collective-permute-start | bytes 1966088 | tf_op jit(solution)/shard_map/ppermute | solution.py:710
  439.0 76.2 %collective-permute-start.33 = (bf16[384,2048]{1,0:T(8,128)(2,1)}, bf16[384,2048]{1,0:T(8,128)(2,1)}, u32[]{:S(2)}, u32[]{:S(2)}) collective-permute-start(bf16[384,2048]{1,0:T(8,128)(2,1)} %get-tuple-element.214), channel_id=1, source_target_pairs={{0,8},{8,0},{16,24},{24,16},{1,9},{9,1},{17,25},{25,17},{2,10},{10... | collective-permute-start | bytes 4718600 | tf_op jit(solution)/shard_map/ppermute | solution.py:710
  440.0 75.2 %collective-permute-start.34 = (bf16[384,2048]{1,0:T(8,128)(2,1)}, bf16[384,2048]{1,0:T(8,128)(2,1)}, u32[]{:S(2)}, u32[]{:S(2)}) collective-permute-start(bf16[384,2048]{1,0:T(8,128)(2,1)} %get-tuple-element.215), channel_id=1, source_target_pairs={{0,16},{8,24},{16,0},{24,8},{1,17},{9,25},{17,1},{25,9},{2,18},{10... | collective-permute-start | bytes 4718600 | tf_op jit(solution)/shard_map/ppermute | solution.py:710
  455.7 59.5 %collective-permute-start.39 = (bf16[384,2048]{1,0:T(8,128)(2,1)}, bf16[384,2048]{1,0:T(8,128)(2,1)}, u32[]{:S(2)}, u32[]{:S(2)}) collective-permute-start(bf16[384,2048]{1,0:T(8,128)(2,1)} %get-tuple-element.221), channel_id=1, source_target_pairs={{0,24},{8,16},{16,8},{24,0},{1,25},{9,17},{17,9},{25,1},{2,26},{10... | collective-permute-start | bytes 4718600 | tf_op jit(solution)/shard_map/ppermute | solution.py:710
  458.1 57.1 %collective-permute-start.40 = (bf16[160,2048]{1,0:T(8,128)(2,1)}, bf16[160,2048]{1,0:T(8,128)(2,1)S(1)}, u32[]{:S(2)}, u32[]{:S(2)}) collective-permute-start(bf16[160,2048]{1,0:T(8,128)(2,1)} %get-tuple-element.234), channel_id=1, source_target_pairs={{0,8},{8,0},{16,24},{24,16},{1,9},{9,1},{17,25},{25,17},{2,10},{10... | collective-permute-start | bytes 1966088 | tf_op jit(solution)/shard_map/ppermute | solution.py:710
  459.0 56.2 %collective-permute-start.41 = (bf16[160,2048]{1,0:T(8,128)(2,1)S(1)}, bf16[160,2048]{1,0:T(8,128)(2,1)S(1)}, u32[]{:S(2)}, u32[]{:S(2)}) collective-permute-start(bf16[160,2048]{1,0:T(8,128)(2,1)S(1)} %copy-done.49), channel_id=1, source_target_pairs={{0,16},{8,24},{16,0},{24,8},{1,17},{9,25},{17,1},{25,9},{2,18},{10... | collective-permute-start | bytes 1966088 | tf_op jit(solution)/shard_map/ppermute | solution.py:710
  526.0 12.1 %all-to-all-start.2 = ((f32[32,1,768]{2,1,0:T(1,128)}), f32[32,1,768]{2,1,0:T(1,128)S(1)}, u32[]{:S(2)}, u32[]{:S(2)}) async-start(f32[32,1,768]{2,1,0:T(1,128)} %all_to_all.20), calls=%async_computation.3 | async-start | bytes 196608 | tf_op jit(solution)/shard_map/all_to_all | solution.py:768
  529.1 19.4 %collective-permute-start.44 = (bf16[50,2048]{1,0:T(8,128)(2,1)S(1)}, bf16[50,2048]{1,0:T(8,128)(2,1)S(1)}, u32[]{:S(2)}, u32[]{:S(2)}) collective-permute-start(bf16[50,2048]{1,0:T(8,128)(2,1)S(1)} %slice.159), channel_id=1, source_target_pairs={{1,0},{2,1},{3,2},{4,3},{5,4},{6,5},{7,6},{8,7},{9,8},{10,9},{11,1... | collective-permute-start | bytes 614408 | tf_op jit(solution)/shard_map/ppermute | solution.py:999
  538.8 38.2 %all-to-all-start.4 = ((bf16[4,64,2048]{2,1,0:T(8,128)(2,1)}), bf16[4,64,2048]{2,1,0:T(8,128)(2,1)S(1)}, u32[]{:S(2)}, u32[]{:S(2)}) async-start(bf16[4,64,2048]{2,1,0:T(8,128)(2,1)} %reduce-scatter.6.cloned.1.call-done), calls=%async_computation.7 | async-start | bytes 2097152 | tf_op jit(solution)/shard_map/all_to_all | solution.py:752
  542.6 28.7 %collective-permute-start.42 = (bf16[160,2048]{1,0:T(8,128)(2,1)S(1)}, bf16[160,2048]{1,0:T(8,128)(2,1)S(1)}, u32[]{:S(2)}, u32[]{:S(2)}) collective-permute-start(bf16[160,2048]{1,0:T(8,128)(2,1)S(1)} %add_convert_fusion.1), channel_id=1, source_target_pairs={{0,16},{8,24},{16,0},{24,8},{1,17},{9,25},{17,1},{25,9},{2,18},{10... | collective-permute-start | bytes 1966088 | tf_op jit(solution)/shard_map/ppermute | solution.py:710
  544.8 26.7 %collective-permute-start.43 = (bf16[160,2048]{1,0:T(8,128)(2,1)S(1)}, bf16[160,2048]{1,0:T(8,128)(2,1)S(1)}, u32[]{:S(2)}, u32[]{:S(2)}) collective-permute-start(bf16[160,2048]{1,0:T(8,128)(2,1)S(1)} %add_convert_fusion), channel_id=1, source_target_pairs={{0,8},{8,0},{16,24},{24,16},{1,9},{9,1},{17,25},{25,17},{2,10},{10... | collective-permute-start | bytes 1966088 | tf_op jit(solution)/shard_map/ppermute | solution.py:710
  546.3 24.9 %copy-start.32 = (bf16[160,2048]{1,0:T(8,128)(2,1)S(1)}, bf16[160,2048]{1,0:T(8,128)(2,1)}, u32[]{:S(2)}) copy-start(bf16[160,2048]{1,0:T(8,128)(2,1)} %copy-done.31) | copy-start | bytes 1966084
  547.9 23.4 %copy-start.18 = (f32[160,2048]{1,0:T(8,128)S(1)}, f32[160,2048]{1,0:T(8,128)}, u32[]{:S(2)}) copy-start(f32[160,2048]{1,0:T(8,128)} %get-tuple-element.254) | copy-start | bytes 3932164
  549.7 21.8 %copy-start.17 = (f32[160,2048]{1,0:T(8,128)S(1)}, f32[160,2048]{1,0:T(8,128)}, u32[]{:S(2)}) copy-start(f32[160,2048]{1,0:T(8,128)} %get-tuple-element.256) | copy-start | bytes 3932164
  549.7 21.8 %copy-start.30 = (bf16[160,2048]{1,0:T(8,128)(2,1)S(1)}, bf16[160,2048]{1,0:T(8,128)(2,1)}, u32[]{:S(2)}) copy-start(bf16[160,2048]{1,0:T(8,128)(2,1)} %copy-done.29) | copy-start | bytes 1966084
  577.0 14.9 %all-to-all-start.3 = ((bf16[4,64,1536]{2,1,0:T(8,128)(2,1)}), bf16[4,64,1536]{2,1,0:T(8,128)(2,1)S(1)}, u32[]{:S(2)}, u32[]{:S(2)}) async-start(bf16[4,64,1536]{2,1,0:T(8,128)(2,1)} %slice.192), calls=%async_computation.6 | async-start | bytes 1572864 | tf_op jit(solution)/shard_map/all_to_all | solution.py:752
  (44 other events, 369.9 us)
Sparse Core Ops, SparseCore 0:
  29.2 83.5 all-gather.3
  114.4 80.4 all-gather.5
  196.5 80.5 all-gather.7
  293.5 89.1 reduce-scatter.3
  384.8 87.9 reduce-scatter.5
  480.9 93.9 reduce-scatter.7

commit v6 on v5

--- a/solution.py
+++ b/solution.py
@@ -703,6 +703,38 @@
     )(*parts, joined, middle_grad, gain)
 
 
+def beside_blocks(weights, members):
+    rows, width = weights[0].shape
+    cols = width // members
+    count = len(weights)
+
+    def kernel(*refs):
+        out, sems = refs[count:]
+        copies = []
+        for member in range(members):
+            for index in range(count):
+                copies.append(
+                    pltpu.make_async_copy(
+                        refs[index].at[:, pl.ds(member * cols, cols)],
+                        out.at[member, :, pl.ds(index * cols, cols)],
+                        sems.at[member * count + index],
+                    )
+                )
+        for copy in copies:
+            copy.start()
+        wait_all(copies)
+
+    return pl.pallas_call(
+        kernel,
+        out_shape=jax.ShapeDtypeStruct((members, rows, count * cols), BF16),
+        in_specs=[HBM] * count,
+        out_specs=HBM,
+        scratch_shapes=[pltpu.SemaphoreType.DMA((members * count,))],
+        name="beside_blocks",
+        **kernel_params(1),
+    )(*weights)
+
+
 def swap(value, rel):
     if rel == 0:
         return value
@@ -720,14 +752,18 @@
     return [[swap(half, rel) for half in halves] for rel in near]
 
 
-def spread_far(halves, near, *others):
+def spread_cut(near):
+    return [halves_of(near[0][0])[0], halves_of(near[-1][0])[1]]
+
+
+def spread_far(halves, near, *others, cut=None):
     members = lax.axis_size("fsdp")
-    near = lax.optimization_barrier((near, others))[0]
+    near, cut = lax.optimization_barrier((near, cut, others))[:2]
     pieces = [halves, *near]
     if members > 3:
         top, bottom = near[0][0], near[1][-1]
         if len(halves) == 1:
-            top, bottom = halves_of(top)[0], halves_of(bottom)[1]
+            top, bottom = cut or spread_cut(near)
         pieces.append([swap(top, 2), swap(bottom, 1)])
     return pieces + [[swap(half, rel) for half in halves] for rel in range(4, members)]
 
@@ -826,7 +862,7 @@
     prior = lax.ppermute(prior, BOTH, [(i, i + 1) for i in range(total - 1)])
     joined = jnp.concatenate([tokens, prior], 0)
 
-    qkv_blocks = jnp.concatenate([blocks_of(w_query), blocks_of(w_key), blocks_of(w_value)], 2)
+    qkv_blocks = beside_blocks([w_query, w_key, w_value], members)
     qkv_blocks = trade_blocks(qkv_blocks)
     up_blocks, packed = lax.optimization_barrier((blocks_of(w_up), packed, qkv_blocks, joined))[:2]
     up_blocks = trade_blocks(up_blocks)
@@ -865,7 +901,7 @@
 
 
     def part_type(rel):
-        return BF16 if rel else F32
+        return BF16
 
     attn = {}
     middle_parts = {}
@@ -891,8 +927,9 @@
         middle_parts[2] = [add_low(two[0], middle_over[0]), two[1]]
         middle_parts[1] = [one[0], add_low(one[1], middle_over[1])]
     middle_parts = {rel: [swap(half, rel) for half in part] for rel, part in middle_parts.items()}
+    cot_cut = spread_cut(cot_near)
     middle, *second_own = middle_norm(
-        tokens, list(middle_parts.values()), out_off, gain_two, bias_two
+        after(tokens, cot_cut), list(middle_parts.values()), out_off, gain_two, bias_two
     )
     def ordered(values):
         return [values[rel] for rel in own_last]
@@ -912,7 +949,7 @@
             hidden[rel], slope[rel] = one, other
         previous = hiddens[:1]
         if low_rel == 1:
-            group_cot = spread_far(cot_rows, cot_near, previous)
+            group_cot = spread_far(cot_rows, cot_near, previous, cut=cot_cut)
     down_partial = weight_grad(ordered(hidden), flat_list(ordered(group_cot)))
     down_share = scatter_dp(down_partial, 0)
     pre, up_sums, second_parts = [], [], {}

time: 607 us -> 602 us (level)
  transfers between devices with their start and end apart: 55 -> 55, of which waited for: 21 -> 22; matrix products, arithmetic and copies ran while one was open for 5% -> 6% of each run, Pallas kernels for 47% -> 47%
where the time goes in v6:
time: 602 us; the launch traced here: 597 us
  Pallas kernels  282 us (47%)
  waiting for transfers between devices  170 us (28%)
  starting transfers between devices  61.6 us (10%)
  local copies, waits for them, and re-layouts  34.8 us (6%)
  blocking collectives  18.7 us (3%)
  between operations  15.4 us (3%)
  other arithmetic  14.6 us (2%)
    ppermute x38, waiting for transfers between devices, swap(): return lax.ppermute(value, 'fsdp', [(i, i ^ rel) for i in range(count)])  134 us
    pallas_call x3, Pallas kernels, attn_forward(): pl.pallas_call(kernel, out_shape=shapes, in_specs=[HBM] * given + [VMEM]...  54.8 us
    pallas_call x3, Pallas kernels, attn_backward(): pl.pallas_call(kernel, out_shape=shapes, in_specs=[HBM] * given + [VMEM]...  52.9 us
    pallas_call x2, Pallas kernels, ffn_back(): pl.pallas_call(kernel, out_shape=(shape_of(rows, wide), shape_of(1, wide,...  38.4 us
    ppermute x38, starting transfers between devices, swap(): return lax.ppermute(value, 'fsdp', [(i, i ^ rel) for i in range(count)])  37.7 us
    pallas_call x2, Pallas kernels, weight_grad(): pl.pallas_call(kernel, grid=(tall // GRAD_ROWS,), out_shape=shape_of(tall...  35.6 us
    pallas_call x3, Pallas kernels, ffn_hidden(): pl.pallas_call(kernel, out_shape=[shape_of(seg, wide)] * (2 * count), in_...  35.1 us
    pallas_call x1, Pallas kernels, attn_weight_grad(): pl.pallas_call(kernel, grid=(width // GRAD_ROWS,), out_shape=shape_of(wid...  21.4 us
  transfers between devices with their start and end apart: 55, of which 22 were waited for; matrix products, arithmetic and copies ran while one was open for 6% of the time, Pallas kernels for 47%

profile of v6, /device:TPU:0, one launch (start us, length us, event | category | flops | bytes accessed | tf_op | source)
XLA Modules:
  0.0 597.1 jit_solution(4875909713036254400)
XLA Ops:
  11.0 5.2 all-to-all-start
  16.2 10.8 %all-to-all-done = bf16[4,64,1536]{2,1,0:T(8,128)(2,1)S(1)} async-done(((bf16[4,64,1536]{2,1,0:T(8,128)(2,1)}), bf16[4,64,1536]{2,1,0:T(8,128)(2,1)S(1)}, u32[]{:S(2)}, u32[]{:S(2)}) %all-to-all-start) | async-done | bytes 786464 | tf_op jit(solution)/shard_map/all_to_all | solution.py:788
  28.5 1.5 collective-permute-start.1
  32.2 1.5 collective-permute-start.2
  33.9 1.8 reshape.197
  36.6 18.7 %all_to_all.29 = bf16[4,64,2048]{2,1,0:T(8,128)(2,1)} all-to-all(bf16[4,64,2048]{2,1,0:T(8,128)(2,1)S(1)} %copy.71), channel_id=1, replica_groups=mesh['fsdp'=4,'dp'=8] {'fsdp'}, dimensions={0} | all-to-all | bytes 2097152 | tf_op jit(solution)/shard_map/all_to_all | solution.py:788
  59.1 1.6 collective-permute-start.8
  60.8 4.2 collective-permute-done.8
  67.1 3.6 collective-permute-done.9
  72.8 21.3 %collective-permute-done.4.refs_1_ = bf16[384,2048]{1,0:T(8,128)(2,1)S(1)} collective-permute-done((bf16[384,2048]{1,0:T(8,128)(2,1)S(1)}, bf16[384,2048]{1,0:T(8,128)(2,1)S(1)}, u32[]{:S(2)}, u32[]{:S(2)}) %collective-permute-start.4) | collective-permute-done | bytes 1572896 | tf_op jit(solution)/shard_map/ppermute | solution.py:742
  94.8 2.1 slice.133
  104.2 12.5 %collective-permute-done.5.refs_0_ = bf16[192,2048]{1,0:T(8,128)(2,1)S(1)} collective-permute-done((bf16[192,2048]{1,0:T(8,128)(2,1)}, bf16[192,2048]{1,0:T(8,128)(2,1)S(1)}, u32[]{:S(2)}, u32[]{:S(2)}) %collective-permute-start.5) | collective-permute-done | bytes 786464 | tf_op jit(solution)/shard_map/ppermute | solution.py:742
  117.5 15.5 %attn_forward.3 = (bf16[384,2048]{1,0:T(8,128)(2,1)}, bf16[384,1536]{1,0:T(8,128)(2,1)}, f32[320,128]{1,0:T(8,128)S(1)}, bf16[320,512]{1,0:T(8,128)(2,1)S(1)}, b...) custom-call(bf16[192,2048]{1,0:T(8,128)(2,1)} %copy-done.21, bf16[192,2048]{1,0:T(8,128)(2,1)} %collective-permute-done.6.refs_1_, ...), custom_call_target="tpu_custom_call" | custom-call | flops 12000000 | bytes 1 | tf_op jit(solution)/shard_map/attn_forward/pallas_call | solution.py:199
  134.0 1.8 collective-permute-start.17
  136.4 1.4 collective-permute-start.16
  137.8 25.3 %attn_forward.4 = (bf16[384,2048]{1,0:T(8,128)(2,1)}, bf16[384,1536]{1,0:T(8,128)(2,1)}, f32[320,128]{1,0:T(8,128)S(1)}, bf16[320,512]{1,0:T(8,128)(2,1)S(1)}, b...) custom-call(bf16[384,2048]{1,0:T(8,128)(2,1)} %collective-permute-do, ...), custom_call_target="tpu_custom_call" | custom-call | flops 24000000 | bytes 1 | tf_op jit(solution)/shard_map/attn_forward/pallas_call | solution.py:199
  164.5 2.2 add_convert_fusion.3
  168.7 11.0 %collective-permute-done.17.refs_6_.refs_2_ = bf16[320,2048]{1,0:T(8,128)(2,1)S(1)} collective-permute-done((bf16[320,2048]{1,0:T(8,128)(2,1)S(1)}, bf16[320,2048]{1,0:T(8,128)(2,1)S(1)}, u32[]{:S(2)}, u32[]{:S(2)}) %collective-permute-start.17) | collective-permute-done | bytes 1310752 | tf_op jit(solution)/shard_map/ppermute | solution.py:742
  181.0 2.0 slice.184
  183.1 2.0 slice.183
  185.1 14.1 %attn_forward.5 = (bf16[384,2048]{1,0:T(8,128)(2,1)}, bf16[384,1536]{1,0:T(8,128)(2,1)}, f32[320,128]{1,0:T(8,128)S(1)}, bf16[320,512]{1,0:T(8,128)(2,1)S(1)}, b...) custom-call(bf16[384,2048]{1,0:T(8,128)(2,1)} %copy-done.11, f32[1,2048]{1,0:T(1,128)S(1)} %reshape.229.refs_2_.refs_1_.refs_6_, ...), custom_call_target="tpu_custom_call" | custom-call | flops 12000000 | bytes 1 | tf_op jit(solution)/shard_map/attn_forward/pallas_call | solution.py:199
  199.2 6.6 %collective-permute-done.12.refs_1_ = bf16[160,2048]{1,0:T(8,128)(2,1)} collective-permute-done((bf16[160,2048]{1,0:T(8,128)(2,1)}, bf16[160,2048]{1,0:T(8,128)(2,1)}, u32[]{:S(2)}, u32[]{:S(2)}) %collective-permute-start.12) | collective-permute-done | bytes 655392 | tf_op jit(solution)/shard_map/ppermute | solution.py:742
  205.8 6.9 %middle_norm.1 = (f32[320,2048]{1,0:T(8,128)}, bf16[160,2048]{1,0:T(8,128)(2,1)S(1)}, bf16[160,2048]{1,0:T(8,128)(2,1)}) custom-call(bf16[160,2048]{1,0:T(8,128)(2,1)} %copy-done.22, bf16[160,2048]{1,0:T(8,128)(2,1)} %collective-permute-done.12.refs_1_, bf16[160,2048]{1,0:T(8,128)(2,1)} %collective-permute-done.14.refs_2_, ...), custom_call_target="tpu_custom_call" | custom-call | flops 5000000 | bytes 1 | tf_op jit(solution)/shard_map/middle_norm/pallas_call | solution.py:608
  214.2 1.4 collective-permute-start.21
  217.0 10.1 %ffn_hidden.3 = (bf16[320,2048]{1,0:T(8,128)(2,1)}, bf16[320,2048]{1,0:T(8,128)(2,1)}) custom-call(bf16[160,2048]{1,0:T(8,128)(2,1)S(1)} %get-tuple-element.164.refs_0_.refs_6_, bf16[160,2048]{1,0:T(8,128)(2,1)} %get-tuple-element.165.refs_1_.refs_7_, f32[1,2048]{1,0:T(1,128)S(1)} %constant_dynamic-slice_fusion.refs_2_.refs_4_, bf16[8,4,64,2048]{3,2,1,0:T(8,128)(2,1)} %bitcast.59), custom_call_target="tpu_custom_call" | custom-call | flops 6000000 | bytes 1 | tf_op jit(solution)/shard_map/ffn_hidden/pallas_call | solution.py:349
  227.1 3.4 collective-permute-done.20.refs_2_
  230.8 10.9 %collective-permute-done.21.refs_3_ = bf16[160,2048]{1,0:T(8,128)(2,1)} collective-permute-done((bf16[160,2048]{1,0:T(8,128)(2,1)}, bf16[160,2048]{1,0:T(8,128)(2,1)}, u32[]{:S(2)}, u32[]{:S(2)}) %collective-permute-start.21) | collective-permute-done | bytes 655392 | tf_op jit(solution)/shard_map/ppermute | solution.py:742
  241.6 1.5 collective-permute-start.22
  244.0 14.9 %ffn_hidden.4 = (bf16[320,2048]{1,0:T(8,128)(2,1)}, bf16[320,2048]{1,0:T(8,128)(2,1)}, bf16[320,2048]{1,0:T(8,128)(2,1)}, bf16[320,2048]{1,0:T(8,128)(2,1)}) custom-call(bf16[160,2048]{1,0:T(8,128)(2,1)S(1)} %collective-permute-done.18.refs_0_.refs_4_, bf16[160,2048]{1,0:T(8,128)(2,1)} %collective-permute-done.19.refs_1_.refs_5_, ...), custom_call_target="tpu_custom_call" | custom-call | flops 12000000 | bytes 1 | tf_op jit(solution)/shard_map/ffn_hidden/pallas_call | solution.py:349
  261.6 10.2 %ffn_hidden.5 = (bf16[320,2048]{1,0:T(8,128)(2,1)}, bf16[320,2048]{1,0:T(8,128)(2,1)}) custom-call(bf16[160,2048]{1,0:T(8,128)(2,1)S(1)} %collective-permute-done.22.refs_0_, bf16[160,2048]{1,0:T(8,128)(2,1)} %copy-done.19, f32[1,2048]{1,0:T(1,128)S(1)} %constant_dynamic-slice_fusion.refs_2_.refs_4_, bf16[8,4,64,2048]{3,2,1,0:T(8,128)(2,1)} %bitcast.61), custom_call_target="tpu_custom_call" | custom-call | flops 6000000 | bytes 1 | tf_op jit(solution)/shard_map/ffn_hidden/pallas_call | solution.py:349
  272.6 17.6 %weight_grad.2 = bf16[2048,2048]{1,0:T(8,128)(2,1)} custom-call(bf16[320,2048]{1,0:T(8,128)(2,1)} %get-tuple-element.188.refs_0_, bf16[320,2048]{1,0:T(8,128)(2,1)} %get-tuple-element.176.refs_1_, bf16[320,2048]{1,0:T(8,128)(2,1)} %get-tuple-element.172.refs_2_, bf16[320,2048]{1,0:T(8,128)(2,1)} %get-tuple-element.166.refs_3_, ...), custom_call_target="tpu_custom_call" | custom-call | flops 17000000 | bytes 1 | tf_op jit(solution)/shard_map/weight_grad/pallas_call | solution.py:486
  290.4 26.0 %ffn_back.2 = (bf16[960,2048]{1,0:T(8,128)(2,1)}, f32[1,2048]{1,0:T(1,128)S(1)}, bf16[320,2048]{1,0:T(8,128)(2,1)}, bf16[320,2048]{1,0:T(8,128)(2,1)}, bf16[320,2048]{1,0:T(8,128)(2,1)}) custom-call(bf16[160,2048]{1,0:T(8,128)(2,1)S(1)} %collective-permute-done.24.refs_4_.refs_0_, bf16[160,2048]{1,0:T(8,128)(2,1)} %copy-done.16, ...), custom_call_target="tpu_custom_call" | custom-call | flops 30000000 | bytes 1 | tf_op jit(solution)/shard_map/ffn_back/pallas_call | solution.py:406
  316.9 1.4 collective-permute-start.27
  318.3 1.5 collective-permute-start.28
  319.9 12.5 %ffn_back.3 = (bf16[320,2048]{1,0:T(8,128)(2,1)}, f32[1,2048]{1,0:T(1,128)S(1)}, bf16[320,2048]{1,0:T(8,128)(2,1)}) custom-call(bf16[320,2048]{1,0:T(8,128)(2,1)} %refs_5_.1, bf16[320,2048]{1,0:T(8,128)(2,1)} %get-tuple-element.186.refs_1_, bf16[8,4,64,2048]{3,2,1,0:T(8,128)(2,1)} %bitcast.63, ...), custom_call_target="tpu_custom_call" | custom-call | flops 10000000 | bytes 1 | tf_op jit(solution)/shard_map/ffn_back/pallas_call | solution.py:406
  332.3 18.0 %weight_grad.3 = bf16[2048,2048]{1,0:T(8,128)(2,1)} custom-call(bf16[160,2048]{1,0:T(8,128)(2,1)S(1)} %collective-permute-done.22.refs_0_, bf16[160,2048]{1,0:T(8,128)(2,1)} %copy-done.19, bf16[160,2048]{1,0:T(8,128)(2,1)} %copy-done.15, bf16[160,2048]{1,0:T(8,128)(2,1)} %collective-permute-done.21.refs_3_, bf16[160,2048]{1,0:T(8,128)(2,1)} %copy-done, ...), custom_call_target="tpu_custom_call" | custom-call | flops 17000000 | bytes 1 | tf_op jit(solution)/shard_map/weight_grad/pallas_call | solution.py:486
  350.3 19.4 %ffn_out.1 = (bf16[160,2048]{1,0:T(8,128)(2,1)S(1)}, bf16[160,2048]{1,0:T(8,128)(2,1)}, bf16[160,2048]{1,0:T(8,128)(2,1)}, bf16[160,2048]{1,0:T(8,128)(2,1)}, bf...) custom-call(bf16[320,2048]{1,0:T(8,128)(2,1)} %get-tuple-element.188, ...), custom_call_target="tpu_custom_call" | custom-call | flops 18000000 | bytes 1 | tf_op jit(solution)/shard_map/ffn_out/pallas_call | solution.py:450
  369.9 7.2 %middle_back.1 = (f32[320,2048]{1,0:T(8,128)}, bf16[160,2048]{1,0:T(8,128)(2,1)S(1)}, bf16[160,2048]{1,0:T(8,128)(2,1)}, f32[4,2048]{1,0:T(4,128)S(1)}) custom-call(bf16[320,2048]{1,0:T(8,128)(2,1)} %get-tuple-element.201.refs_0_, bf16[320,2048]{1,0:T(8,128)(2,1)} %collective-permute-done.26.refs_1_, bf16[320,2048]{1,0:T(8,128)(2,1)} %collective-permute-done.27.refs_2_, ...), custom_call_target="tpu_custom_call" | custom-call | flops 5000000 | bytes 1 | tf_op jit(solution)/shard_map/middle_back/pallas_call | solution.py:642
  379.8 1.4 collective-permute-start.30
  381.3 14.6 %attn_backward.3 = (bf16[384,1536]{1,0:T(8,128)(2,1)}, f32[1,1536]{1,0:T(1,128)S(1)}, bf16[384,2048]{1,0:T(8,128)(2,1)}) custom-call(bf16[160,2048]{1,0:T(8,128)(2,1)} %copy-done.1, bf16[160,2048]{1,0:T(8,128)(2,1)} %get-tuple-element.207.refs_1_.refs_13_, bf16[384,1536]{1,0:T(8,128)(2,1)} %get-tuple-element.208.refs_2_, ...), custom_call_target="tpu_custom_call" | custom-call | flops 12000000 | bytes 1 | tf_op jit(solution)/shard_map/attn_backward/pallas_call | solution.py:299
  396.0 8.9 %collective-permute-done.32.refs_3_.refs_17_ = bf16[160,2048]{1,0:T(8,128)(2,1)} collective-permute-done((bf16[160,2048]{1,0:T(8,128)(2,1)}, bf16[160,2048]{1,0:T(8,128)(2,1)}, u32[]{:S(2)}, u32[]{:S(2)}) %collective-permute-start.32) | collective-permute-done | bytes 655392 | tf_op jit(solution)/shard_map/ppermute | solution.py:742
  404.9 2.1 collective-permute-done.30.refs_1_.refs_15_
  407.2 1.8 collective-permute-start.37
  409.0 2.0 collective-permute-start.38
  411.3 23.8 %attn_backward.4 = (bf16[384,1536]{1,0:T(8,128)(2,1)}, f32[1,1536]{1,0:T(1,128)S(1)}, bf16[384,2048]{1,0:T(8,128)(2,1)}, bf16[384,1536]{1,0:T(8,128)(2,1)}, f32[...) custom-call(bf16[160,2048]{1,0:T(8,128)(2,1)} %collective-permute-done.29.refs_0_.refs_14_, ...), custom_call_target="tpu_custom_call" | custom-call | flops 24000000 | bytes 1 | tf_op jit(solution)/shard_map/attn_backward/pallas_call | solution.py:299
  437.0 14.5 %attn_backward.5 = (bf16[384,1536]{1,0:T(8,128)(2,1)}, f32[1,1536]{1,0:T(1,128)S(1)}, bf16[384,2048]{1,0:T(8,128)(2,1)}) custom-call(bf16[160,2048]{1,0:T(8,128)(2,1)} %copy-done.17, bf16[160,2048]{1,0:T(8,128)(2,1)} %copy-done.18, bf16[384,1536]{1,0:T(8,128)(2,1)} %get-tuple-element.226.refs_2_, f32[320,128]{1,0:T(8,128)S(1)} %get-tuple-element.149.refs_3_, ...), custom_call_target="tpu_custom_call" | custom-call | flops 12000000 | bytes 1 | tf_op jit(solution)/shard_map/attn_backward/pallas_call | solution.py:299
  451.4 2.7 collective-permute-start.39
  455.0 21.4 %attn_weight_grad.1 = bf16[2048,2048]{1,0:T(8,128)(2,1)} custom-call(bf16[384,2048]{1,0:T(8,128)(2,1)} %get-tuple-element.228.refs_0_, bf16[384,2048]{1,0:T(8,128)(2,1)} %get-tuple-element.229.refs_1_, bf16[384,2048]{1,0:T(8,128)(2,1)} %get-tuple-element.230.refs_2_, bf16[384,2048]{1,0:T(8,128)(2,1)} %get-tuple-element.231.refs_3_, ...), custom_call_target="tpu_custom_call" | custom-call | flops 21000000 | bytes 1 | tf_op jit(solution)/shard_map/attn_weight_grad/pallas_call | solution.py:527
  476.5 34.5 %collective-permute-done.40 = bf16[160,2048]{1,0:T(8,128)(2,1)S(1)} collective-permute-done((bf16[160,2048]{1,0:T(8,128)(2,1)}, bf16[160,2048]{1,0:T(8,128)(2,1)S(1)}, u32[]{:S(2)}, u32[]{:S(2)}) %collective-permute-start.40) | collective-permute-done | bytes 655392 | tf_op jit(solution)/shard_map/ppermute | solution.py:742
  511.0 8.8 %first_back.1 = (f32[320,2048]{1,0:T(8,128)}, bf16[64,2048]{1,0:T(8,128)(2,1)S(1)}, f32[2,2048]{1,0:T(2,128)S(1)}) custom-call(bf16[384,2048]{1,0:T(8,128)(2,1)} %get-tuple-element.242.refs_0_, bf16[384,2048]{1,0:T(8,128)(2,1)} %collective-permute-done.33.refs_1_, bf16[384,2048]{1,0:T(8,128)(2,1)} %collective-permute-done.34.refs_2_, ...), custom_call_target="tpu_custom_call" | custom-call | flops 499999997952 | bytes 1 | tf_op jit(solution)/shard_map/first_back/pallas_call | solution.py:691
  521.5 3.0 all-to-all-start.2
  524.5 1.4 collective-permute-start.44
  526.0 7.5 %all-to-all-done.2 = f32[32,1,768]{2,1,0:T(1,128)S(1)} async-done(((f32[32,1,768]{2,1,0:T(1,128)}), f32[32,1,768]{2,1,0:T(1,128)S(1)}, u32[]{:S(2)}, u32[]{:S(2)}) %all-to-all-start.2) | async-done | bytes 98336 | tf_op jit(solution)/shard_map/all_to_all | solution.py:804
  534.2 3.5 all-to-all-start.4
  538.0 2.0 collective-permute-start.42
  540.3 1.5 collective-permute-start.43
  541.8 1.6 convert_element_type.166
  545.2 21.5 %collective-permute-done.42 = bf16[160,2048]{1,0:T(8,128)(2,1)S(1)} collective-permute-done((bf16[160,2048]{1,0:T(8,128)(2,1)S(1)}, bf16[160,2048]{1,0:T(8,128)(2,1)S(1)}, u32[]{:S(2)}, u32[]{:S(2)}) %collective-permute-start.42) | collective-permute-done | bytes 655392 | tf_op jit(solution)/shard_map/ppermute | solution.py:742
  567.4 1.5 copy-done.9
  568.8 1.6 fusion.1
  570.7 2.1 slice.194
  572.8 3.7 all-to-all-start.3
  576.7 1.5 copy.85
  580.0 7.3 %all-to-all-done.3 = bf16[4,64,1536]{2,1,0:T(8,128)(2,1)S(1)} async-done(((bf16[4,64,1536]{2,1,0:T(8,128)(2,1)}), bf16[4,64,1536]{2,1,0:T(8,128)(2,1)S(1)}, u32[]{:S(2)}, u32[]{:S(2)}) %all-to-all-start.3) | async-done | bytes 786464 | tf_op jit(solution)/shard_map/all_to_all | solution.py:788
  (291 shorter events, 56.1 us)
Async XLA Ops:
  11.0 16.0 %all-to-all-start = ((bf16[4,64,1536]{2,1,0:T(8,128)(2,1)}), bf16[4,64,1536]{2,1,0:T(8,128)(2,1)S(1)}, u32[]{:S(2)}, u32[]{:S(2)}) async-start(bf16[4,64,1536]{2,1,0:T(8,128)(2,1)} %beside_blocks.1), calls=%async_computation | async-start | bytes 1572864 | tf_op jit(solution)/shard_map/all_to_all | solution.py:788
  16.2 100.5 %all-gather.4.cloned.1.call-start = ((), (), s32[]{:S(2)}) async-start(), calls=%async_computation.8 | async-start | bytes 9437184 | tf_op jit(solution)/shard_map/all_gather | solution.py:808
  28.3 188.7 %all-gather.6.cloned.1.call-start = ((), (), s32[]{:S(2)}) async-start(), calls=%async_computation.9 | async-start | bytes 9437184 | tf_op jit(solution)/shard_map/all_gather | solution.py:808
  28.5 3.7 collective-permute-start.1
  30.0 5.9 collective-permute-start
  32.2 3.7 collective-permute-start.2
  36.0 22.6 %copy-start.11 = (bf16[384,2048]{1,0:T(8,128)(2,1)}, bf16[384,2048]{1,0:T(8,128)(2,1)S(1)}, u32[]{:S(2)}) copy-start(bf16[384,2048]{1,0:T(8,128)(2,1)S(1)} %constant_dynamic-update-slice_fusion.refs_0_.refs_4_) | copy-start | bytes 4718596
  55.3 235.0 %all-gather.8.cloned.1.call-start = ((), (), s32[]{:S(2)}) async-start(), calls=%async_computation.10 | async-start | bytes 9437184 | tf_op jit(solution)/shard_map/all_gather | solution.py:808
  56.1 325.1 %reduce-scatter.4.cloned.1.call-start = ((), (), s32[]{:S(2)}) async-start(), calls=%async_computation.11 | async-start | bytes 9437184 | tf_op jit(solution)/shard_map/reduce_scatter | solution.py:812
  56.3 1.2 collective-permute-start.7
  57.6 36.5 %collective-permute-start.4 = (bf16[384,2048]{1,0:T(8,128)(2,1)S(1)}, bf16[384,2048]{1,0:T(8,128)(2,1)S(1)}, u32[]{:S(2)}, u32[]{:S(2)}) collective-permute-start(bf16[384,2048]{1,0:T(8,128)(2,1)S(1)} %constant_dynamic-update-slice_fusion.refs_0_.refs_4_), channel_id=1, source_target_pairs={{0,16},{8,24},{16,0},{24,8},{1,17},{9,25},{17,1},{25,9},{2,18},{10... | collective-permute-start | bytes 4718600 | tf_op jit(solution)/shard_map/ppermute | solution.py:742
  58.6 36.3 %collective-permute-start.3 = (bf16[384,2048]{1,0:T(8,128)(2,1)S(1)}, bf16[384,2048]{1,0:T(8,128)(2,1)}, u32[]{:S(2)}, u32[]{:S(2)}) collective-permute-start(bf16[384,2048]{1,0:T(8,128)(2,1)S(1)} %constant_dynamic-update-slice_fusion.refs_0_.refs_4_), channel_id=1, source_target_pairs={{0,8},{8,0},{16,24},{24,16},{1,9},{9,1},{17,25},{25,17},{2,10},{10... | collective-permute-start | bytes 4718600 | tf_op jit(solution)/shard_map/ppermute | solution.py:742
  59.1 5.9 collective-permute-start.8
  65.0 5.6 collective-permute-start.9
  97.0 19.6 %collective-permute-start.6 = (bf16[192,2048]{1,0:T(8,128)(2,1)S(1)}, bf16[192,2048]{1,0:T(8,128)(2,1)}, u32[]{:S(2)}, u32[]{:S(2)}) collective-permute-start(bf16[192,2048]{1,0:T(8,128)(2,1)S(1)} %slice.134), channel_id=1, source_target_pairs={{0,8},{8,0},{16,24},{24,16},{1,9},{9,1},{17,25},{25,17},{2,10},{10... | collective-permute-start | bytes 2359304 | tf_op jit(solution)/shard_map/ppermute | solution.py:742
  97.8 18.9 %collective-permute-start.5 = (bf16[192,2048]{1,0:T(8,128)(2,1)}, bf16[192,2048]{1,0:T(8,128)(2,1)S(1)}, u32[]{:S(2)}, u32[]{:S(2)}) collective-permute-start(bf16[192,2048]{1,0:T(8,128)(2,1)} %slice.133), channel_id=1, source_target_pairs={{0,16},{8,24},{16,0},{24,8},{1,17},{9,25},{17,1},{25,9},{2,18},{10... | collective-permute-start | bytes 2359304 | tf_op jit(solution)/shard_map/ppermute | solution.py:742
  133.7 30.0 %collective-permute-start.11 = (bf16[160,2048]{1,0:T(8,128)(2,1)}, bf16[160,2048]{1,0:T(8,128)(2,1)S(1)}, u32[]{:S(2)}, u32[]{:S(2)}) collective-permute-start(bf16[160,2048]{1,0:T(8,128)(2,1)} %get-tuple-element.153), channel_id=1, source_target_pairs={{0,16},{8,24},{16,0},{24,8},{1,17},{9,25},{17,1},{25,9},{2,18},{10... | collective-permute-start | bytes 1966088 | tf_op jit(solution)/shard_map/ppermute | solution.py:742
  134.0 45.7 %collective-permute-start.17 = (bf16[320,2048]{1,0:T(8,128)(2,1)S(1)}, bf16[320,2048]{1,0:T(8,128)(2,1)S(1)}, u32[]{:S(2)}, u32[]{:S(2)}) collective-permute-start(bf16[320,2048]{1,0:T(8,128)(2,1)S(1)} %copy-done.8), channel_id=1, source_target_pairs={{0,16},{8,24},{16,0},{24,8},{1,17},{9,25},{17,1},{25,9},{2,18},{10... | collective-permute-start | bytes 3932168 | tf_op jit(solution)/shard_map/ppermute | solution.py:742
  135.8 30.9 %collective-permute-start.13 = (bf16[160,2048]{1,0:T(8,128)(2,1)}, bf16[160,2048]{1,0:T(8,128)(2,1)S(1)}, u32[]{:S(2)}, u32[]{:S(2)}) collective-permute-start(bf16[160,2048]{1,0:T(8,128)(2,1)} %get-tuple-element.155), channel_id=1, source_target_pairs={{0,8},{8,0},{16,24},{24,16},{1,9},{9,1},{17,25},{25,17},{2,10},{10... | collective-permute-start | bytes 1966088 | tf_op jit(solution)/shard_map/ppermute | solution.py:742
  136.4 46.6 %collective-permute-start.16 = (bf16[320,2048]{1,0:T(8,128)(2,1)S(1)}, bf16[320,2048]{1,0:T(8,128)(2,1)}, u32[]{:S(2)}, u32[]{:S(2)}) collective-permute-start(bf16[320,2048]{1,0:T(8,128)(2,1)S(1)} %copy-done.8), channel_id=1, source_target_pairs={{0,8},{8,0},{16,24},{24,16},{1,9},{9,1},{17,25},{25,17},{2,10},{10... | collective-permute-start | bytes 3932168 | tf_op jit(solution)/shard_map/ppermute | solution.py:742
  163.1 36.1 %collective-permute-start.10 = (bf16[160,2048]{1,0:T(8,128)(2,1)}, bf16[160,2048]{1,0:T(8,128)(2,1)S(1)}, u32[]{:S(2)}, u32[]{:S(2)}) collective-permute-start(bf16[160,2048]{1,0:T(8,128)(2,1)} %get-tuple-element.151), channel_id=1, source_target_pairs={{0,8},{8,0},{16,24},{24,16},{1,9},{9,1},{17,25},{25,17},{2,10},{10... | collective-permute-start | bytes 1966088 | tf_op jit(solution)/shard_map/ppermute | solution.py:742
  163.8 35.4 %collective-permute-start.15 = (bf16[160,2048]{1,0:T(8,128)(2,1)}, bf16[160,2048]{1,0:T(8,128)(2,1)}, u32[]{:S(2)}, u32[]{:S(2)}) collective-permute-start(bf16[160,2048]{1,0:T(8,128)(2,1)} %get-tuple-element.156), channel_id=1, source_target_pairs={{0,16},{8,24},{16,0},{24,8},{1,17},{9,25},{17,1},{25,9},{2,18},{10... | collective-permute-start | bytes 1966088 | tf_op jit(solution)/shard_map/ppermute | solution.py:742
  166.7 39.1 %collective-permute-start.12 = (bf16[160,2048]{1,0:T(8,128)(2,1)}, bf16[160,2048]{1,0:T(8,128)(2,1)}, u32[]{:S(2)}, u32[]{:S(2)}) collective-permute-start(bf16[160,2048]{1,0:T(8,128)(2,1)} %add_convert_fusion.3), channel_id=1, source_target_pairs={{0,8},{8,0},{16,24},{24,16},{1,9},{9,1},{17,25},{25,17},{2,10},{10... | collective-permute-start | bytes 1966088 | tf_op jit(solution)/shard_map/ppermute | solution.py:742
  179.7 26.1 %collective-permute-start.14 = (bf16[160,2048]{1,0:T(8,128)(2,1)}, bf16[160,2048]{1,0:T(8,128)(2,1)}, u32[]{:S(2)}, u32[]{:S(2)}) collective-permute-start(bf16[160,2048]{1,0:T(8,128)(2,1)} %add_convert_fusion.2), channel_id=1, source_target_pairs={{0,16},{8,24},{16,0},{24,8},{1,17},{9,25},{17,1},{25,9},{2,18},{10... | collective-permute-start | bytes 1966088 | tf_op jit(solution)/shard_map/ppermute | solution.py:742
  212.7 17.7 %collective-permute-start.20 = (bf16[160,2048]{1,0:T(8,128)(2,1)S(1)}, bf16[160,2048]{1,0:T(8,128)(2,1)S(1)}, u32[]{:S(2)}, u32[]{:S(2)}) collective-permute-start(bf16[160,2048]{1,0:T(8,128)(2,1)S(1)} %get-tuple-element.164.refs_0_.refs_6_), channel_id=1, source_target_pairs={{0,16},{8,24},{16,0},{24,8},{1,17},{9,25},{17,1},{25,9},{2,18},{10... | collective-permute-start | bytes 1966088 | tf_op jit(solution)/shard_map/ppermute | solution.py:742
  213.1 17.7 %collective-permute-start.18 = (bf16[160,2048]{1,0:T(8,128)(2,1)S(1)}, bf16[160,2048]{1,0:T(8,128)(2,1)S(1)}, u32[]{:S(2)}, u32[]{:S(2)}) collective-permute-start(bf16[160,2048]{1,0:T(8,128)(2,1)S(1)} %get-tuple-element.164.refs_0_.refs_6_), channel_id=1, source_target_pairs={{0,8},{8,0},{16,24},{24,16},{1,9},{9,1},{17,25},{25,17},{2,10},{10... | collective-permute-start | bytes 1966088 | tf_op jit(solution)/shard_map/ppermute | solution.py:742
  214.2 27.5 %collective-permute-start.21 = (bf16[160,2048]{1,0:T(8,128)(2,1)}, bf16[160,2048]{1,0:T(8,128)(2,1)}, u32[]{:S(2)}, u32[]{:S(2)}) collective-permute-start(bf16[160,2048]{1,0:T(8,128)(2,1)} %get-tuple-element.165.refs_1_.refs_7_), channel_id=1, source_target_pairs={{0,16},{8,24},{16,0},{24,8},{1,17},{9,25},{17,1},{25,9},{2,18},{10... | collective-permute-start | bytes 1966088 | tf_op jit(solution)/shard_map/ppermute | solution.py:742
  215.6 26.0 %collective-permute-start.19 = (bf16[160,2048]{1,0:T(8,128)(2,1)}, bf16[160,2048]{1,0:T(8,128)(2,1)}, u32[]{:S(2)}, u32[]{:S(2)}) collective-permute-start(bf16[160,2048]{1,0:T(8,128)(2,1)} %get-tuple-element.165.refs_1_.refs_7_), channel_id=1, source_target_pairs={{0,8},{8,0},{16,24},{24,16},{1,9},{9,1},{17,25},{25,17},{2,10},{10... | collective-permute-start | bytes 1966088 | tf_op jit(solution)/shard_map/ppermute | solution.py:742
  230.8 28.1 %copy-start = (bf16[160,2048]{1,0:T(8,128)(2,1)}, bf16[160,2048]{1,0:T(8,128)(2,1)S(1)}, u32[]{:S(2)}) copy-start(bf16[160,2048]{1,0:T(8,128)(2,1)S(1)} %collective-permute-done.18.refs_0_.refs_4_) | copy-start | bytes 1966084
  241.6 19.1 %collective-permute-start.22 = (bf16[160,2048]{1,0:T(8,128)(2,1)S(1)}, bf16[160,2048]{1,0:T(8,128)(2,1)S(1)}, u32[]{:S(2)}, u32[]{:S(2)}) collective-permute-start(bf16[160,2048]{1,0:T(8,128)(2,1)S(1)} %collective-permute-done.18.refs_0_.refs_4_), channel_id=1, source_target_pairs={{0,16},{8,24},{16,0},{24,8},{1,17},{9,25},{17,1},{25,9},{2,18},{10... | collective-permute-start | bytes 1966088 | tf_op jit(solution)/shard_map/ppermute | solution.py:742
  243.2 17.6 %collective-permute-start.23 = (bf16[160,2048]{1,0:T(8,128)(2,1)}, bf16[160,2048]{1,0:T(8,128)(2,1)S(1)}, u32[]{:S(2)}, u32[]{:S(2)}) collective-permute-start(bf16[160,2048]{1,0:T(8,128)(2,1)} %collective-permute-done.21.refs_3_), channel_id=1, source_target_pairs={{0,8},{8,0},{16,24},{24,16},{1,9},{9,1},{17,25},{25,17},{2,10},{10... | collective-permute-start | bytes 1966088 | tf_op jit(solution)/shard_map/ppermute | solution.py:742
  258.9 12.9 %collective-permute-start.24 = (bf16[160,2048]{1,0:T(8,128)(2,1)S(1)}, bf16[160,2048]{1,0:T(8,128)(2,1)S(1)}, u32[]{:S(2)}, u32[]{:S(2)}) collective-permute-start(bf16[160,2048]{1,0:T(8,128)(2,1)S(1)} %copy-done.24), channel_id=1, source_target_pairs={{0,16},{8,24},{16,0},{24,8},{1,17},{9,25},{17,1},{25,9},{2,18},{10... | collective-permute-start | bytes 1966088 | tf_op jit(solution)/shard_map/ppermute | solution.py:742
  259.5 12.3 %collective-permute-start.25 = (bf16[160,2048]{1,0:T(8,128)(2,1)S(1)}, bf16[160,2048]{1,0:T(8,128)(2,1)S(1)}, u32[]{:S(2)}, u32[]{:S(2)}) collective-permute-start(bf16[160,2048]{1,0:T(8,128)(2,1)S(1)} %copy-done.23), channel_id=1, source_target_pairs={{0,8},{8,0},{16,24},{24,16},{1,9},{9,1},{17,25},{25,17},{2,10},{10... | collective-permute-start | bytes 1966088 | tf_op jit(solution)/shard_map/ppermute | solution.py:742
  290.3 186.2 %reduce-scatter.6.cloned.1.call-start = ((), (), s32[]{:S(2)}) async-start(), calls=%async_computation.12 | async-start | bytes 9437184 | tf_op jit(solution)/shard_map/reduce_scatter | solution.py:812
  316.3 53.4 %collective-permute-start.26 = (bf16[320,2048]{1,0:T(8,128)(2,1)}, bf16[320,2048]{1,0:T(8,128)(2,1)}, u32[]{:S(2)}, u32[]{:S(2)}) collective-permute-start(bf16[320,2048]{1,0:T(8,128)(2,1)} %get-tuple-element.196), channel_id=1, source_target_pairs={{0,8},{8,0},{16,24},{24,16},{1,9},{9,1},{17,25},{25,17},{2,10},{10... | collective-permute-start | bytes 3932168 | tf_op jit(solution)/shard_map/ppermute | solution.py:742
  316.9 52.9 %collective-permute-start.27 = (bf16[320,2048]{1,0:T(8,128)(2,1)}, bf16[320,2048]{1,0:T(8,128)(2,1)}, u32[]{:S(2)}, u32[]{:S(2)}) collective-permute-start(bf16[320,2048]{1,0:T(8,128)(2,1)} %get-tuple-element.197), channel_id=1, source_target_pairs={{0,16},{8,24},{16,0},{24,8},{1,17},{9,25},{17,1},{25,9},{2,18},{10... | collective-permute-start | bytes 3932168 | tf_op jit(solution)/shard_map/ppermute | solution.py:742
  318.3 51.4 %collective-permute-start.28 = (bf16[320,2048]{1,0:T(8,128)(2,1)}, bf16[320,2048]{1,0:T(8,128)(2,1)}, u32[]{:S(2)}, u32[]{:S(2)}) collective-permute-start(bf16[320,2048]{1,0:T(8,128)(2,1)} %get-tuple-element.198), channel_id=1, source_target_pairs={{0,24},{8,16},{16,8},{24,0},{1,25},{9,17},{17,9},{25,1},{2,26},{10... | collective-permute-start | bytes 3932168 | tf_op jit(solution)/shard_map/ppermute | solution.py:742
  369.8 200.9 %reduce-scatter.8.cloned.1.call-start = ((), (), s32[]{:S(2)}) async-start(), calls=%async_computation.13 | async-start | bytes 9437184 | tf_op jit(solution)/shard_map/reduce_scatter | solution.py:812
  377.0 18.9 %collective-permute-start.31 = (bf16[160,2048]{1,0:T(8,128)(2,1)S(1)}, bf16[160,2048]{1,0:T(8,128)(2,1)S(1)}, u32[]{:S(2)}, u32[]{:S(2)}) collective-permute-start(bf16[160,2048]{1,0:T(8,128)(2,1)S(1)} %get-tuple-element.206.refs_0_.refs_12_), channel_id=1, source_target_pairs={{0,16},{8,24},{16,0},{24,8},{1,17},{9,25},{17,1},{25,9},{2,18},{10... | collective-permute-start | bytes 1966088 | tf_op jit(solution)/shard_map/ppermute | solution.py:742
  378.3 17.6 %collective-permute-start.29 = (bf16[160,2048]{1,0:T(8,128)(2,1)S(1)}, bf16[160,2048]{1,0:T(8,128)(2,1)}, u32[]{:S(2)}, u32[]{:S(2)}) collective-permute-start(bf16[160,2048]{1,0:T(8,128)(2,1)S(1)} %get-tuple-element.206.refs_0_.refs_12_), channel_id=1, source_target_pairs={{0,8},{8,0},{16,24},{24,16},{1,9},{9,1},{17,25},{25,17},{2,10},{10... | collective-permute-start | bytes 1966088 | tf_op jit(solution)/shard_map/ppermute | solution.py:742
  379.1 25.7 %collective-permute-start.32 = (bf16[160,2048]{1,0:T(8,128)(2,1)}, bf16[160,2048]{1,0:T(8,128)(2,1)}, u32[]{:S(2)}, u32[]{:S(2)}) collective-permute-start(bf16[160,2048]{1,0:T(8,128)(2,1)} %get-tuple-element.207.refs_1_.refs_13_), channel_id=1, source_target_pairs={{0,16},{8,24},{16,0},{24,8},{1,17},{9,25},{17,1},{25,9},{2,18},{10... | collective-permute-start | bytes 1966088 | tf_op jit(solution)/shard_map/ppermute | solution.py:742
  379.8 27.2 %collective-permute-start.30 = (bf16[160,2048]{1,0:T(8,128)(2,1)}, bf16[160,2048]{1,0:T(8,128)(2,1)}, u32[]{:S(2)}, u32[]{:S(2)}) collective-permute-start(bf16[160,2048]{1,0:T(8,128)(2,1)} %get-tuple-element.207.refs_1_.refs_13_), channel_id=1, source_target_pairs={{0,8},{8,0},{16,24},{24,16},{1,9},{9,1},{17,25},{25,17},{2,10},{10... | collective-permute-start | bytes 1966088 | tf_op jit(solution)/shard_map/ppermute | solution.py:742
  381.3 25.9 %copy-start.55 = (bf16[160,2048]{1,0:T(8,128)(2,1)S(1)}, bf16[160,2048]{1,0:T(8,128)(2,1)}, u32[]{:S(2)}) copy-start(bf16[160,2048]{1,0:T(8,128)(2,1)} %get-tuple-element.224) | copy-start | bytes 1966084
  381.3 29.8 %copy-start.43 = (f32[384]{0:T(512)S(1)}, f32[384]{0:T(512)}, u32[]{:S(2)}) copy-start(f32[384]{0:T(512)} %get-tuple-element.370) | copy-start | bytes 4612
  381.3 29.9 %copy-start.42 = (f32[384]{0:T(512)S(1)}, f32[384]{0:T(512)}, u32[]{:S(2)}) copy-start(f32[384]{0:T(512)} %get-tuple-element.371) | copy-start | bytes 4612
  407.0 28.3 %collective-permute-start.35 = (bf16[160,2048]{1,0:T(8,128)(2,1)}, bf16[160,2048]{1,0:T(8,128)(2,1)S(1)}, u32[]{:S(2)}, u32[]{:S(2)}) collective-permute-start(bf16[160,2048]{1,0:T(8,128)(2,1)} %collective-permute-done.29.refs_0_.refs_14_), channel_id=1, source_target_pairs={{0,16},{8,24},{16,0},{24,8},{1,17},{9,25},{17,1},{25,9},{2,18},{10... | collective-permute-start | bytes 1966088 | tf_op jit(solution)/shard_map/ppermute | solution.py:742
  407.1 28.4 %collective-permute-start.36 = (bf16[160,2048]{1,0:T(8,128)(2,1)S(1)}, bf16[160,2048]{1,0:T(8,128)(2,1)S(1)}, u32[]{:S(2)}, u32[]{:S(2)}) collective-permute-start(bf16[160,2048]{1,0:T(8,128)(2,1)S(1)} %get-tuple-element.223), channel_id=1, source_target_pairs={{0,8},{8,0},{16,24},{24,16},{1,9},{9,1},{17,25},{25,17},{2,10},{10... | collective-permute-start | bytes 1966088 | tf_op jit(solution)/shard_map/ppermute | solution.py:742
  407.2 28.2 %collective-permute-start.37 = (bf16[160,2048]{1,0:T(8,128)(2,1)S(1)}, bf16[160,2048]{1,0:T(8,128)(2,1)S(1)}, u32[]{:S(2)}, u32[]{:S(2)}) collective-permute-start(bf16[160,2048]{1,0:T(8,128)(2,1)S(1)} %copy-done.55), channel_id=1, source_target_pairs={{0,16},{8,24},{16,0},{24,8},{1,17},{9,25},{17,1},{25,9},{2,18},{10... | collective-permute-start | bytes 1966088 | tf_op jit(solution)/shard_map/ppermute | solution.py:742
  409.0 27.1 %collective-permute-start.38 = (bf16[160,2048]{1,0:T(8,128)(2,1)}, bf16[160,2048]{1,0:T(8,128)(2,1)S(1)}, u32[]{:S(2)}, u32[]{:S(2)}) collective-permute-start(bf16[160,2048]{1,0:T(8,128)(2,1)} %collective-permute-done.32.refs_3_.refs_17_), channel_id=1, source_target_pairs={{0,8},{8,0},{16,24},{24,16},{1,9},{9,1},{17,25},{25,17},{2,10},{10... | collective-permute-start | bytes 1966088 | tf_op jit(solution)/shard_map/ppermute | solution.py:742
  435.1 75.8 %collective-permute-start.33 = (bf16[384,2048]{1,0:T(8,128)(2,1)}, bf16[384,2048]{1,0:T(8,128)(2,1)}, u32[]{:S(2)}, u32[]{:S(2)}) collective-permute-start(bf16[384,2048]{1,0:T(8,128)(2,1)} %get-tuple-element.220), channel_id=1, source_target_pairs={{0,8},{8,0},{16,24},{24,16},{1,9},{9,1},{17,25},{25,17},{2,10},{10... | collective-permute-start | bytes 4718600 | tf_op jit(solution)/shard_map/ppermute | solution.py:742
  435.3 75.7 %collective-permute-start.34 = (bf16[384,2048]{1,0:T(8,128)(2,1)}, bf16[384,2048]{1,0:T(8,128)(2,1)}, u32[]{:S(2)}, u32[]{:S(2)}) collective-permute-start(bf16[384,2048]{1,0:T(8,128)(2,1)} %get-tuple-element.221), channel_id=1, source_target_pairs={{0,16},{8,24},{16,0},{24,8},{1,17},{9,25},{17,1},{25,9},{2,18},{10... | collective-permute-start | bytes 4718600 | tf_op jit(solution)/shard_map/ppermute | solution.py:742
  451.4 59.5 %collective-permute-start.39 = (bf16[384,2048]{1,0:T(8,128)(2,1)}, bf16[384,2048]{1,0:T(8,128)(2,1)}, u32[]{:S(2)}, u32[]{:S(2)}) collective-permute-start(bf16[384,2048]{1,0:T(8,128)(2,1)} %get-tuple-element.227), channel_id=1, source_target_pairs={{0,24},{8,16},{16,8},{24,0},{1,25},{9,17},{17,9},{25,1},{2,26},{10... | collective-permute-start | bytes 4718600 | tf_op jit(solution)/shard_map/ppermute | solution.py:742
  454.1 56.8 %collective-permute-start.40 = (bf16[160,2048]{1,0:T(8,128)(2,1)}, bf16[160,2048]{1,0:T(8,128)(2,1)S(1)}, u32[]{:S(2)}, u32[]{:S(2)}) collective-permute-start(bf16[160,2048]{1,0:T(8,128)(2,1)} %get-tuple-element.240), channel_id=1, source_target_pairs={{0,8},{8,0},{16,24},{24,16},{1,9},{9,1},{17,25},{25,17},{2,10},{10... | collective-permute-start | bytes 1966088 | tf_op jit(solution)/shard_map/ppermute | solution.py:742
  454.2 56.7 %collective-permute-start.41 = (bf16[160,2048]{1,0:T(8,128)(2,1)S(1)}, bf16[160,2048]{1,0:T(8,128)(2,1)S(1)}, u32[]{:S(2)}, u32[]{:S(2)}) collective-permute-start(bf16[160,2048]{1,0:T(8,128)(2,1)S(1)} %copy-done.54), channel_id=1, source_target_pairs={{0,16},{8,24},{16,0},{24,8},{1,17},{9,25},{17,1},{25,9},{2,18},{10... | collective-permute-start | bytes 1966088 | tf_op jit(solution)/shard_map/ppermute | solution.py:742
  521.5 12.0 %all-to-all-start.2 = ((f32[32,1,768]{2,1,0:T(1,128)}), f32[32,1,768]{2,1,0:T(1,128)S(1)}, u32[]{:S(2)}, u32[]{:S(2)}) async-start(f32[32,1,768]{2,1,0:T(1,128)} %all_to_all.20), calls=%async_computation.3 | async-start | bytes 196608 | tf_op jit(solution)/shard_map/all_to_all | solution.py:804
  524.5 19.4 %collective-permute-start.44 = (bf16[50,2048]{1,0:T(8,128)(2,1)S(1)}, bf16[50,2048]{1,0:T(8,128)(2,1)S(1)}, u32[]{:S(2)}, u32[]{:S(2)}) collective-permute-start(bf16[50,2048]{1,0:T(8,128)(2,1)S(1)} %slice.159), channel_id=1, source_target_pairs={{1,0},{2,1},{3,2},{4,3},{5,4},{6,5},{7,6},{8,7},{9,8},{10,9},{11,1... | collective-permute-start | bytes 614408 | tf_op jit(solution)/shard_map/ppermute | solution.py:1036
  534.2 38.6 %all-to-all-start.4 = ((bf16[4,64,2048]{2,1,0:T(8,128)(2,1)}), bf16[4,64,2048]{2,1,0:T(8,128)(2,1)S(1)}, u32[]{:S(2)}, u32[]{:S(2)}) async-start(bf16[4,64,2048]{2,1,0:T(8,128)(2,1)} %reduce-scatter.6.cloned.1.call-done), calls=%async_computation.7 | async-start | bytes 2097152 | tf_op jit(solution)/shard_map/all_to_all | solution.py:788
  538.0 28.7 %collective-permute-start.42 = (bf16[160,2048]{1,0:T(8,128)(2,1)S(1)}, bf16[160,2048]{1,0:T(8,128)(2,1)S(1)}, u32[]{:S(2)}, u32[]{:S(2)}) collective-permute-start(bf16[160,2048]{1,0:T(8,128)(2,1)S(1)} %add_convert_fusion.1), channel_id=1, source_target_pairs={{0,16},{8,24},{16,0},{24,8},{1,17},{9,25},{17,1},{25,9},{2,18},{10... | collective-permute-start | bytes 1966088 | tf_op jit(solution)/shard_map/ppermute | solution.py:742
  540.3 26.8 %collective-permute-start.43 = (bf16[160,2048]{1,0:T(8,128)(2,1)S(1)}, bf16[160,2048]{1,0:T(8,128)(2,1)S(1)}, u32[]{:S(2)}, u32[]{:S(2)}) collective-permute-start(bf16[160,2048]{1,0:T(8,128)(2,1)S(1)} %add_convert_fusion), channel_id=1, source_target_pairs={{0,8},{8,0},{16,24},{24,16},{1,9},{9,1},{17,25},{25,17},{2,10},{10... | collective-permute-start | bytes 1966088 | tf_op jit(solution)/shard_map/ppermute | solution.py:742
  543.3 23.4 %copy-start.26 = (bf16[160,2048]{1,0:T(8,128)(2,1)S(1)}, bf16[160,2048]{1,0:T(8,128)(2,1)}, u32[]{:S(2)}) copy-start(bf16[160,2048]{1,0:T(8,128)(2,1)} %get-tuple-element.260) | copy-start | bytes 1966084
  543.3 23.4 %copy-start.36 = (bf16[160,2048]{1,0:T(8,128)(2,1)S(1)}, bf16[160,2048]{1,0:T(8,128)(2,1)}, u32[]{:S(2)}) copy-start(bf16[160,2048]{1,0:T(8,128)(2,1)} %copy-done.35) | copy-start | bytes 1966084
  545.2 21.9 %copy-start.25 = (bf16[160,2048]{1,0:T(8,128)(2,1)S(1)}, bf16[160,2048]{1,0:T(8,128)(2,1)}, u32[]{:S(2)}) copy-start(bf16[160,2048]{1,0:T(8,128)(2,1)} %get-tuple-element.262) | copy-start | bytes 1966084
  545.2 21.9 %copy-start.34 = (bf16[160,2048]{1,0:T(8,128)(2,1)S(1)}, bf16[160,2048]{1,0:T(8,128)(2,1)}, u32[]{:S(2)}) copy-start(bf16[160,2048]{1,0:T(8,128)(2,1)} %copy-done.33) | copy-start | bytes 1966084
  572.8 14.6 %all-to-all-start.3 = ((bf16[4,64,1536]{2,1,0:T(8,128)(2,1)}), bf16[4,64,1536]{2,1,0:T(8,128)(2,1)S(1)}, u32[]{:S(2)}, u32[]{:S(2)}) async-start(bf16[4,64,1536]{2,1,0:T(8,128)(2,1)} %slice.194), calls=%async_computation.6 | async-start | bytes 1572864 | tf_op jit(solution)/shard_map/all_to_all | solution.py:788
  (49 other events, 303.7 us)
Sparse Core Ops, SparseCore 0:
  28.4 83.5 all-gather.3
  113.6 80.4 all-gather.5
  195.7 80.5 all-gather.7
  290.4 89.0 reduce-scatter.3
  381.6 87.9 reduce-scatter.5
  476.6 94.1 reduce-scatter.7

commit v7 on v6

--- a/solution.py
+++ b/solution.py
@@ -146,13 +146,8 @@
         col = lax.broadcasted_iota(jnp.int32, (seg, keys), 1)
         mask[...] = jnp.where(jnp.logical_or(col <= row, ok_row > 0.5), 0.0, MASKED)
 
-        def project(part, _):
-            at = pl.ds(pl.multiple_of(part * cols, PAIR), cols)
-            value = dot(low_ref[...], rows_of(weights, at)) + off_ref[:, at]
-            qkv_ref[:, at] = value.astype(BF16)
-            return _
-
-        lax.fori_loop(0, 3, project, 0)
+        value = dot(low_ref[...], rows_of(weights, pl.ds(0, 3 * cols))) + off_ref[...]
+        qkv_ref[...] = value.astype(BF16)
         lane = lax.broadcasted_iota(jnp.int32, (seg, PAIR), 1)
 
         def attend(pair, _):
@@ -322,7 +317,7 @@
     count = len(seconds)
     seg = sum(piece.shape[0] for piece in pieces) // count
     columns, members, share, wide = up_w.shape
-    step = 512
+    step = min(1024, wide)
 
     def kernel(*refs):
         off_ref, up_hbm = refs[given : given + 2]
@@ -429,7 +424,7 @@
     seg, wide = hiddens[0].shape
     rows = seg // 2
     width = down_w.shape[1]
-    step = 512
+    step = min(1024, width)
 
     def kernel(*refs):
         down_ref = refs[count]
@@ -462,13 +457,11 @@
     return [outs[2 * index : 2 * index + 2] for index in range(count)]
 
 
-GRAD_ROWS = 256
-
-
 def weight_grad(lefts, rights):
     tall, wide = lefts[0].shape[1], rights[0].shape[1]
     deep = sum(left.shape[0] for left in lefts)
     counts = len(lefts), len(rights)
+    rows_each = min(512, tall)
     both = sum(counts)
 
     def kernel(*refs):
@@ -480,15 +473,15 @@
             copies = load_rows(refs[: counts[0]], left, sems)
             wait_all(copies + load_rows(refs[counts[0] : both], right, sems.at[pl.ds(counts[0], counts[1])]))
 
-        at = pl.ds(pl.multiple_of(step * GRAD_ROWS, GRAD_ROWS), GRAD_ROWS)
+        at = pl.ds(pl.multiple_of(step * rows_each, rows_each), rows_each)
         out_ref[...] = t_dot(left[:, at], right[...]).astype(BF16)
 
     return pl.pallas_call(
         kernel,
-        grid=(tall // GRAD_ROWS,),
+        grid=(tall // rows_each,),
         out_shape=shape_of(tall, wide),
         in_specs=[HBM] * both,
-        out_specs=pl.BlockSpec((GRAD_ROWS, wide), lambda i: (i, 0)),
+        out_specs=pl.BlockSpec((rows_each, wide), lambda i: (i, 0)),
         scratch_shapes=[
             pltpu.VMEM((deep, tall), BF16),
             pltpu.VMEM((deep, wide), BF16),
@@ -502,7 +495,8 @@
 def attn_weight_grad(lows, grads, mixeds, branches):
     lists = lows, grads, mixeds, branches
     width, cols = lows[0].shape[1], mixeds[0].shape[1]
-    halves = cols // GRAD_ROWS
+    rows_each = min(512, cols)
+    halves = cols // rows_each
     ends = [0]
     for some in lists:
         ends.append(ends[-1] + len(some))
@@ -518,18 +512,18 @@
                 copies += load_rows(refs[first:last], scratch, sems.at[pl.ds(first, last - first)])
             wait_all(copies)
 
-        at = pl.ds(pl.multiple_of(step * GRAD_ROWS, GRAD_ROWS), GRAD_ROWS)
+        at = pl.ds(pl.multiple_of(step * rows_each, rows_each), rows_each)
         out_ref[:, : 3 * cols] = t_dot(low[:, at], grad[...]).astype(BF16)
-        half = pl.ds(pl.multiple_of((step % halves) * GRAD_ROWS, GRAD_ROWS), GRAD_ROWS)
+        half = pl.ds(pl.multiple_of((step % halves) * rows_each, rows_each), rows_each)
         block = pl.ds(pl.multiple_of((step // halves) * cols, PAIR), cols)
         out_ref[:, 3 * cols :] = t_dot(mixed[:, half], branch[:, block]).astype(BF16)
 
     return pl.pallas_call(
         kernel,
-        grid=(width // GRAD_ROWS,),
+        grid=(width // rows_each,),
         out_shape=shape_of(width, 4 * cols),
         in_specs=[HBM] * ends[-1],
-        out_specs=pl.BlockSpec((GRAD_ROWS, 4 * cols), lambda i: (i, 0)),
+        out_specs=pl.BlockSpec((rows_each, 4 * cols), lambda i: (i, 0)),
         scratch_shapes=[
             pltpu.VMEM((sum(one.shape[0] for one in some), some[0].shape[1]), BF16)
             for some in lists

time: 602 us -> 597 us (level)
  Pallas kernels: 282 us -> 275 us
  transfers between devices with their start and end apart: 55 -> 55, of which waited for: 22 -> 20; matrix products, arithmetic and copies ran while one was open for 6% -> 6% of each run, Pallas kernels for 47% -> 46%
where the time goes in v7:
time: 597 us; the launch traced here: 594 us
  Pallas kernels  275 us (46%)
  waiting for transfers between devices  171 us (29%)
  starting transfers between devices  63.9 us (11%)
  local copies, waits for them, and re-layouts  34.8 us (6%)
  blocking collectives  18.7 us (3%)
  between operations  15.7 us (3%)
  other arithmetic  14.6 us (2%)
    ppermute x38, waiting for transfers between devices, swap(): return lax.ppermute(value, 'fsdp', [(i, i ^ rel) for i in range(count)])  135 us
    pallas_call x3, Pallas kernels, attn_forward(): pl.pallas_call(kernel, out_shape=shapes, in_specs=[HBM] * given + [VMEM]...  53.3 us
    pallas_call x3, Pallas kernels, attn_backward(): pl.pallas_call(kernel, out_shape=shapes, in_specs=[HBM] * given + [VMEM]...  52.4 us
    ppermute x38, starting transfers between devices, swap(): return lax.ppermute(value, 'fsdp', [(i, i ^ rel) for i in range(count)])  39.8 us
    pallas_call x2, Pallas kernels, ffn_back(): pl.pallas_call(kernel, out_shape=(shape_of(rows, wide), shape_of(1, wide,...  38.4 us
    pallas_call x2, Pallas kernels, weight_grad(): pl.pallas_call(kernel, grid=(tall // rows_each,), out_shape=shape_of(tall...  34.5 us
    pallas_call x3, Pallas kernels, ffn_hidden(): pl.pallas_call(kernel, out_shape=[shape_of(seg, wide)] * (2 * count), in_...  33.1 us
    pallas_call x1, Pallas kernels, attn_weight_grad(): pl.pallas_call(kernel, grid=(width // rows_each,), out_shape=shape_of(wid...  20.8 us
  transfers between devices with their start and end apart: 55, of which 20 were waited for; matrix products, arithmetic and copies ran while one was open for 6% of the time, Pallas kernels for 46%

profile of v7, /device:TPU:0, one launch (start us, length us, event | category | flops | bytes accessed | tf_op | source)
XLA Modules:
  0.0 593.8 jit_solution(13880178817375333851)
XLA Ops:
  11.0 5.2 all-to-all-start
  16.2 10.8 %all-to-all-done = bf16[4,64,1536]{2,1,0:T(8,128)(2,1)S(1)} async-done(((bf16[4,64,1536]{2,1,0:T(8,128)(2,1)}), bf16[4,64,1536]{2,1,0:T(8,128)(2,1)S(1)}, u32[]{:S(2)}, u32[]{:S(2)}) %all-to-all-start) | async-done | bytes 786464 | tf_op jit(solution)/shard_map/all_to_all | solution.py:782
  28.5 1.5 collective-permute-start.1
  32.2 1.5 collective-permute-start.2
  33.9 1.8 reshape.197
  36.6 18.7 %all_to_all.29 = bf16[4,64,2048]{2,1,0:T(8,128)(2,1)} all-to-all(bf16[4,64,2048]{2,1,0:T(8,128)(2,1)S(1)} %copy.71), channel_id=1, replica_groups=mesh['fsdp'=4,'dp'=8] {'fsdp'}, dimensions={0} | all-to-all | bytes 2097152 | tf_op jit(solution)/shard_map/all_to_all | solution.py:782
  59.3 1.6 collective-permute-start.8
  61.0 4.0 collective-permute-done.8
  67.3 3.6 collective-permute-done.9
  73.0 21.3 %collective-permute-done.4.refs_1_ = bf16[384,2048]{1,0:T(8,128)(2,1)S(1)} collective-permute-done((bf16[384,2048]{1,0:T(8,128)(2,1)S(1)}, bf16[384,2048]{1,0:T(8,128)(2,1)S(1)}, u32[]{:S(2)}, u32[]{:S(2)}) %collective-permute-start.4) | collective-permute-done | bytes 1572896 | tf_op jit(solution)/shard_map/ppermute | solution.py:736
  95.1 2.1 slice.133
  104.4 12.5 %collective-permute-done.5.refs_0_ = bf16[192,2048]{1,0:T(8,128)(2,1)S(1)} collective-permute-done((bf16[192,2048]{1,0:T(8,128)(2,1)}, bf16[192,2048]{1,0:T(8,128)(2,1)S(1)}, u32[]{:S(2)}, u32[]{:S(2)}) %collective-permute-start.5) | collective-permute-done | bytes 786464 | tf_op jit(solution)/shard_map/ppermute | solution.py:736
  117.7 15.1 %attn_forward.3 = (bf16[384,2048]{1,0:T(8,128)(2,1)}, bf16[384,1536]{1,0:T(8,128)(2,1)}, f32[320,128]{1,0:T(8,128)S(1)}, bf16[320,512]{1,0:T(8,128)(2,1)S(1)}, b...) custom-call(bf16[192,2048]{1,0:T(8,128)(2,1)} %copy-done.21, bf16[192,2048]{1,0:T(8,128)(2,1)} %collective-permute-done.6.refs_1_, ...), custom_call_target="tpu_custom_call" | custom-call | flops 12000000 | bytes 1 | tf_op jit(solution)/shard_map/attn_forward/pallas_call | solution.py:194
  133.9 1.7 collective-permute-start.17
  136.3 1.3 collective-permute-start.16
  137.6 24.5 %attn_forward.4 = (bf16[384,2048]{1,0:T(8,128)(2,1)}, bf16[384,1536]{1,0:T(8,128)(2,1)}, f32[320,128]{1,0:T(8,128)S(1)}, bf16[320,512]{1,0:T(8,128)(2,1)S(1)}, b...) custom-call(bf16[384,2048]{1,0:T(8,128)(2,1)} %collective-permute-do, ...), custom_call_target="tpu_custom_call" | custom-call | flops 24000000 | bytes 1 | tf_op jit(solution)/shard_map/attn_forward/pallas_call | solution.py:194
  163.6 2.2 add_convert_fusion.3
  167.8 11.7 %collective-permute-done.17.refs_6_.refs_2_ = bf16[320,2048]{1,0:T(8,128)(2,1)S(1)} collective-permute-done((bf16[320,2048]{1,0:T(8,128)(2,1)S(1)}, bf16[320,2048]{1,0:T(8,128)(2,1)S(1)}, u32[]{:S(2)}, u32[]{:S(2)}) %collective-permute-start.17) | collective-permute-done | bytes 1310752 | tf_op jit(solution)/shard_map/ppermute | solution.py:736
  180.9 2.0 slice.184
  182.9 2.0 slice.183
  184.9 13.7 %attn_forward.5 = (bf16[384,2048]{1,0:T(8,128)(2,1)}, bf16[384,1536]{1,0:T(8,128)(2,1)}, f32[320,128]{1,0:T(8,128)S(1)}, bf16[320,512]{1,0:T(8,128)(2,1)S(1)}, b...) custom-call(bf16[384,2048]{1,0:T(8,128)(2,1)} %copy-done.11, f32[1,2048]{1,0:T(1,128)S(1)} %reshape.229.refs_2_.refs_1_.refs_6_, ...), custom_call_target="tpu_custom_call" | custom-call | flops 12000000 | bytes 1 | tf_op jit(solution)/shard_map/attn_forward/pallas_call | solution.py:194
  198.6 7.0 %collective-permute-done.12.refs_1_ = bf16[160,2048]{1,0:T(8,128)(2,1)} collective-permute-done((bf16[160,2048]{1,0:T(8,128)(2,1)}, bf16[160,2048]{1,0:T(8,128)(2,1)}, u32[]{:S(2)}, u32[]{:S(2)}) %collective-permute-start.12) | collective-permute-done | bytes 655392 | tf_op jit(solution)/shard_map/ppermute | solution.py:736
  205.7 6.9 %middle_norm.1 = (f32[320,2048]{1,0:T(8,128)}, bf16[160,2048]{1,0:T(8,128)(2,1)S(1)}, bf16[160,2048]{1,0:T(8,128)(2,1)}) custom-call(bf16[160,2048]{1,0:T(8,128)(2,1)} %copy-done.22, bf16[160,2048]{1,0:T(8,128)(2,1)} %collective-permute-done.12.refs_1_, bf16[160,2048]{1,0:T(8,128)(2,1)} %collective-permute-done.14.refs_2_, ...), custom_call_target="tpu_custom_call" | custom-call | flops 5000000 | bytes 1 | tf_op jit(solution)/shard_map/middle_norm/pallas_call | solution.py:602
  214.0 1.3 collective-permute-start.21
  216.8 9.7 %ffn_hidden.3 = (bf16[320,2048]{1,0:T(8,128)(2,1)}, bf16[320,2048]{1,0:T(8,128)(2,1)}) custom-call(bf16[160,2048]{1,0:T(8,128)(2,1)S(1)} %get-tuple-element.164.refs_0_.refs_6_, bf16[160,2048]{1,0:T(8,128)(2,1)} %get-tuple-element.165.refs_1_.refs_7_, f32[1,2048]{1,0:T(1,128)S(1)} %constant_dynamic-slice_fusion.refs_2_.refs_4_, bf16[8,4,64,2048]{3,2,1,0:T(8,128)(2,1)} %bitcast.59), custom_call_target="tpu_custom_call" | custom-call | flops 6000000 | bytes 1 | tf_op jit(solution)/shard_map/ffn_hidden/pallas_call | solution.py:344
  226.5 3.7 collective-permute-done.20.refs_2_
  230.7 10.8 %collective-permute-done.21.refs_3_ = bf16[160,2048]{1,0:T(8,128)(2,1)} collective-permute-done((bf16[160,2048]{1,0:T(8,128)(2,1)}, bf16[160,2048]{1,0:T(8,128)(2,1)}, u32[]{:S(2)}, u32[]{:S(2)}) %collective-permute-start.21) | collective-permute-done | bytes 655392 | tf_op jit(solution)/shard_map/ppermute | solution.py:736
  241.5 1.5 collective-permute-start.22
  243.8 13.8 %ffn_hidden.4 = (bf16[320,2048]{1,0:T(8,128)(2,1)}, bf16[320,2048]{1,0:T(8,128)(2,1)}, bf16[320,2048]{1,0:T(8,128)(2,1)}, bf16[320,2048]{1,0:T(8,128)(2,1)}) custom-call(bf16[160,2048]{1,0:T(8,128)(2,1)S(1)} %collective-permute-done.18.refs_0_.refs_4_, bf16[160,2048]{1,0:T(8,128)(2,1)} %collective-permute-done.19.refs_1_.refs_5_, ...), custom_call_target="tpu_custom_call" | custom-call | flops 12000000 | bytes 1 | tf_op jit(solution)/shard_map/ffn_hidden/pallas_call | solution.py:344
  260.4 9.6 %ffn_hidden.5 = (bf16[320,2048]{1,0:T(8,128)(2,1)}, bf16[320,2048]{1,0:T(8,128)(2,1)}) custom-call(bf16[160,2048]{1,0:T(8,128)(2,1)S(1)} %collective-permute-done.22.refs_0_, bf16[160,2048]{1,0:T(8,128)(2,1)} %copy-done.19, f32[1,2048]{1,0:T(1,128)S(1)} %constant_dynamic-slice_fusion.refs_2_.refs_4_, bf16[8,4,64,2048]{3,2,1,0:T(8,128)(2,1)} %bitcast.61), custom_call_target="tpu_custom_call" | custom-call | flops 6000000 | bytes 1 | tf_op jit(solution)/shard_map/ffn_hidden/pallas_call | solution.py:344
  270.9 17.1 %weight_grad.2 = bf16[2048,2048]{1,0:T(8,128)(2,1)} custom-call(bf16[320,2048]{1,0:T(8,128)(2,1)} %get-tuple-element.188.refs_0_, bf16[320,2048]{1,0:T(8,128)(2,1)} %get-tuple-element.176.refs_1_, bf16[320,2048]{1,0:T(8,128)(2,1)} %get-tuple-element.172.refs_2_, bf16[320,2048]{1,0:T(8,128)(2,1)} %get-tuple-element.166.refs_3_, ...), custom_call_target="tpu_custom_call" | custom-call | flops 17000000 | bytes 1 | tf_op jit(solution)/shard_map/weight_grad/pallas_call | solution.py:479
  288.1 26.0 %ffn_back.2 = (bf16[960,2048]{1,0:T(8,128)(2,1)}, f32[1,2048]{1,0:T(1,128)S(1)}, bf16[320,2048]{1,0:T(8,128)(2,1)}, bf16[320,2048]{1,0:T(8,128)(2,1)}, bf16[320,2048]{1,0:T(8,128)(2,1)}) custom-call(bf16[160,2048]{1,0:T(8,128)(2,1)S(1)} %collective-permute-done.24.refs_4_.refs_0_, bf16[160,2048]{1,0:T(8,128)(2,1)} %copy-done.16, ...), custom_call_target="tpu_custom_call" | custom-call | flops 30000000 | bytes 1 | tf_op jit(solution)/shard_map/ffn_back/pallas_call | solution.py:401
  314.7 1.5 collective-permute-start.27
  316.2 1.5 collective-permute-start.28
  317.6 12.5 %ffn_back.3 = (bf16[320,2048]{1,0:T(8,128)(2,1)}, f32[1,2048]{1,0:T(1,128)S(1)}, bf16[320,2048]{1,0:T(8,128)(2,1)}) custom-call(bf16[320,2048]{1,0:T(8,128)(2,1)} %refs_5_.1, bf16[320,2048]{1,0:T(8,128)(2,1)} %get-tuple-element.186.refs_1_, bf16[8,4,64,2048]{3,2,1,0:T(8,128)(2,1)} %bitcast.63, ...), custom_call_target="tpu_custom_call" | custom-call | flops 10000000 | bytes 1 | tf_op jit(solution)/shard_map/ffn_back/pallas_call | solution.py:401
  330.1 17.4 %weight_grad.3 = bf16[2048,2048]{1,0:T(8,128)(2,1)} custom-call(bf16[160,2048]{1,0:T(8,128)(2,1)S(1)} %collective-permute-done.22.refs_0_, bf16[160,2048]{1,0:T(8,128)(2,1)} %copy-done.19, bf16[160,2048]{1,0:T(8,128)(2,1)} %copy-done.15, bf16[160,2048]{1,0:T(8,128)(2,1)} %collective-permute-done.21.refs_3_, bf16[160,2048]{1,0:T(8,128)(2,1)} %copy-done, ...), custom_call_target="tpu_custom_call" | custom-call | flops 17000000 | bytes 1 | tf_op jit(solution)/shard_map/weight_grad/pallas_call | solution.py:479
  347.5 19.1 %ffn_out.1 = (bf16[160,2048]{1,0:T(8,128)(2,1)S(1)}, bf16[160,2048]{1,0:T(8,128)(2,1)}, bf16[160,2048]{1,0:T(8,128)(2,1)}, bf16[160,2048]{1,0:T(8,128)(2,1)}, bf...) custom-call(bf16[320,2048]{1,0:T(8,128)(2,1)} %get-tuple-element.188, ...), custom_call_target="tpu_custom_call" | custom-call | flops 18000000 | bytes 1 | tf_op jit(solution)/shard_map/ffn_out/pallas_call | solution.py:445
  367.3 7.0 %middle_back.1 = (f32[320,2048]{1,0:T(8,128)}, bf16[160,2048]{1,0:T(8,128)(2,1)S(1)}, bf16[160,2048]{1,0:T(8,128)(2,1)}, f32[4,2048]{1,0:T(4,128)S(1)}) custom-call(bf16[320,2048]{1,0:T(8,128)(2,1)} %get-tuple-element.201.refs_0_, bf16[320,2048]{1,0:T(8,128)(2,1)} %collective-permute-done.26.refs_1_, bf16[320,2048]{1,0:T(8,128)(2,1)} %collective-permute-done.27.refs_2_, ...), custom_call_target="tpu_custom_call" | custom-call | flops 5000000 | bytes 1 | tf_op jit(solution)/shard_map/middle_back/pallas_call | solution.py:636
  375.1 1.5 collective-permute-start.29
  378.6 14.1 %attn_backward.3 = (bf16[384,1536]{1,0:T(8,128)(2,1)}, f32[1,1536]{1,0:T(1,128)S(1)}, bf16[384,2048]{1,0:T(8,128)(2,1)}) custom-call(bf16[160,2048]{1,0:T(8,128)(2,1)} %copy-done.1, bf16[160,2048]{1,0:T(8,128)(2,1)} %get-tuple-element.207.refs_1_.refs_13_, bf16[384,1536]{1,0:T(8,128)(2,1)} %get-tuple-element.208.refs_2_, ...), custom_call_target="tpu_custom_call" | custom-call | flops 12000000 | bytes 1 | tf_op jit(solution)/shard_map/attn_backward/pallas_call | solution.py:294
  392.7 9.8 %collective-permute-done.32.refs_3_.refs_17_ = bf16[160,2048]{1,0:T(8,128)(2,1)} collective-permute-done((bf16[160,2048]{1,0:T(8,128)(2,1)}, bf16[160,2048]{1,0:T(8,128)(2,1)}, u32[]{:S(2)}, u32[]{:S(2)}) %collective-permute-start.32) | collective-permute-done | bytes 655392 | tf_op jit(solution)/shard_map/ppermute | solution.py:736
  402.6 2.0 collective-permute-start.35
  404.6 2.0 collective-permute-start.38
  406.9 23.7 %attn_backward.4 = (bf16[384,1536]{1,0:T(8,128)(2,1)}, f32[1,1536]{1,0:T(1,128)S(1)}, bf16[384,2048]{1,0:T(8,128)(2,1)}, bf16[384,1536]{1,0:T(8,128)(2,1)}, f32[...) custom-call(bf16[160,2048]{1,0:T(8,128)(2,1)} %collective-permute-done.29.refs_0_.refs_14_, ...), custom_call_target="tpu_custom_call" | custom-call | flops 24000000 | bytes 1 | tf_op jit(solution)/shard_map/attn_backward/pallas_call | solution.py:294
  430.8 2.1 collective-permute-start.34
  433.8 14.5 %attn_backward.5 = (bf16[384,1536]{1,0:T(8,128)(2,1)}, f32[1,1536]{1,0:T(1,128)S(1)}, bf16[384,2048]{1,0:T(8,128)(2,1)}) custom-call(bf16[160,2048]{1,0:T(8,128)(2,1)} %copy-done.17, bf16[160,2048]{1,0:T(8,128)(2,1)} %copy-done.18, bf16[384,1536]{1,0:T(8,128)(2,1)} %get-tuple-element.226.refs_2_, f32[320,128]{1,0:T(8,128)S(1)} %get-tuple-element.149.refs_3_, ...), custom_call_target="tpu_custom_call" | custom-call | flops 12000000 | bytes 1 | tf_op jit(solution)/shard_map/attn_backward/pallas_call | solution.py:294
  448.3 1.6 collective-permute-start.39
  451.9 20.8 %attn_weight_grad.1 = bf16[2048,2048]{1,0:T(8,128)(2,1)} custom-call(bf16[384,2048]{1,0:T(8,128)(2,1)} %get-tuple-element.228.refs_0_, bf16[384,2048]{1,0:T(8,128)(2,1)} %get-tuple-element.229.refs_1_, bf16[384,2048]{1,0:T(8,128)(2,1)} %get-tuple-element.230.refs_2_, bf16[384,2048]{1,0:T(8,128)(2,1)} %get-tuple-element.231.refs_3_, ...), custom_call_target="tpu_custom_call" | custom-call | flops 21000000 | bytes 1 | tf_op jit(solution)/shard_map/attn_weight_grad/pallas_call | solution.py:521
  472.7 34.6 %collective-permute-done.40 = bf16[160,2048]{1,0:T(8,128)(2,1)S(1)} collective-permute-done((bf16[160,2048]{1,0:T(8,128)(2,1)}, bf16[160,2048]{1,0:T(8,128)(2,1)S(1)}, u32[]{:S(2)}, u32[]{:S(2)}) %collective-permute-start.40) | collective-permute-done | bytes 655392 | tf_op jit(solution)/shard_map/ppermute | solution.py:736
  507.4 8.9 %first_back.1 = (f32[320,2048]{1,0:T(8,128)}, bf16[64,2048]{1,0:T(8,128)(2,1)S(1)}, f32[2,2048]{1,0:T(2,128)S(1)}) custom-call(bf16[384,2048]{1,0:T(8,128)(2,1)} %get-tuple-element.242.refs_0_, bf16[384,2048]{1,0:T(8,128)(2,1)} %collective-permute-done.33.refs_1_, bf16[384,2048]{1,0:T(8,128)(2,1)} %collective-permute-done.34.refs_2_, ...), custom_call_target="tpu_custom_call" | custom-call | flops 499999997952 | bytes 1 | tf_op jit(solution)/shard_map/first_back/pallas_call | solution.py:685
  517.9 3.1 all-to-all-start.2
  521.1 1.4 collective-permute-start.44
  522.5 7.5 %all-to-all-done.2 = f32[32,1,768]{2,1,0:T(1,128)S(1)} async-done(((f32[32,1,768]{2,1,0:T(1,128)}), f32[32,1,768]{2,1,0:T(1,128)S(1)}, u32[]{:S(2)}, u32[]{:S(2)}) %all-to-all-start.2) | async-done | bytes 98336 | tf_op jit(solution)/shard_map/all_to_all | solution.py:798
  530.8 3.5 all-to-all-start.4
  534.5 2.0 collective-permute-start.42
  536.8 1.5 collective-permute-start.43
  538.3 1.6 convert_element_type.166
  541.7 21.5 %collective-permute-done.42 = bf16[160,2048]{1,0:T(8,128)(2,1)S(1)} collective-permute-done((bf16[160,2048]{1,0:T(8,128)(2,1)S(1)}, bf16[160,2048]{1,0:T(8,128)(2,1)S(1)}, u32[]{:S(2)}, u32[]{:S(2)}) %collective-permute-start.42) | collective-permute-done | bytes 655392 | tf_op jit(solution)/shard_map/ppermute | solution.py:736
  563.9 1.5 copy-done.9
  565.4 1.6 fusion.1
  567.0 2.1 slice.194
  569.0 3.5 all-to-all-start.3
  572.8 1.5 copy.85
  576.1 7.7 %all-to-all-done.3 = bf16[4,64,1536]{2,1,0:T(8,128)(2,1)S(1)} async-done(((bf16[4,64,1536]{2,1,0:T(8,128)(2,1)}), bf16[4,64,1536]{2,1,0:T(8,128)(2,1)S(1)}, u32[]{:S(2)}, u32[]{:S(2)}) %all-to-all-start.3) | async-done | bytes 786464 | tf_op jit(solution)/shard_map/all_to_all | solution.py:782
  (291 shorter events, 57.1 us)
Async XLA Ops:
  11.0 16.0 %all-to-all-start = ((bf16[4,64,1536]{2,1,0:T(8,128)(2,1)}), bf16[4,64,1536]{2,1,0:T(8,128)(2,1)S(1)}, u32[]{:S(2)}, u32[]{:S(2)}) async-start(bf16[4,64,1536]{2,1,0:T(8,128)(2,1)} %beside_blocks.1), calls=%async_computation | async-start | bytes 1572864 | tf_op jit(solution)/shard_map/all_to_all | solution.py:782
  16.2 100.7 %all-gather.4.cloned.1.call-start = ((), (), s32[]{:S(2)}) async-start(), calls=%async_computation.8 | async-start | bytes 9437184 | tf_op jit(solution)/shard_map/all_gather | solution.py:802
  28.3 188.6 %all-gather.6.cloned.1.call-start = ((), (), s32[]{:S(2)}) async-start(), calls=%async_computation.9 | async-start | bytes 9437184 | tf_op jit(solution)/shard_map/all_gather | solution.py:802
  28.5 3.7 collective-permute-start.1
  30.0 5.9 collective-permute-start
  32.2 3.7 collective-permute-start.2
  36.0 22.8 %copy-start.11 = (bf16[384,2048]{1,0:T(8,128)(2,1)}, bf16[384,2048]{1,0:T(8,128)(2,1)S(1)}, u32[]{:S(2)}) copy-start(bf16[384,2048]{1,0:T(8,128)(2,1)S(1)} %constant_dynamic-update-slice_fusion.refs_0_.refs_4_) | copy-start | bytes 4718596
  55.3 232.8 %all-gather.8.cloned.1.call-start = ((), (), s32[]{:S(2)}) async-start(), calls=%async_computation.10 | async-start | bytes 9437184 | tf_op jit(solution)/shard_map/all_gather | solution.py:802
  56.1 322.3 %reduce-scatter.4.cloned.1.call-start = ((), (), s32[]{:S(2)}) async-start(), calls=%async_computation.11 | async-start | bytes 9437184 | tf_op jit(solution)/shard_map/reduce_scatter | solution.py:806
  56.5 1.2 collective-permute-start.7
  57.8 36.5 %collective-permute-start.4 = (bf16[384,2048]{1,0:T(8,128)(2,1)S(1)}, bf16[384,2048]{1,0:T(8,128)(2,1)S(1)}, u32[]{:S(2)}, u32[]{:S(2)}) collective-permute-start(bf16[384,2048]{1,0:T(8,128)(2,1)S(1)} %constant_dynamic-update-slice_fusion.refs_0_.refs_4_), channel_id=1, source_target_pairs={{0,16},{8,24},{16,0},{24,8},{1,17},{9,25},{17,1},{25,9},{2,18},{10... | collective-permute-start | bytes 4718600 | tf_op jit(solution)/shard_map/ppermute | solution.py:736
  58.8 36.3 %collective-permute-start.3 = (bf16[384,2048]{1,0:T(8,128)(2,1)S(1)}, bf16[384,2048]{1,0:T(8,128)(2,1)}, u32[]{:S(2)}, u32[]{:S(2)}) collective-permute-start(bf16[384,2048]{1,0:T(8,128)(2,1)S(1)} %constant_dynamic-update-slice_fusion.refs_0_.refs_4_), channel_id=1, source_target_pairs={{0,8},{8,0},{16,24},{24,16},{1,9},{9,1},{17,25},{25,17},{2,10},{10... | collective-permute-start | bytes 4718600 | tf_op jit(solution)/shard_map/ppermute | solution.py:736
  59.3 5.7 collective-permute-start.8
  65.1 5.8 collective-permute-start.9
  97.2 19.6 %collective-permute-start.6 = (bf16[192,2048]{1,0:T(8,128)(2,1)S(1)}, bf16[192,2048]{1,0:T(8,128)(2,1)}, u32[]{:S(2)}, u32[]{:S(2)}) collective-permute-start(bf16[192,2048]{1,0:T(8,128)(2,1)S(1)} %slice.134), channel_id=1, source_target_pairs={{0,8},{8,0},{16,24},{24,16},{1,9},{9,1},{17,25},{25,17},{2,10},{10... | collective-permute-start | bytes 2359304 | tf_op jit(solution)/shard_map/ppermute | solution.py:736
  98.0 18.8 %collective-permute-start.5 = (bf16[192,2048]{1,0:T(8,128)(2,1)}, bf16[192,2048]{1,0:T(8,128)(2,1)S(1)}, u32[]{:S(2)}, u32[]{:S(2)}) collective-permute-start(bf16[192,2048]{1,0:T(8,128)(2,1)} %slice.133), channel_id=1, source_target_pairs={{0,16},{8,24},{16,0},{24,8},{1,17},{9,25},{17,1},{25,9},{2,18},{10... | collective-permute-start | bytes 2359304 | tf_op jit(solution)/shard_map/ppermute | solution.py:736
  133.6 29.3 %collective-permute-start.11 = (bf16[160,2048]{1,0:T(8,128)(2,1)}, bf16[160,2048]{1,0:T(8,128)(2,1)S(1)}, u32[]{:S(2)}, u32[]{:S(2)}) collective-permute-start(bf16[160,2048]{1,0:T(8,128)(2,1)} %get-tuple-element.153), channel_id=1, source_target_pairs={{0,16},{8,24},{16,0},{24,8},{1,17},{9,25},{17,1},{25,9},{2,18},{10... | collective-permute-start | bytes 1966088 | tf_op jit(solution)/shard_map/ppermute | solution.py:736
  133.9 45.6 %collective-permute-start.17 = (bf16[320,2048]{1,0:T(8,128)(2,1)S(1)}, bf16[320,2048]{1,0:T(8,128)(2,1)S(1)}, u32[]{:S(2)}, u32[]{:S(2)}) collective-permute-start(bf16[320,2048]{1,0:T(8,128)(2,1)S(1)} %copy-done.8), channel_id=1, source_target_pairs={{0,16},{8,24},{16,0},{24,8},{1,17},{9,25},{17,1},{25,9},{2,18},{10... | collective-permute-start | bytes 3932168 | tf_op jit(solution)/shard_map/ppermute | solution.py:736
  135.6 30.2 %collective-permute-start.13 = (bf16[160,2048]{1,0:T(8,128)(2,1)}, bf16[160,2048]{1,0:T(8,128)(2,1)S(1)}, u32[]{:S(2)}, u32[]{:S(2)}) collective-permute-start(bf16[160,2048]{1,0:T(8,128)(2,1)} %get-tuple-element.155), channel_id=1, source_target_pairs={{0,8},{8,0},{16,24},{24,16},{1,9},{9,1},{17,25},{25,17},{2,10},{10... | collective-permute-start | bytes 1966088 | tf_op jit(solution)/shard_map/ppermute | solution.py:736
  136.3 46.6 %collective-permute-start.16 = (bf16[320,2048]{1,0:T(8,128)(2,1)S(1)}, bf16[320,2048]{1,0:T(8,128)(2,1)}, u32[]{:S(2)}, u32[]{:S(2)}) collective-permute-start(bf16[320,2048]{1,0:T(8,128)(2,1)S(1)} %copy-done.8), channel_id=1, source_target_pairs={{0,8},{8,0},{16,24},{24,16},{1,9},{9,1},{17,25},{25,17},{2,10},{10... | collective-permute-start | bytes 3932168 | tf_op jit(solution)/shard_map/ppermute | solution.py:736
  162.2 36.4 %collective-permute-start.10 = (bf16[160,2048]{1,0:T(8,128)(2,1)}, bf16[160,2048]{1,0:T(8,128)(2,1)S(1)}, u32[]{:S(2)}, u32[]{:S(2)}) collective-permute-start(bf16[160,2048]{1,0:T(8,128)(2,1)} %get-tuple-element.151), channel_id=1, source_target_pairs={{0,8},{8,0},{16,24},{24,16},{1,9},{9,1},{17,25},{25,17},{2,10},{10... | collective-permute-start | bytes 1966088 | tf_op jit(solution)/shard_map/ppermute | solution.py:736
  162.9 35.7 %collective-permute-start.15 = (bf16[160,2048]{1,0:T(8,128)(2,1)}, bf16[160,2048]{1,0:T(8,128)(2,1)}, u32[]{:S(2)}, u32[]{:S(2)}) collective-permute-start(bf16[160,2048]{1,0:T(8,128)(2,1)} %get-tuple-element.156), channel_id=1, source_target_pairs={{0,16},{8,24},{16,0},{24,8},{1,17},{9,25},{17,1},{25,9},{2,18},{10... | collective-permute-start | bytes 1966088 | tf_op jit(solution)/shard_map/ppermute | solution.py:736
  165.8 39.9 %collective-permute-start.12 = (bf16[160,2048]{1,0:T(8,128)(2,1)}, bf16[160,2048]{1,0:T(8,128)(2,1)}, u32[]{:S(2)}, u32[]{:S(2)}) collective-permute-start(bf16[160,2048]{1,0:T(8,128)(2,1)} %add_convert_fusion.3), channel_id=1, source_target_pairs={{0,8},{8,0},{16,24},{24,16},{1,9},{9,1},{17,25},{25,17},{2,10},{10... | collective-permute-start | bytes 1966088 | tf_op jit(solution)/shard_map/ppermute | solution.py:736
  179.5 26.1 %collective-permute-start.14 = (bf16[160,2048]{1,0:T(8,128)(2,1)}, bf16[160,2048]{1,0:T(8,128)(2,1)}, u32[]{:S(2)}, u32[]{:S(2)}) collective-permute-start(bf16[160,2048]{1,0:T(8,128)(2,1)} %add_convert_fusion.2), channel_id=1, source_target_pairs={{0,16},{8,24},{16,0},{24,8},{1,17},{9,25},{17,1},{25,9},{2,18},{10... | collective-permute-start | bytes 1966088 | tf_op jit(solution)/shard_map/ppermute | solution.py:736
  212.6 17.7 %collective-permute-start.20 = (bf16[160,2048]{1,0:T(8,128)(2,1)S(1)}, bf16[160,2048]{1,0:T(8,128)(2,1)S(1)}, u32[]{:S(2)}, u32[]{:S(2)}) collective-permute-start(bf16[160,2048]{1,0:T(8,128)(2,1)S(1)} %get-tuple-element.164.refs_0_.refs_6_), channel_id=1, source_target_pairs={{0,16},{8,24},{16,0},{24,8},{1,17},{9,25},{17,1},{25,9},{2,18},{10... | collective-permute-start | bytes 1966088 | tf_op jit(solution)/shard_map/ppermute | solution.py:736
  213.0 17.7 %collective-permute-start.18 = (bf16[160,2048]{1,0:T(8,128)(2,1)S(1)}, bf16[160,2048]{1,0:T(8,128)(2,1)S(1)}, u32[]{:S(2)}, u32[]{:S(2)}) collective-permute-start(bf16[160,2048]{1,0:T(8,128)(2,1)S(1)} %get-tuple-element.164.refs_0_.refs_6_), channel_id=1, source_target_pairs={{0,8},{8,0},{16,24},{24,16},{1,9},{9,1},{17,25},{25,17},{2,10},{10... | collective-permute-start | bytes 1966088 | tf_op jit(solution)/shard_map/ppermute | solution.py:736
  214.0 27.4 %collective-permute-start.21 = (bf16[160,2048]{1,0:T(8,128)(2,1)}, bf16[160,2048]{1,0:T(8,128)(2,1)}, u32[]{:S(2)}, u32[]{:S(2)}) collective-permute-start(bf16[160,2048]{1,0:T(8,128)(2,1)} %get-tuple-element.165.refs_1_.refs_7_), channel_id=1, source_target_pairs={{0,16},{8,24},{16,0},{24,8},{1,17},{9,25},{17,1},{25,9},{2,18},{10... | collective-permute-start | bytes 1966088 | tf_op jit(solution)/shard_map/ppermute | solution.py:736
  215.4 26.1 %collective-permute-start.19 = (bf16[160,2048]{1,0:T(8,128)(2,1)}, bf16[160,2048]{1,0:T(8,128)(2,1)}, u32[]{:S(2)}, u32[]{:S(2)}) collective-permute-start(bf16[160,2048]{1,0:T(8,128)(2,1)} %get-tuple-element.165.refs_1_.refs_7_), channel_id=1, source_target_pairs={{0,8},{8,0},{16,24},{24,16},{1,9},{9,1},{17,25},{25,17},{2,10},{10... | collective-permute-start | bytes 1966088 | tf_op jit(solution)/shard_map/ppermute | solution.py:736
  230.7 26.9 %copy-start = (bf16[160,2048]{1,0:T(8,128)(2,1)}, bf16[160,2048]{1,0:T(8,128)(2,1)S(1)}, u32[]{:S(2)}) copy-start(bf16[160,2048]{1,0:T(8,128)(2,1)S(1)} %collective-permute-done.18.refs_0_.refs_4_) | copy-start | bytes 1966084
  241.5 18.1 %collective-permute-start.22 = (bf16[160,2048]{1,0:T(8,128)(2,1)S(1)}, bf16[160,2048]{1,0:T(8,128)(2,1)S(1)}, u32[]{:S(2)}, u32[]{:S(2)}) collective-permute-start(bf16[160,2048]{1,0:T(8,128)(2,1)S(1)} %collective-permute-done.18.refs_0_.refs_4_), channel_id=1, source_target_pairs={{0,16},{8,24},{16,0},{24,8},{1,17},{9,25},{17,1},{25,9},{2,18},{10... | collective-permute-start | bytes 1966088 | tf_op jit(solution)/shard_map/ppermute | solution.py:736
  243.0 16.6 %collective-permute-start.23 = (bf16[160,2048]{1,0:T(8,128)(2,1)}, bf16[160,2048]{1,0:T(8,128)(2,1)S(1)}, u32[]{:S(2)}, u32[]{:S(2)}) collective-permute-start(bf16[160,2048]{1,0:T(8,128)(2,1)} %collective-permute-done.21.refs_3_), channel_id=1, source_target_pairs={{0,8},{8,0},{16,24},{24,16},{1,9},{9,1},{17,25},{25,17},{2,10},{10... | collective-permute-start | bytes 1966088 | tf_op jit(solution)/shard_map/ppermute | solution.py:736
  257.6 12.4 %collective-permute-start.24 = (bf16[160,2048]{1,0:T(8,128)(2,1)S(1)}, bf16[160,2048]{1,0:T(8,128)(2,1)S(1)}, u32[]{:S(2)}, u32[]{:S(2)}) collective-permute-start(bf16[160,2048]{1,0:T(8,128)(2,1)S(1)} %copy-done.24), channel_id=1, source_target_pairs={{0,16},{8,24},{16,0},{24,8},{1,17},{9,25},{17,1},{25,9},{2,18},{10... | collective-permute-start | bytes 1966088 | tf_op jit(solution)/shard_map/ppermute | solution.py:736
  258.3 11.8 %collective-permute-start.25 = (bf16[160,2048]{1,0:T(8,128)(2,1)S(1)}, bf16[160,2048]{1,0:T(8,128)(2,1)S(1)}, u32[]{:S(2)}, u32[]{:S(2)}) collective-permute-start(bf16[160,2048]{1,0:T(8,128)(2,1)S(1)} %copy-done.23), channel_id=1, source_target_pairs={{0,8},{8,0},{16,24},{24,16},{1,9},{9,1},{17,25},{25,17},{2,10},{10... | collective-permute-start | bytes 1966088 | tf_op jit(solution)/shard_map/ppermute | solution.py:736
  288.0 184.6 %reduce-scatter.6.cloned.1.call-start = ((), (), s32[]{:S(2)}) async-start(), calls=%async_computation.12 | async-start | bytes 9437184 | tf_op jit(solution)/shard_map/reduce_scatter | solution.py:806
  314.1 52.5 %collective-permute-start.26 = (bf16[320,2048]{1,0:T(8,128)(2,1)}, bf16[320,2048]{1,0:T(8,128)(2,1)}, u32[]{:S(2)}, u32[]{:S(2)}) collective-permute-start(bf16[320,2048]{1,0:T(8,128)(2,1)} %get-tuple-element.196), channel_id=1, source_target_pairs={{0,8},{8,0},{16,24},{24,16},{1,9},{9,1},{17,25},{25,17},{2,10},{10... | collective-permute-start | bytes 3932168 | tf_op jit(solution)/shard_map/ppermute | solution.py:736
  314.7 51.9 %collective-permute-start.27 = (bf16[320,2048]{1,0:T(8,128)(2,1)}, bf16[320,2048]{1,0:T(8,128)(2,1)}, u32[]{:S(2)}, u32[]{:S(2)}) collective-permute-start(bf16[320,2048]{1,0:T(8,128)(2,1)} %get-tuple-element.197), channel_id=1, source_target_pairs={{0,16},{8,24},{16,0},{24,8},{1,17},{9,25},{17,1},{25,9},{2,18},{10... | collective-permute-start | bytes 3932168 | tf_op jit(solution)/shard_map/ppermute | solution.py:736
  316.2 51.0 %collective-permute-start.28 = (bf16[320,2048]{1,0:T(8,128)(2,1)}, bf16[320,2048]{1,0:T(8,128)(2,1)}, u32[]{:S(2)}, u32[]{:S(2)}) collective-permute-start(bf16[320,2048]{1,0:T(8,128)(2,1)} %get-tuple-element.198), channel_id=1, source_target_pairs={{0,24},{8,16},{16,8},{24,0},{1,25},{9,17},{17,9},{25,1},{2,26},{10... | collective-permute-start | bytes 3932168 | tf_op jit(solution)/shard_map/ppermute | solution.py:736
  367.2 199.8 %reduce-scatter.8.cloned.1.call-start = ((), (), s32[]{:S(2)}) async-start(), calls=%async_computation.13 | async-start | bytes 9437184 | tf_op jit(solution)/shard_map/reduce_scatter | solution.py:806
  374.3 18.4 %collective-permute-start.31 = (bf16[160,2048]{1,0:T(8,128)(2,1)S(1)}, bf16[160,2048]{1,0:T(8,128)(2,1)S(1)}, u32[]{:S(2)}, u32[]{:S(2)}) collective-permute-start(bf16[160,2048]{1,0:T(8,128)(2,1)S(1)} %get-tuple-element.206.refs_0_.refs_12_), channel_id=1, source_target_pairs={{0,16},{8,24},{16,0},{24,8},{1,17},{9,25},{17,1},{25,9},{2,18},{10... | collective-permute-start | bytes 1966088 | tf_op jit(solution)/shard_map/ppermute | solution.py:736
  375.1 17.6 %collective-permute-start.29 = (bf16[160,2048]{1,0:T(8,128)(2,1)S(1)}, bf16[160,2048]{1,0:T(8,128)(2,1)}, u32[]{:S(2)}, u32[]{:S(2)}) collective-permute-start(bf16[160,2048]{1,0:T(8,128)(2,1)S(1)} %get-tuple-element.206.refs_0_.refs_12_), channel_id=1, source_target_pairs={{0,8},{8,0},{16,24},{24,16},{1,9},{9,1},{17,25},{25,17},{2,10},{10... | collective-permute-start | bytes 1966088 | tf_op jit(solution)/shard_map/ppermute | solution.py:736
  376.6 25.9 %collective-permute-start.32 = (bf16[160,2048]{1,0:T(8,128)(2,1)}, bf16[160,2048]{1,0:T(8,128)(2,1)}, u32[]{:S(2)}, u32[]{:S(2)}) collective-permute-start(bf16[160,2048]{1,0:T(8,128)(2,1)} %get-tuple-element.207.refs_1_.refs_13_), channel_id=1, source_target_pairs={{0,16},{8,24},{16,0},{24,8},{1,17},{9,25},{17,1},{25,9},{2,18},{10... | collective-permute-start | bytes 1966088 | tf_op jit(solution)/shard_map/ppermute | solution.py:736
  377.3 25.2 %collective-permute-start.30 = (bf16[160,2048]{1,0:T(8,128)(2,1)}, bf16[160,2048]{1,0:T(8,128)(2,1)}, u32[]{:S(2)}, u32[]{:S(2)}) collective-permute-start(bf16[160,2048]{1,0:T(8,128)(2,1)} %get-tuple-element.207.refs_1_.refs_13_), channel_id=1, source_target_pairs={{0,8},{8,0},{16,24},{24,16},{1,9},{9,1},{17,25},{25,17},{2,10},{10... | collective-permute-start | bytes 1966088 | tf_op jit(solution)/shard_map/ppermute | solution.py:736
  378.5 26.0 %copy-start.55 = (bf16[160,2048]{1,0:T(8,128)(2,1)S(1)}, bf16[160,2048]{1,0:T(8,128)(2,1)}, u32[]{:S(2)}) copy-start(bf16[160,2048]{1,0:T(8,128)(2,1)} %get-tuple-element.224) | copy-start | bytes 1966084
  378.5 28.1 %copy-start.43 = (f32[384]{0:T(512)S(1)}, f32[384]{0:T(512)}, u32[]{:S(2)}) copy-start(f32[384]{0:T(512)} %get-tuple-element.370) | copy-start | bytes 4612
  378.5 28.2 %copy-start.42 = (f32[384]{0:T(512)S(1)}, f32[384]{0:T(512)}, u32[]{:S(2)}) copy-start(f32[384]{0:T(512)} %get-tuple-element.371) | copy-start | bytes 4612
  402.6 28.2 %collective-permute-start.35 = (bf16[160,2048]{1,0:T(8,128)(2,1)}, bf16[160,2048]{1,0:T(8,128)(2,1)S(1)}, u32[]{:S(2)}, u32[]{:S(2)}) collective-permute-start(bf16[160,2048]{1,0:T(8,128)(2,1)} %collective-permute-done.29.refs_0_.refs_14_), channel_id=1, source_target_pairs={{0,16},{8,24},{16,0},{24,8},{1,17},{9,25},{17,1},{25,9},{2,18},{10... | collective-permute-start | bytes 1966088 | tf_op jit(solution)/shard_map/ppermute | solution.py:736
  404.5 28.3 %collective-permute-start.36 = (bf16[160,2048]{1,0:T(8,128)(2,1)S(1)}, bf16[160,2048]{1,0:T(8,128)(2,1)S(1)}, u32[]{:S(2)}, u32[]{:S(2)}) collective-permute-start(bf16[160,2048]{1,0:T(8,128)(2,1)S(1)} %get-tuple-element.223), channel_id=1, source_target_pairs={{0,8},{8,0},{16,24},{24,16},{1,9},{9,1},{17,25},{25,17},{2,10},{10... | collective-permute-start | bytes 1966088 | tf_op jit(solution)/shard_map/ppermute | solution.py:736
  404.5 28.3 %collective-permute-start.37 = (bf16[160,2048]{1,0:T(8,128)(2,1)S(1)}, bf16[160,2048]{1,0:T(8,128)(2,1)S(1)}, u32[]{:S(2)}, u32[]{:S(2)}) collective-permute-start(bf16[160,2048]{1,0:T(8,128)(2,1)S(1)} %copy-done.55), channel_id=1, source_target_pairs={{0,16},{8,24},{16,0},{24,8},{1,17},{9,25},{17,1},{25,9},{2,18},{10... | collective-permute-start | bytes 1966088 | tf_op jit(solution)/shard_map/ppermute | solution.py:736
  404.6 28.3 %collective-permute-start.38 = (bf16[160,2048]{1,0:T(8,128)(2,1)}, bf16[160,2048]{1,0:T(8,128)(2,1)S(1)}, u32[]{:S(2)}, u32[]{:S(2)}) collective-permute-start(bf16[160,2048]{1,0:T(8,128)(2,1)} %collective-permute-done.32.refs_3_.refs_17_), channel_id=1, source_target_pairs={{0,8},{8,0},{16,24},{24,16},{1,9},{9,1},{17,25},{25,17},{2,10},{10... | collective-permute-start | bytes 1966088 | tf_op jit(solution)/shard_map/ppermute | solution.py:736
  430.6 76.7 %collective-permute-start.33 = (bf16[384,2048]{1,0:T(8,128)(2,1)}, bf16[384,2048]{1,0:T(8,128)(2,1)}, u32[]{:S(2)}, u32[]{:S(2)}) collective-permute-start(bf16[384,2048]{1,0:T(8,128)(2,1)} %get-tuple-element.220), channel_id=1, source_target_pairs={{0,8},{8,0},{16,24},{24,16},{1,9},{9,1},{17,25},{25,17},{2,10},{10... | collective-permute-start | bytes 4718600 | tf_op jit(solution)/shard_map/ppermute | solution.py:736
  430.8 76.6 %collective-permute-start.34 = (bf16[384,2048]{1,0:T(8,128)(2,1)}, bf16[384,2048]{1,0:T(8,128)(2,1)}, u32[]{:S(2)}, u32[]{:S(2)}) collective-permute-start(bf16[384,2048]{1,0:T(8,128)(2,1)} %get-tuple-element.221), channel_id=1, source_target_pairs={{0,16},{8,24},{16,0},{24,8},{1,17},{9,25},{17,1},{25,9},{2,18},{10... | collective-permute-start | bytes 4718600 | tf_op jit(solution)/shard_map/ppermute | solution.py:736
  448.3 59.0 %collective-permute-start.39 = (bf16[384,2048]{1,0:T(8,128)(2,1)}, bf16[384,2048]{1,0:T(8,128)(2,1)}, u32[]{:S(2)}, u32[]{:S(2)}) collective-permute-start(bf16[384,2048]{1,0:T(8,128)(2,1)} %get-tuple-element.227), channel_id=1, source_target_pairs={{0,24},{8,16},{16,8},{24,0},{1,25},{9,17},{17,9},{25,1},{2,26},{10... | collective-permute-start | bytes 4718600 | tf_op jit(solution)/shard_map/ppermute | solution.py:736
  450.0 57.4 %collective-permute-start.40 = (bf16[160,2048]{1,0:T(8,128)(2,1)}, bf16[160,2048]{1,0:T(8,128)(2,1)S(1)}, u32[]{:S(2)}, u32[]{:S(2)}) collective-permute-start(bf16[160,2048]{1,0:T(8,128)(2,1)} %get-tuple-element.240), channel_id=1, source_target_pairs={{0,8},{8,0},{16,24},{24,16},{1,9},{9,1},{17,25},{25,17},{2,10},{10... | collective-permute-start | bytes 1966088 | tf_op jit(solution)/shard_map/ppermute | solution.py:736
  450.6 56.7 %collective-permute-start.41 = (bf16[160,2048]{1,0:T(8,128)(2,1)S(1)}, bf16[160,2048]{1,0:T(8,128)(2,1)S(1)}, u32[]{:S(2)}, u32[]{:S(2)}) collective-permute-start(bf16[160,2048]{1,0:T(8,128)(2,1)S(1)} %copy-done.54), channel_id=1, source_target_pairs={{0,16},{8,24},{16,0},{24,8},{1,17},{9,25},{17,1},{25,9},{2,18},{10... | collective-permute-start | bytes 1966088 | tf_op jit(solution)/shard_map/ppermute | solution.py:736
  517.9 12.1 %all-to-all-start.2 = ((f32[32,1,768]{2,1,0:T(1,128)}), f32[32,1,768]{2,1,0:T(1,128)S(1)}, u32[]{:S(2)}, u32[]{:S(2)}) async-start(f32[32,1,768]{2,1,0:T(1,128)} %all_to_all.20), calls=%async_computation.3 | async-start | bytes 196608 | tf_op jit(solution)/shard_map/all_to_all | solution.py:798
  521.1 19.4 %collective-permute-start.44 = (bf16[50,2048]{1,0:T(8,128)(2,1)S(1)}, bf16[50,2048]{1,0:T(8,128)(2,1)S(1)}, u32[]{:S(2)}, u32[]{:S(2)}) collective-permute-start(bf16[50,2048]{1,0:T(8,128)(2,1)S(1)} %slice.159), channel_id=1, source_target_pairs={{1,0},{2,1},{3,2},{4,3},{5,4},{6,5},{7,6},{8,7},{9,8},{10,9},{11,1... | collective-permute-start | bytes 614408 | tf_op jit(solution)/shard_map/ppermute | solution.py:1030
  530.8 38.3 %all-to-all-start.4 = ((bf16[4,64,2048]{2,1,0:T(8,128)(2,1)}), bf16[4,64,2048]{2,1,0:T(8,128)(2,1)S(1)}, u32[]{:S(2)}, u32[]{:S(2)}) async-start(bf16[4,64,2048]{2,1,0:T(8,128)(2,1)} %reduce-scatter.6.cloned.1.call-done), calls=%async_computation.7 | async-start | bytes 2097152 | tf_op jit(solution)/shard_map/all_to_all | solution.py:782
  534.5 28.7 %collective-permute-start.42 = (bf16[160,2048]{1,0:T(8,128)(2,1)S(1)}, bf16[160,2048]{1,0:T(8,128)(2,1)S(1)}, u32[]{:S(2)}, u32[]{:S(2)}) collective-permute-start(bf16[160,2048]{1,0:T(8,128)(2,1)S(1)} %add_convert_fusion.1), channel_id=1, source_target_pairs={{0,16},{8,24},{16,0},{24,8},{1,17},{9,25},{17,1},{25,9},{2,18},{10... | collective-permute-start | bytes 1966088 | tf_op jit(solution)/shard_map/ppermute | solution.py:736
  536.8 26.8 %collective-permute-start.43 = (bf16[160,2048]{1,0:T(8,128)(2,1)S(1)}, bf16[160,2048]{1,0:T(8,128)(2,1)S(1)}, u32[]{:S(2)}, u32[]{:S(2)}) collective-permute-start(bf16[160,2048]{1,0:T(8,128)(2,1)S(1)} %add_convert_fusion), channel_id=1, source_target_pairs={{0,8},{8,0},{16,24},{24,16},{1,9},{9,1},{17,25},{25,17},{2,10},{10... | collective-permute-start | bytes 1966088 | tf_op jit(solution)/shard_map/ppermute | solution.py:736
  539.9 23.4 %copy-start.26 = (bf16[160,2048]{1,0:T(8,128)(2,1)S(1)}, bf16[160,2048]{1,0:T(8,128)(2,1)}, u32[]{:S(2)}) copy-start(bf16[160,2048]{1,0:T(8,128)(2,1)} %get-tuple-element.260) | copy-start | bytes 1966084
  539.9 23.4 %copy-start.36 = (bf16[160,2048]{1,0:T(8,128)(2,1)S(1)}, bf16[160,2048]{1,0:T(8,128)(2,1)}, u32[]{:S(2)}) copy-start(bf16[160,2048]{1,0:T(8,128)(2,1)} %copy-done.35) | copy-start | bytes 1966084
  541.7 21.9 %copy-start.25 = (bf16[160,2048]{1,0:T(8,128)(2,1)S(1)}, bf16[160,2048]{1,0:T(8,128)(2,1)}, u32[]{:S(2)}) copy-start(bf16[160,2048]{1,0:T(8,128)(2,1)} %get-tuple-element.262) | copy-start | bytes 1966084
  541.7 21.9 %copy-start.34 = (bf16[160,2048]{1,0:T(8,128)(2,1)S(1)}, bf16[160,2048]{1,0:T(8,128)(2,1)}, u32[]{:S(2)}) copy-start(bf16[160,2048]{1,0:T(8,128)(2,1)} %copy-done.33) | copy-start | bytes 1966084
  569.0 14.8 %all-to-all-start.3 = ((bf16[4,64,1536]{2,1,0:T(8,128)(2,1)}), bf16[4,64,1536]{2,1,0:T(8,128)(2,1)S(1)}, u32[]{:S(2)}, u32[]{:S(2)}) async-start(bf16[4,64,1536]{2,1,0:T(8,128)(2,1)} %slice.194), calls=%async_computation.6 | async-start | bytes 1572864 | tf_op jit(solution)/shard_map/all_to_all | solution.py:782
  (49 other events, 300.2 us)
Sparse Core Ops, SparseCore 0:
  28.4 83.5 all-gather.3
  113.6 80.4 all-gather.5
  195.7 80.6 all-gather.7
  288.2 89.0 reduce-scatter.3
  379.4 87.9 reduce-scatter.5
  472.8 91.7 reduce-scatter.7

commit v8 on v7

--- a/solution.py
+++ b/solution.py
@@ -579,7 +579,7 @@
     seg, width = tokens.shape
     count = len(parts)
     rows = seg // 2
-    step = 32
+    step = 80
 
     def kernel(*refs):
         tokens_ref, off_ref, gain_ref, bias_ref, middle_ref, *seconds = refs[2 * count :]
@@ -902,8 +902,6 @@
     previous = []
     for some in ([[3], [1, 2], [0]] if members == 4 else [[rel] for rel in own_last]):
         xs = [group_joined[rel] for rel in some]
-        if some == [0]:
-            previous = previous + flat_list(cot_near)
         xs[0] = [after(xs[0][0], *previous), *xs[0][1:]]
         oks = jnp.concatenate([ok_rows[rel : rel + 1] for rel in some], 0)
         outs = attn_forward(

time: 597 us -> 597 us (level)
  no operation moved by 1% of the time
where the time goes in v8:
time: 597 us; the launch traced here: 593 us
  Pallas kernels  275 us (46%)
  waiting for transfers between devices  170 us (28%)
  starting transfers between devices  63.9 us (11%)
  local copies, waits for them, and re-layouts  34.7 us (6%)
  blocking collectives  18.7 us (3%)
  between operations  15.7 us (3%)
  other arithmetic  14.6 us (2%)
    ppermute x38, waiting for transfers between devices, swap(): return lax.ppermute(value, 'fsdp', [(i, i ^ rel) for i in range(count)])  134 us
    pallas_call x3, Pallas kernels, attn_forward(): pl.pallas_call(kernel, out_shape=shapes, in_specs=[HBM] * given + [VMEM]...  53.3 us
    pallas_call x3, Pallas kernels, attn_backward(): pl.pallas_call(kernel, out_shape=shapes, in_specs=[HBM] * given + [VMEM]...  52.7 us
    ppermute x38, starting transfers between devices, swap(): return lax.ppermute(value, 'fsdp', [(i, i ^ rel) for i in range(count)])  39.7 us
    pallas_call x2, Pallas kernels, ffn_back(): pl.pallas_call(kernel, out_shape=(shape_of(rows, wide), shape_of(1, wide,...  38.7 us
    pallas_call x2, Pallas kernels, weight_grad(): pl.pallas_call(kernel, grid=(tall // rows_each,), out_shape=shape_of(tall...  34.5 us
    pallas_call x3, Pallas kernels, ffn_hidden(): pl.pallas_call(kernel, out_shape=[shape_of(seg, wide)] * (2 * count), in_...  33.2 us
    pallas_call x1, Pallas kernels, attn_weight_grad(): pl.pallas_call(kernel, grid=(width // rows_each,), out_shape=shape_of(wid...  20.7 us
  transfers between devices with their start and end apart: 55, of which 20 were waited for; matrix products, arithmetic and copies ran while one was open for 6% of the time, Pallas kernels for 46%

profile of v8, /device:TPU:0, one launch (start us, length us, event | category | flops | bytes accessed | tf_op | source)
XLA Modules:
  0.0 593.0 jit_solution(8645017863044026758)
XLA Ops:
  11.0 5.2 all-to-all-start
  16.2 10.8 %all-to-all-done = bf16[4,64,1536]{2,1,0:T(8,128)(2,1)S(1)} async-done(((bf16[4,64,1536]{2,1,0:T(8,128)(2,1)}), bf16[4,64,1536]{2,1,0:T(8,128)(2,1)S(1)}, u32[]{:S(2)}, u32[]{:S(2)}) %all-to-all-start) | async-done | bytes 786464 | tf_op jit(solution)/shard_map/all_to_all | solution.py:782
  28.5 1.5 collective-permute-start.1
  32.2 1.5 collective-permute-start.2
  33.9 1.8 reshape.197
  36.6 18.7 %all_to_all.29 = bf16[4,64,2048]{2,1,0:T(8,128)(2,1)} all-to-all(bf16[4,64,2048]{2,1,0:T(8,128)(2,1)S(1)} %copy.71), channel_id=1, replica_groups=mesh['fsdp'=4,'dp'=8] {'fsdp'}, dimensions={0} | all-to-all | bytes 2097152 | tf_op jit(solution)/shard_map/all_to_all | solution.py:782
  59.3 1.6 collective-permute-start.8
  61.0 4.0 collective-permute-done.8
  67.3 3.6 collective-permute-done.9
  73.0 21.3 %collective-permute-done.4.refs_1_ = bf16[384,2048]{1,0:T(8,128)(2,1)S(1)} collective-permute-done((bf16[384,2048]{1,0:T(8,128)(2,1)S(1)}, bf16[384,2048]{1,0:T(8,128)(2,1)S(1)}, u32[]{:S(2)}, u32[]{:S(2)}) %collective-permute-start.4) | collective-permute-done | bytes 1572896 | tf_op jit(solution)/shard_map/ppermute | solution.py:736
  95.1 2.1 slice.133
  104.4 12.5 %collective-permute-done.5.refs_0_ = bf16[192,2048]{1,0:T(8,128)(2,1)S(1)} collective-permute-done((bf16[192,2048]{1,0:T(8,128)(2,1)}, bf16[192,2048]{1,0:T(8,128)(2,1)S(1)}, u32[]{:S(2)}, u32[]{:S(2)}) %collective-permute-start.5) | collective-permute-done | bytes 786464 | tf_op jit(solution)/shard_map/ppermute | solution.py:736
  117.7 15.1 %attn_forward.3 = (bf16[384,2048]{1,0:T(8,128)(2,1)}, bf16[384,1536]{1,0:T(8,128)(2,1)}, f32[320,128]{1,0:T(8,128)S(1)}, bf16[320,512]{1,0:T(8,128)(2,1)S(1)}, b...) custom-call(bf16[192,2048]{1,0:T(8,128)(2,1)} %copy-done.21, bf16[192,2048]{1,0:T(8,128)(2,1)} %collective-permute-done.6.refs_1_, ...), custom_call_target="tpu_custom_call" | custom-call | flops 12000000 | bytes 1 | tf_op jit(solution)/shard_map/attn_forward/pallas_call | solution.py:194
  133.9 1.7 collective-permute-start.17
  137.6 24.5 %attn_forward.4 = (bf16[384,2048]{1,0:T(8,128)(2,1)}, bf16[384,1536]{1,0:T(8,128)(2,1)}, f32[320,128]{1,0:T(8,128)S(1)}, bf16[320,512]{1,0:T(8,128)(2,1)S(1)}, b...) custom-call(bf16[384,2048]{1,0:T(8,128)(2,1)} %collective-permute-do, ...), custom_call_target="tpu_custom_call" | custom-call | flops 24000000 | bytes 1 | tf_op jit(solution)/shard_map/attn_forward/pallas_call | solution.py:194
  163.6 2.2 add_convert_fusion.3
  167.8 11.7 %collective-permute-done.17.refs_6_.refs_2_ = bf16[320,2048]{1,0:T(8,128)(2,1)S(1)} collective-permute-done((bf16[320,2048]{1,0:T(8,128)(2,1)S(1)}, bf16[320,2048]{1,0:T(8,128)(2,1)S(1)}, u32[]{:S(2)}, u32[]{:S(2)}) %collective-permute-start.17) | collective-permute-done | bytes 1310752 | tf_op jit(solution)/shard_map/ppermute | solution.py:736
  180.9 2.0 slice.184
  182.9 2.0 slice.183
  184.9 13.7 %attn_forward.5 = (bf16[384,2048]{1,0:T(8,128)(2,1)}, bf16[384,1536]{1,0:T(8,128)(2,1)}, f32[320,128]{1,0:T(8,128)S(1)}, bf16[320,512]{1,0:T(8,128)(2,1)S(1)}, b...) custom-call(bf16[384,2048]{1,0:T(8,128)(2,1)} %copy-done.11, f32[1,2048]{1,0:T(1,128)S(1)} %reshape.229.refs_2_.refs_1_.refs_6_, ...), custom_call_target="tpu_custom_call" | custom-call | flops 12000000 | bytes 1 | tf_op jit(solution)/shard_map/attn_forward/pallas_call | solution.py:194
  198.6 7.0 %collective-permute-done.12.refs_1_ = bf16[160,2048]{1,0:T(8,128)(2,1)} collective-permute-done((bf16[160,2048]{1,0:T(8,128)(2,1)}, bf16[160,2048]{1,0:T(8,128)(2,1)}, u32[]{:S(2)}, u32[]{:S(2)}) %collective-permute-start.12) | collective-permute-done | bytes 655392 | tf_op jit(solution)/shard_map/ppermute | solution.py:736
  205.7 5.7 middle_norm.1
  212.8 1.4 collective-permute-start.21
  215.6 9.7 %ffn_hidden.3 = (bf16[320,2048]{1,0:T(8,128)(2,1)}, bf16[320,2048]{1,0:T(8,128)(2,1)}) custom-call(bf16[160,2048]{1,0:T(8,128)(2,1)S(1)} %get-tuple-element.164.refs_0_.refs_6_, bf16[160,2048]{1,0:T(8,128)(2,1)} %get-tuple-element.165.refs_1_.refs_7_, f32[1,2048]{1,0:T(1,128)S(1)} %constant_dynamic-slice_fusion.refs_2_.refs_4_, bf16[8,4,64,2048]{3,2,1,0:T(8,128)(2,1)} %bitcast.59), custom_call_target="tpu_custom_call" | custom-call | flops 6000000 | bytes 1 | tf_op jit(solution)/shard_map/ffn_hidden/pallas_call | solution.py:344
  225.3 3.8 collective-permute-done.20.refs_2_
  229.5 10.8 %collective-permute-done.21.refs_3_ = bf16[160,2048]{1,0:T(8,128)(2,1)} collective-permute-done((bf16[160,2048]{1,0:T(8,128)(2,1)}, bf16[160,2048]{1,0:T(8,128)(2,1)}, u32[]{:S(2)}, u32[]{:S(2)}) %collective-permute-start.21) | collective-permute-done | bytes 655392 | tf_op jit(solution)/shard_map/ppermute | solution.py:736
  240.3 1.5 collective-permute-start.22
  242.6 13.9 %ffn_hidden.4 = (bf16[320,2048]{1,0:T(8,128)(2,1)}, bf16[320,2048]{1,0:T(8,128)(2,1)}, bf16[320,2048]{1,0:T(8,128)(2,1)}, bf16[320,2048]{1,0:T(8,128)(2,1)}) custom-call(bf16[160,2048]{1,0:T(8,128)(2,1)S(1)} %collective-permute-done.18.refs_0_.refs_4_, bf16[160,2048]{1,0:T(8,128)(2,1)} %collective-permute-done.19.refs_1_.refs_5_, ...), custom_call_target="tpu_custom_call" | custom-call | flops 12000000 | bytes 1 | tf_op jit(solution)/shard_map/ffn_hidden/pallas_call | solution.py:344
  259.4 9.6 %ffn_hidden.5 = (bf16[320,2048]{1,0:T(8,128)(2,1)}, bf16[320,2048]{1,0:T(8,128)(2,1)}) custom-call(bf16[160,2048]{1,0:T(8,128)(2,1)S(1)} %collective-permute-done.22.refs_0_, bf16[160,2048]{1,0:T(8,128)(2,1)} %copy-done.19, f32[1,2048]{1,0:T(1,128)S(1)} %constant_dynamic-slice_fusion.refs_2_.refs_4_, bf16[8,4,64,2048]{3,2,1,0:T(8,128)(2,1)} %bitcast.61), custom_call_target="tpu_custom_call" | custom-call | flops 6000000 | bytes 1 | tf_op jit(solution)/shard_map/ffn_hidden/pallas_call | solution.py:344
  269.9 17.2 %weight_grad.2 = bf16[2048,2048]{1,0:T(8,128)(2,1)} custom-call(bf16[320,2048]{1,0:T(8,128)(2,1)} %get-tuple-element.188.refs_0_, bf16[320,2048]{1,0:T(8,128)(2,1)} %get-tuple-element.176.refs_1_, bf16[320,2048]{1,0:T(8,128)(2,1)} %get-tuple-element.172.refs_2_, bf16[320,2048]{1,0:T(8,128)(2,1)} %get-tuple-element.166.refs_3_, ...), custom_call_target="tpu_custom_call" | custom-call | flops 17000000 | bytes 1 | tf_op jit(solution)/shard_map/weight_grad/pallas_call | solution.py:479
  287.1 26.2 %ffn_back.2 = (bf16[960,2048]{1,0:T(8,128)(2,1)}, f32[1,2048]{1,0:T(1,128)S(1)}, bf16[320,2048]{1,0:T(8,128)(2,1)}, bf16[320,2048]{1,0:T(8,128)(2,1)}, bf16[320,2048]{1,0:T(8,128)(2,1)}) custom-call(bf16[160,2048]{1,0:T(8,128)(2,1)S(1)} %collective-permute-done.24.refs_4_.refs_0_, bf16[160,2048]{1,0:T(8,128)(2,1)} %copy-done.16, ...), custom_call_target="tpu_custom_call" | custom-call | flops 30000000 | bytes 1 | tf_op jit(solution)/shard_map/ffn_back/pallas_call | solution.py:401
  313.8 1.4 collective-permute-start.27
  315.2 1.7 collective-permute-start.28
  316.9 12.4 %ffn_back.3 = (bf16[320,2048]{1,0:T(8,128)(2,1)}, f32[1,2048]{1,0:T(1,128)S(1)}, bf16[320,2048]{1,0:T(8,128)(2,1)}) custom-call(bf16[320,2048]{1,0:T(8,128)(2,1)} %refs_5_.1, bf16[320,2048]{1,0:T(8,128)(2,1)} %get-tuple-element.186.refs_1_, bf16[8,4,64,2048]{3,2,1,0:T(8,128)(2,1)} %bitcast.63, ...), custom_call_target="tpu_custom_call" | custom-call | flops 10000000 | bytes 1 | tf_op jit(solution)/shard_map/ffn_back/pallas_call | solution.py:401
  329.4 17.4 %weight_grad.3 = bf16[2048,2048]{1,0:T(8,128)(2,1)} custom-call(bf16[160,2048]{1,0:T(8,128)(2,1)S(1)} %collective-permute-done.22.refs_0_, bf16[160,2048]{1,0:T(8,128)(2,1)} %copy-done.19, bf16[160,2048]{1,0:T(8,128)(2,1)} %copy-done.15, bf16[160,2048]{1,0:T(8,128)(2,1)} %collective-permute-done.21.refs_3_, bf16[160,2048]{1,0:T(8,128)(2,1)} %copy-done, ...), custom_call_target="tpu_custom_call" | custom-call | flops 17000000 | bytes 1 | tf_op jit(solution)/shard_map/weight_grad/pallas_call | solution.py:479
  346.8 19.1 %ffn_out.1 = (bf16[160,2048]{1,0:T(8,128)(2,1)S(1)}, bf16[160,2048]{1,0:T(8,128)(2,1)}, bf16[160,2048]{1,0:T(8,128)(2,1)}, bf16[160,2048]{1,0:T(8,128)(2,1)}, bf...) custom-call(bf16[320,2048]{1,0:T(8,128)(2,1)} %get-tuple-element.188, ...), custom_call_target="tpu_custom_call" | custom-call | flops 18000000 | bytes 1 | tf_op jit(solution)/shard_map/ffn_out/pallas_call | solution.py:445
  366.3 7.0 %middle_back.1 = (f32[320,2048]{1,0:T(8,128)}, bf16[160,2048]{1,0:T(8,128)(2,1)S(1)}, bf16[160,2048]{1,0:T(8,128)(2,1)}, f32[4,2048]{1,0:T(4,128)S(1)}) custom-call(bf16[320,2048]{1,0:T(8,128)(2,1)} %get-tuple-element.201.refs_0_, bf16[320,2048]{1,0:T(8,128)(2,1)} %collective-permute-done.26.refs_1_, bf16[320,2048]{1,0:T(8,128)(2,1)} %collective-permute-done.27.refs_2_, ...), custom_call_target="tpu_custom_call" | custom-call | flops 5000000 | bytes 1 | tf_op jit(solution)/shard_map/middle_back/pallas_call | solution.py:636
  374.1 1.6 collective-permute-start.29
  377.6 14.3 %attn_backward.3 = (bf16[384,1536]{1,0:T(8,128)(2,1)}, f32[1,1536]{1,0:T(1,128)S(1)}, bf16[384,2048]{1,0:T(8,128)(2,1)}) custom-call(bf16[160,2048]{1,0:T(8,128)(2,1)} %copy-done.1, bf16[160,2048]{1,0:T(8,128)(2,1)} %get-tuple-element.207.refs_1_.refs_13_, bf16[384,1536]{1,0:T(8,128)(2,1)} %get-tuple-element.208.refs_2_, ...), custom_call_target="tpu_custom_call" | custom-call | flops 12000000 | bytes 1 | tf_op jit(solution)/shard_map/attn_backward/pallas_call | solution.py:294
  391.9 10.0 %collective-permute-done.32.refs_3_.refs_17_ = bf16[160,2048]{1,0:T(8,128)(2,1)} collective-permute-done((bf16[160,2048]{1,0:T(8,128)(2,1)}, bf16[160,2048]{1,0:T(8,128)(2,1)}, u32[]{:S(2)}, u32[]{:S(2)}) %collective-permute-start.32) | collective-permute-done | bytes 655392 | tf_op jit(solution)/shard_map/ppermute | solution.py:736
  401.9 2.0 collective-permute-start.35
  404.0 2.0 collective-permute-start.38
  406.2 23.9 %attn_backward.4 = (bf16[384,1536]{1,0:T(8,128)(2,1)}, f32[1,1536]{1,0:T(1,128)S(1)}, bf16[384,2048]{1,0:T(8,128)(2,1)}, bf16[384,1536]{1,0:T(8,128)(2,1)}, f32[...) custom-call(bf16[160,2048]{1,0:T(8,128)(2,1)} %collective-permute-done.29.refs_0_.refs_14_, ...), custom_call_target="tpu_custom_call" | custom-call | flops 24000000 | bytes 1 | tf_op jit(solution)/shard_map/attn_backward/pallas_call | solution.py:294
  430.2 2.0 collective-permute-start.34
  433.2 14.5 %attn_backward.5 = (bf16[384,1536]{1,0:T(8,128)(2,1)}, f32[1,1536]{1,0:T(1,128)S(1)}, bf16[384,2048]{1,0:T(8,128)(2,1)}) custom-call(bf16[160,2048]{1,0:T(8,128)(2,1)} %copy-done.17, bf16[160,2048]{1,0:T(8,128)(2,1)} %copy-done.18, bf16[384,1536]{1,0:T(8,128)(2,1)} %get-tuple-element.226.refs_2_, f32[320,128]{1,0:T(8,128)S(1)} %get-tuple-element.149.refs_3_, ...), custom_call_target="tpu_custom_call" | custom-call | flops 12000000 | bytes 1 | tf_op jit(solution)/shard_map/attn_backward/pallas_call | solution.py:294
  447.7 1.6 collective-permute-start.39
  449.9 1.3 collective-permute-start.41
  451.3 20.7 %attn_weight_grad.1 = bf16[2048,2048]{1,0:T(8,128)(2,1)} custom-call(bf16[384,2048]{1,0:T(8,128)(2,1)} %get-tuple-element.228.refs_0_, bf16[384,2048]{1,0:T(8,128)(2,1)} %get-tuple-element.229.refs_1_, bf16[384,2048]{1,0:T(8,128)(2,1)} %get-tuple-element.230.refs_2_, bf16[384,2048]{1,0:T(8,128)(2,1)} %get-tuple-element.231.refs_3_, ...), custom_call_target="tpu_custom_call" | custom-call | flops 21000000 | bytes 1 | tf_op jit(solution)/shard_map/attn_weight_grad/pallas_call | solution.py:521
  472.1 34.3 %collective-permute-done.40 = bf16[160,2048]{1,0:T(8,128)(2,1)S(1)} collective-permute-done((bf16[160,2048]{1,0:T(8,128)(2,1)}, bf16[160,2048]{1,0:T(8,128)(2,1)S(1)}, u32[]{:S(2)}, u32[]{:S(2)}) %collective-permute-start.40) | collective-permute-done | bytes 655392 | tf_op jit(solution)/shard_map/ppermute | solution.py:736
  506.4 8.9 %first_back.1 = (f32[320,2048]{1,0:T(8,128)}, bf16[64,2048]{1,0:T(8,128)(2,1)S(1)}, f32[2,2048]{1,0:T(2,128)S(1)}) custom-call(bf16[384,2048]{1,0:T(8,128)(2,1)} %get-tuple-element.242.refs_0_, bf16[384,2048]{1,0:T(8,128)(2,1)} %collective-permute-done.33.refs_1_, bf16[384,2048]{1,0:T(8,128)(2,1)} %collective-permute-done.34.refs_2_, ...), custom_call_target="tpu_custom_call" | custom-call | flops 499999997952 | bytes 1 | tf_op jit(solution)/shard_map/first_back/pallas_call | solution.py:685
  517.0 3.1 all-to-all-start.2
  520.2 1.4 collective-permute-start.44
  521.6 7.5 %all-to-all-done.2 = f32[32,1,768]{2,1,0:T(1,128)S(1)} async-done(((f32[32,1,768]{2,1,0:T(1,128)}), f32[32,1,768]{2,1,0:T(1,128)S(1)}, u32[]{:S(2)}, u32[]{:S(2)}) %all-to-all-start.2) | async-done | bytes 98336 | tf_op jit(solution)/shard_map/all_to_all | solution.py:798
  529.9 3.5 all-to-all-start.4
  533.7 2.0 collective-permute-start.42
  535.9 1.5 collective-permute-start.43
  537.4 1.6 convert_element_type.166
  540.8 21.5 %collective-permute-done.42 = bf16[160,2048]{1,0:T(8,128)(2,1)S(1)} collective-permute-done((bf16[160,2048]{1,0:T(8,128)(2,1)S(1)}, bf16[160,2048]{1,0:T(8,128)(2,1)S(1)}, u32[]{:S(2)}, u32[]{:S(2)}) %collective-permute-start.42) | collective-permute-done | bytes 655392 | tf_op jit(solution)/shard_map/ppermute | solution.py:736
  563.0 1.4 copy-done.9
  564.5 1.6 fusion.1
  566.1 2.1 slice.194
  568.1 3.5 all-to-all-start.3
  571.9 1.5 copy.85
  575.2 7.8 %all-to-all-done.3 = bf16[4,64,1536]{2,1,0:T(8,128)(2,1)S(1)} async-done(((bf16[4,64,1536]{2,1,0:T(8,128)(2,1)}), bf16[4,64,1536]{2,1,0:T(8,128)(2,1)S(1)}, u32[]{:S(2)}, u32[]{:S(2)}) %all-to-all-start.3) | async-done | bytes 786464 | tf_op jit(solution)/shard_map/all_to_all | solution.py:782
  (291 shorter events, 56.6 us)
Async XLA Ops:
  11.0 16.0 %all-to-all-start = ((bf16[4,64,1536]{2,1,0:T(8,128)(2,1)}), bf16[4,64,1536]{2,1,0:T(8,128)(2,1)S(1)}, u32[]{:S(2)}, u32[]{:S(2)}) async-start(bf16[4,64,1536]{2,1,0:T(8,128)(2,1)} %beside_blocks.1), calls=%async_computation | async-start | bytes 1572864 | tf_op jit(solution)/shard_map/all_to_all | solution.py:782
  16.2 100.7 %all-gather.4.cloned.1.call-start = ((), (), s32[]{:S(2)}) async-start(), calls=%async_computation.8 | async-start | bytes 9437184 | tf_op jit(solution)/shard_map/all_gather | solution.py:802
  28.3 187.4 %all-gather.6.cloned.1.call-start = ((), (), s32[]{:S(2)}) async-start(), calls=%async_computation.9 | async-start | bytes 9437184 | tf_op jit(solution)/shard_map/all_gather | solution.py:802
  28.5 3.7 collective-permute-start.1
  30.0 5.9 collective-permute-start
  32.2 3.7 collective-permute-start.2
  36.0 22.8 %copy-start.11 = (bf16[384,2048]{1,0:T(8,128)(2,1)}, bf16[384,2048]{1,0:T(8,128)(2,1)S(1)}, u32[]{:S(2)}) copy-start(bf16[384,2048]{1,0:T(8,128)(2,1)S(1)} %constant_dynamic-update-slice_fusion.refs_0_.refs_4_) | copy-start | bytes 4718596
  55.3 231.8 %all-gather.8.cloned.1.call-start = ((), (), s32[]{:S(2)}) async-start(), calls=%async_computation.10 | async-start | bytes 9437184 | tf_op jit(solution)/shard_map/all_gather | solution.py:802
  56.1 321.3 %reduce-scatter.4.cloned.1.call-start = ((), (), s32[]{:S(2)}) async-start(), calls=%async_computation.11 | async-start | bytes 9437184 | tf_op jit(solution)/shard_map/reduce_scatter | solution.py:806
  56.5 1.2 collective-permute-start.7
  57.8 36.5 %collective-permute-start.4 = (bf16[384,2048]{1,0:T(8,128)(2,1)S(1)}, bf16[384,2048]{1,0:T(8,128)(2,1)S(1)}, u32[]{:S(2)}, u32[]{:S(2)}) collective-permute-start(bf16[384,2048]{1,0:T(8,128)(2,1)S(1)} %constant_dynamic-update-slice_fusion.refs_0_.refs_4_), channel_id=1, source_target_pairs={{0,16},{8,24},{16,0},{24,8},{1,17},{9,25},{17,1},{25,9},{2,18},{10... | collective-permute-start | bytes 4718600 | tf_op jit(solution)/shard_map/ppermute | solution.py:736
  58.8 36.3 %collective-permute-start.3 = (bf16[384,2048]{1,0:T(8,128)(2,1)S(1)}, bf16[384,2048]{1,0:T(8,128)(2,1)}, u32[]{:S(2)}, u32[]{:S(2)}) collective-permute-start(bf16[384,2048]{1,0:T(8,128)(2,1)S(1)} %constant_dynamic-update-slice_fusion.refs_0_.refs_4_), channel_id=1, source_target_pairs={{0,8},{8,0},{16,24},{24,16},{1,9},{9,1},{17,25},{25,17},{2,10},{10... | collective-permute-start | bytes 4718600 | tf_op jit(solution)/shard_map/ppermute | solution.py:736
  59.3 5.7 collective-permute-start.8
  65.1 5.8 collective-permute-start.9
  97.2 19.6 %collective-permute-start.6 = (bf16[192,2048]{1,0:T(8,128)(2,1)S(1)}, bf16[192,2048]{1,0:T(8,128)(2,1)}, u32[]{:S(2)}, u32[]{:S(2)}) collective-permute-start(bf16[192,2048]{1,0:T(8,128)(2,1)S(1)} %slice.134), channel_id=1, source_target_pairs={{0,8},{8,0},{16,24},{24,16},{1,9},{9,1},{17,25},{25,17},{2,10},{10... | collective-permute-start | bytes 2359304 | tf_op jit(solution)/shard_map/ppermute | solution.py:736
  98.0 18.8 %collective-permute-start.5 = (bf16[192,2048]{1,0:T(8,128)(2,1)}, bf16[192,2048]{1,0:T(8,128)(2,1)S(1)}, u32[]{:S(2)}, u32[]{:S(2)}) collective-permute-start(bf16[192,2048]{1,0:T(8,128)(2,1)} %slice.133), channel_id=1, source_target_pairs={{0,16},{8,24},{16,0},{24,8},{1,17},{9,25},{17,1},{25,9},{2,18},{10... | collective-permute-start | bytes 2359304 | tf_op jit(solution)/shard_map/ppermute | solution.py:736
  133.6 29.3 %collective-permute-start.11 = (bf16[160,2048]{1,0:T(8,128)(2,1)}, bf16[160,2048]{1,0:T(8,128)(2,1)S(1)}, u32[]{:S(2)}, u32[]{:S(2)}) collective-permute-start(bf16[160,2048]{1,0:T(8,128)(2,1)} %get-tuple-element.153), channel_id=1, source_target_pairs={{0,16},{8,24},{16,0},{24,8},{1,17},{9,25},{17,1},{25,9},{2,18},{10... | collective-permute-start | bytes 1966088 | tf_op jit(solution)/shard_map/ppermute | solution.py:736
  133.9 45.6 %collective-permute-start.17 = (bf16[320,2048]{1,0:T(8,128)(2,1)S(1)}, bf16[320,2048]{1,0:T(8,128)(2,1)S(1)}, u32[]{:S(2)}, u32[]{:S(2)}) collective-permute-start(bf16[320,2048]{1,0:T(8,128)(2,1)S(1)} %copy-done.8), channel_id=1, source_target_pairs={{0,16},{8,24},{16,0},{24,8},{1,17},{9,25},{17,1},{25,9},{2,18},{10... | collective-permute-start | bytes 3932168 | tf_op jit(solution)/shard_map/ppermute | solution.py:736
  135.6 30.2 %collective-permute-start.13 = (bf16[160,2048]{1,0:T(8,128)(2,1)}, bf16[160,2048]{1,0:T(8,128)(2,1)S(1)}, u32[]{:S(2)}, u32[]{:S(2)}) collective-permute-start(bf16[160,2048]{1,0:T(8,128)(2,1)} %get-tuple-element.155), channel_id=1, source_target_pairs={{0,8},{8,0},{16,24},{24,16},{1,9},{9,1},{17,25},{25,17},{2,10},{10... | collective-permute-start | bytes 1966088 | tf_op jit(solution)/shard_map/ppermute | solution.py:736
  136.3 46.6 %collective-permute-start.16 = (bf16[320,2048]{1,0:T(8,128)(2,1)S(1)}, bf16[320,2048]{1,0:T(8,128)(2,1)}, u32[]{:S(2)}, u32[]{:S(2)}) collective-permute-start(bf16[320,2048]{1,0:T(8,128)(2,1)S(1)} %copy-done.8), channel_id=1, source_target_pairs={{0,8},{8,0},{16,24},{24,16},{1,9},{9,1},{17,25},{25,17},{2,10},{10... | collective-permute-start | bytes 3932168 | tf_op jit(solution)/shard_map/ppermute | solution.py:736
  162.2 36.4 %collective-permute-start.10 = (bf16[160,2048]{1,0:T(8,128)(2,1)}, bf16[160,2048]{1,0:T(8,128)(2,1)S(1)}, u32[]{:S(2)}, u32[]{:S(2)}) collective-permute-start(bf16[160,2048]{1,0:T(8,128)(2,1)} %get-tuple-element.151), channel_id=1, source_target_pairs={{0,8},{8,0},{16,24},{24,16},{1,9},{9,1},{17,25},{25,17},{2,10},{10... | collective-permute-start | bytes 1966088 | tf_op jit(solution)/shard_map/ppermute | solution.py:736
  162.9 35.7 %collective-permute-start.15 = (bf16[160,2048]{1,0:T(8,128)(2,1)}, bf16[160,2048]{1,0:T(8,128)(2,1)}, u32[]{:S(2)}, u32[]{:S(2)}) collective-permute-start(bf16[160,2048]{1,0:T(8,128)(2,1)} %get-tuple-element.156), channel_id=1, source_target_pairs={{0,16},{8,24},{16,0},{24,8},{1,17},{9,25},{17,1},{25,9},{2,18},{10... | collective-permute-start | bytes 1966088 | tf_op jit(solution)/shard_map/ppermute | solution.py:736
  165.8 39.9 %collective-permute-start.12 = (bf16[160,2048]{1,0:T(8,128)(2,1)}, bf16[160,2048]{1,0:T(8,128)(2,1)}, u32[]{:S(2)}, u32[]{:S(2)}) collective-permute-start(bf16[160,2048]{1,0:T(8,128)(2,1)} %add_convert_fusion.3), channel_id=1, source_target_pairs={{0,8},{8,0},{16,24},{24,16},{1,9},{9,1},{17,25},{25,17},{2,10},{10... | collective-permute-start | bytes 1966088 | tf_op jit(solution)/shard_map/ppermute | solution.py:736
  179.5 26.1 %collective-permute-start.14 = (bf16[160,2048]{1,0:T(8,128)(2,1)}, bf16[160,2048]{1,0:T(8,128)(2,1)}, u32[]{:S(2)}, u32[]{:S(2)}) collective-permute-start(bf16[160,2048]{1,0:T(8,128)(2,1)} %add_convert_fusion.2), channel_id=1, source_target_pairs={{0,16},{8,24},{16,0},{24,8},{1,17},{9,25},{17,1},{25,9},{2,18},{10... | collective-permute-start | bytes 1966088 | tf_op jit(solution)/shard_map/ppermute | solution.py:736
  211.4 17.7 %collective-permute-start.20 = (bf16[160,2048]{1,0:T(8,128)(2,1)S(1)}, bf16[160,2048]{1,0:T(8,128)(2,1)S(1)}, u32[]{:S(2)}, u32[]{:S(2)}) collective-permute-start(bf16[160,2048]{1,0:T(8,128)(2,1)S(1)} %get-tuple-element.164.refs_0_.refs_6_), channel_id=1, source_target_pairs={{0,16},{8,24},{16,0},{24,8},{1,17},{9,25},{17,1},{25,9},{2,18},{10... | collective-permute-start | bytes 1966088 | tf_op jit(solution)/shard_map/ppermute | solution.py:736
  211.8 17.7 %collective-permute-start.18 = (bf16[160,2048]{1,0:T(8,128)(2,1)S(1)}, bf16[160,2048]{1,0:T(8,128)(2,1)S(1)}, u32[]{:S(2)}, u32[]{:S(2)}) collective-permute-start(bf16[160,2048]{1,0:T(8,128)(2,1)S(1)} %get-tuple-element.164.refs_0_.refs_6_), channel_id=1, source_target_pairs={{0,8},{8,0},{16,24},{24,16},{1,9},{9,1},{17,25},{25,17},{2,10},{10... | collective-permute-start | bytes 1966088 | tf_op jit(solution)/shard_map/ppermute | solution.py:736
  212.8 27.4 %collective-permute-start.21 = (bf16[160,2048]{1,0:T(8,128)(2,1)}, bf16[160,2048]{1,0:T(8,128)(2,1)}, u32[]{:S(2)}, u32[]{:S(2)}) collective-permute-start(bf16[160,2048]{1,0:T(8,128)(2,1)} %get-tuple-element.165.refs_1_.refs_7_), channel_id=1, source_target_pairs={{0,16},{8,24},{16,0},{24,8},{1,17},{9,25},{17,1},{25,9},{2,18},{10... | collective-permute-start | bytes 1966088 | tf_op jit(solution)/shard_map/ppermute | solution.py:736
  214.2 26.1 %collective-permute-start.19 = (bf16[160,2048]{1,0:T(8,128)(2,1)}, bf16[160,2048]{1,0:T(8,128)(2,1)}, u32[]{:S(2)}, u32[]{:S(2)}) collective-permute-start(bf16[160,2048]{1,0:T(8,128)(2,1)} %get-tuple-element.165.refs_1_.refs_7_), channel_id=1, source_target_pairs={{0,8},{8,0},{16,24},{24,16},{1,9},{9,1},{17,25},{25,17},{2,10},{10... | collective-permute-start | bytes 1966088 | tf_op jit(solution)/shard_map/ppermute | solution.py:736
  229.5 27.0 %copy-start = (bf16[160,2048]{1,0:T(8,128)(2,1)}, bf16[160,2048]{1,0:T(8,128)(2,1)S(1)}, u32[]{:S(2)}) copy-start(bf16[160,2048]{1,0:T(8,128)(2,1)S(1)} %collective-permute-done.18.refs_0_.refs_4_) | copy-start | bytes 1966084
  240.3 18.2 %collective-permute-start.22 = (bf16[160,2048]{1,0:T(8,128)(2,1)S(1)}, bf16[160,2048]{1,0:T(8,128)(2,1)S(1)}, u32[]{:S(2)}, u32[]{:S(2)}) collective-permute-start(bf16[160,2048]{1,0:T(8,128)(2,1)S(1)} %collective-permute-done.18.refs_0_.refs_4_), channel_id=1, source_target_pairs={{0,16},{8,24},{16,0},{24,8},{1,17},{9,25},{17,1},{25,9},{2,18},{10... | collective-permute-start | bytes 1966088 | tf_op jit(solution)/shard_map/ppermute | solution.py:736
  241.8 16.7 %collective-permute-start.23 = (bf16[160,2048]{1,0:T(8,128)(2,1)}, bf16[160,2048]{1,0:T(8,128)(2,1)S(1)}, u32[]{:S(2)}, u32[]{:S(2)}) collective-permute-start(bf16[160,2048]{1,0:T(8,128)(2,1)} %collective-permute-done.21.refs_3_), channel_id=1, source_target_pairs={{0,8},{8,0},{16,24},{24,16},{1,9},{9,1},{17,25},{25,17},{2,10},{10... | collective-permute-start | bytes 1966088 | tf_op jit(solution)/shard_map/ppermute | solution.py:736
  256.5 12.5 %collective-permute-start.24 = (bf16[160,2048]{1,0:T(8,128)(2,1)S(1)}, bf16[160,2048]{1,0:T(8,128)(2,1)S(1)}, u32[]{:S(2)}, u32[]{:S(2)}) collective-permute-start(bf16[160,2048]{1,0:T(8,128)(2,1)S(1)} %copy-done.24), channel_id=1, source_target_pairs={{0,16},{8,24},{16,0},{24,8},{1,17},{9,25},{17,1},{25,9},{2,18},{10... | collective-permute-start | bytes 1966088 | tf_op jit(solution)/shard_map/ppermute | solution.py:736
  257.2 11.8 %collective-permute-start.25 = (bf16[160,2048]{1,0:T(8,128)(2,1)S(1)}, bf16[160,2048]{1,0:T(8,128)(2,1)S(1)}, u32[]{:S(2)}, u32[]{:S(2)}) collective-permute-start(bf16[160,2048]{1,0:T(8,128)(2,1)S(1)} %copy-done.23), channel_id=1, source_target_pairs={{0,8},{8,0},{16,24},{24,16},{1,9},{9,1},{17,25},{25,17},{2,10},{10... | collective-permute-start | bytes 1966088 | tf_op jit(solution)/shard_map/ppermute | solution.py:736
  287.1 185.0 %reduce-scatter.6.cloned.1.call-start = ((), (), s32[]{:S(2)}) async-start(), calls=%async_computation.12 | async-start | bytes 9437184 | tf_op jit(solution)/shard_map/reduce_scatter | solution.py:806
  313.4 52.5 %collective-permute-start.26 = (bf16[320,2048]{1,0:T(8,128)(2,1)}, bf16[320,2048]{1,0:T(8,128)(2,1)}, u32[]{:S(2)}, u32[]{:S(2)}) collective-permute-start(bf16[320,2048]{1,0:T(8,128)(2,1)} %get-tuple-element.196), channel_id=1, source_target_pairs={{0,8},{8,0},{16,24},{24,16},{1,9},{9,1},{17,25},{25,17},{2,10},{10... | collective-permute-start | bytes 3932168 | tf_op jit(solution)/shard_map/ppermute | solution.py:736
  313.8 52.1 %collective-permute-start.27 = (bf16[320,2048]{1,0:T(8,128)(2,1)}, bf16[320,2048]{1,0:T(8,128)(2,1)}, u32[]{:S(2)}, u32[]{:S(2)}) collective-permute-start(bf16[320,2048]{1,0:T(8,128)(2,1)} %get-tuple-element.197), channel_id=1, source_target_pairs={{0,16},{8,24},{16,0},{24,8},{1,17},{9,25},{17,1},{25,9},{2,18},{10... | collective-permute-start | bytes 3932168 | tf_op jit(solution)/shard_map/ppermute | solution.py:736
  315.2 51.0 %collective-permute-start.28 = (bf16[320,2048]{1,0:T(8,128)(2,1)}, bf16[320,2048]{1,0:T(8,128)(2,1)}, u32[]{:S(2)}, u32[]{:S(2)}) collective-permute-start(bf16[320,2048]{1,0:T(8,128)(2,1)} %get-tuple-element.198), channel_id=1, source_target_pairs={{0,24},{8,16},{16,8},{24,0},{1,25},{9,17},{17,9},{25,1},{2,26},{10... | collective-permute-start | bytes 3932168 | tf_op jit(solution)/shard_map/ppermute | solution.py:736
  366.2 199.8 %reduce-scatter.8.cloned.1.call-start = ((), (), s32[]{:S(2)}) async-start(), calls=%async_computation.13 | async-start | bytes 9437184 | tf_op jit(solution)/shard_map/reduce_scatter | solution.py:806
  373.3 18.6 %collective-permute-start.31 = (bf16[160,2048]{1,0:T(8,128)(2,1)S(1)}, bf16[160,2048]{1,0:T(8,128)(2,1)S(1)}, u32[]{:S(2)}, u32[]{:S(2)}) collective-permute-start(bf16[160,2048]{1,0:T(8,128)(2,1)S(1)} %get-tuple-element.206.refs_0_.refs_12_), channel_id=1, source_target_pairs={{0,16},{8,24},{16,0},{24,8},{1,17},{9,25},{17,1},{25,9},{2,18},{10... | collective-permute-start | bytes 1966088 | tf_op jit(solution)/shard_map/ppermute | solution.py:736
  374.1 17.9 %collective-permute-start.29 = (bf16[160,2048]{1,0:T(8,128)(2,1)S(1)}, bf16[160,2048]{1,0:T(8,128)(2,1)}, u32[]{:S(2)}, u32[]{:S(2)}) collective-permute-start(bf16[160,2048]{1,0:T(8,128)(2,1)S(1)} %get-tuple-element.206.refs_0_.refs_12_), channel_id=1, source_target_pairs={{0,8},{8,0},{16,24},{24,16},{1,9},{9,1},{17,25},{25,17},{2,10},{10... | collective-permute-start | bytes 1966088 | tf_op jit(solution)/shard_map/ppermute | solution.py:736
  375.7 26.3 %collective-permute-start.32 = (bf16[160,2048]{1,0:T(8,128)(2,1)}, bf16[160,2048]{1,0:T(8,128)(2,1)}, u32[]{:S(2)}, u32[]{:S(2)}) collective-permute-start(bf16[160,2048]{1,0:T(8,128)(2,1)} %get-tuple-element.207.refs_1_.refs_13_), channel_id=1, source_target_pairs={{0,16},{8,24},{16,0},{24,8},{1,17},{9,25},{17,1},{25,9},{2,18},{10... | collective-permute-start | bytes 1966088 | tf_op jit(solution)/shard_map/ppermute | solution.py:736
  376.4 25.6 %collective-permute-start.30 = (bf16[160,2048]{1,0:T(8,128)(2,1)}, bf16[160,2048]{1,0:T(8,128)(2,1)}, u32[]{:S(2)}, u32[]{:S(2)}) collective-permute-start(bf16[160,2048]{1,0:T(8,128)(2,1)} %get-tuple-element.207.refs_1_.refs_13_), channel_id=1, source_target_pairs={{0,8},{8,0},{16,24},{24,16},{1,9},{9,1},{17,25},{25,17},{2,10},{10... | collective-permute-start | bytes 1966088 | tf_op jit(solution)/shard_map/ppermute | solution.py:736
  377.5 26.4 %copy-start.55 = (bf16[160,2048]{1,0:T(8,128)(2,1)S(1)}, bf16[160,2048]{1,0:T(8,128)(2,1)}, u32[]{:S(2)}) copy-start(bf16[160,2048]{1,0:T(8,128)(2,1)} %get-tuple-element.224) | copy-start | bytes 1966084
  377.5 28.4 %copy-start.43 = (f32[384]{0:T(512)S(1)}, f32[384]{0:T(512)}, u32[]{:S(2)}) copy-start(f32[384]{0:T(512)} %get-tuple-element.370) | copy-start | bytes 4612
  377.6 28.6 %copy-start.42 = (f32[384]{0:T(512)S(1)}, f32[384]{0:T(512)}, u32[]{:S(2)}) copy-start(f32[384]{0:T(512)} %get-tuple-element.371) | copy-start | bytes 4612
  401.9 28.3 %collective-permute-start.35 = (bf16[160,2048]{1,0:T(8,128)(2,1)}, bf16[160,2048]{1,0:T(8,128)(2,1)S(1)}, u32[]{:S(2)}, u32[]{:S(2)}) collective-permute-start(bf16[160,2048]{1,0:T(8,128)(2,1)} %collective-permute-done.29.refs_0_.refs_14_), channel_id=1, source_target_pairs={{0,16},{8,24},{16,0},{24,8},{1,17},{9,25},{17,1},{25,9},{2,18},{10... | collective-permute-start | bytes 1966088 | tf_op jit(solution)/shard_map/ppermute | solution.py:736
  403.9 28.3 %collective-permute-start.36 = (bf16[160,2048]{1,0:T(8,128)(2,1)S(1)}, bf16[160,2048]{1,0:T(8,128)(2,1)S(1)}, u32[]{:S(2)}, u32[]{:S(2)}) collective-permute-start(bf16[160,2048]{1,0:T(8,128)(2,1)S(1)} %get-tuple-element.223), channel_id=1, source_target_pairs={{0,8},{8,0},{16,24},{24,16},{1,9},{9,1},{17,25},{25,17},{2,10},{10... | collective-permute-start | bytes 1966088 | tf_op jit(solution)/shard_map/ppermute | solution.py:736
  403.9 28.3 %collective-permute-start.37 = (bf16[160,2048]{1,0:T(8,128)(2,1)S(1)}, bf16[160,2048]{1,0:T(8,128)(2,1)S(1)}, u32[]{:S(2)}, u32[]{:S(2)}) collective-permute-start(bf16[160,2048]{1,0:T(8,128)(2,1)S(1)} %copy-done.55), channel_id=1, source_target_pairs={{0,16},{8,24},{16,0},{24,8},{1,17},{9,25},{17,1},{25,9},{2,18},{10... | collective-permute-start | bytes 1966088 | tf_op jit(solution)/shard_map/ppermute | solution.py:736
  404.0 28.3 %collective-permute-start.38 = (bf16[160,2048]{1,0:T(8,128)(2,1)}, bf16[160,2048]{1,0:T(8,128)(2,1)S(1)}, u32[]{:S(2)}, u32[]{:S(2)}) collective-permute-start(bf16[160,2048]{1,0:T(8,128)(2,1)} %collective-permute-done.32.refs_3_.refs_17_), channel_id=1, source_target_pairs={{0,8},{8,0},{16,24},{24,16},{1,9},{9,1},{17,25},{25,17},{2,10},{10... | collective-permute-start | bytes 1966088 | tf_op jit(solution)/shard_map/ppermute | solution.py:736
  430.1 76.3 %collective-permute-start.33 = (bf16[384,2048]{1,0:T(8,128)(2,1)}, bf16[384,2048]{1,0:T(8,128)(2,1)}, u32[]{:S(2)}, u32[]{:S(2)}) collective-permute-start(bf16[384,2048]{1,0:T(8,128)(2,1)} %get-tuple-element.220), channel_id=1, source_target_pairs={{0,8},{8,0},{16,24},{24,16},{1,9},{9,1},{17,25},{25,17},{2,10},{10... | collective-permute-start | bytes 4718600 | tf_op jit(solution)/shard_map/ppermute | solution.py:736
  430.2 76.2 %collective-permute-start.34 = (bf16[384,2048]{1,0:T(8,128)(2,1)}, bf16[384,2048]{1,0:T(8,128)(2,1)}, u32[]{:S(2)}, u32[]{:S(2)}) collective-permute-start(bf16[384,2048]{1,0:T(8,128)(2,1)} %get-tuple-element.221), channel_id=1, source_target_pairs={{0,16},{8,24},{16,0},{24,8},{1,17},{9,25},{17,1},{25,9},{2,18},{10... | collective-permute-start | bytes 4718600 | tf_op jit(solution)/shard_map/ppermute | solution.py:736
  447.7 58.7 %collective-permute-start.39 = (bf16[384,2048]{1,0:T(8,128)(2,1)}, bf16[384,2048]{1,0:T(8,128)(2,1)}, u32[]{:S(2)}, u32[]{:S(2)}) collective-permute-start(bf16[384,2048]{1,0:T(8,128)(2,1)} %get-tuple-element.227), channel_id=1, source_target_pairs={{0,24},{8,16},{16,8},{24,0},{1,25},{9,17},{17,9},{25,1},{2,26},{10... | collective-permute-start | bytes 4718600 | tf_op jit(solution)/shard_map/ppermute | solution.py:736
  449.3 57.1 %collective-permute-start.40 = (bf16[160,2048]{1,0:T(8,128)(2,1)}, bf16[160,2048]{1,0:T(8,128)(2,1)S(1)}, u32[]{:S(2)}, u32[]{:S(2)}) collective-permute-start(bf16[160,2048]{1,0:T(8,128)(2,1)} %get-tuple-element.240), channel_id=1, source_target_pairs={{0,8},{8,0},{16,24},{24,16},{1,9},{9,1},{17,25},{25,17},{2,10},{10... | collective-permute-start | bytes 1966088 | tf_op jit(solution)/shard_map/ppermute | solution.py:736
  449.9 56.5 %collective-permute-start.41 = (bf16[160,2048]{1,0:T(8,128)(2,1)S(1)}, bf16[160,2048]{1,0:T(8,128)(2,1)S(1)}, u32[]{:S(2)}, u32[]{:S(2)}) collective-permute-start(bf16[160,2048]{1,0:T(8,128)(2,1)S(1)} %copy-done.54), channel_id=1, source_target_pairs={{0,16},{8,24},{16,0},{24,8},{1,17},{9,25},{17,1},{25,9},{2,18},{10... | collective-permute-start | bytes 1966088 | tf_op jit(solution)/shard_map/ppermute | solution.py:736
  517.0 12.2 %all-to-all-start.2 = ((f32[32,1,768]{2,1,0:T(1,128)}), f32[32,1,768]{2,1,0:T(1,128)S(1)}, u32[]{:S(2)}, u32[]{:S(2)}) async-start(f32[32,1,768]{2,1,0:T(1,128)} %all_to_all.20), calls=%async_computation.3 | async-start | bytes 196608 | tf_op jit(solution)/shard_map/all_to_all | solution.py:798
  520.2 19.4 %collective-permute-start.44 = (bf16[50,2048]{1,0:T(8,128)(2,1)S(1)}, bf16[50,2048]{1,0:T(8,128)(2,1)S(1)}, u32[]{:S(2)}, u32[]{:S(2)}) collective-permute-start(bf16[50,2048]{1,0:T(8,128)(2,1)S(1)} %slice.159), channel_id=1, source_target_pairs={{1,0},{2,1},{3,2},{4,3},{5,4},{6,5},{7,6},{8,7},{9,8},{10,9},{11,1... | collective-permute-start | bytes 614408 | tf_op jit(solution)/shard_map/ppermute | solution.py:1028
  529.9 38.2 %all-to-all-start.4 = ((bf16[4,64,2048]{2,1,0:T(8,128)(2,1)}), bf16[4,64,2048]{2,1,0:T(8,128)(2,1)S(1)}, u32[]{:S(2)}, u32[]{:S(2)}) async-start(bf16[4,64,2048]{2,1,0:T(8,128)(2,1)} %reduce-scatter.6.cloned.1.call-done), calls=%async_computation.7 | async-start | bytes 2097152 | tf_op jit(solution)/shard_map/all_to_all | solution.py:782
  533.7 28.7 %collective-permute-start.42 = (bf16[160,2048]{1,0:T(8,128)(2,1)S(1)}, bf16[160,2048]{1,0:T(8,128)(2,1)S(1)}, u32[]{:S(2)}, u32[]{:S(2)}) collective-permute-start(bf16[160,2048]{1,0:T(8,128)(2,1)S(1)} %add_convert_fusion.1), channel_id=1, source_target_pairs={{0,16},{8,24},{16,0},{24,8},{1,17},{9,25},{17,1},{25,9},{2,18},{10... | collective-permute-start | bytes 1966088 | tf_op jit(solution)/shard_map/ppermute | solution.py:736
  535.9 26.8 %collective-permute-start.43 = (bf16[160,2048]{1,0:T(8,128)(2,1)S(1)}, bf16[160,2048]{1,0:T(8,128)(2,1)S(1)}, u32[]{:S(2)}, u32[]{:S(2)}) collective-permute-start(bf16[160,2048]{1,0:T(8,128)(2,1)S(1)} %add_convert_fusion), channel_id=1, source_target_pairs={{0,8},{8,0},{16,24},{24,16},{1,9},{9,1},{17,25},{25,17},{2,10},{10... | collective-permute-start | bytes 1966088 | tf_op jit(solution)/shard_map/ppermute | solution.py:736
  539.0 23.4 %copy-start.26 = (bf16[160,2048]{1,0:T(8,128)(2,1)S(1)}, bf16[160,2048]{1,0:T(8,128)(2,1)}, u32[]{:S(2)}) copy-start(bf16[160,2048]{1,0:T(8,128)(2,1)} %get-tuple-element.260) | copy-start | bytes 1966084
  539.0 23.4 %copy-start.36 = (bf16[160,2048]{1,0:T(8,128)(2,1)S(1)}, bf16[160,2048]{1,0:T(8,128)(2,1)}, u32[]{:S(2)}) copy-start(bf16[160,2048]{1,0:T(8,128)(2,1)} %copy-done.35) | copy-start | bytes 1966084
  540.8 21.9 %copy-start.25 = (bf16[160,2048]{1,0:T(8,128)(2,1)S(1)}, bf16[160,2048]{1,0:T(8,128)(2,1)}, u32[]{:S(2)}) copy-start(bf16[160,2048]{1,0:T(8,128)(2,1)} %get-tuple-element.262) | copy-start | bytes 1966084
  540.8 21.9 %copy-start.34 = (bf16[160,2048]{1,0:T(8,128)(2,1)S(1)}, bf16[160,2048]{1,0:T(8,128)(2,1)}, u32[]{:S(2)}) copy-start(bf16[160,2048]{1,0:T(8,128)(2,1)} %copy-done.33) | copy-start | bytes 1966084
  568.1 14.8 %all-to-all-start.3 = ((bf16[4,64,1536]{2,1,0:T(8,128)(2,1)}), bf16[4,64,1536]{2,1,0:T(8,128)(2,1)S(1)}, u32[]{:S(2)}, u32[]{:S(2)}) async-start(bf16[4,64,1536]{2,1,0:T(8,128)(2,1)} %slice.194), calls=%async_computation.6 | async-start | bytes 1572864 | tf_op jit(solution)/shard_map/all_to_all | solution.py:782
  (49 other events, 300.7 us)
Sparse Core Ops, SparseCore 0:
  28.4 83.5 all-gather.3
  113.6 80.4 all-gather.5
  195.7 80.5 all-gather.7
  287.2 88.7 reduce-scatter.3
  378.2 87.9 reduce-scatter.5
  472.2 91.8 reduce-scatter.7

commit v9 on v8

--- a/solution.py
+++ b/solution.py
@@ -363,7 +363,7 @@
     count = len(slopes)
     seg, width = slopes[0].shape[0], pieces[0].shape[1]
     columns, members, share, wide = up_w.shape
-    step = 512
+    step = wide // 2
     rows = count * seg
     loads = given + count
 

time: 597 us -> 596 us (level)
  no operation moved by 1% of the time
where the time goes in v9:
time: 596 us; the launch traced here: 592 us
  Pallas kernels  274 us (46%)
  waiting for transfers between devices  171 us (29%)
  starting transfers between devices  64.3 us (11%)
  local copies, waits for them, and re-layouts  34.7 us (6%)
  blocking collectives  18.7 us (3%)
  between operations  15.7 us (3%)
  other arithmetic  14.7 us (2%)
    ppermute x38, waiting for transfers between devices, swap(): return lax.ppermute(value, 'fsdp', [(i, i ^ rel) for i in range(count)])  135 us
    pallas_call x3, Pallas kernels, attn_forward(): pl.pallas_call(kernel, out_shape=shapes, in_specs=[HBM] * given + [VMEM]...  53.3 us
    pallas_call x3, Pallas kernels, attn_backward(): pl.pallas_call(kernel, out_shape=shapes, in_specs=[HBM] * given + [VMEM]...  52.4 us
    ppermute x38, starting transfers between devices, swap(): return lax.ppermute(value, 'fsdp', [(i, i ^ rel) for i in range(count)])  39.9 us
    pallas_call x2, Pallas kernels, ffn_back(): pl.pallas_call(kernel, out_shape=(shape_of(rows, wide), shape_of(1, wide,...  37.8 us
    pallas_call x2, Pallas kernels, weight_grad(): pl.pallas_call(kernel, grid=(tall // rows_each,), out_shape=shape_of(tall...  34.5 us
    pallas_call x3, Pallas kernels, ffn_hidden(): pl.pallas_call(kernel, out_shape=[shape_of(seg, wide)] * (2 * count), in_...  33.1 us
    pallas_call x1, Pallas kernels, attn_weight_grad(): pl.pallas_call(kernel, grid=(width // rows_each,), out_shape=shape_of(wid...  20.8 us
  transfers between devices with their start and end apart: 55, of which 20 were waited for; matrix products, arithmetic and copies ran while one was open for 6% of the time, Pallas kernels for 46%

profile of v9, /device:TPU:0, one launch (start us, length us, event | category | flops | bytes accessed | tf_op | source)
XLA Modules:
  0.0 592.5 jit_solution(1469283295644763618)
XLA Ops:
  11.0 5.2 all-to-all-start
  16.2 10.8 %all-to-all-done = bf16[4,64,1536]{2,1,0:T(8,128)(2,1)S(1)} async-done(((bf16[4,64,1536]{2,1,0:T(8,128)(2,1)}), bf16[4,64,1536]{2,1,0:T(8,128)(2,1)S(1)}, u32[]{:S(2)}, u32[]{:S(2)}) %all-to-all-start) | async-done | bytes 786464 | tf_op jit(solution)/shard_map/all_to_all | solution.py:782
  28.5 1.5 collective-permute-start.1
  32.2 1.5 collective-permute-start.2
  33.9 1.8 reshape.197
  36.6 18.7 %all_to_all.29 = bf16[4,64,2048]{2,1,0:T(8,128)(2,1)} all-to-all(bf16[4,64,2048]{2,1,0:T(8,128)(2,1)S(1)} %copy.71), channel_id=1, replica_groups=mesh['fsdp'=4,'dp'=8] {'fsdp'}, dimensions={0} | all-to-all | bytes 2097152 | tf_op jit(solution)/shard_map/all_to_all | solution.py:782
  59.3 1.6 collective-permute-start.8
  61.0 4.0 collective-permute-done.8
  67.3 3.6 collective-permute-done.9
  73.0 21.3 %collective-permute-done.4.refs_1_ = bf16[384,2048]{1,0:T(8,128)(2,1)S(1)} collective-permute-done((bf16[384,2048]{1,0:T(8,128)(2,1)S(1)}, bf16[384,2048]{1,0:T(8,128)(2,1)S(1)}, u32[]{:S(2)}, u32[]{:S(2)}) %collective-permute-start.4) | collective-permute-done | bytes 1572896 | tf_op jit(solution)/shard_map/ppermute | solution.py:736
  95.1 2.1 slice.133
  104.4 12.4 %collective-permute-done.5.refs_0_ = bf16[192,2048]{1,0:T(8,128)(2,1)S(1)} collective-permute-done((bf16[192,2048]{1,0:T(8,128)(2,1)}, bf16[192,2048]{1,0:T(8,128)(2,1)S(1)}, u32[]{:S(2)}, u32[]{:S(2)}) %collective-permute-start.5) | collective-permute-done | bytes 786464 | tf_op jit(solution)/shard_map/ppermute | solution.py:736
  117.8 15.1 %attn_forward.3 = (bf16[384,2048]{1,0:T(8,128)(2,1)}, bf16[384,1536]{1,0:T(8,128)(2,1)}, f32[320,128]{1,0:T(8,128)S(1)}, bf16[320,512]{1,0:T(8,128)(2,1)S(1)}, b...) custom-call(bf16[192,2048]{1,0:T(8,128)(2,1)} %copy-done.21, bf16[192,2048]{1,0:T(8,128)(2,1)} %collective-permute-done.6.refs_1_, ...), custom_call_target="tpu_custom_call" | custom-call | flops 12000000 | bytes 1 | tf_op jit(solution)/shard_map/attn_forward/pallas_call | solution.py:194
  133.9 1.7 collective-permute-start.17
  136.3 1.3 collective-permute-start.16
  137.6 24.5 %attn_forward.4 = (bf16[384,2048]{1,0:T(8,128)(2,1)}, bf16[384,1536]{1,0:T(8,128)(2,1)}, f32[320,128]{1,0:T(8,128)S(1)}, bf16[320,512]{1,0:T(8,128)(2,1)S(1)}, b...) custom-call(bf16[384,2048]{1,0:T(8,128)(2,1)} %collective-permute-do, ...), custom_call_target="tpu_custom_call" | custom-call | flops 24000000 | bytes 1 | tf_op jit(solution)/shard_map/attn_forward/pallas_call | solution.py:194
  163.6 2.2 add_convert_fusion.3
  167.8 11.7 %collective-permute-done.17.refs_6_.refs_2_ = bf16[320,2048]{1,0:T(8,128)(2,1)S(1)} collective-permute-done((bf16[320,2048]{1,0:T(8,128)(2,1)S(1)}, bf16[320,2048]{1,0:T(8,128)(2,1)S(1)}, u32[]{:S(2)}, u32[]{:S(2)}) %collective-permute-start.17) | collective-permute-done | bytes 1310752 | tf_op jit(solution)/shard_map/ppermute | solution.py:736
  180.8 2.0 slice.184
  182.9 2.0 slice.183
  184.9 13.7 %attn_forward.5 = (bf16[384,2048]{1,0:T(8,128)(2,1)}, bf16[384,1536]{1,0:T(8,128)(2,1)}, f32[320,128]{1,0:T(8,128)S(1)}, bf16[320,512]{1,0:T(8,128)(2,1)S(1)}, b...) custom-call(bf16[384,2048]{1,0:T(8,128)(2,1)} %copy-done.11, f32[1,2048]{1,0:T(1,128)S(1)} %reshape.229.refs_2_.refs_1_.refs_6_, ...), custom_call_target="tpu_custom_call" | custom-call | flops 12000000 | bytes 1 | tf_op jit(solution)/shard_map/attn_forward/pallas_call | solution.py:194
  198.6 7.1 %collective-permute-done.12.refs_1_ = bf16[160,2048]{1,0:T(8,128)(2,1)} collective-permute-done((bf16[160,2048]{1,0:T(8,128)(2,1)}, bf16[160,2048]{1,0:T(8,128)(2,1)}, u32[]{:S(2)}, u32[]{:S(2)}) %collective-permute-start.12) | collective-permute-done | bytes 655392 | tf_op jit(solution)/shard_map/ppermute | solution.py:736
  205.7 5.7 middle_norm.1
  212.9 1.4 collective-permute-start.21
  215.6 9.6 %ffn_hidden.3 = (bf16[320,2048]{1,0:T(8,128)(2,1)}, bf16[320,2048]{1,0:T(8,128)(2,1)}) custom-call(bf16[160,2048]{1,0:T(8,128)(2,1)S(1)} %get-tuple-element.164.refs_0_.refs_6_, bf16[160,2048]{1,0:T(8,128)(2,1)} %get-tuple-element.165.refs_1_.refs_7_, f32[1,2048]{1,0:T(1,128)S(1)} %constant_dynamic-slice_fusion.refs_2_.refs_4_, bf16[8,4,64,2048]{3,2,1,0:T(8,128)(2,1)} %bitcast.59), custom_call_target="tpu_custom_call" | custom-call | flops 6000000 | bytes 1 | tf_op jit(solution)/shard_map/ffn_hidden/pallas_call | solution.py:344
  225.3 3.8 collective-permute-done.20.refs_2_
  229.5 10.8 %collective-permute-done.21.refs_3_ = bf16[160,2048]{1,0:T(8,128)(2,1)} collective-permute-done((bf16[160,2048]{1,0:T(8,128)(2,1)}, bf16[160,2048]{1,0:T(8,128)(2,1)}, u32[]{:S(2)}, u32[]{:S(2)}) %collective-permute-start.21) | collective-permute-done | bytes 655392 | tf_op jit(solution)/shard_map/ppermute | solution.py:736
  240.3 1.5 collective-permute-start.22
  242.6 13.9 %ffn_hidden.4 = (bf16[320,2048]{1,0:T(8,128)(2,1)}, bf16[320,2048]{1,0:T(8,128)(2,1)}, bf16[320,2048]{1,0:T(8,128)(2,1)}, bf16[320,2048]{1,0:T(8,128)(2,1)}) custom-call(bf16[160,2048]{1,0:T(8,128)(2,1)S(1)} %collective-permute-done.18.refs_0_.refs_4_, bf16[160,2048]{1,0:T(8,128)(2,1)} %collective-permute-done.19.refs_1_.refs_5_, ...), custom_call_target="tpu_custom_call" | custom-call | flops 12000000 | bytes 1 | tf_op jit(solution)/shard_map/ffn_hidden/pallas_call | solution.py:344
  259.4 9.6 %ffn_hidden.5 = (bf16[320,2048]{1,0:T(8,128)(2,1)}, bf16[320,2048]{1,0:T(8,128)(2,1)}) custom-call(bf16[160,2048]{1,0:T(8,128)(2,1)S(1)} %collective-permute-done.22.refs_0_, bf16[160,2048]{1,0:T(8,128)(2,1)} %copy-done.19, f32[1,2048]{1,0:T(1,128)S(1)} %constant_dynamic-slice_fusion.refs_2_.refs_4_, bf16[8,4,64,2048]{3,2,1,0:T(8,128)(2,1)} %bitcast.61), custom_call_target="tpu_custom_call" | custom-call | flops 6000000 | bytes 1 | tf_op jit(solution)/shard_map/ffn_hidden/pallas_call | solution.py:344
  269.9 17.2 %weight_grad.2 = bf16[2048,2048]{1,0:T(8,128)(2,1)} custom-call(bf16[320,2048]{1,0:T(8,128)(2,1)} %get-tuple-element.188.refs_0_, bf16[320,2048]{1,0:T(8,128)(2,1)} %get-tuple-element.176.refs_1_, bf16[320,2048]{1,0:T(8,128)(2,1)} %get-tuple-element.172.refs_2_, bf16[320,2048]{1,0:T(8,128)(2,1)} %get-tuple-element.166.refs_3_, ...), custom_call_target="tpu_custom_call" | custom-call | flops 17000000 | bytes 1 | tf_op jit(solution)/shard_map/weight_grad/pallas_call | solution.py:479
  287.2 25.7 %ffn_back.2 = (bf16[960,2048]{1,0:T(8,128)(2,1)}, f32[1,2048]{1,0:T(1,128)S(1)}, bf16[320,2048]{1,0:T(8,128)(2,1)}, bf16[320,2048]{1,0:T(8,128)(2,1)}, bf16[320,2048]{1,0:T(8,128)(2,1)}) custom-call(bf16[160,2048]{1,0:T(8,128)(2,1)S(1)} %collective-permute-done.24.refs_4_.refs_0_, bf16[160,2048]{1,0:T(8,128)(2,1)} %copy-done.16, ...), custom_call_target="tpu_custom_call" | custom-call | flops 30000000 | bytes 1 | tf_op jit(solution)/shard_map/ffn_back/pallas_call | solution.py:401
  313.3 1.3 collective-permute-start.27
  314.6 1.8 collective-permute-start.28
  316.5 12.1 %ffn_back.3 = (bf16[320,2048]{1,0:T(8,128)(2,1)}, f32[1,2048]{1,0:T(1,128)S(1)}, bf16[320,2048]{1,0:T(8,128)(2,1)}) custom-call(bf16[320,2048]{1,0:T(8,128)(2,1)} %refs_5_.1, bf16[320,2048]{1,0:T(8,128)(2,1)} %get-tuple-element.186.refs_1_, bf16[8,4,64,2048]{3,2,1,0:T(8,128)(2,1)} %bitcast.63, ...), custom_call_target="tpu_custom_call" | custom-call | flops 10000000 | bytes 1 | tf_op jit(solution)/shard_map/ffn_back/pallas_call | solution.py:401
  328.5 17.4 %weight_grad.3 = bf16[2048,2048]{1,0:T(8,128)(2,1)} custom-call(bf16[160,2048]{1,0:T(8,128)(2,1)S(1)} %collective-permute-done.22.refs_0_, bf16[160,2048]{1,0:T(8,128)(2,1)} %copy-done.19, bf16[160,2048]{1,0:T(8,128)(2,1)} %copy-done.15, bf16[160,2048]{1,0:T(8,128)(2,1)} %collective-permute-done.21.refs_3_, bf16[160,2048]{1,0:T(8,128)(2,1)} %copy-done, ...), custom_call_target="tpu_custom_call" | custom-call | flops 17000000 | bytes 1 | tf_op jit(solution)/shard_map/weight_grad/pallas_call | solution.py:479
  345.9 19.1 %ffn_out.1 = (bf16[160,2048]{1,0:T(8,128)(2,1)S(1)}, bf16[160,2048]{1,0:T(8,128)(2,1)}, bf16[160,2048]{1,0:T(8,128)(2,1)}, bf16[160,2048]{1,0:T(8,128)(2,1)}, bf...) custom-call(bf16[320,2048]{1,0:T(8,128)(2,1)} %get-tuple-element.188, ...), custom_call_target="tpu_custom_call" | custom-call | flops 18000000 | bytes 1 | tf_op jit(solution)/shard_map/ffn_out/pallas_call | solution.py:445
  365.9 7.0 %middle_back.1 = (f32[320,2048]{1,0:T(8,128)}, bf16[160,2048]{1,0:T(8,128)(2,1)S(1)}, bf16[160,2048]{1,0:T(8,128)(2,1)}, f32[4,2048]{1,0:T(4,128)S(1)}) custom-call(bf16[320,2048]{1,0:T(8,128)(2,1)} %get-tuple-element.201.refs_0_, bf16[320,2048]{1,0:T(8,128)(2,1)} %collective-permute-done.26.refs_1_, bf16[320,2048]{1,0:T(8,128)(2,1)} %collective-permute-done.27.refs_2_, ...), custom_call_target="tpu_custom_call" | custom-call | flops 5000000 | bytes 1 | tf_op jit(solution)/shard_map/middle_back/pallas_call | solution.py:636
  373.6 1.6 collective-permute-start.29
  377.2 14.1 %attn_backward.3 = (bf16[384,1536]{1,0:T(8,128)(2,1)}, f32[1,1536]{1,0:T(1,128)S(1)}, bf16[384,2048]{1,0:T(8,128)(2,1)}) custom-call(bf16[160,2048]{1,0:T(8,128)(2,1)} %copy-done.1, bf16[160,2048]{1,0:T(8,128)(2,1)} %get-tuple-element.207.refs_1_.refs_13_, bf16[384,1536]{1,0:T(8,128)(2,1)} %get-tuple-element.208.refs_2_, ...), custom_call_target="tpu_custom_call" | custom-call | flops 12000000 | bytes 1 | tf_op jit(solution)/shard_map/attn_backward/pallas_call | solution.py:294
  391.3 9.8 %collective-permute-done.32.refs_3_.refs_17_ = bf16[160,2048]{1,0:T(8,128)(2,1)} collective-permute-done((bf16[160,2048]{1,0:T(8,128)(2,1)}, bf16[160,2048]{1,0:T(8,128)(2,1)}, u32[]{:S(2)}, u32[]{:S(2)}) %collective-permute-start.32) | collective-permute-done | bytes 655392 | tf_op jit(solution)/shard_map/ppermute | solution.py:736
  401.1 2.0 collective-permute-start.35
  403.2 2.0 collective-permute-start.38
  405.4 23.8 %attn_backward.4 = (bf16[384,1536]{1,0:T(8,128)(2,1)}, f32[1,1536]{1,0:T(1,128)S(1)}, bf16[384,2048]{1,0:T(8,128)(2,1)}, bf16[384,1536]{1,0:T(8,128)(2,1)}, f32[...) custom-call(bf16[160,2048]{1,0:T(8,128)(2,1)} %collective-permute-done.29.refs_0_.refs_14_, ...), custom_call_target="tpu_custom_call" | custom-call | flops 24000000 | bytes 1 | tf_op jit(solution)/shard_map/attn_backward/pallas_call | solution.py:294
  429.3 2.0 collective-permute-start.34
  432.3 14.6 %attn_backward.5 = (bf16[384,1536]{1,0:T(8,128)(2,1)}, f32[1,1536]{1,0:T(1,128)S(1)}, bf16[384,2048]{1,0:T(8,128)(2,1)}) custom-call(bf16[160,2048]{1,0:T(8,128)(2,1)} %copy-done.17, bf16[160,2048]{1,0:T(8,128)(2,1)} %copy-done.18, bf16[384,1536]{1,0:T(8,128)(2,1)} %get-tuple-element.226.refs_2_, f32[320,128]{1,0:T(8,128)S(1)} %get-tuple-element.149.refs_3_, ...), custom_call_target="tpu_custom_call" | custom-call | flops 12000000 | bytes 1 | tf_op jit(solution)/shard_map/attn_backward/pallas_call | solution.py:294
  446.9 1.6 collective-permute-start.39
  450.4 20.8 %attn_weight_grad.1 = bf16[2048,2048]{1,0:T(8,128)(2,1)} custom-call(bf16[384,2048]{1,0:T(8,128)(2,1)} %get-tuple-element.228.refs_0_, bf16[384,2048]{1,0:T(8,128)(2,1)} %get-tuple-element.229.refs_1_, bf16[384,2048]{1,0:T(8,128)(2,1)} %get-tuple-element.230.refs_2_, bf16[384,2048]{1,0:T(8,128)(2,1)} %get-tuple-element.231.refs_3_, ...), custom_call_target="tpu_custom_call" | custom-call | flops 21000000 | bytes 1 | tf_op jit(solution)/shard_map/attn_weight_grad/pallas_call | solution.py:521
  471.2 34.4 %collective-permute-done.40 = bf16[160,2048]{1,0:T(8,128)(2,1)S(1)} collective-permute-done((bf16[160,2048]{1,0:T(8,128)(2,1)}, bf16[160,2048]{1,0:T(8,128)(2,1)S(1)}, u32[]{:S(2)}, u32[]{:S(2)}) %collective-permute-start.40) | collective-permute-done | bytes 655392 | tf_op jit(solution)/shard_map/ppermute | solution.py:736
  505.7 8.9 %first_back.1 = (f32[320,2048]{1,0:T(8,128)}, bf16[64,2048]{1,0:T(8,128)(2,1)S(1)}, f32[2,2048]{1,0:T(2,128)S(1)}) custom-call(bf16[384,2048]{1,0:T(8,128)(2,1)} %get-tuple-element.242.refs_0_, bf16[384,2048]{1,0:T(8,128)(2,1)} %collective-permute-done.33.refs_1_, bf16[384,2048]{1,0:T(8,128)(2,1)} %collective-permute-done.34.refs_2_, ...), custom_call_target="tpu_custom_call" | custom-call | flops 499999997952 | bytes 1 | tf_op jit(solution)/shard_map/first_back/pallas_call | solution.py:685
  516.3 3.3 all-to-all-start.2
  519.7 1.4 collective-permute-start.44
  521.2 7.5 %all-to-all-done.2 = f32[32,1,768]{2,1,0:T(1,128)S(1)} async-done(((f32[32,1,768]{2,1,0:T(1,128)}), f32[32,1,768]{2,1,0:T(1,128)S(1)}, u32[]{:S(2)}, u32[]{:S(2)}) %all-to-all-start.2) | async-done | bytes 98336 | tf_op jit(solution)/shard_map/all_to_all | solution.py:798
  529.4 3.5 all-to-all-start.4
  533.2 2.0 collective-permute-start.42
  535.4 1.5 collective-permute-start.43
  537.0 1.6 convert_element_type.166
  540.3 21.5 %collective-permute-done.42 = bf16[160,2048]{1,0:T(8,128)(2,1)S(1)} collective-permute-done((bf16[160,2048]{1,0:T(8,128)(2,1)S(1)}, bf16[160,2048]{1,0:T(8,128)(2,1)S(1)}, u32[]{:S(2)}, u32[]{:S(2)}) %collective-permute-start.42) | collective-permute-done | bytes 655392 | tf_op jit(solution)/shard_map/ppermute | solution.py:736
  562.5 1.5 copy-done.9
  564.0 1.6 fusion.1
  565.6 2.1 slice.194
  567.7 3.5 all-to-all-start.3
  571.4 1.5 copy.85
  574.7 7.7 %all-to-all-done.3 = bf16[4,64,1536]{2,1,0:T(8,128)(2,1)S(1)} async-done(((bf16[4,64,1536]{2,1,0:T(8,128)(2,1)}), bf16[4,64,1536]{2,1,0:T(8,128)(2,1)S(1)}, u32[]{:S(2)}, u32[]{:S(2)}) %all-to-all-start.3) | async-done | bytes 786464 | tf_op jit(solution)/shard_map/all_to_all | solution.py:782
  (291 shorter events, 57.1 us)
Async XLA Ops:
  11.0 16.0 %all-to-all-start = ((bf16[4,64,1536]{2,1,0:T(8,128)(2,1)}), bf16[4,64,1536]{2,1,0:T(8,128)(2,1)S(1)}, u32[]{:S(2)}, u32[]{:S(2)}) async-start(bf16[4,64,1536]{2,1,0:T(8,128)(2,1)} %beside_blocks.1), calls=%async_computation | async-start | bytes 1572864 | tf_op jit(solution)/shard_map/all_to_all | solution.py:782
  16.2 100.7 %all-gather.4.cloned.1.call-start = ((), (), s32[]{:S(2)}) async-start(), calls=%async_computation.8 | async-start | bytes 9437184 | tf_op jit(solution)/shard_map/all_gather | solution.py:802
  28.3 187.4 %all-gather.6.cloned.1.call-start = ((), (), s32[]{:S(2)}) async-start(), calls=%async_computation.9 | async-start | bytes 9437184 | tf_op jit(solution)/shard_map/all_gather | solution.py:802
  28.5 3.7 collective-permute-start.1
  30.0 5.9 collective-permute-start
  32.2 3.7 collective-permute-start.2
  36.0 22.8 %copy-start.11 = (bf16[384,2048]{1,0:T(8,128)(2,1)}, bf16[384,2048]{1,0:T(8,128)(2,1)S(1)}, u32[]{:S(2)}) copy-start(bf16[384,2048]{1,0:T(8,128)(2,1)S(1)} %constant_dynamic-update-slice_fusion.refs_0_.refs_4_) | copy-start | bytes 4718596
  55.3 231.8 %all-gather.8.cloned.1.call-start = ((), (), s32[]{:S(2)}) async-start(), calls=%async_computation.10 | async-start | bytes 9437184 | tf_op jit(solution)/shard_map/all_gather | solution.py:802
  56.1 320.9 %reduce-scatter.4.cloned.1.call-start = ((), (), s32[]{:S(2)}) async-start(), calls=%async_computation.11 | async-start | bytes 9437184 | tf_op jit(solution)/shard_map/reduce_scatter | solution.py:806
  56.5 1.2 collective-permute-start.7
  57.8 36.5 %collective-permute-start.4 = (bf16[384,2048]{1,0:T(8,128)(2,1)S(1)}, bf16[384,2048]{1,0:T(8,128)(2,1)S(1)}, u32[]{:S(2)}, u32[]{:S(2)}) collective-permute-start(bf16[384,2048]{1,0:T(8,128)(2,1)S(1)} %constant_dynamic-update-slice_fusion.refs_0_.refs_4_), channel_id=1, source_target_pairs={{0,16},{8,24},{16,0},{24,8},{1,17},{9,25},{17,1},{25,9},{2,18},{10... | collective-permute-start | bytes 4718600 | tf_op jit(solution)/shard_map/ppermute | solution.py:736
  58.8 36.3 %collective-permute-start.3 = (bf16[384,2048]{1,0:T(8,128)(2,1)S(1)}, bf16[384,2048]{1,0:T(8,128)(2,1)}, u32[]{:S(2)}, u32[]{:S(2)}) collective-permute-start(bf16[384,2048]{1,0:T(8,128)(2,1)S(1)} %constant_dynamic-update-slice_fusion.refs_0_.refs_4_), channel_id=1, source_target_pairs={{0,8},{8,0},{16,24},{24,16},{1,9},{9,1},{17,25},{25,17},{2,10},{10... | collective-permute-start | bytes 4718600 | tf_op jit(solution)/shard_map/ppermute | solution.py:736
  59.3 5.7 collective-permute-start.8
  65.1 5.8 collective-permute-start.9
  97.2 19.6 %collective-permute-start.6 = (bf16[192,2048]{1,0:T(8,128)(2,1)S(1)}, bf16[192,2048]{1,0:T(8,128)(2,1)}, u32[]{:S(2)}, u32[]{:S(2)}) collective-permute-start(bf16[192,2048]{1,0:T(8,128)(2,1)S(1)} %slice.134), channel_id=1, source_target_pairs={{0,8},{8,0},{16,24},{24,16},{1,9},{9,1},{17,25},{25,17},{2,10},{10... | collective-permute-start | bytes 2359304 | tf_op jit(solution)/shard_map/ppermute | solution.py:736
  98.0 18.8 %collective-permute-start.5 = (bf16[192,2048]{1,0:T(8,128)(2,1)}, bf16[192,2048]{1,0:T(8,128)(2,1)S(1)}, u32[]{:S(2)}, u32[]{:S(2)}) collective-permute-start(bf16[192,2048]{1,0:T(8,128)(2,1)} %slice.133), channel_id=1, source_target_pairs={{0,16},{8,24},{16,0},{24,8},{1,17},{9,25},{17,1},{25,9},{2,18},{10... | collective-permute-start | bytes 2359304 | tf_op jit(solution)/shard_map/ppermute | solution.py:736
  133.5 29.4 %collective-permute-start.11 = (bf16[160,2048]{1,0:T(8,128)(2,1)}, bf16[160,2048]{1,0:T(8,128)(2,1)S(1)}, u32[]{:S(2)}, u32[]{:S(2)}) collective-permute-start(bf16[160,2048]{1,0:T(8,128)(2,1)} %get-tuple-element.153), channel_id=1, source_target_pairs={{0,16},{8,24},{16,0},{24,8},{1,17},{9,25},{17,1},{25,9},{2,18},{10... | collective-permute-start | bytes 1966088 | tf_op jit(solution)/shard_map/ppermute | solution.py:736
  133.9 45.6 %collective-permute-start.17 = (bf16[320,2048]{1,0:T(8,128)(2,1)S(1)}, bf16[320,2048]{1,0:T(8,128)(2,1)S(1)}, u32[]{:S(2)}, u32[]{:S(2)}) collective-permute-start(bf16[320,2048]{1,0:T(8,128)(2,1)S(1)} %copy-done.8), channel_id=1, source_target_pairs={{0,16},{8,24},{16,0},{24,8},{1,17},{9,25},{17,1},{25,9},{2,18},{10... | collective-permute-start | bytes 3932168 | tf_op jit(solution)/shard_map/ppermute | solution.py:736
  135.6 30.2 %collective-permute-start.13 = (bf16[160,2048]{1,0:T(8,128)(2,1)}, bf16[160,2048]{1,0:T(8,128)(2,1)S(1)}, u32[]{:S(2)}, u32[]{:S(2)}) collective-permute-start(bf16[160,2048]{1,0:T(8,128)(2,1)} %get-tuple-element.155), channel_id=1, source_target_pairs={{0,8},{8,0},{16,24},{24,16},{1,9},{9,1},{17,25},{25,17},{2,10},{10... | collective-permute-start | bytes 1966088 | tf_op jit(solution)/shard_map/ppermute | solution.py:736
  136.3 46.6 %collective-permute-start.16 = (bf16[320,2048]{1,0:T(8,128)(2,1)S(1)}, bf16[320,2048]{1,0:T(8,128)(2,1)}, u32[]{:S(2)}, u32[]{:S(2)}) collective-permute-start(bf16[320,2048]{1,0:T(8,128)(2,1)S(1)} %copy-done.8), channel_id=1, source_target_pairs={{0,8},{8,0},{16,24},{24,16},{1,9},{9,1},{17,25},{25,17},{2,10},{10... | collective-permute-start | bytes 3932168 | tf_op jit(solution)/shard_map/ppermute | solution.py:736
  162.2 36.4 %collective-permute-start.10 = (bf16[160,2048]{1,0:T(8,128)(2,1)}, bf16[160,2048]{1,0:T(8,128)(2,1)S(1)}, u32[]{:S(2)}, u32[]{:S(2)}) collective-permute-start(bf16[160,2048]{1,0:T(8,128)(2,1)} %get-tuple-element.151), channel_id=1, source_target_pairs={{0,8},{8,0},{16,24},{24,16},{1,9},{9,1},{17,25},{25,17},{2,10},{10... | collective-permute-start | bytes 1966088 | tf_op jit(solution)/shard_map/ppermute | solution.py:736
  162.9 35.7 %collective-permute-start.15 = (bf16[160,2048]{1,0:T(8,128)(2,1)}, bf16[160,2048]{1,0:T(8,128)(2,1)}, u32[]{:S(2)}, u32[]{:S(2)}) collective-permute-start(bf16[160,2048]{1,0:T(8,128)(2,1)} %get-tuple-element.156), channel_id=1, source_target_pairs={{0,16},{8,24},{16,0},{24,8},{1,17},{9,25},{17,1},{25,9},{2,18},{10... | collective-permute-start | bytes 1966088 | tf_op jit(solution)/shard_map/ppermute | solution.py:736
  165.8 39.9 %collective-permute-start.12 = (bf16[160,2048]{1,0:T(8,128)(2,1)}, bf16[160,2048]{1,0:T(8,128)(2,1)}, u32[]{:S(2)}, u32[]{:S(2)}) collective-permute-start(bf16[160,2048]{1,0:T(8,128)(2,1)} %add_convert_fusion.3), channel_id=1, source_target_pairs={{0,8},{8,0},{16,24},{24,16},{1,9},{9,1},{17,25},{25,17},{2,10},{10... | collective-permute-start | bytes 1966088 | tf_op jit(solution)/shard_map/ppermute | solution.py:736
  179.5 26.2 %collective-permute-start.14 = (bf16[160,2048]{1,0:T(8,128)(2,1)}, bf16[160,2048]{1,0:T(8,128)(2,1)}, u32[]{:S(2)}, u32[]{:S(2)}) collective-permute-start(bf16[160,2048]{1,0:T(8,128)(2,1)} %add_convert_fusion.2), channel_id=1, source_target_pairs={{0,16},{8,24},{16,0},{24,8},{1,17},{9,25},{17,1},{25,9},{2,18},{10... | collective-permute-start | bytes 1966088 | tf_op jit(solution)/shard_map/ppermute | solution.py:736
  211.4 17.7 %collective-permute-start.20 = (bf16[160,2048]{1,0:T(8,128)(2,1)S(1)}, bf16[160,2048]{1,0:T(8,128)(2,1)S(1)}, u32[]{:S(2)}, u32[]{:S(2)}) collective-permute-start(bf16[160,2048]{1,0:T(8,128)(2,1)S(1)} %get-tuple-element.164.refs_0_.refs_6_), channel_id=1, source_target_pairs={{0,16},{8,24},{16,0},{24,8},{1,17},{9,25},{17,1},{25,9},{2,18},{10... | collective-permute-start | bytes 1966088 | tf_op jit(solution)/shard_map/ppermute | solution.py:736
  211.8 17.7 %collective-permute-start.18 = (bf16[160,2048]{1,0:T(8,128)(2,1)S(1)}, bf16[160,2048]{1,0:T(8,128)(2,1)S(1)}, u32[]{:S(2)}, u32[]{:S(2)}) collective-permute-start(bf16[160,2048]{1,0:T(8,128)(2,1)S(1)} %get-tuple-element.164.refs_0_.refs_6_), channel_id=1, source_target_pairs={{0,8},{8,0},{16,24},{24,16},{1,9},{9,1},{17,25},{25,17},{2,10},{10... | collective-permute-start | bytes 1966088 | tf_op jit(solution)/shard_map/ppermute | solution.py:736
  212.9 27.4 %collective-permute-start.21 = (bf16[160,2048]{1,0:T(8,128)(2,1)}, bf16[160,2048]{1,0:T(8,128)(2,1)}, u32[]{:S(2)}, u32[]{:S(2)}) collective-permute-start(bf16[160,2048]{1,0:T(8,128)(2,1)} %get-tuple-element.165.refs_1_.refs_7_), channel_id=1, source_target_pairs={{0,16},{8,24},{16,0},{24,8},{1,17},{9,25},{17,1},{25,9},{2,18},{10... | collective-permute-start | bytes 1966088 | tf_op jit(solution)/shard_map/ppermute | solution.py:736
  214.2 26.1 %collective-permute-start.19 = (bf16[160,2048]{1,0:T(8,128)(2,1)}, bf16[160,2048]{1,0:T(8,128)(2,1)}, u32[]{:S(2)}, u32[]{:S(2)}) collective-permute-start(bf16[160,2048]{1,0:T(8,128)(2,1)} %get-tuple-element.165.refs_1_.refs_7_), channel_id=1, source_target_pairs={{0,8},{8,0},{16,24},{24,16},{1,9},{9,1},{17,25},{25,17},{2,10},{10... | collective-permute-start | bytes 1966088 | tf_op jit(solution)/shard_map/ppermute | solution.py:736
  229.5 26.9 %copy-start = (bf16[160,2048]{1,0:T(8,128)(2,1)}, bf16[160,2048]{1,0:T(8,128)(2,1)S(1)}, u32[]{:S(2)}) copy-start(bf16[160,2048]{1,0:T(8,128)(2,1)S(1)} %collective-permute-done.18.refs_0_.refs_4_) | copy-start | bytes 1966084
  240.3 18.2 %collective-permute-start.22 = (bf16[160,2048]{1,0:T(8,128)(2,1)S(1)}, bf16[160,2048]{1,0:T(8,128)(2,1)S(1)}, u32[]{:S(2)}, u32[]{:S(2)}) collective-permute-start(bf16[160,2048]{1,0:T(8,128)(2,1)S(1)} %collective-permute-done.18.refs_0_.refs_4_), channel_id=1, source_target_pairs={{0,16},{8,24},{16,0},{24,8},{1,17},{9,25},{17,1},{25,9},{2,18},{10... | collective-permute-start | bytes 1966088 | tf_op jit(solution)/shard_map/ppermute | solution.py:736
  241.8 16.7 %collective-permute-start.23 = (bf16[160,2048]{1,0:T(8,128)(2,1)}, bf16[160,2048]{1,0:T(8,128)(2,1)S(1)}, u32[]{:S(2)}, u32[]{:S(2)}) collective-permute-start(bf16[160,2048]{1,0:T(8,128)(2,1)} %collective-permute-done.21.refs_3_), channel_id=1, source_target_pairs={{0,8},{8,0},{16,24},{24,16},{1,9},{9,1},{17,25},{25,17},{2,10},{10... | collective-permute-start | bytes 1966088 | tf_op jit(solution)/shard_map/ppermute | solution.py:736
  256.5 12.6 %collective-permute-start.24 = (bf16[160,2048]{1,0:T(8,128)(2,1)S(1)}, bf16[160,2048]{1,0:T(8,128)(2,1)S(1)}, u32[]{:S(2)}, u32[]{:S(2)}) collective-permute-start(bf16[160,2048]{1,0:T(8,128)(2,1)S(1)} %copy-done.24), channel_id=1, source_target_pairs={{0,16},{8,24},{16,0},{24,8},{1,17},{9,25},{17,1},{25,9},{2,18},{10... | collective-permute-start | bytes 1966088 | tf_op jit(solution)/shard_map/ppermute | solution.py:736
  257.3 11.8 %collective-permute-start.25 = (bf16[160,2048]{1,0:T(8,128)(2,1)S(1)}, bf16[160,2048]{1,0:T(8,128)(2,1)S(1)}, u32[]{:S(2)}, u32[]{:S(2)}) collective-permute-start(bf16[160,2048]{1,0:T(8,128)(2,1)S(1)} %copy-done.23), channel_id=1, source_target_pairs={{0,8},{8,0},{16,24},{24,16},{1,9},{9,1},{17,25},{25,17},{2,10},{10... | collective-permute-start | bytes 1966088 | tf_op jit(solution)/shard_map/ppermute | solution.py:736
  287.1 184.1 %reduce-scatter.6.cloned.1.call-start = ((), (), s32[]{:S(2)}) async-start(), calls=%async_computation.12 | async-start | bytes 9437184 | tf_op jit(solution)/shard_map/reduce_scatter | solution.py:806
  312.9 52.2 %collective-permute-start.26 = (bf16[320,2048]{1,0:T(8,128)(2,1)}, bf16[320,2048]{1,0:T(8,128)(2,1)}, u32[]{:S(2)}, u32[]{:S(2)}) collective-permute-start(bf16[320,2048]{1,0:T(8,128)(2,1)} %get-tuple-element.196), channel_id=1, source_target_pairs={{0,8},{8,0},{16,24},{24,16},{1,9},{9,1},{17,25},{25,17},{2,10},{10... | collective-permute-start | bytes 3932168 | tf_op jit(solution)/shard_map/ppermute | solution.py:736
  313.3 51.8 %collective-permute-start.27 = (bf16[320,2048]{1,0:T(8,128)(2,1)}, bf16[320,2048]{1,0:T(8,128)(2,1)}, u32[]{:S(2)}, u32[]{:S(2)}) collective-permute-start(bf16[320,2048]{1,0:T(8,128)(2,1)} %get-tuple-element.197), channel_id=1, source_target_pairs={{0,16},{8,24},{16,0},{24,8},{1,17},{9,25},{17,1},{25,9},{2,18},{10... | collective-permute-start | bytes 3932168 | tf_op jit(solution)/shard_map/ppermute | solution.py:736
  314.6 51.1 %collective-permute-start.28 = (bf16[320,2048]{1,0:T(8,128)(2,1)}, bf16[320,2048]{1,0:T(8,128)(2,1)}, u32[]{:S(2)}, u32[]{:S(2)}) collective-permute-start(bf16[320,2048]{1,0:T(8,128)(2,1)} %get-tuple-element.198), channel_id=1, source_target_pairs={{0,24},{8,16},{16,8},{24,0},{1,25},{9,17},{17,9},{25,1},{2,26},{10... | collective-permute-start | bytes 3932168 | tf_op jit(solution)/shard_map/ppermute | solution.py:736
  365.8 199.8 %reduce-scatter.8.cloned.1.call-start = ((), (), s32[]{:S(2)}) async-start(), calls=%async_computation.13 | async-start | bytes 9437184 | tf_op jit(solution)/shard_map/reduce_scatter | solution.py:806
  372.9 18.4 %collective-permute-start.31 = (bf16[160,2048]{1,0:T(8,128)(2,1)S(1)}, bf16[160,2048]{1,0:T(8,128)(2,1)S(1)}, u32[]{:S(2)}, u32[]{:S(2)}) collective-permute-start(bf16[160,2048]{1,0:T(8,128)(2,1)S(1)} %get-tuple-element.206.refs_0_.refs_12_), channel_id=1, source_target_pairs={{0,16},{8,24},{16,0},{24,8},{1,17},{9,25},{17,1},{25,9},{2,18},{10... | collective-permute-start | bytes 1966088 | tf_op jit(solution)/shard_map/ppermute | solution.py:736
  373.6 17.8 %collective-permute-start.29 = (bf16[160,2048]{1,0:T(8,128)(2,1)S(1)}, bf16[160,2048]{1,0:T(8,128)(2,1)}, u32[]{:S(2)}, u32[]{:S(2)}) collective-permute-start(bf16[160,2048]{1,0:T(8,128)(2,1)S(1)} %get-tuple-element.206.refs_0_.refs_12_), channel_id=1, source_target_pairs={{0,8},{8,0},{16,24},{24,16},{1,9},{9,1},{17,25},{25,17},{2,10},{10... | collective-permute-start | bytes 1966088 | tf_op jit(solution)/shard_map/ppermute | solution.py:736
  375.2 25.9 %collective-permute-start.32 = (bf16[160,2048]{1,0:T(8,128)(2,1)}, bf16[160,2048]{1,0:T(8,128)(2,1)}, u32[]{:S(2)}, u32[]{:S(2)}) collective-permute-start(bf16[160,2048]{1,0:T(8,128)(2,1)} %get-tuple-element.207.refs_1_.refs_13_), channel_id=1, source_target_pairs={{0,16},{8,24},{16,0},{24,8},{1,17},{9,25},{17,1},{25,9},{2,18},{10... | collective-permute-start | bytes 1966088 | tf_op jit(solution)/shard_map/ppermute | solution.py:736
  375.9 25.2 %collective-permute-start.30 = (bf16[160,2048]{1,0:T(8,128)(2,1)}, bf16[160,2048]{1,0:T(8,128)(2,1)}, u32[]{:S(2)}, u32[]{:S(2)}) collective-permute-start(bf16[160,2048]{1,0:T(8,128)(2,1)} %get-tuple-element.207.refs_1_.refs_13_), channel_id=1, source_target_pairs={{0,8},{8,0},{16,24},{24,16},{1,9},{9,1},{17,25},{25,17},{2,10},{10... | collective-permute-start | bytes 1966088 | tf_op jit(solution)/shard_map/ppermute | solution.py:736
  377.1 26.0 %copy-start.55 = (bf16[160,2048]{1,0:T(8,128)(2,1)S(1)}, bf16[160,2048]{1,0:T(8,128)(2,1)}, u32[]{:S(2)}) copy-start(bf16[160,2048]{1,0:T(8,128)(2,1)} %get-tuple-element.224) | copy-start | bytes 1966084
  377.1 28.0 %copy-start.43 = (f32[384]{0:T(512)S(1)}, f32[384]{0:T(512)}, u32[]{:S(2)}) copy-start(f32[384]{0:T(512)} %get-tuple-element.370) | copy-start | bytes 4612
  377.1 28.1 %copy-start.42 = (f32[384]{0:T(512)S(1)}, f32[384]{0:T(512)}, u32[]{:S(2)}) copy-start(f32[384]{0:T(512)} %get-tuple-element.371) | copy-start | bytes 4612
  401.1 28.2 %collective-permute-start.35 = (bf16[160,2048]{1,0:T(8,128)(2,1)}, bf16[160,2048]{1,0:T(8,128)(2,1)S(1)}, u32[]{:S(2)}, u32[]{:S(2)}) collective-permute-start(bf16[160,2048]{1,0:T(8,128)(2,1)} %collective-permute-done.29.refs_0_.refs_14_), channel_id=1, source_target_pairs={{0,16},{8,24},{16,0},{24,8},{1,17},{9,25},{17,1},{25,9},{2,18},{10... | collective-permute-start | bytes 1966088 | tf_op jit(solution)/shard_map/ppermute | solution.py:736
  403.1 28.3 %collective-permute-start.36 = (bf16[160,2048]{1,0:T(8,128)(2,1)S(1)}, bf16[160,2048]{1,0:T(8,128)(2,1)S(1)}, u32[]{:S(2)}, u32[]{:S(2)}) collective-permute-start(bf16[160,2048]{1,0:T(8,128)(2,1)S(1)} %get-tuple-element.223), channel_id=1, source_target_pairs={{0,8},{8,0},{16,24},{24,16},{1,9},{9,1},{17,25},{25,17},{2,10},{10... | collective-permute-start | bytes 1966088 | tf_op jit(solution)/shard_map/ppermute | solution.py:736
  403.1 28.3 %collective-permute-start.37 = (bf16[160,2048]{1,0:T(8,128)(2,1)S(1)}, bf16[160,2048]{1,0:T(8,128)(2,1)S(1)}, u32[]{:S(2)}, u32[]{:S(2)}) collective-permute-start(bf16[160,2048]{1,0:T(8,128)(2,1)S(1)} %copy-done.55), channel_id=1, source_target_pairs={{0,16},{8,24},{16,0},{24,8},{1,17},{9,25},{17,1},{25,9},{2,18},{10... | collective-permute-start | bytes 1966088 | tf_op jit(solution)/shard_map/ppermute | solution.py:736
  403.2 28.2 %collective-permute-start.38 = (bf16[160,2048]{1,0:T(8,128)(2,1)}, bf16[160,2048]{1,0:T(8,128)(2,1)S(1)}, u32[]{:S(2)}, u32[]{:S(2)}) collective-permute-start(bf16[160,2048]{1,0:T(8,128)(2,1)} %collective-permute-done.32.refs_3_.refs_17_), channel_id=1, source_target_pairs={{0,8},{8,0},{16,24},{24,16},{1,9},{9,1},{17,25},{25,17},{2,10},{10... | collective-permute-start | bytes 1966088 | tf_op jit(solution)/shard_map/ppermute | solution.py:736
  429.2 76.5 %collective-permute-start.33 = (bf16[384,2048]{1,0:T(8,128)(2,1)}, bf16[384,2048]{1,0:T(8,128)(2,1)}, u32[]{:S(2)}, u32[]{:S(2)}) collective-permute-start(bf16[384,2048]{1,0:T(8,128)(2,1)} %get-tuple-element.220), channel_id=1, source_target_pairs={{0,8},{8,0},{16,24},{24,16},{1,9},{9,1},{17,25},{25,17},{2,10},{10... | collective-permute-start | bytes 4718600 | tf_op jit(solution)/shard_map/ppermute | solution.py:736
  429.3 76.4 %collective-permute-start.34 = (bf16[384,2048]{1,0:T(8,128)(2,1)}, bf16[384,2048]{1,0:T(8,128)(2,1)}, u32[]{:S(2)}, u32[]{:S(2)}) collective-permute-start(bf16[384,2048]{1,0:T(8,128)(2,1)} %get-tuple-element.221), channel_id=1, source_target_pairs={{0,16},{8,24},{16,0},{24,8},{1,17},{9,25},{17,1},{25,9},{2,18},{10... | collective-permute-start | bytes 4718600 | tf_op jit(solution)/shard_map/ppermute | solution.py:736
  446.9 58.8 %collective-permute-start.39 = (bf16[384,2048]{1,0:T(8,128)(2,1)}, bf16[384,2048]{1,0:T(8,128)(2,1)}, u32[]{:S(2)}, u32[]{:S(2)}) collective-permute-start(bf16[384,2048]{1,0:T(8,128)(2,1)} %get-tuple-element.227), channel_id=1, source_target_pairs={{0,24},{8,16},{16,8},{24,0},{1,25},{9,17},{17,9},{25,1},{2,26},{10... | collective-permute-start | bytes 4718600 | tf_op jit(solution)/shard_map/ppermute | solution.py:736
  448.5 57.2 %collective-permute-start.40 = (bf16[160,2048]{1,0:T(8,128)(2,1)}, bf16[160,2048]{1,0:T(8,128)(2,1)S(1)}, u32[]{:S(2)}, u32[]{:S(2)}) collective-permute-start(bf16[160,2048]{1,0:T(8,128)(2,1)} %get-tuple-element.240), channel_id=1, source_target_pairs={{0,8},{8,0},{16,24},{24,16},{1,9},{9,1},{17,25},{25,17},{2,10},{10... | collective-permute-start | bytes 1966088 | tf_op jit(solution)/shard_map/ppermute | solution.py:736
  449.2 56.5 %collective-permute-start.41 = (bf16[160,2048]{1,0:T(8,128)(2,1)S(1)}, bf16[160,2048]{1,0:T(8,128)(2,1)S(1)}, u32[]{:S(2)}, u32[]{:S(2)}) collective-permute-start(bf16[160,2048]{1,0:T(8,128)(2,1)S(1)} %copy-done.54), channel_id=1, source_target_pairs={{0,16},{8,24},{16,0},{24,8},{1,17},{9,25},{17,1},{25,9},{2,18},{10... | collective-permute-start | bytes 1966088 | tf_op jit(solution)/shard_map/ppermute | solution.py:736
  516.3 12.4 %all-to-all-start.2 = ((f32[32,1,768]{2,1,0:T(1,128)}), f32[32,1,768]{2,1,0:T(1,128)S(1)}, u32[]{:S(2)}, u32[]{:S(2)}) async-start(f32[32,1,768]{2,1,0:T(1,128)} %all_to_all.20), calls=%async_computation.3 | async-start | bytes 196608 | tf_op jit(solution)/shard_map/all_to_all | solution.py:798
  519.7 19.4 %collective-permute-start.44 = (bf16[50,2048]{1,0:T(8,128)(2,1)S(1)}, bf16[50,2048]{1,0:T(8,128)(2,1)S(1)}, u32[]{:S(2)}, u32[]{:S(2)}) collective-permute-start(bf16[50,2048]{1,0:T(8,128)(2,1)S(1)} %slice.159), channel_id=1, source_target_pairs={{1,0},{2,1},{3,2},{4,3},{5,4},{6,5},{7,6},{8,7},{9,8},{10,9},{11,1... | collective-permute-start | bytes 614408 | tf_op jit(solution)/shard_map/ppermute | solution.py:1028
  529.4 38.3 %all-to-all-start.4 = ((bf16[4,64,2048]{2,1,0:T(8,128)(2,1)}), bf16[4,64,2048]{2,1,0:T(8,128)(2,1)S(1)}, u32[]{:S(2)}, u32[]{:S(2)}) async-start(bf16[4,64,2048]{2,1,0:T(8,128)(2,1)} %reduce-scatter.6.cloned.1.call-done), calls=%async_computation.7 | async-start | bytes 2097152 | tf_op jit(solution)/shard_map/all_to_all | solution.py:782
  533.2 28.7 %collective-permute-start.42 = (bf16[160,2048]{1,0:T(8,128)(2,1)S(1)}, bf16[160,2048]{1,0:T(8,128)(2,1)S(1)}, u32[]{:S(2)}, u32[]{:S(2)}) collective-permute-start(bf16[160,2048]{1,0:T(8,128)(2,1)S(1)} %add_convert_fusion.1), channel_id=1, source_target_pairs={{0,16},{8,24},{16,0},{24,8},{1,17},{9,25},{17,1},{25,9},{2,18},{10... | collective-permute-start | bytes 1966088 | tf_op jit(solution)/shard_map/ppermute | solution.py:736
  535.4 26.8 %collective-permute-start.43 = (bf16[160,2048]{1,0:T(8,128)(2,1)S(1)}, bf16[160,2048]{1,0:T(8,128)(2,1)S(1)}, u32[]{:S(2)}, u32[]{:S(2)}) collective-permute-start(bf16[160,2048]{1,0:T(8,128)(2,1)S(1)} %add_convert_fusion), channel_id=1, source_target_pairs={{0,8},{8,0},{16,24},{24,16},{1,9},{9,1},{17,25},{25,17},{2,10},{10... | collective-permute-start | bytes 1966088 | tf_op jit(solution)/shard_map/ppermute | solution.py:736
  538.5 23.4 %copy-start.26 = (bf16[160,2048]{1,0:T(8,128)(2,1)S(1)}, bf16[160,2048]{1,0:T(8,128)(2,1)}, u32[]{:S(2)}) copy-start(bf16[160,2048]{1,0:T(8,128)(2,1)} %get-tuple-element.260) | copy-start | bytes 1966084
  538.5 23.4 %copy-start.36 = (bf16[160,2048]{1,0:T(8,128)(2,1)S(1)}, bf16[160,2048]{1,0:T(8,128)(2,1)}, u32[]{:S(2)}) copy-start(bf16[160,2048]{1,0:T(8,128)(2,1)} %copy-done.35) | copy-start | bytes 1966084
  540.3 21.9 %copy-start.25 = (bf16[160,2048]{1,0:T(8,128)(2,1)S(1)}, bf16[160,2048]{1,0:T(8,128)(2,1)}, u32[]{:S(2)}) copy-start(bf16[160,2048]{1,0:T(8,128)(2,1)} %get-tuple-element.262) | copy-start | bytes 1966084
  540.3 21.9 %copy-start.34 = (bf16[160,2048]{1,0:T(8,128)(2,1)S(1)}, bf16[160,2048]{1,0:T(8,128)(2,1)}, u32[]{:S(2)}) copy-start(bf16[160,2048]{1,0:T(8,128)(2,1)} %copy-done.33) | copy-start | bytes 1966084
  567.7 14.8 %all-to-all-start.3 = ((bf16[4,64,1536]{2,1,0:T(8,128)(2,1)}), bf16[4,64,1536]{2,1,0:T(8,128)(2,1)S(1)}, u32[]{:S(2)}, u32[]{:S(2)}) async-start(bf16[4,64,1536]{2,1,0:T(8,128)(2,1)} %slice.194), calls=%async_computation.6 | async-start | bytes 1572864 | tf_op jit(solution)/shard_map/all_to_all | solution.py:782
  (49 other events, 300.7 us)
Sparse Core Ops, SparseCore 0:
  28.4 83.5 all-gather.3
  113.6 80.4 all-gather.5
  195.7 80.5 all-gather.7
  287.2 88.8 reduce-scatter.3
  378.2 87.9 reduce-scatter.5
  471.4 91.7 reduce-scatter.7
